TPU v7x, 32 devices: a whole 2x2x4 slice. The times are simulated.
32 devices in a mesh: slab: 4 (over x, core), coil: 8 (over z, y).
Axes of the slice: x: 2, y: 2, z: 4, core: 2. Of those that a mesh axis runs over, the one named last changes fastest.
Arguments:
- prior_image: float32 [256, 128, 128], P(('slab', 'coil')), may hold values from -12 to 12
- coil_maps: bfloat16 [8, 256, 128, 128], P('coil', 'slab'), may hold values from -3 to 3
- kspace: bfloat16 [8, 128, 256, 128], P('coil', 'slab'), may hold values from -6 to 6
- sampling: int32 [128, 256], P('slab'), may hold values 0 or 1
- weight_first: bfloat16 [3, 3, 3, 32, 2], replicated, may hold values from -0.875 to 0.875
- bias_first: float32 [32], replicated, may hold values from -3 to 3
- weight_middle: bfloat16 [3, 3, 3, 32, 32], replicated, may hold values from -0.21875 to 0.21875
- bias_middle: float32 [32], replicated, may hold values from -3 to 3
- weight_last: bfloat16 [3, 3, 3, 2, 32], replicated, may hold values from -0.21875 to 0.21875
- bias_last: float32 [2], replicated, may hold values from -3 to 3
Outputs:
- solution: float32 [256, 128, 128], P(('slab', 'coil'))
- residual: float32 [256, 128, 128], P(('slab', 'coil'))
All inputs are finite; a program needn't handle non-finite values. No bound on the sum of `sampling` on one device may be relied on, other than what follows from the above.
Results may differ from a plain program's by a relative error of at most 0.0018.
Values may be sent and summed in bfloat16 or wider, within the bound.
No kernel may reach another device: no remote copies, remote signals or barrier semaphores. Data moves between devices by JAX's collectives and lax.ppermute only.
A program may use at most 192 MiB of HBM per device.

v0:
```python
import math

import jax
import jax.numpy as jnp
from jax import lax
from jax.sharding import PartitionSpec as P

CG_ITERS = 2


penalty = 0.5
highest = lax.Precision.HIGHEST


def padded_2(cells, sides, width):
    for axis, dim in sides:
        count = lax.axis_size(axis)
        ends = count - 1
        head = lax.slice_in_dim(cells, 0, width, axis=dim)
        tail = lax.slice_in_dim(cells, cells.shape[dim] - width, cells.shape[dim], axis=dim)
        cells = jnp.concatenate(
            [
                lax.ppermute(tail, axis, [(i, (i + 1) % count) for i in range(ends)]),
                cells,
                lax.ppermute(head, axis, [((i + 1) % count, i) for i in range(ends)]),
            ],
            axis=dim,
        )
    return cells


def dft_table(length):
    positions = jnp.arange(length, dtype=jnp.int32)
    phases = positions[:, None] * positions[None, :] % length
    angles = phases.astype(jnp.float32) * (2.0 * math.pi / length)
    return jnp.concatenate([jnp.cos(angles), jnp.sin(angles)], axis=0) / math.sqrt(length)


def combine(stacked, along_axis, inverse):
    length = stacked.shape[along_axis] // 2
    cos_part = lax.slice_in_dim(stacked, 0, length, axis=along_axis)
    sin_part = lax.slice_in_dim(stacked, length, 2 * length, axis=along_axis)
    half_width = stacked.shape[-1] // 2
    if inverse:
        real_part = cos_part[..., :half_width] - sin_part[..., half_width:]
        imag_part = cos_part[..., half_width:] + sin_part[..., :half_width]
    else:
        real_part = cos_part[..., :half_width] + sin_part[..., half_width:]
        imag_part = cos_part[..., half_width:] - sin_part[..., :half_width]
    return jnp.concatenate([real_part, imag_part], axis=-1)


def complex_product(coil_map, volume, conjugate):
    half_width = volume.shape[-1] // 2
    map_real = coil_map[..., :half_width].astype(jnp.float32)
    map_imag = coil_map[..., half_width:].astype(jnp.float32)
    if conjugate:
        map_imag = -map_imag
    field_real = volume[..., :half_width]
    field_imag = volume[..., half_width:]
    return jnp.concatenate(
        [
            map_real * field_real - map_imag * field_imag,
            map_real * field_imag + map_imag * field_real,
        ],
        axis=-1,
    )


def forward_planes(transform, volume):
    stacked = jnp.einsum(
        "kz,yzn->ykn", transform, volume, precision=highest, preferred_element_type=jnp.float32
    )
    return combine(stacked, 1, False)


def inverse_planes(transform, spectrum):
    stacked = jnp.einsum(
        "jk,kyn->yjn", transform, spectrum, precision=highest, preferred_element_type=jnp.float32
    )
    return combine(stacked, 1, True)


def transpose_slab(volume):
    return lax.all_to_all(volume, "slab", split_axis=1, concat_axis=0, tiled=True)


def from_kspace(spectrum, y_table):
    stacked = jnp.einsum(
        "jk,zkn->zjn", y_table, spectrum, precision=highest, preferred_element_type=jnp.float32
    )
    return transpose_slab(combine(stacked, 1, True))


def through_kspace(spectrum_rows, y_table, sampled):
    moved = transpose_slab(spectrum_rows)
    stacked = jnp.einsum(
        "ky,yzn->zkn", y_table, moved, precision=highest, preferred_element_type=jnp.float32
    )
    spectrum = combine(stacked, 1, False) * sampled
    return from_kspace(spectrum, y_table)


def single_total(value):
    return lax.psum(value, ("slab", "coil"))


def convolve_layer(features, weights, offsets, readout):
    row_total = features.shape[0]
    in_channels = features.shape[1]
    span_cells = features.shape[2]
    out_channels = weights.shape[3]
    extended = padded_2(features, ((("slab", "coil"), 0),), 1)
    padded = jnp.pad(extended, ((0, 0), (0, 0), (readout + 1, readout + 1)))
    column = (jnp.arange(padded.shape[2], dtype=jnp.int32) - 1) % readout
    zero_value = jnp.zeros((), padded.dtype)
    sources = (
        jnp.where(column != readout - 1, padded, zero_value),
        padded,
        jnp.where(column != 0, padded, zero_value),
    )
    running = jnp.zeros((row_total, out_channels, span_cells), jnp.float32)
    for row_shift in range(3):
        for plane_shift in range(3):
            pieces = []
            for column_shift in range(3):
                first_cell = plane_shift * readout + column_shift
                pieces.append(
                    lax.slice(
                        sources[column_shift],
                        (row_shift, 0, first_cell),
                        (row_shift + row_total, in_channels, first_cell + span_cells),
                    )
                )
            stacked = jnp.concatenate(pieces, axis=1)
            kernel = jnp.transpose(weights[row_shift, plane_shift], (1, 0, 2)).reshape(
                out_channels, 3 * in_channels
            )
            running = running + jnp.einsum(
                "oc,ycn->yon", kernel, stacked, preferred_element_type=jnp.float32
            )
    return running + offsets[None, :, None]


def body(
    prior_image,
    coil_maps,
    kspace,
    sampling,
    weight_first,
    bias_first,
    weight_middle,
    bias_middle,
    weight_last,
    bias_last,
):
    readout = prior_image.shape[2] // 2
    own_rows = prior_image.shape[0]
    planes = prior_image.shape[1]
    features = (
        jnp.stack([prior_image[..., :readout], prior_image[..., readout:]], axis=1)
        .reshape(own_rows, 2, planes * readout)
        .astype(jnp.bfloat16)
    )
    hidden = jax.nn.relu(convolve_layer(features, weight_first, bias_first, readout)).astype(
        jnp.bfloat16
    )
    hidden = jax.nn.relu(convolve_layer(hidden, weight_middle, bias_middle, readout)).astype(
        jnp.bfloat16
    )
    output = convolve_layer(hidden, weight_last, bias_last, readout).reshape(
        own_rows, 2, planes, readout
    )
    denoised = prior_image + jnp.concatenate([output[:, 0], output[:, 1]], axis=-1)
    z_table = dft_table(planes)
    y_table = dft_table(sampling.shape[1])
    sampled = sampling.astype(jnp.float32)[:, :, None]
    slab_maps = coil_maps[0]
    measured = kspace[0].astype(jnp.float32) * sampled
    data_side = from_kspace(measured, y_table)

    def reduce_coils(image_side):
        return lax.psum_scatter(
            complex_product(slab_maps, inverse_planes(z_table, image_side), True),
            "coil",
            scatter_dimension=0,
            tiled=True,
        )

    right_side = reduce_coils(data_side) + penalty * denoised

    def own_inner(left_side, other_side):
        return jnp.sum(left_side * other_side)

    solution = jnp.zeros_like(right_side)
    residual = right_side
    direction = right_side
    norm_now = single_total(own_inner(residual, residual))
    for iteration in range(CG_ITERS):
        spectrum = forward_planes(
            z_table,
            complex_product(
                slab_maps, lax.all_gather(direction, "coil", axis=0, tiled=True), False
            ),
        )
        image_dir = reduce_coils(through_kspace(spectrum, y_table, sampled)) + penalty * direction
        step_size = norm_now / single_total(own_inner(direction, image_dir))
        solution = solution + step_size * direction
        residual = residual - step_size * image_dir
        if iteration + 1 < CG_ITERS:
            norm_next = single_total(own_inner(residual, residual))
            direction = residual + norm_next / norm_now * direction
            norm_now = norm_next
    return (solution, residual)


def solution(mesh):
    placed = (
        P(("slab", "coil"), None, None),
        P("coil", "slab", None, None),
        P("coil", "slab", None, None),
        P("slab", None),
        P(),
        P(),
        P(),
        P(),
        P(),
        P(),
    )
    return jax.shard_map(
        body,
        mesh=mesh,
        in_specs=placed,
        out_specs=(P(("slab", "coil"), None, None), P(("slab", "coil"), None, None)),
        check_vma=False,
    )
```

profile of v0, /device:TPU:0, one launch (start us, length us, event | category | flops | bytes accessed | tf_op | source)
XLA Modules:
  0.0 1302.3 jit_solution(5200178267232932711)
XLA Ops:
  72.8 13.9 %collective-permute-done.2 = bf16[1,32,8192]{2,1,0:T(8,128)(2,1)S(1)} collective-permute-done((bf16[1,32,8192]{2,1,0:T(8,128)(2,1)S(1)}, bf16[1,32,8192]{2,1,0:T(8,128)(2,1)S(1)}, u32[]{:S(2)}, u32[]{:S(2)}) %collective-permute-start.2) | collective-permute-done | bytes 524320 | tf_op jit(solution)/shard_map/ppermute | solution.py:23
  99.0 22.7 %fusion.390 = (bf16[8,32,8192]{2,1,0:T(8,128)(2,1)}, bf16[8,32,8192]{2,1,0:T(8,128)(2,1)}, bf16[8,32,8192]{2,1,0:T(8,128)(2,1)}, bf16[8,32,8192]{2,1,0:T(8,128)(...) fusion(bf16[10,32,8322]{2,1,0:T(8,128)(2,1)} %copy-done.1), kind=kLoop, calls=%fused_computation.443 | loop fusion | bytes 50331648 | tf_op jit(solution)/shard_map/slice | solution.py:129
  121.6 30.8 %fusion.391 = (bf16[8,32,8192]{2,1,0:T(8,128)(2,1)}, bf16[8,32,8192]{2,1,0:T(8,128)(2,1)}, bf16[8,32,8192]{2,1,0:T(8,128)(2,1)}, bf16[8,32,8192]{2,1,0:T(8,128)(...) fusion(bf16[10,32,8322]{2,1,0:T(8,128)(2,1)} %broadcast_select_, ...), kind=kLoop, calls=%fused_computation.444 | loop fusion | bytes 75497472 | tf_op jit(solution)/shard_map/slice | solution.py:129
  152.5 13.4 %fusion.389 = (bf16[8,32,8192]{2,1,0:T(8,128)(2,1)}, bf16[8,32,8192]{2,1,0:T(8,128)(2,1)}, bf16[8,32,8192]{2,1,0:T(8,128)(2,1)}, bf16[8,32,8192]{2,1,0:T(8,128)(...) fusion(bf16[10,32,8322]{2,1,0:T(8,128)(2,1)S(1)} %bitcast.223), kind=kLoop, calls=%fused_computation.442 | loop fusion | bytes 75497472 | tf_op jit(solution)/shard_map/slice | solution.py:129
  172.7 11.7 fusion.127
  194.1 11.7 fusion.121
  241.8 13.2 %fusion.144 = bf16[8,32,8192]{2,1,0:T(8,128)(2,1)S(1)} fusion(f32[8,8192,32]{1,2,0:T(8,128)} %fusion.54, f32[8,8192,32]{1,2,0:T(8,128)} %fusion.6, f32[8,8192,32]{1,2,0:T(8,128)} %fusion.115, bf16[32,96,1]{1,0,2:T(8,128)(2,1)S(1)} %reshape.147, bf16[8,32,8192]{2,1,0:T(8,128)(2,1)} %get-tuple-element.81, bf16[8,32,8192]{2,1,0:T(8,128)(2,1)} %get-tuple-element.75, ...), kind=kOutput, calls=%fused_computation.132 | convolution fusion | flops 452984832 | bytes 41949312 | tf_op jit(solution)/shard_map/oc,ycn->yon/dot_general | solution.py:139
  298.0 16.2 %fusion.388 = (bf16[8,32,8192]{2,1,0:T(8,128)(2,1)}, bf16[8,32,8192]{2,1,0:T(8,128)(2,1)}, bf16[8,32,8192]{2,1,0:T(8,128)(2,1)}, bf16[8,32,8192]{2,1,0:T(8,128)(...) fusion(bf16[10,32,8322]{2,1,0:T(8,128)(2,1)S(1)} %broadcast_sel, ...), kind=kLoop, calls=%fused_computation.441 | loop fusion | bytes 75497472 | tf_op jit(solution)/shard_map/slice | solution.py:129
  314.1 13.3 %fusion.386 = (bf16[8,32,8192]{2,1,0:T(8,128)(2,1)}, bf16[8,32,8192]{2,1,0:T(8,128)(2,1)}, bf16[8,32,8192]{2,1,0:T(8,128)(2,1)}, bf16[8,32,8192]{2,1,0:T(8,128)(...) fusion(bf16[10,32,8322]{2,1,0:T(8,128)(2,1)S(1)} %get-tuple-ele, ...), kind=kLoop, calls=%fused_computation.439 | loop fusion | bytes 75497472 | tf_op jit(solution)/shard_map/slice | solution.py:129
  333.2 22.3 %fusion.387 = (bf16[8,32,8192]{2,1,0:T(8,128)(2,1)}, bf16[8,32,8192]{2,1,0:T(8,128)(2,1)}, bf16[8,32,8192]{2,1,0:T(8,128)(2,1)}, bf16[8,32,8192]{2,1,0:T(8,128)(...) fusion(bf16[10,32,8322]{2,1,0:T(8,128)(2,1)} %copy-done), kind=kLoop, calls=%fused_computation.440 | loop fusion | bytes 50331648 | tf_op jit(solution)/shard_map/slice | solution.py:129
  419.7 40.6 %reduce-scatter.4.cloned.1.call-done = f32[8,128,128]{1,2,0:T(8,128)} async-done(((f32[64,128,128]{1,2,0:T(8,128)}), f32[8,128,128]{1,2,0:T(8,128)}) %reduce-scatter.4.cloned.1.call-update) | async-done | bytes 524304 | tf_op jit(solution)/shard_map/reduce_scatter | solution.py:183
  463.0 73.4 %all-gather.3.cloned.1.call-done = f32[64,128,128]{2,1,0:T(8,128)} async-done(((f32[8,128,128]{2,1,0:T(8,128)}), f32[64,128,128]{2,1,0:T(8,128)}) %all-gather.3.cloned.1.call-update) | async-done | bytes 4194320 | tf_op jit(solution)/shard_map/all_gather | solution.py:203
  570.2 51.9 %all_to_all.90 = f32[64,128,128]{2,0,1:T(8,128)S(1)} all-to-all(f32[64,128,128]{2,0,1:T(8,128)} %copy.120), channel_id=1, replica_groups=mesh['slab'=4,'coil'=8] {'slab'}, dimensions={1} | all-to-all | bytes 8388608 | tf_op jit(solution)/shard_map/all_to_all | solution.py:85
  624.6 16.0 %fusion.213 = f32[32,512,128]{1,2,0:T(8,128)S(1)} fusion(f32[256,32,128]{2,1,0:T(8,128)S(1)} %bitcast.231, f32[256,256]{1,0:T(8,128)S(1)} %copy-done.10, f32[256,256]{1,0:T(8,128)S(1)} %copy-done.12), kind=kOutput, calls=%fused_computation.211 | convolution fusion | flops 6442713088 | bytes 13107200 | tf_op jit(solution)/shard_map/ky,yzn->zkn/dot_general | solution.py:97
  657.9 51.9 %all_to_all.91 = f32[32,256,128]{2,0,1:T(8,128)S(1)} all-to-all(f32[32,256,128]{2,0,1:T(8,128)} %copy.124), channel_id=1, replica_groups=mesh['slab'=4,'coil'=8] {'slab'}, dimensions={1} | all-to-all | bytes 8388608 | tf_op jit(solution)/shard_map/all_to_all | solution.py:85
  725.0 85.6 %reduce-scatter.6.cloned.1.call-done = f32[8,128,128]{1,2,0:T(8,128)} async-done(((f32[64,128,128]{1,2,0:T(8,128)}), f32[8,128,128]{1,2,0:T(8,128)}) %reduce-scatter.6.cloned.1.call-update) | async-done | bytes 524304 | tf_op jit(solution)/shard_map/reduce_scatter | solution.py:183
  812.4 40.6 %all-reduce.3 = (f32[]{:T(128)}, f32[]{:T(128)}) all-reduce(f32[]{:T(128)} %get-tuple-element.9, f32[]{:T(128)} %get-tuple-element.8), channel_id=1, replica_groups=mesh['slab'=4,'coil'=8] {'slab','coil'}, use_global_device_ids=true, to_apply=%region_2.3 | all-reduce | flops 2 | bytes 16 | tf_op jit(solution)/shard_map/psum | solution.py:105
  856.1 39.2 %psum.30 = f32[]{:T(128)} all-reduce(f32[]{:T(128)} %multiply_reduce_fusion.1), channel_id=1, replica_groups=mesh['slab'=4,'coil'=8] {'slab','coil'}, use_global_device_ids=true, to_apply=%region_7.8 | all-reduce | flops 1 | bytes 8 | tf_op jit(solution)/shard_map/psum | solution.py:105
  900.7 74.5 %all-gather.5.cloned.1.call-done = f32[64,128,128]{2,1,0:T(8,128)} async-done(((f32[8,128,128]{2,1,0:T(8,128)}), f32[64,128,128]{2,1,0:T(8,128)}) %all-gather.5.cloned.1.call-update) | async-done | bytes 4194320 | tf_op jit(solution)/shard_map/all_gather | solution.py:203
  1009.0 51.9 %all_to_all.92 = f32[64,128,128]{2,0,1:T(8,128)S(1)} all-to-all(f32[64,128,128]{2,0,1:T(8,128)} %copy.131), channel_id=1, replica_groups=mesh['slab'=4,'coil'=8] {'slab'}, dimensions={1} | all-to-all | bytes 8388608 | tf_op jit(solution)/shard_map/all_to_all | solution.py:85
  1063.4 16.0 %fusion.216 = f32[32,512,128]{1,2,0:T(8,128)S(1)} fusion(f32[256,32,128]{2,1,0:T(8,128)S(1)} %bitcast.233, f32[256,256]{1,0:T(8,128)S(1)} %copy-done.10, f32[256,256]{1,0:T(8,128)S(1)} %copy-done.12), kind=kOutput, calls=%fused_computation.212 | convolution fusion | flops 6442713088 | bytes 13107200 | tf_op jit(solution)/shard_map/ky,yzn->zkn/dot_general | solution.py:97
  1096.5 51.9 %all_to_all.93 = f32[32,256,128]{2,0,1:T(8,128)S(1)} all-to-all(f32[32,256,128]{2,0,1:T(8,128)} %copy.135), channel_id=1, replica_groups=mesh['slab'=4,'coil'=8] {'slab'}, dimensions={1} | all-to-all | bytes 8388608 | tf_op jit(solution)/shard_map/all_to_all | solution.py:85
  1163.2 85.4 %reduce-scatter.8.cloned.1.call-done = f32[8,128,128]{1,2,0:T(8,128)} async-done(((f32[64,128,128]{1,2,0:T(8,128)}), f32[8,128,128]{1,2,0:T(8,128)}) %reduce-scatter.8.cloned.1.call-update) | async-done | bytes 524304 | tf_op jit(solution)/shard_map/reduce_scatter | solution.py:183
  1250.4 40.5 %psum.31 = f32[]{:T(128)} all-reduce(f32[]{:T(128)} %multiply_reduce_fusion), channel_id=1, replica_groups=mesh['slab'=4,'coil'=8] {'slab','coil'}, use_global_device_ids=true, to_apply=%region_10.11 | all-reduce | flops 1 | bytes 8 | tf_op jit(solution)/shard_map/psum | solution.py:105
  (271 shorter events, 394.5 us)
Async XLA Ops:
  8.9 20.7 %collective-permute-start = (bf16[1,2,8192]{2,1,0:T(2,128)(2,1)S(1)}, bf16[1,2,8192]{2,1,0:T(2,128)(2,1)S(1)}, u32[]{:S(2)}, u32[]{:S(2)}) collective-permute-start(bf16[1,2,8192]{2,1,0:T(2,128)(2,1)S(1)} %get-tuple-element.102), channel_id=1, source_target_pairs={{0,1},{1,2},{2,3},{3,4},{4,5},{5,6},{6,7},{7,8},{8,9},{9,10},{10,1... | collective-permute-start | bytes 98312 | tf_op jit(solution)/shard_map/ppermute | solution.py:23
  13.7 15.8 %collective-permute-start.1 = (bf16[1,2,8192]{2,1,0:T(2,128)(2,1)S(1)}, bf16[1,2,8192]{2,1,0:T(2,128)(2,1)S(1)}, u32[]{:S(2)}, u32[]{:S(2)}) collective-permute-start(bf16[1,2,8192]{2,1,0:T(2,128)(2,1)S(1)} %get-tuple-element.103), channel_id=1, source_target_pairs={{1,0},{2,1},{3,2},{4,3},{5,4},{6,5},{7,6},{8,7},{9,8},{10,9},{11,1... | collective-permute-start | bytes 98312 | tf_op jit(solution)/shard_map/ppermute | solution.py:25
  15.1 71.7 %copy-start.34 = (pred[8322]{0:T(1024)(128)(4,1)}, pred[8322]{0:T(1024)(128)(4,1)S(1)}, u32[]{:S(2)}) copy-start(pred[8322]{0:T(1024)(128)(4,1)S(1)} %broadcast_compare_fusion) | copy-start | bytes 24970
  15.1 78.6 %copy-start.36 = (pred[8322]{0:T(1024)(128)(4,1)}, pred[8322]{0:T(1024)(128)(4,1)S(1)}, u32[]{:S(2)}) copy-start(pred[8322]{0:T(1024)(128)(4,1)S(1)} %broadcast_compare_fusion.1) | copy-start | bytes 24970
  16.2 13.2 %copy-start.9 = (f32[256,256]{1,0:T(8,128)}, f32[256,256]{1,0:T(8,128)S(1)}, u32[]{:S(2)}) copy-start(f32[256,256]{1,0:T(8,128)S(1)} %get-tuple-element.157) | copy-start | bytes 786436
  59.1 27.7 %collective-permute-start.2 = (bf16[1,32,8192]{2,1,0:T(8,128)(2,1)S(1)}, bf16[1,32,8192]{2,1,0:T(8,128)(2,1)S(1)}, u32[]{:S(2)}, u32[]{:S(2)}) collective-permute-start(bf16[1,32,8192]{2,1,0:T(8,128)(2,1)S(1)} %get-tuple-element.96), channel_id=1, source_target_pairs={{0,1},{1,2},{2,3},{3,4},{4,5},{5,6},{6,7},{7,8},{8,9},{9,10},{10,1... | collective-permute-start | bytes 1572872 | tf_op jit(solution)/shard_map/ppermute | solution.py:23
  63.7 23.1 %collective-permute-start.3 = (bf16[1,32,8192]{2,1,0:T(8,128)(2,1)S(1)}, bf16[1,32,8192]{2,1,0:T(8,128)(2,1)S(1)}, u32[]{:S(2)}, u32[]{:S(2)}) collective-permute-start(bf16[1,32,8192]{2,1,0:T(8,128)(2,1)S(1)} %get-tuple-element.97), channel_id=1, source_target_pairs={{1,0},{2,1},{3,2},{4,3},{5,4},{6,5},{7,6},{8,7},{9,8},{10,9},{11,1... | collective-permute-start | bytes 1572872 | tf_op jit(solution)/shard_map/ppermute | solution.py:25
  66.0 20.8 %copy-start.6 = (bf16[8,32,8192]{2,1,0:T(8,128)(2,1)S(1)}, bf16[8,32,8192]{2,1,0:T(8,128)(2,1)}, u32[]{:S(2)}) copy-start(bf16[8,32,8192]{2,1,0:T(8,128)(2,1)} %copy-done.5) | copy-start | bytes 12582916
  99.0 53.5 %slice-start = ((s8[5406720]{0:T(1024)(128)(4,1)}), s8[1212416]{0:T(1024)(128)(4,1)S(1)}, s32[]{:S(2)}) async-start(s8[5406720]{0:T(1024)(128)(4,1)} %bitcast.222), calls=%async_computation.13 | async-start | bytes 2424832
  121.6 30.9 %slice-start.1 = ((s8[5406720]{0:T(1024)(128)(4,1)}), s8[4194304]{0:T(1024)(128)(4,1)S(1)}, s32[]{:S(2)}) async-start(s8[5406720]{0:T(1024)(128)(4,1)} %bitcast.222), calls=%async_computation.14 | async-start | bytes 8388608
  152.5 13.4 %copy-start.7 = (bf16[8,32,8192]{2,1,0:T(8,128)(2,1)S(1)}, bf16[8,32,8192]{2,1,0:T(8,128)(2,1)}, u32[]{:S(2)}) copy-start(bf16[8,32,8192]{2,1,0:T(8,128)(2,1)} %copy-done.5) | copy-start | bytes 12582916
  241.8 22.0 %copy-start.15 = (f32[32,256,64]{1,2,0:T(8,128)S(1)}, f32[32,256,64]{1,2,0:T(8,128)}, u32[]{:S(2)}) copy-start(f32[32,256,64]{1,2,0:T(8,128)} %get-tuple-element.36) | copy-start | bytes 6291460
  241.8 22.0 %copy-start.16 = (f32[32,256,64]{1,2,0:T(8,128)S(1)}, f32[32,256,64]{1,2,0:T(8,128)}, u32[]{:S(2)}) copy-start(f32[32,256,64]{1,2,0:T(8,128)} %get-tuple-element.37) | copy-start | bytes 6291460
  258.1 30.6 %collective-permute-start.4 = (bf16[1,32,8192]{2,1,0:T(8,128)(2,1)}, bf16[1,32,8192]{2,1,0:T(8,128)(2,1)S(1)}, u32[]{:S(2)}, u32[]{:S(2)}) collective-permute-start(bf16[1,32,8192]{2,1,0:T(8,128)(2,1)} %get-tuple-element.94), channel_id=1, source_target_pairs={{0,1},{1,2},{2,3},{3,4},{4,5},{5,6},{6,7},{7,8},{8,9},{9,10},{10,1... | collective-permute-start | bytes 1572872 | tf_op jit(solution)/shard_map/ppermute | solution.py:23
  262.5 26.2 %collective-permute-start.5 = (bf16[1,32,8192]{2,1,0:T(8,128)(2,1)}, bf16[1,32,8192]{2,1,0:T(8,128)(2,1)S(1)}, u32[]{:S(2)}, u32[]{:S(2)}) collective-permute-start(bf16[1,32,8192]{2,1,0:T(8,128)(2,1)} %get-tuple-element.95), channel_id=1, source_target_pairs={{1,0},{2,1},{3,2},{4,3},{5,4},{6,5},{7,6},{8,7},{9,8},{10,9},{11,1... | collective-permute-start | bytes 1572872 | tf_op jit(solution)/shard_map/ppermute | solution.py:25
  271.6 84.0 %all-to-all-start = ((f32[32,256,128]{2,0,1:T(8,128)}), f32[32,256,128]{2,0,1:T(8,128)}, u32[]{:S(2)}, u32[]{:S(2)}) async-start(f32[32,256,128]{2,0,1:T(8,128)} %copy.87), calls=%async_computation | async-start | bytes 8388608 | tf_op jit(solution)/shard_map/all_to_all | solution.py:85
  282.8 177.4 %reduce-scatter.4.cloned.1.call-start = ((), (), s32[]{:S(2)}) async-start(), calls=%async_computation.8 | async-start | bytes 4718592 | tf_op jit(solution)/shard_map/reduce_scatter | solution.py:183
  314.1 13.3 %copy-start.3 = (bf16[8,32,8192]{2,1,0:T(8,128)(2,1)S(1)}, bf16[8,32,8192]{2,1,0:T(8,128)(2,1)}, u32[]{:S(2)}) copy-start(bf16[8,32,8192]{2,1,0:T(8,128)(2,1)} %copy-done.2) | copy-start | bytes 12582916
  372.6 163.7 %all-gather.3.cloned.1.call-start = ((), (), s32[]{:S(2)}) async-start(), calls=%async_computation.9 | async-start | bytes 4718592 | tf_op jit(solution)/shard_map/all_gather | solution.py:203
  462.6 348.0 %reduce-scatter.6.cloned.1.call-start = ((), (), s32[]{:S(2)}) async-start(), calls=%async_computation.10 | async-start | bytes 4718592 | tf_op jit(solution)/shard_map/reduce_scatter | solution.py:183
  725.0 250.3 %all-gather.5.cloned.1.call-start = ((), (), s32[]{:S(2)}) async-start(), calls=%async_computation.11 | async-start | bytes 4718592 | tf_op jit(solution)/shard_map/all_gather | solution.py:203
  900.7 347.9 %reduce-scatter.8.cloned.1.call-start = ((), (), s32[]{:S(2)}) async-start(), calls=%async_computation.12 | async-start | bytes 4718592 | tf_op jit(solution)/shard_map/reduce_scatter | solution.py:183
  1163.2 85.4 %copy-start.14 = (f32[8,128,128]{1,2,0:T(8,128)S(1)}, f32[8,128,128]{1,2,0:T(8,128)}, u32[]{:S(2)}) copy-start(f32[8,128,128]{1,2,0:T(8,128)} %multiply_add_fusion.2) | copy-start | bytes 1572868
  1163.2 129.1 %copy-start.13 = (f32[8,128,128]{1,2,0:T(8,128)S(1)}, f32[8,128,128]{1,2,0:T(8,128)}, u32[]{:S(2)}) copy-start(f32[8,128,128]{1,2,0:T(8,128)} %reduce-scatter.6.cloned.1.call-done) | copy-start | bytes 1572868
  (35 other events, 213.1 us)
Sparse Core Ops, SparseCore 0:
  372.8 87.4 reduce-scatter.3
  463.2 73.1 all-gather.2
  725.1 85.4 reduce-scatter.5
  900.8 74.4 all-gather.4
  1163.4 85.2 reduce-scatter.7
where the time goes:
time: 1310 us; the launch traced here: 1300 us
  waiting for transfers between devices  373 us (28%)
  blocking collectives  328 us (25%)
  matrix products  247 us (19%)
  local copies, waits for them, and re-layouts  234 us (18%)
  other arithmetic  71.1 us (5%)
  starting transfers between devices  29.6 us (2%)
  between operations  19 us (1%)
    reduce_scatter x3, waiting for transfers between devices, reduce_coils(): lax.psum_scatter(complex_product(slab_maps, inverse_planes(z_table, image...  212 us
    all_to_all x4, blocking collectives, transpose_slab(): lax.all_to_all(volume, 'slab', split_axis=1, concat_axis=0, tiled=True)  208 us
    dot_general x27, matrix products, convolve_layer(): jnp.einsum('oc,ycn->yon', kernel, stacked, preferred_element_type=jnp.flo...  150 us
    all_gather x2, waiting for transfers between devices, body(): lax.all_gather(direction, 'coil', axis=0, tiled=True)  148 us
    slice x8, local copies, waits for them, and re-layouts, convolve_layer(): lax.slice(sources[column_shift], (row_shift, 0, first_cell), (row_shift +...  126 us
    psum x3, blocking collectives, single_total(): return lax.psum(value, ('slab', 'coil'))  120 us
    unnamed x105, local copies, waits for them, and re-layouts  40.5 us
    dot_general x2, matrix products, through_kspace(): jnp.einsum('ky,yzn->zkn', y_table, moved, precision=highest, preferred_el...  32.1 us
  transfers between devices with their start and end apart: 12, of which 6 were waited for; matrix products, arithmetic and copies ran while one was open for 11% of the time, Pallas kernels for 0%

commit v1 on v0

v1 whole, which is shorter than its diff:
```python
import functools
import math

import jax
import jax.numpy as jnp
import numpy as np
from jax import lax
from jax.experimental import pallas as pl
from jax.experimental.pallas import tpu as pltpu
from jax.sharding import PartitionSpec as P

CG_ITERS = 2


penalty = 0.5
axes = ("slab", "coil")


def padded_2(cells, sides, width):
    for axis, dim in sides:
        count = lax.axis_size(axis)
        ends = count - 1
        head = lax.slice_in_dim(cells, 0, width, axis=dim)
        tail = lax.slice_in_dim(cells, cells.shape[dim] - width, cells.shape[dim], axis=dim)
        cells = jnp.concatenate(
            [
                lax.ppermute(tail, axis, [(i, (i + 1) % count) for i in range(ends)]),
                cells,
                lax.ppermute(head, axis, [((i + 1) % count, i) for i in range(ends)]),
            ],
            axis=dim,
        )
    return cells


def convolve_layer(features, weights, offsets, readout):
    row_total = features.shape[0]
    in_channels = features.shape[1]
    span_cells = features.shape[2]
    out_channels = weights.shape[3]
    extended = padded_2(features, ((("slab", "coil"), 0),), 1)
    padded = jnp.pad(extended, ((0, 0), (0, 0), (readout + 1, readout + 1)))
    column = (jnp.arange(padded.shape[2], dtype=jnp.int32) - 1) % readout
    zero_value = jnp.zeros((), padded.dtype)
    sources = (
        jnp.where(column != readout - 1, padded, zero_value),
        padded,
        jnp.where(column != 0, padded, zero_value),
    )
    running = jnp.zeros((row_total, out_channels, span_cells), jnp.float32)
    for row_shift in range(3):
        for plane_shift in range(3):
            pieces = []
            for column_shift in range(3):
                first_cell = plane_shift * readout + column_shift
                pieces.append(
                    lax.slice(
                        sources[column_shift],
                        (row_shift, 0, first_cell),
                        (row_shift + row_total, in_channels, first_cell + span_cells),
                    )
                )
            stacked = jnp.concatenate(pieces, axis=1)
            kernel = jnp.transpose(weights[row_shift, plane_shift], (1, 0, 2)).reshape(
                out_channels, 3 * in_channels
            )
            running = running + jnp.einsum(
                "oc,ycn->yon", kernel, stacked, preferred_element_type=jnp.float32
            )
    return running + offsets[None, :, None]


def denoise(
    prior_image, weight_first, bias_first, weight_middle, bias_middle, weight_last, bias_last
):
    readout = prior_image.shape[2] // 2
    own_rows = prior_image.shape[0]
    planes = prior_image.shape[1]
    features = (
        jnp.stack([prior_image[..., :readout], prior_image[..., readout:]], axis=1)
        .reshape(own_rows, 2, planes * readout)
        .astype(jnp.bfloat16)
    )
    hidden = jax.nn.relu(convolve_layer(features, weight_first, bias_first, readout)).astype(
        jnp.bfloat16
    )
    hidden = jax.nn.relu(convolve_layer(hidden, weight_middle, bias_middle, readout)).astype(
        jnp.bfloat16
    )
    output = convolve_layer(hidden, weight_last, bias_last, readout).reshape(
        own_rows, 2, planes, readout
    )
    return prior_image + jnp.concatenate([output[:, 0], output[:, 1]], axis=-1)


def table_parts(table):
    high = table.astype(jnp.bfloat16)
    low = (table - high.astype(np.float64)).astype(jnp.bfloat16)
    return high, low


def dft_parts(length):
    positions = np.arange(length, dtype=np.int64)
    angles = (positions[:, None] * positions[None, :] % length) * (2.0 * math.pi / length)
    scale = 1.0 / math.sqrt(length)
    return np.cos(angles) * scale, np.sin(angles) * scale


def row_table(length):
    cos_part, sin_part = dft_parts(length)
    high, low = table_parts(np.concatenate([cos_part, sin_part], axis=0))
    return np.concatenate([high, low, high], axis=1)


def plane_table(length, inverse):
    cos_part, sin_part = dft_parts(length)
    if inverse:
        sin_part = -sin_part
    table = np.concatenate(
        [
            np.concatenate([cos_part, -sin_part], axis=1),
            np.concatenate([sin_part, cos_part], axis=1),
        ],
        axis=0,
    )
    high, low = table_parts(table)
    return np.concatenate([high, low, high], axis=0)


def value_parts(value):
    high = value.astype(jnp.bfloat16)
    low = (value - high.astype(jnp.float32)).astype(jnp.bfloat16)
    return high, low


def along_planes(value, table):
    high, low = value_parts(value)
    return jnp.dot(
        jnp.concatenate([high, high, low], axis=1), table, preferred_element_type=jnp.float32
    )


def along_rows(table, value):
    high, low = value_parts(value)
    return jnp.dot(
        table, jnp.concatenate([high, high, low], axis=0), preferred_element_type=jnp.float32
    )


def rows_combined(stacked, inverse):
    rows = stacked.shape[0] // 2
    half = stacked.shape[1] // 2
    cos_real, cos_imag = stacked[:rows, :half], stacked[:rows, half:]
    sin_real, sin_imag = stacked[rows:, :half], stacked[rows:, half:]
    if inverse:
        return cos_real - sin_imag, cos_imag + sin_real
    return cos_real + sin_imag, cos_imag - sin_real


def plane_of(ref, part):
    value = ref[:, part, 0]
    return value.reshape(value.shape[0] * value.shape[1], value.shape[2])


def map_of(ref, part):
    value = ref[:, 0, part, 0]
    return value.reshape(value.shape[0] * value.shape[1], value.shape[2]).astype(jnp.float32)


def normal_product(map_real, map_imag, real, imag, mask, rows, planes, inverse_planes):
    half = real.shape[1]
    coil_real = map_real * real - map_imag * imag
    coil_imag = map_real * imag + map_imag * real
    field = along_planes(jnp.concatenate([coil_real, coil_imag], axis=1), planes)
    real, imag = rows_combined(along_rows(rows, field), False)
    spectrum = jnp.concatenate([real * mask, imag * mask], axis=1)
    real, imag = rows_combined(along_rows(rows, spectrum), True)
    field = along_planes(jnp.concatenate([real, imag], axis=1), inverse_planes)
    real, imag = field[:, :half], field[:, half:]
    return map_real * real + map_imag * imag, map_real * imag - map_imag * real


def adjoint_kernel(kspace_ref, maps_ref, mask_ref, rows_ref, inverse_ref, out_ref):
    mask = mask_ref[...]
    parts = []
    for part in range(2):
        parts.append((jnp.transpose(map_of(kspace_ref, part)) * mask).astype(jnp.bfloat16))
    spectrum = jnp.concatenate(parts, axis=1)
    length = spectrum.shape[0]
    stacked = jnp.dot(
        rows_ref[:, : 2 * length],
        jnp.concatenate([spectrum, spectrum], axis=0),
        preferred_element_type=jnp.float32,
    )
    real, imag = rows_combined(stacked, True)
    half = real.shape[1]
    field = along_planes(jnp.concatenate([real, imag], axis=1), inverse_ref[...])
    real, imag = field[:, :half], field[:, half:]
    map_real, map_imag = map_of(maps_ref, 0), map_of(maps_ref, 1)
    shape = out_ref.shape[0], out_ref.shape[3], out_ref.shape[4]
    sums = (map_real * real + map_imag * imag, map_real * imag - map_imag * real)

    @pl.when(pl.program_id(1) == 0)
    def _():
        for part in range(2):
            out_ref[:, part, 0] = sums[part].reshape(shape)

    @pl.when(pl.program_id(1) > 0)
    def _():
        for part in range(2):
            out_ref[:, part, 0] += sums[part].reshape(shape)


def first_kernel(
    maps_ref, adjoint_ref, denoised_ref, mask_ref, rows_ref, planes_ref, inverse_ref, right_ref, out_ref
):
    @pl.when(pl.program_id(1) == 0)
    def _():
        right = adjoint_ref[...] + penalty * denoised_ref[...]
        right_ref[...] = right
        out_ref[...] = jnp.zeros_like(out_ref)

    sums = normal_product(
        map_of(maps_ref, 0),
        map_of(maps_ref, 1),
        plane_of(right_ref, 0),
        plane_of(right_ref, 1),
        mask_ref[...],
        rows_ref[...],
        planes_ref[...],
        inverse_ref[...],
    )
    shape = out_ref.shape[0], out_ref.shape[3], out_ref.shape[4]
    for part in range(2):
        out_ref[:, part, 0] += sums[part].reshape(shape)


def second_kernel(
    maps_ref, right_ref, field_ref, mask_ref, rows_ref, planes_ref, inverse_ref, out_ref, total_ref
):
    x_index = pl.program_id(0)
    x_count = pl.num_programs(0)
    blocks, block_rows, planes = out_ref.shape[0], out_ref.shape[2], out_ref.shape[3]
    shape = blocks, block_rows, planes

    @pl.when(pl.program_id(1) == 0)
    def _():
        for part in range(2):
            out_ref[:, part * x_count + x_index] = jnp.zeros(shape, jnp.float32)

    sums = normal_product(
        map_of(maps_ref, 0),
        map_of(maps_ref, 1),
        plane_of(field_ref, 0),
        plane_of(field_ref, 1),
        mask_ref[...],
        rows_ref[...],
        planes_ref[...],
        inverse_ref[...],
    )
    for part in range(2):
        out_ref[:, part * x_count + x_index] += sums[part].reshape(shape)

    @pl.when(pl.program_id(1) == pl.num_programs(1) - 1)
    def _():
        rights = [right_ref[:, part, 0] for part in range(2)]
        fields = [field_ref[:, part, 0] for part in range(2)]
        images = [out_ref[:, part * x_count + x_index] for part in range(2)]

        def lane_sums(left, other):
            product = left[0] * other[0] + left[1] * other[1]
            return jnp.sum(jnp.sum(product, axis=0), axis=0, keepdims=True)

        totals = jnp.concatenate(
            [
                lane_sums(rights, rights),
                lane_sums(rights, fields),
                lane_sums(fields, fields),
                lane_sums(fields, images),
                jnp.zeros((4, planes), jnp.float32),
            ],
            axis=0,
        )

        @pl.when(x_index == 0)
        def _():
            total_ref[...] = totals

        @pl.when(x_index > 0)
        def _():
            total_ref[...] += totals


def plan_specs(maps, blocks, block_rows, mask):
    slabs, coils, _, x_count, slab_rows, planes = maps.shape
    row_count = slabs * slab_rows
    maps_spec = pl.BlockSpec(
        (slabs, 1, 2, 1, slab_rows, planes), lambda x, c: (0, c, 0, x, 0, 0)
    )
    field_spec = pl.BlockSpec((blocks, 2, 1, block_rows, planes), lambda x, c: (0, 0, x, 0, 0))

    def whole(shape):
        return pl.BlockSpec(shape, lambda x, c: (0,) * len(shape))

    rows = row_table(row_count)
    forward = plane_table(planes, False)
    inverse = plane_table(planes, True)
    return maps_spec, field_spec, whole, rows, forward, inverse


def compute_params():
    return pltpu.CompilerParams(
        dimension_semantics=("arbitrary", "arbitrary"), vmem_limit_bytes=48 * 1024 * 1024
    )


def product_cost(maps, passes):
    slabs, coils, _, x_count, slab_rows, planes = maps.shape
    rows = slabs * slab_rows
    per_plane = 2 * 2 * rows * planes * (2 * rows + 2 * planes)
    return pl.CostEstimate(
        flops=int(coils * x_count * per_plane * passes), bytes_accessed=int(2 * maps.size), transcendentals=0
    )


def adjoint_call(spectra, maps, mask, blocks):
    slabs, coils, _, x_count, slab_planes, row_count = spectra.shape
    planes = slabs * slab_planes
    block_rows = row_count // blocks
    maps_spec, field_spec, whole, rows, _, inverse = plan_specs(maps, blocks, block_rows, mask)
    spectra_spec = pl.BlockSpec(
        (slabs, 1, 2, 1, slab_planes, row_count), lambda x, c: (0, c, 0, x, 0, 0)
    )
    return pl.pallas_call(
        adjoint_kernel,
        grid=(x_count, coils),
        in_specs=[spectra_spec, maps_spec, whole(mask.shape), whole(rows.shape), whole(inverse.shape)],
        out_specs=field_spec,
        out_shape=jax.ShapeDtypeStruct((blocks, 2, x_count, block_rows, planes), jnp.float32),
        compiler_params=compute_params(),
        cost_estimate=product_cost(maps, 3),
        name="adjoint",
    )(spectra, maps, mask, rows, inverse)


def first_call(maps, adjoint, denoised, mask):
    blocks, _, x_count, block_rows, planes = adjoint.shape
    maps_spec, field_spec, whole, rows, forward, inverse = plan_specs(
        maps, blocks, block_rows, mask
    )
    return pl.pallas_call(
        first_kernel,
        grid=(x_count, maps.shape[1]),
        in_specs=[
            maps_spec,
            field_spec,
            field_spec,
            whole(mask.shape),
            whole(rows.shape),
            whole(forward.shape),
            whole(inverse.shape),
        ],
        out_specs=[field_spec, field_spec],
        out_shape=[jax.ShapeDtypeStruct(adjoint.shape, jnp.float32)] * 2,
        compiler_params=compute_params(),
        cost_estimate=product_cost(maps, 6),
        name="first_product",
    )(maps, adjoint, denoised, mask, rows, forward, inverse)


def second_call(maps, right, field, mask):
    blocks, _, x_count, block_rows, planes = field.shape
    maps_spec, field_spec, whole, rows, forward, inverse = plan_specs(
        maps, blocks, block_rows, mask
    )
    out_shape = (blocks, 2 * x_count, block_rows, planes)
    return pl.pallas_call(
        second_kernel,
        grid=(x_count, maps.shape[1]),
        in_specs=[
            maps_spec,
            field_spec,
            field_spec,
            whole(mask.shape),
            whole(rows.shape),
            whole(forward.shape),
            whole(inverse.shape),
        ],
        out_specs=[whole(out_shape), whole((8, planes))],
        out_shape=[
            jax.ShapeDtypeStruct(out_shape, jnp.float32),
            jax.ShapeDtypeStruct((8, planes), jnp.float32),
        ],
        compiler_params=compute_params(),
        cost_estimate=product_cost(maps, 6),
        name="second_product",
    )(maps, right, field, mask, rows, forward, inverse)


def exchange(blocks, axis):
    return lax.all_to_all(blocks, axis, split_axis=0, concat_axis=0, tiled=True)


def x_first(cells, parts):
    rows, planes, width = cells.shape
    split = cells.reshape(rows, planes, 2, parts, width // (2 * parts))
    return jnp.transpose(split, (3, 2, 4, 0, 1))


def x_last(blocks):
    parts, _, x_count, rows, planes = blocks.shape
    return jnp.transpose(blocks, (3, 4, 1, 0, 2)).reshape(rows, planes, 2 * parts * x_count)


def combined(right, field, image, squares):
    right_right, right_field, field_field, field_image = (squares[i] for i in range(4))
    ratio = right_field / right_right
    alpha = right_right / (right_field + penalty * right_right)
    fresh = alpha * alpha * (field_field - ratio * right_field)
    weight = alpha * ratio + fresh / right_right
    mixed = weight * alpha
    curvature = (
        weight * weight * right_field - 2.0 * mixed * field_field + alpha * alpha * field_image
    ) + penalty * (
        weight * weight * right_right - 2.0 * mixed * right_field + alpha * alpha * field_field
    )
    second = fresh / curvature
    solution = (alpha + second * weight) * right - (second * alpha) * field
    residual = (
        (alpha * ratio - penalty * second * weight) * right
        - (alpha + second * weight - penalty * second * alpha) * field
        + (second * alpha) * image
    )
    return solution, residual


def body(
    prior_image,
    coil_maps,
    kspace,
    sampling,
    weight_first,
    bias_first,
    weight_middle,
    bias_middle,
    weight_last,
    bias_last,
):
    readout = prior_image.shape[2] // 2
    own_rows = prior_image.shape[0]
    planes = prior_image.shape[1]
    slabs = lax.axis_size("slab")
    coils = lax.axis_size("coil")
    devices = slabs * coils
    mask = jnp.transpose(
        lax.all_gather(sampling.astype(jnp.bfloat16), "slab", axis=0, tiled=True)
    ).astype(jnp.float32)
    spread = readout % devices == 0
    parts = devices if spread else coils

    def coils_to_x(values):
        blocks = x_first(values, parts)
        tail = blocks.shape[1:]
        if spread:
            return exchange(blocks, axes).reshape((slabs, coils) + tail)
        blocks = exchange(blocks, "coil").reshape((slabs, coils // slabs) + tail)
        return exchange(blocks, "slab")

    spectra = coils_to_x(kspace[0])
    maps = coils_to_x(coil_maps[0])
    denoised = denoise(
        prior_image, weight_first, bias_first, weight_middle, bias_middle, weight_last, bias_last
    )
    blocks = x_first(denoised, parts)
    if spread:
        denoised = exchange(blocks, axes)
        adjoint = adjoint_call(spectra, maps, mask, devices)
        right, field = first_call(maps, adjoint, denoised, mask)
        right_rows = x_last(exchange(right, axes))
        field_rows = x_last(exchange(field, axes))
        image, totals = second_call(maps, right, field, mask)
        payload = jnp.concatenate(
            [image, jnp.broadcast_to(totals[None, None], (devices, 1) + totals.shape)], axis=1
        )
        payload = exchange(payload, axes)
        squares = jnp.sum(payload[:, -1], axis=(0, 2))
        image_rows = x_last(payload[:, :-1].reshape(blocks.shape))
        return combined(right_rows, field_rows, image_rows, squares)

    tail = blocks.shape[1:3]

    def whole_rows(parts_in):
        moved = lax.all_gather(exchange(parts_in, "coil"), "slab", axis=0, tiled=True)
        return jnp.transpose(moved, (1, 2, 0, 3, 4)).reshape((1,) + tail + (-1, planes))

    def own_part(whole):
        rows = whole.shape[3] // slabs
        mine = lax.dynamic_slice_in_dim(whole, lax.axis_index("slab") * rows, rows, axis=3)
        split = jnp.transpose(mine.reshape(tail + (coils, own_rows, planes)), (2, 0, 1, 3, 4))
        return x_last(exchange(split, "coil"))

    adjoint = lax.psum(adjoint_call(spectra, maps, mask, 1), "slab")
    right = adjoint + penalty * whole_rows(blocks)
    _, field = first_call(maps, right, jnp.zeros_like(right), mask)
    field = lax.psum(field, "slab")
    image, _ = second_call(maps, right, field, mask)
    image = lax.psum(image.reshape(field.shape), "slab")
    squares = lax.psum(
        jnp.stack(
            [
                jnp.sum(right * right),
                jnp.sum(right * field),
                jnp.sum(field * field),
                jnp.sum(field * image),
            ]
        ),
        "coil",
    )
    return combined(own_part(right), own_part(field), own_part(image), squares)


def solution(mesh):
    placed = (
        P(("slab", "coil"), None, None),
        P("coil", "slab", None, None),
        P("coil", "slab", None, None),
        P("slab", None),
        P(),
        P(),
        P(),
        P(),
        P(),
        P(),
    )
    return jax.shard_map(
        body,
        mesh=mesh,
        in_specs=placed,
        out_specs=(P(("slab", "coil"), None, None), P(("slab", "coil"), None, None)),
        check_vma=False,
    )
```

time: 1310 us -> 608 us (0.46)
  waiting for transfers between devices: 373 us -> 63.1 us
  blocking collectives: 328 us -> 30.3 us
  matrix products: 247 us -> 150 us
  Pallas kernels: 0 us -> 70.9 us
  other arithmetic: 71.1 us -> 27.1 us
  local copies, waits for them, and re-layouts: 234 us -> 197 us
  starting transfers between devices: 29.6 us -> 53.7 us
    reduce_scatter x3 -> x0, waiting for transfers between devices: 212 us -> none  [reduce_coils(): lax.psum_scatter(complex_product(slab_maps, inverse_planes(z_table, image...]
    all_to_all x4 -> x1, blocking collectives: 208 us -> 24.8 us  [exchange(): return lax.all_to_all(blocks, axis, split_axis=0, concat_axis=0, tiled=True)]
    all_gather x2 -> x0, waiting for transfers between devices: 148 us -> none  [body(): lax.all_gather(direction, 'coil', axis=0, tiled=True)]
    psum x3 -> x0, blocking collectives: 120 us -> none  [single_total(): return lax.psum(value, ('slab', 'coil'))]
    dot_general x10 -> x0, matrix products: 96.6 us -> none  [the longest x2 32.1 us: through_kspace(): jnp.einsum('ky,yzn->zkn', y_table, moved, precision=highest, preferred_el...]
    pallas_call x0 -> x3, Pallas kernels: none -> 70.9 us  [the longest x1 28.5 us: second_call(): pl.pallas_call(second_kernel, grid=(x_count, maps.shape[1]), in_specs=[ma...]
    all_to_all x1 -> x5, waiting for transfers between devices: 0.01 us -> 33 us  [exchange(): return lax.all_to_all(blocks, axis, split_axis=0, concat_axis=0, tiled=True)]
    concatenate x5 -> x0, local copies, waits for them, and re-layouts: 27.3 us -> none  [combine(): return jnp.concatenate([real_part, imag_part], axis=-1)]
  transfers between devices with their start and end apart: 12 -> 11, of which waited for: 6 -> 5; matrix products, arithmetic and copies ran while one was open for 11% -> 26% of each run, Pallas kernels for 0% -> 7%
where the time goes in v1:
time: 608 us; the launch traced here: 602 us
  local copies, waits for them, and re-layouts  197 us (32%)
  matrix products  150 us (25%)
  Pallas kernels  70.9 us (12%)
  waiting for transfers between devices  63.1 us (10%)
  starting transfers between devices  53.7 us (9%)
  blocking collectives  30.3 us (5%)
  other arithmetic  27.1 us (4%)
  between operations  10.4 us (2%)
    slice x8, local copies, waits for them, and re-layouts, convolve_layer(): lax.slice(sources[column_shift], (row_shift, 0, first_cell), (row_shift +...  153 us
    dot_general x27, matrix products, convolve_layer(): jnp.einsum('oc,ycn->yon', kernel, stacked, preferred_element_type=jnp.flo...  150 us
    all_to_all x5, starting transfers between devices, exchange(): return lax.all_to_all(blocks, axis, split_axis=0, concat_axis=0, tiled=True)  36.2 us
    all_to_all x5, waiting for transfers between devices, exchange(): return lax.all_to_all(blocks, axis, split_axis=0, concat_axis=0, tiled=True)  33 us
    pallas_call x1, Pallas kernels, second_call(): pl.pallas_call(second_kernel, grid=(x_count, maps.shape[1]), in_specs=[ma...  28.5 us
    pallas_call x1, Pallas kernels, first_call(): pl.pallas_call(first_kernel, grid=(x_count, maps.shape[1]), in_specs=[map...  28 us
    unnamed x78, local copies, waits for them, and re-layouts  28 us
    ppermute x3, waiting for transfers between devices, padded_2(): lax.ppermute(tail, axis, [(i, (i + 1) % count) for i in range(ends)])  26.7 us
  transfers between devices with their start and end apart: 11, of which 5 were waited for; matrix products, arithmetic and copies ran while one was open for 26% of the time, Pallas kernels for 7%

profile of v1, /device:TPU:0, one launch (start us, length us, event | category | flops | bytes accessed | tf_op | source)
XLA Modules:
  0.0 602.3 jit_solution(7248926247921793336)
XLA Ops:
  49.6 18.6 %collective-permute-done.2 = bf16[1,32,8192]{2,1,0:T(8,128)(2,1)S(1)} collective-permute-done((bf16[1,32,8192]{2,1,0:T(8,128)(2,1)S(1)}, bf16[1,32,8192]{2,1,0:T(8,128)(2,1)S(1)}, u32[]{:S(2)}, u32[]{:S(2)}) %collective-permute-start.2) | collective-permute-done | bytes 524320 | tf_op jit(solution)/shard_map/ppermute | solution.py:27
  68.2 8.0 %broadcast_select_fusion.3 = (bf16[10,32,8322]{2,1,0:T(8,128)(2,1)}, bf16[10,32,8322]{2,1,0:T(8,128)(2,1)S(1)}) fusion(pred[8322]{0:T(1024)(128)(4,1)S(1)} %broadcast_compare_fusion, bf16[1,32,8192]{2,1,0:T(8,128)(2,1)S(1)} %collective-permute-done.3, bf16[8,32,8192]{2,1,0:T(8,128)(2,1)} %copy-done.14, bf16[1,32,8192]{2,1,0:T(8,128)(2,1)S(1)} %collective-permute-done.2), kind=kLoop, calls=%fused_computation.153 | loop fusion | flops 34619520 | bytes 15903362 | tf_op jit(solution)/shard_map/jit(_where)/select_n | solution.py:46
  81.4 22.8 %fusion.271 = (bf16[8,32,8192]{2,1,0:T(8,128)(2,1)}, bf16[8,32,8192]{2,1,0:T(8,128)(2,1)}, bf16[8,32,8192]{2,1,0:T(8,128)(2,1)}, bf16[8,32,8192]{2,1,0:T(8,128)(...) fusion(bf16[10,32,8322]{2,1,0:T(8,128)(2,1)} %copy-done.9), kind=kLoop, calls=%fused_computation.293 | loop fusion | bytes 50331648 | tf_op jit(solution)/shard_map/slice | solution.py:57
  104.2 31.3 %fusion.272 = (bf16[8,32,8192]{2,1,0:T(8,128)(2,1)}, bf16[8,32,8192]{2,1,0:T(8,128)(2,1)}, bf16[8,32,8192]{2,1,0:T(8,128)(2,1)}, bf16[8,32,8192]{2,1,0:T(8,128)(...) fusion(bf16[10,32,8322]{2,1,0:T(8,128)(2,1)} %broadcast_select_, ...), kind=kLoop, calls=%fused_computation.294 | loop fusion | bytes 75497472 | tf_op jit(solution)/shard_map/slice | solution.py:57
  135.5 13.3 %fusion.270 = (bf16[8,32,8192]{2,1,0:T(8,128)(2,1)}, bf16[8,32,8192]{2,1,0:T(8,128)(2,1)}, bf16[8,32,8192]{2,1,0:T(8,128)(2,1)}, bf16[8,32,8192]{2,1,0:T(8,128)(...) fusion(bf16[10,32,8322]{2,1,0:T(8,128)(2,1)S(1)} %bitcast.194), kind=kLoop, calls=%fused_computation.292 | loop fusion | bytes 75497472 | tf_op jit(solution)/shard_map/slice | solution.py:57
  148.8 6.8 %fusion.11 = f32[8,8192,32]{1,2,0:T(8,128)} fusion(bf16[32,96,1]{1,0,2:T(8,128)(2,1)S(1)} %reshape.170, bf16[8,32,8192]{2,1,0:T(8,128)(2,1)S(1)} %copy-done.15, bf16[1,32,8192]{2,1,0:T(8,128)(2,1)S(1)} %collective-permute-done.2, bf16[8,32,8192]{2,1,0:T(8,128)(2,1)S(1)} %get-tuple-element.66, bf16[8,32,8192]{2,1,0:T(8,128)(2,1)} %get-tuple-element.51), kind=kOutput, calls=%fused_computation.16 | convolution fusion | flops 452984832 | bytes 21501952 | tf_op jit(solution)/shard_map/oc,ycn->yon/dot_general | solution.py:67
  155.6 11.7 %fusion.127 = f32[8,8192,32]{1,2,0:T(8,128)} fusion(f32[8,8192,32]{1,2,0:T(8,128)} %fusion.11, bf16[32,96,1]{1,0,2:T(8,128)(2,1)S(1)} %reshape.169, bf16[8,32,8192]{2,1,0:T(8,128)(2,1)} %get-tuple-element.67, bf16[8,32,8192]{2,1,0:T(8,128)(2,1)} %get-tuple-element.57, bf16[8,32,8192]{2,1,0:T(8,128)(2,1)} %get-tuple-element.52), kind=kOutput, calls=%fused_computation.125 | convolution fusion | flops 442499072 | bytes 29366272 | tf_op jit(solution)/shard_map/oc,ycn->yon/dot_general | solution.py:67
  167.3 9.7 %fusion.124 = f32[8,8192,32]{1,2,0:T(8,128)} fusion(f32[8,8192,32]{1,2,0:T(8,128)} %fusion.127, bf16[32,96,1]{1,0,2:T(8,128)(2,1)S(1)} %reshape.171, bf16[8,32,8192]{2,1,0:T(8,128)(2,1)} %get-tuple-element.65, bf16[8,32,8192]{2,1,0:T(8,128)(2,1)S(1)} %copy-done.22, bf16[8,32,8192]{2,1,0:T(8,128)(2,1)} %get-tuple-element.50), kind=kOutput, calls=%fused_computation.124 | convolution fusion | flops 442499072 | bytes 29366272 | tf_op jit(solution)/shard_map/oc,ycn->yon/dot_general | solution.py:67
  177.0 11.7 %fusion.121 = f32[8,8192,32]{1,2,0:T(8,128)} fusion(f32[8,8192,32]{1,2,0:T(8,128)} %fusion.124, bf16[32,96,1]{1,0,2:T(8,128)(2,1)S(1)} %reshape.172, bf16[8,32,8192]{2,1,0:T(8,128)(2,1)} %get-tuple-element.64, bf16[8,32,8192]{2,1,0:T(8,128)(2,1)} %get-tuple-element.55, bf16[8,32,8192]{2,1,0:T(8,128)(2,1)} %get-tuple-element.49), kind=kOutput, calls=%fused_computation.123 | convolution fusion | flops 442499072 | bytes 29366272 | tf_op jit(solution)/shard_map/oc,ycn->yon/dot_general | solution.py:67
  188.7 9.7 %fusion.118 = f32[8,8192,32]{1,2,0:T(8,128)} fusion(f32[8,8192,32]{1,2,0:T(8,128)} %fusion.121, bf16[32,96,1]{1,0,2:T(8,128)(2,1)S(1)} %reshape.173, bf16[8,32,8192]{2,1,0:T(8,128)(2,1)} %get-tuple-element.63, bf16[8,32,8192]{2,1,0:T(8,128)(2,1)S(1)} %copy-done.16, bf16[8,32,8192]{2,1,0:T(8,128)(2,1)} %get-tuple-element.48), kind=kOutput, calls=%fused_computation.122 | convolution fusion | flops 442499072 | bytes 29366272 | tf_op jit(solution)/shard_map/oc,ycn->yon/dot_general | solution.py:67
  198.4 8.1 %fusion.54 = f32[8,8192,32]{1,2,0:T(8,128)} fusion(bf16[32,96,1]{1,0,2:T(8,128)(2,1)S(1)} %reshape.177, bf16[8,32,8192]{2,1,0:T(8,128)(2,1)} %get-tuple-element.60, bf16[8,32,8192]{2,1,0:T(8,128)(2,1)} %get-tuple-element.58, bf16[8,32,8192]{2,1,0:T(8,128)(2,1)} %get-tuple-element.45), kind=kOutput, calls=%fused_computation.58 | convolution fusion | flops 440401920 | bytes 20977664 | tf_op jit(solution)/shard_map/oc,ycn->yon/dot_general | solution.py:67
  206.5 11.6 %fusion.115 = f32[8,8192,32]{1,2,0:T(8,128)} fusion(f32[8,8192,32]{1,2,0:T(8,128)} %fusion.118, bf16[32,96,1]{1,0,2:T(8,128)(2,1)S(1)} %reshape.174, bf16[8,32,8192]{2,1,0:T(8,128)(2,1)} %get-tuple-element.62, bf16[8,32,8192]{2,1,0:T(8,128)(2,1)} %get-tuple-element.54, bf16[8,32,8192]{2,1,0:T(8,128)(2,1)} %get-tuple-element.47), kind=kOutput, calls=%fused_computation.121 | convolution fusion | flops 442499072 | bytes 29366272 | tf_op jit(solution)/shard_map/oc,ycn->yon/dot_general | solution.py:67
  224.7 13.1 %fusion.144 = bf16[8,32,8192]{2,1,0:T(8,128)(2,1)S(1)} fusion(f32[8,8192,32]{1,2,0:T(8,128)} %fusion.54, f32[8,8192,32]{1,2,0:T(8,128)} %fusion.6, f32[8,8192,32]{1,2,0:T(8,128)} %fusion.115, bf16[32,96,1]{1,0,2:T(8,128)(2,1)S(1)} %reshape.175, bf16[8,32,8192]{2,1,0:T(8,128)(2,1)} %get-tuple-element.59, bf16[8,32,8192]{2,1,0:T(8,128)(2,1)} %get-tuple-element.53, ...), kind=kOutput, calls=%fused_computation.132 | convolution fusion | flops 452984832 | bytes 41949312 | tf_op jit(solution)/shard_map/oc,ycn->yon/dot_general | solution.py:67
  251.4 9.4 %all-to-all-start = ((bf16[32,2,2,64,128]{4,3,2,1,0:T(8,128)(2,1)}), bf16[32,2,2,64,128]{4,3,2,1,0:T(8,128)(2,1)S(1)}, u32[]{:S(2)}, u32[]{:S(2)}) async-start(bf16[32,2,2,64,128]{4,3,2,1,0:T(8,128)(2,1)} %copy.78), calls=%async_computation | async-start | bytes 4194304 | tf_op jit(solution)/shard_map/all_to_all | solution.py:401
  269.7 8.1 %collective-permute-done.4 = bf16[1,32,8192]{2,1,0:T(8,128)(2,1)S(1)} collective-permute-done((bf16[1,32,8192]{2,1,0:T(8,128)(2,1)}, bf16[1,32,8192]{2,1,0:T(8,128)(2,1)S(1)}, u32[]{:S(2)}, u32[]{:S(2)}) %collective-permute-start.4) | collective-permute-done | bytes 524320 | tf_op jit(solution)/shard_map/ppermute | solution.py:27
  289.6 22.2 %fusion.268 = (bf16[8,32,8192]{2,1,0:T(8,128)(2,1)}, bf16[8,32,8192]{2,1,0:T(8,128)(2,1)}, bf16[8,32,8192]{2,1,0:T(8,128)(2,1)}, bf16[8,32,8192]{2,1,0:T(8,128)(...) fusion(bf16[10,32,8322]{2,1,0:T(8,128)(2,1)} %copy-done.8), kind=kLoop, calls=%fused_computation.290 | loop fusion | bytes 50331648 | tf_op jit(solution)/shard_map/slice | solution.py:57
  311.8 31.0 %fusion.269 = (bf16[8,32,8192]{2,1,0:T(8,128)(2,1)}, bf16[8,32,8192]{2,1,0:T(8,128)(2,1)}, bf16[8,32,8192]{2,1,0:T(8,128)(2,1)}, bf16[8,32,8192]{2,1,0:T(8,128)(...) fusion(bf16[10,32,8322]{2,1,0:T(8,128)(2,1)} %broadcast_select_, ...), kind=kLoop, calls=%fused_computation.291 | loop fusion | bytes 75497472 | tf_op jit(solution)/shard_map/slice | solution.py:57
  342.8 24.7 %fusion.267 = (bf16[8,32,8192]{2,1,0:T(8,128)(2,1)}, bf16[8,32,8192]{2,1,0:T(8,128)(2,1)}, bf16[8,32,8192]{2,1,0:T(8,128)(2,1)}, bf16[8,32,8192]{2,1,0:T(8,128)(...) fusion(bf16[10,32,8322]{2,1,0:T(8,128)(2,1)} %get-tuple-element.14), kind=kLoop, calls=%fused_computation.289 | loop fusion | bytes 75497472 | tf_op jit(solution)/shard_map/slice | solution.py:57
  396.0 15.8 %all-to-all-start.1 = ((bf16[32,2,2,32,256]{4,3,2,1,0:T(8,128)(2,1)}), bf16[32,2,2,32,256]{4,3,2,1,0:T(8,128)(2,1)}, u32[]{:S(2)}, u32[]{:S(2)}) async-start(bf16[32,2,2,32,256]{4,3,2,1,0:T(8,128)(2,1)} %copy.80), calls=%async_computation.1 | async-start | bytes 4194304 | tf_op jit(solution)/shard_map/all_to_all | solution.py:401
  435.7 26.2 %all-to-all-done.1 = bf16[32,2,2,32,256]{4,3,2,1,0:T(8,128)(2,1)} async-done(((bf16[32,2,2,32,256]{4,3,2,1,0:T(8,128)(2,1)}), bf16[32,2,2,32,256]{4,3,2,1,0:T(8,128)(2,1)}, u32[]{:S(2)}, u32[]{:S(2)}) %all-to-all-start.1) | async-done | bytes 2097184 | tf_op jit(solution)/shard_map/all_to_all | solution.py:401
  473.4 14.4 %adjoint.1.adjoint_ref = f32[32,2,2,8,128]{4,3,2,1,0:T(8,128)S(1)} custom-call(bf16[4,8,2,2,32,256]{5,4,3,2,1,0:T(8,128)(2,1)} %bitcast.5.kspace_ref, bf16[4,8,2,2,64,128]{5,4,3,2,1,0:T(8,128)(2,1)S(1)} %bitcast.190, f32[256,128]{1,0:T(8,128)S(1)} %convert_bitcast_fusion.mask_ref, bf16[512,768]{1,0:T(8,128)(2,1)S(1)} %copy-done, bf16[768,256]{1,0:T(8,128)(2,1)S(1)} %copy-done.1), custom_call_target="tpu_custom_call" | custom-call | flops 4831838208 | bytes 2097152 | tf_op jit(solution)/shard_map/adjoint/pallas_call | solution.py:334
  491.7 28.0 %first_product.1 = (f32[32,2,2,8,128]{4,3,2,1,0:T(8,128)}, f32[32,2,2,8,128]{4,3,2,1,0:T(8,128)}) custom-call(bf16[4,8,2,2,64,128]{5,4,3,2,1,0:T(8,128)(2,1)S(1)} %bitcast.191, f32[32,2,2,8,128]{4,3,2,1,0:T(8,128)S(1)} %copy-done.7, f32[32,2,2,8,128]{4,3,2,1,0:T(8,128)S(1)} %all-to-all-done.2.denoised_ref, f32[256,128]{1,0:T(8,128)S(1)} %convert_bitcast_fusion.mask_ref, ...), custom_call_target="tpu_custom_call" | custom-call | flops 9663676416 | bytes 2097152 | tf_op jit(solution)/shard_map/first_product/pallas_call | solution.py:351
  527.4 28.5 %second_product.1 = (f32[32,4,8,128]{3,2,1,0:T(8,128)S(1)}, f32[8,128]{1,0:T(8,128)S(1)}) custom-call(bf16[4,8,2,2,64,128]{5,4,3,2,1,0:T(8,128)(2,1)S(1)} %bitcast.192, f32[32,2,2,8,128]{4,3,2,1,0:T(8,128)} %get-tuple-element.6.right_ref, f32[32,2,2,8,128]{4,3,2,1,0:T(8,128)} %get-tuple-element.7.field_ref, f32[256,128]{1,0:T(8,128)S(1)} %convert_bitcast_fusion.mask_ref, ...), custom_call_target="tpu_custom_call" | custom-call | flops 9663676416 | bytes 2097152 | tf_op jit(solution)/shard_map/second_product/pallas_call | solution.py:377
  556.0 24.8 %all_to_all.30 = f32[32,5,8,128]{3,2,1,0:T(8,128)S(1)} all-to-all(f32[32,5,8,128]{3,2,1,0:T(8,128)S(1)} %pad_maximum_fusion.10), channel_id=1, replica_groups=mesh['slab'=4,'coil'=8] {'slab','coil'}, dimensions={0} | all-to-all | bytes 1310720 | tf_op jit(solution)/shard_map/all_to_all | solution.py:401
  (199 shorter events, 182.6 us)
Async XLA Ops:
  2.3 7.2 %collective-permute-start = (bf16[1,2,8192]{2,1,0:T(2,128)(2,1)S(1)}, bf16[1,2,8192]{2,1,0:T(2,128)(2,1)S(1)}, u32[]{:S(2)}, u32[]{:S(2)}) collective-permute-start(bf16[1,2,8192]{2,1,0:T(2,128)(2,1)S(1)} %get-tuple-element.76), channel_id=1, source_target_pairs={{0,1},{1,2},{2,3},{3,4},{4,5},{5,6},{6,7},{7,8},{8,9},{9,10},{10,1... | collective-permute-start | bytes 98312 | tf_op jit(solution)/shard_map/ppermute | solution.py:27
  7.2 5.8 collective-permute-start.1
  8.5 59.7 %copy-start.27 = (pred[8322]{0:T(1024)(128)(4,1)}, pred[8322]{0:T(1024)(128)(4,1)S(1)}, u32[]{:S(2)}) copy-start(pred[8322]{0:T(1024)(128)(4,1)S(1)} %broadcast_compare_fusion) | copy-start | bytes 24970
  8.6 67.7 %copy-start.29 = (pred[8322]{0:T(1024)(128)(4,1)}, pred[8322]{0:T(1024)(128)(4,1)S(1)}, u32[]{:S(2)}) copy-start(pred[8322]{0:T(1024)(128)(4,1)S(1)} %broadcast_compare_fusion.1) | copy-start | bytes 24970
  42.9 25.3 %collective-permute-start.2 = (bf16[1,32,8192]{2,1,0:T(8,128)(2,1)S(1)}, bf16[1,32,8192]{2,1,0:T(8,128)(2,1)S(1)}, u32[]{:S(2)}, u32[]{:S(2)}) collective-permute-start(bf16[1,32,8192]{2,1,0:T(8,128)(2,1)S(1)} %get-tuple-element.70), channel_id=1, source_target_pairs={{0,1},{1,2},{2,3},{3,4},{4,5},{5,6},{6,7},{7,8},{8,9},{9,10},{10,1... | collective-permute-start | bytes 1572872 | tf_op jit(solution)/shard_map/ppermute | solution.py:27
  47.3 20.9 %collective-permute-start.3 = (bf16[1,32,8192]{2,1,0:T(8,128)(2,1)S(1)}, bf16[1,32,8192]{2,1,0:T(8,128)(2,1)S(1)}, u32[]{:S(2)}, u32[]{:S(2)}) collective-permute-start(bf16[1,32,8192]{2,1,0:T(8,128)(2,1)S(1)} %get-tuple-element.71), channel_id=1, source_target_pairs={{1,0},{2,1},{3,2},{4,3},{5,4},{6,5},{7,6},{8,7},{9,8},{10,9},{11,1... | collective-permute-start | bytes 1572872 | tf_op jit(solution)/shard_map/ppermute | solution.py:29
  81.4 54.1 %slice-start = ((s8[5406720]{0:T(1024)(128)(4,1)}), s8[1212416]{0:T(1024)(128)(4,1)S(1)}, s32[]{:S(2)}) async-start(s8[5406720]{0:T(1024)(128)(4,1)} %bitcast.193), calls=%async_computation.6 | async-start | bytes 2424832
  104.2 31.3 %slice-start.1 = ((s8[5406720]{0:T(1024)(128)(4,1)}), s8[4194304]{0:T(1024)(128)(4,1)S(1)}, s32[]{:S(2)}) async-start(s8[5406720]{0:T(1024)(128)(4,1)} %bitcast.193), calls=%async_computation.7 | async-start | bytes 8388608
  135.5 13.3 %copy-start.15 = (bf16[8,32,8192]{2,1,0:T(8,128)(2,1)S(1)}, bf16[8,32,8192]{2,1,0:T(8,128)(2,1)}, u32[]{:S(2)}) copy-start(bf16[8,32,8192]{2,1,0:T(8,128)(2,1)} %copy-done.14) | copy-start | bytes 12582916
  155.6 11.7 %copy-start.22 = (bf16[8,32,8192]{2,1,0:T(8,128)(2,1)S(1)}, bf16[8,32,8192]{2,1,0:T(8,128)(2,1)}, u32[]{:S(2)}) copy-start(bf16[8,32,8192]{2,1,0:T(8,128)(2,1)} %get-tuple-element.56) | copy-start | bytes 12582916
  177.0 11.7 %copy-start.16 = (bf16[8,32,8192]{2,1,0:T(8,128)(2,1)S(1)}, bf16[8,32,8192]{2,1,0:T(8,128)(2,1)}, u32[]{:S(2)}) copy-start(bf16[8,32,8192]{2,1,0:T(8,128)(2,1)} %copy-done.14) | copy-start | bytes 12582916
  240.8 36.9 %collective-permute-start.4 = (bf16[1,32,8192]{2,1,0:T(8,128)(2,1)}, bf16[1,32,8192]{2,1,0:T(8,128)(2,1)S(1)}, u32[]{:S(2)}, u32[]{:S(2)}) collective-permute-start(bf16[1,32,8192]{2,1,0:T(8,128)(2,1)} %get-tuple-element.68), channel_id=1, source_target_pairs={{0,1},{1,2},{2,3},{3,4},{4,5},{5,6},{6,7},{7,8},{8,9},{9,10},{10,1... | collective-permute-start | bytes 1572872 | tf_op jit(solution)/shard_map/ppermute | solution.py:27
  245.2 15.6 %copy-start.31 = (bf16[3,3,3,2,32]{4,3,2,1,0:T(2,128)(2,1)S(1)}, bf16[3,3,3,2,32]{4,3,2,1,0:T(2,128)(2,1)}, u32[]{:S(2)}) copy-start(bf16[3,3,3,2,32]{4,3,2,1,0:T(2,128)(2,1)} %param.26) | copy-start | bytes 10372
  245.2 32.5 %collective-permute-start.5 = (bf16[1,32,8192]{2,1,0:T(8,128)(2,1)}, bf16[1,32,8192]{2,1,0:T(8,128)(2,1)S(1)}, u32[]{:S(2)}, u32[]{:S(2)}) collective-permute-start(bf16[1,32,8192]{2,1,0:T(8,128)(2,1)} %get-tuple-element.69), channel_id=1, source_target_pairs={{1,0},{2,1},{3,2},{4,3},{5,4},{6,5},{7,6},{8,7},{9,8},{10,9},{11,1... | collective-permute-start | bytes 1572872 | tf_op jit(solution)/shard_map/ppermute | solution.py:29
  251.4 26.3 %copy-start.28 = (pred[8322]{0:T(1024)(128)(4,1)S(1)}, pred[8322]{0:T(1024)(128)(4,1)}, u32[]{:S(2)}) copy-start(pred[8322]{0:T(1024)(128)(4,1)} %copy-done.27) | copy-start | bytes 24970
  251.4 144.6 %all-to-all-start = ((bf16[32,2,2,64,128]{4,3,2,1,0:T(8,128)(2,1)}), bf16[32,2,2,64,128]{4,3,2,1,0:T(8,128)(2,1)S(1)}, u32[]{:S(2)}, u32[]{:S(2)}) async-start(bf16[32,2,2,64,128]{4,3,2,1,0:T(8,128)(2,1)} %copy.78), calls=%async_computation | async-start | bytes 4194304 | tf_op jit(solution)/shard_map/all_to_all | solution.py:401
  266.3 11.5 %copy-start.11 = (bf16[8,32,8192]{2,1,0:T(8,128)(2,1)S(1)}, bf16[8,32,8192]{2,1,0:T(8,128)(2,1)}, u32[]{:S(2)}) copy-start(bf16[8,32,8192]{2,1,0:T(8,128)(2,1)} %copy-done.10) | copy-start | bytes 12582916
  269.7 17.2 %copy-start.30 = (pred[8322]{0:T(1024)(128)(4,1)S(1)}, pred[8322]{0:T(1024)(128)(4,1)}, u32[]{:S(2)}) copy-start(pred[8322]{0:T(1024)(128)(4,1)} %copy-done.29) | copy-start | bytes 24970
  342.8 24.7 %copy-start.12 = (bf16[8,32,8192]{2,1,0:T(8,128)(2,1)S(1)}, bf16[8,32,8192]{2,1,0:T(8,128)(2,1)}, u32[]{:S(2)}) copy-start(bf16[8,32,8192]{2,1,0:T(8,128)(2,1)} %copy-done.10) | copy-start | bytes 12582916
  396.0 65.9 %all-to-all-start.1 = ((bf16[32,2,2,32,256]{4,3,2,1,0:T(8,128)(2,1)}), bf16[32,2,2,32,256]{4,3,2,1,0:T(8,128)(2,1)}, u32[]{:S(2)}, u32[]{:S(2)}) async-start(bf16[32,2,2,32,256]{4,3,2,1,0:T(8,128)(2,1)} %copy.80), calls=%async_computation.1 | async-start | bytes 4194304 | tf_op jit(solution)/shard_map/all_to_all | solution.py:401
  428.5 44.0 %copy-start = (bf16[512,768]{1,0:T(8,128)(2,1)S(1)}, bf16[512,768]{1,0:T(8,128)(2,1)}, u32[]{:S(2)}) copy-start(bf16[512,768]{1,0:T(8,128)(2,1)} %constant.45.clone.rows_ref) | copy-start | bytes 2359300
  461.9 26.7 %all-to-all-start.2 = ((f32[32,2,2,8,128]{4,3,2,1,0:T(8,128)}), f32[32,2,2,8,128]{4,3,2,1,0:T(8,128)S(1)}, u32[]{:S(2)}, u32[]{:S(2)}) async-start(f32[32,2,2,8,128]{4,3,2,1,0:T(8,128)} %bitcast.197), calls=%async_computation.2 | async-start | bytes 1048576 | tf_op jit(solution)/shard_map/all_to_all | solution.py:401
  519.7 36.3 %all-to-all-start.4 = ((f32[32,2,2,8,128]{4,3,2,1,0:T(8,128)}), f32[32,2,2,8,128]{4,3,2,1,0:T(8,128)S(1)}, u32[]{:S(2)}, u32[]{:S(2)}) async-start(f32[32,2,2,8,128]{4,3,2,1,0:T(8,128)} %get-tuple-element.6.right_ref), calls=%async_computation.4 | async-start | bytes 1048576 | tf_op jit(solution)/shard_map/all_to_all | solution.py:401
  580.8 19.0 %all-to-all-start.5 = ((f32[32,2,2,8,128]{4,3,2,1,0:T(8,128)}), f32[32,2,2,8,128]{4,3,2,1,0:T(8,128)S(1)}, u32[]{:S(2)}, u32[]{:S(2)}) async-start(f32[32,2,2,8,128]{4,3,2,1,0:T(8,128)} %get-tuple-element.7.field_ref), calls=%async_computation.5 | async-start | bytes 1048576 | tf_op jit(solution)/shard_map/all_to_all | solution.py:401
  (24 other events, 90.2 us)

commit v2 on v1

--- a/solution.py
+++ b/solution.py
@@ -16,81 +16,228 @@
 axes = ("slab", "coil")
 
 
-def padded_2(cells, sides, width):
-    for axis, dim in sides:
-        count = lax.axis_size(axis)
-        ends = count - 1
-        head = lax.slice_in_dim(cells, 0, width, axis=dim)
-        tail = lax.slice_in_dim(cells, cells.shape[dim] - width, cells.shape[dim], axis=dim)
-        cells = jnp.concatenate(
-            [
-                lax.ppermute(tail, axis, [(i, (i + 1) % count) for i in range(ends)]),
-                cells,
-                lax.ppermute(head, axis, [((i + 1) % count, i) for i in range(ends)]),
-            ],
-            axis=dim,
+def with_halo(cells, width):
+    rows = cells.shape[0]
+    count = lax.axis_size("slab") * lax.axis_size("coil")
+    above, below = [], []
+    for hop in range(1, -(-width // rows) + 1):
+        taken = min(width - (hop - 1) * rows, rows)
+        ends = count - hop
+        tail = lax.slice_in_dim(cells, rows - taken, rows, axis=0)
+        head = lax.slice_in_dim(cells, 0, taken, axis=0)
+        above.insert(0, lax.ppermute(tail, axes, [(i, i + hop) for i in range(ends)]))
+        below.append(lax.ppermute(head, axes, [(i + hop, i) for i in range(ends)]))
+    return jnp.concatenate(above + [cells] + below, axis=0)
+
+
+def chunk_rows(rows):
+    return max(size for size in range(1, 7) if rows % size == 0)
+
+
+def chained(lhs_pieces):
+    rows = lhs_pieces[0].shape[0] * lhs_pieces[0].shape[1]
+    lhs = jnp.concatenate(lhs_pieces, axis=2)
+    return lhs.reshape(rows, lhs.shape[2])
+
+
+def denoise_kernel(
+    group,
+    first_ref,
+    features_ref,
+    prior_ref,
+    weight_first_ref,
+    bias_first_ref,
+    weight_middle_ref,
+    bias_middle_ref,
+    weight_last_ref,
+    bias_last_ref,
+    out_ref,
+    one_ref,
+    two_ref,
+    taps_ref,
+):
+    planes = out_ref.shape[1]
+    width = out_ref.shape[2]
+    edge = (one_ref.shape[2] - two_ref.shape[2]) // 2
+    groups = two_ref.shape[2] // group
+    first = first_ref[0]
+    total = first_ref[1]
+    one_ref[:, :, :edge] = jnp.zeros(one_ref.shape[:2] + (edge,), one_ref.dtype)
+    one_ref[:, :, edge + two_ref.shape[2] :] = jnp.zeros(
+        one_ref.shape[:2] + (edge,), one_ref.dtype
+    )
+
+    def store(ref, start, count, lanes, value, reach):
+        value = jnp.maximum(value, 0.0).reshape(count, planes, group)
+        for row in range(count):
+            place = first + (start + row - reach)
+            kept = jnp.where((place >= 0) & (place < total), value[row], 0.0)
+            ref[start + row, :, lanes] = kept.astype(ref.dtype)
+
+    def first_layer(index, carry):
+        lanes = pl.ds(pl.multiple_of(index * group, group), group)
+        placed = pl.ds(pl.multiple_of(edge + index * group, 128), group)
+        count = chunk_rows(one_ref.shape[0])
+        for start in range(0, one_ref.shape[0], count):
+            lhs = chained([features_ref[start + tap : start + tap + count] for tap in range(3)])
+            value = jnp.dot(lhs, weight_first_ref[:, lanes], preferred_element_type=jnp.float32)
+            store(one_ref, start, count, placed, value + bias_first_ref[:, lanes], 2)
+        return carry
+
+    lax.fori_loop(0, groups, first_layer, 0)
+
+    def shifted(value, plane, step):
+        rows = value.shape[0]
+        if step > 0:
+            return jnp.where(plane == 0, 0.0, pltpu.roll(value, 1, 0))
+        return jnp.where(plane == planes - 1, 0.0, pltpu.roll(value, rows - 1, 0))
+
+    def plane_index(count, lanes):
+        return lax.broadcasted_iota(jnp.int32, (count, planes, lanes), 1).reshape(
+            count * planes, lanes
         )
-    return cells
-
-
-def convolve_layer(features, weights, offsets, readout):
-    row_total = features.shape[0]
-    in_channels = features.shape[1]
-    span_cells = features.shape[2]
-    out_channels = weights.shape[3]
-    extended = padded_2(features, ((("slab", "coil"), 0),), 1)
-    padded = jnp.pad(extended, ((0, 0), (0, 0), (readout + 1, readout + 1)))
-    column = (jnp.arange(padded.shape[2], dtype=jnp.int32) - 1) % readout
-    zero_value = jnp.zeros((), padded.dtype)
-    sources = (
-        jnp.where(column != readout - 1, padded, zero_value),
-        padded,
-        jnp.where(column != 0, padded, zero_value),
-    )
-    running = jnp.zeros((row_total, out_channels, span_cells), jnp.float32)
-    for row_shift in range(3):
-        for plane_shift in range(3):
-            pieces = []
-            for column_shift in range(3):
-                first_cell = plane_shift * readout + column_shift
-                pieces.append(
-                    lax.slice(
-                        sources[column_shift],
-                        (row_shift, 0, first_cell),
-                        (row_shift + row_total, in_channels, first_cell + span_cells),
-                    )
-                )
-            stacked = jnp.concatenate(pieces, axis=1)
-            kernel = jnp.transpose(weights[row_shift, plane_shift], (1, 0, 2)).reshape(
-                out_channels, 3 * in_channels
+
+    def middle_layer(index, carry):
+        lanes = pl.ds(pl.multiple_of(index * group, group), group)
+        window = pl.ds(pl.multiple_of(index * group, group), group + 2 * edge)
+        count = chunk_rows(two_ref.shape[0])
+        plane = plane_index(count, group)
+        for start in range(0, two_ref.shape[0], count):
+            lhs = chained([one_ref[start + tap : start + tap + count, :, window] for tap in range(3)])
+            value = jnp.dot(lhs, weight_middle_ref[...], preferred_element_type=jnp.float32)
+            value = (
+                value[:, group : 2 * group]
+                + shifted(value[:, :group], plane, 1)
+                + shifted(value[:, 2 * group :], plane, -1)
             )
-            running = running + jnp.einsum(
-                "oc,ycn->yon", kernel, stacked, preferred_element_type=jnp.float32
-            )
-    return running + offsets[None, :, None]
+            store(two_ref, start, count, lanes, value + bias_middle_ref[:, lanes], 1)
+        return carry
+
+    lax.fori_loop(0, groups, middle_layer, 0)
+
+    count = chunk_rows(two_ref.shape[0])
+
+    def last_layer(index, carry):
+        start = index * count
+        lhs = two_ref[pl.ds(start, count)].reshape(count * planes, two_ref.shape[2])
+        value = jnp.dot(lhs, weight_last_ref[...], preferred_element_type=jnp.float32)
+        taps_ref[pl.ds(start, count)] = value.reshape(count, planes, value.shape[1])
+        return carry
+
+    lax.fori_loop(0, two_ref.shape[0] // count, last_layer, 0)
+    plane = plane_index(1, width)
+
+    def last_sum(row, carry):
+        sums = []
+        for plane_tap in range(3):
+            running = None
+            for row_tap in range(3):
+                lanes = pl.ds((row_tap * 3 + plane_tap) * width, width)
+                value = taps_ref[row + row_tap, :, lanes]
+                running = value if running is None else running + value
+            sums.append(running)
+        value = sums[1] + shifted(sums[0], plane, 1) + shifted(sums[2], plane, -1)
+        out_ref[row] = prior_ref[row] + (value + bias_last_ref[...])
+        return carry
+
+    lax.fori_loop(0, out_ref.shape[0], last_sum, 0)
+
+
+def banded(tiles, inner, outer, offset):
+    shape = jnp.broadcast_shapes(tiles[0].shape, inner.shape, outer.shape)
+    result = jnp.zeros(shape, jnp.bfloat16)
+    for tap in range(3):
+        result = jnp.where(inner - outer + offset == tap, tiles[tap], result)
+    return result
 
 
 def denoise(
     prior_image, weight_first, bias_first, weight_middle, bias_middle, weight_last, bias_last
 ):
-    readout = prior_image.shape[2] // 2
-    own_rows = prior_image.shape[0]
-    planes = prior_image.shape[1]
-    features = (
-        jnp.stack([prior_image[..., :readout], prior_image[..., readout:]], axis=1)
-        .reshape(own_rows, 2, planes * readout)
-        .astype(jnp.bfloat16)
-    )
-    hidden = jax.nn.relu(convolve_layer(features, weight_first, bias_first, readout)).astype(
-        jnp.bfloat16
-    )
-    hidden = jax.nn.relu(convolve_layer(hidden, weight_middle, bias_middle, readout)).astype(
-        jnp.bfloat16
-    )
-    output = convolve_layer(hidden, weight_last, bias_last, readout).reshape(
-        own_rows, 2, planes, readout
-    )
-    return prior_image + jnp.concatenate([output[:, 0], output[:, 1]], axis=-1)
+    own_rows, planes, width = prior_image.shape
+    readout = width // 2
+    channels = weight_first.shape[3]
+    span = readout * channels
+    group = min(256, span)
+    held = group // channels
+    edge = 128
+    reach = edge // channels
+    window = group + 2 * edge
+
+    def lane_place(count, inside):
+        return jnp.arange(count * inside, dtype=jnp.int32) // inside
+
+    tiles = jnp.transpose(weight_first, (2, 0, 1, 4, 3)).reshape(3, 18, 1, 1, channels)
+    tiles = jnp.broadcast_to(tiles, (3, 18, 1, readout, channels)).reshape(3, 18, 1, span)
+    first_table = banded(
+        tiles,
+        jnp.arange(readout, dtype=jnp.int32)[None, :, None],
+        lane_place(readout, channels)[None, None, :],
+        1,
+    ).reshape(18 * readout, span)
+    tiles = jnp.transpose(weight_middle, (2, 0, 4, 1, 3)).reshape(3, 3, 1, channels, 3, 1, channels)
+    tiles = jnp.broadcast_to(tiles, (3, 3, 1, channels, 3, held, channels))
+    tiles = tiles.reshape(3, 3, 1, channels, 3 * group)
+    middle_table = banded(
+        tiles,
+        jnp.arange(window // channels, dtype=jnp.int32)[None, :, None, None] - reach,
+        jnp.tile(lane_place(held, channels), 3)[None, None, None, :],
+        1,
+    ).reshape(3 * window, 3 * group)
+    tiles = jnp.transpose(weight_last, (2, 4, 0, 1, 3)).reshape(3, 1, channels, 18, 1)
+    tiles = jnp.broadcast_to(tiles, (3, 1, channels, 18, readout)).reshape(
+        3, 1, channels, 18 * readout
+    )
+    last_table = banded(
+        tiles,
+        jnp.arange(readout, dtype=jnp.int32)[:, None, None],
+        jnp.tile(jnp.arange(readout, dtype=jnp.int32), 18)[None, None, :],
+        1,
+    ).reshape(span, 18 * readout)
+
+    features = with_halo(prior_image.astype(jnp.bfloat16), 3)
+    rim = jnp.zeros_like(features[:, :1])
+    features = jnp.concatenate(
+        [
+            jnp.concatenate([rim, features[:, :-1]], axis=1),
+            features,
+            jnp.concatenate([features[:, 1:], rim], axis=1),
+        ],
+        axis=2,
+    )
+    total = own_rows * lax.axis_size("slab") * lax.axis_size("coil")
+    first = lax.axis_index(axes) * own_rows
+    places = jnp.stack([first, jnp.asarray(total)]).astype(jnp.int32)
+    vmem = pl.BlockSpec(memory_space=pltpu.VMEM)
+    flops = 2 * own_rows * planes * (
+        features.shape[2] * 3 * span * 3 // 2 + 9 * span * 512 * 5 // 4 + span * 18 * readout * 5 // 4
+    )
+    return pl.pallas_call(
+        functools.partial(denoise_kernel, group),
+        in_specs=[pl.BlockSpec(memory_space=pltpu.SMEM)] + [vmem] * 8,
+        out_specs=vmem,
+        out_shape=jax.ShapeDtypeStruct(prior_image.shape, jnp.float32),
+        scratch_shapes=[
+            pltpu.VMEM((own_rows + 4, planes, span + 2 * edge), jnp.bfloat16),
+            pltpu.VMEM((own_rows + 2, planes, span), jnp.bfloat16),
+            pltpu.VMEM((own_rows + 2, planes, 18 * readout), jnp.float32),
+        ],
+        compiler_params=pltpu.CompilerParams(vmem_limit_bytes=56 * 1024 * 1024),
+        cost_estimate=pl.CostEstimate(
+            flops=int(flops), bytes_accessed=16 * 1024 * 1024, transcendentals=0
+        ),
+        name="denoise",
+    )(
+        places,
+        features,
+        prior_image,
+        first_table,
+        jnp.tile(bias_first, readout)[None, :],
+        middle_table,
+        jnp.tile(bias_middle, readout)[None, :],
+        last_table,
+        jnp.repeat(bias_last, readout)[None, :],
+    )
 
 
 def table_parts(table):

time: 608 us -> 267 us (0.44)
  local copies, waits for them, and re-layouts: 197 us -> 37.9 us
  matrix products: 150 us -> 0 us
  Pallas kernels: 70.9 us -> 120 us
  waiting for transfers between devices: 63.1 us -> 21 us
  starting transfers between devices: 53.7 us -> 29.8 us
  other arithmetic: 27.1 us -> 16.7 us
    slice x11 -> x17, local copies, waits for them, and re-layouts: 154 us -> 3.21 us  [the longest x15 2.31 us: banded(): result = jnp.where(inner - outer + offset == tap, tiles[tap], result)]
    dot_general x27 -> x0, matrix products: 150 us -> none  [convolve_layer(): jnp.einsum('oc,ycn->yon', kernel, stacked, preferred_element_type=jnp.flo...]
    pallas_call x0 -> x1, Pallas kernels: none -> 48.9 us  [denoise(): pl.pallas_call(functools.partial(denoise_kernel, group), in_specs=[pl.Blo...]
    ppermute x6 -> x2, waiting for transfers between devices: 30.1 us -> 0.01 us  [the longest x1 0.01 us: with_halo(): below.append(lax.ppermute(head, axes, [(i + hop, i) for i in range(ends)]))]
    ppermute x6 -> x2, starting transfers between devices: 17.5 us -> 4.96 us  [the longest x1 3.67 us: with_halo(): lax.ppermute(tail, axes, [(i, i + hop) for i in range(ends)])]
    all_to_all x5, waiting for transfers between devices: 33 us -> 20.9 us  [exchange(): return lax.all_to_all(blocks, axis, split_axis=0, concat_axis=0, tiled=True)]
    select_n x6 -> x5, other arithmetic: 21.8 us -> 10.3 us  [the longest x3 10.3 us: banded(): result = jnp.where(inner - outer + offset == tap, tiles[tap], result)]
    all_to_all x5, starting transfers between devices: 36.2 us -> 24.8 us  [exchange(): return lax.all_to_all(blocks, axis, split_axis=0, concat_axis=0, tiled=True)]
  transfers between devices with their start and end apart: 11 -> 7, of which waited for: 5 -> 2; matrix products, arithmetic and copies ran while one was open for 26% -> 15% of each run, Pallas kernels for 7% -> 35%
where the time goes in v2:
time: 267 us; the launch traced here: 265 us
  Pallas kernels  120 us (45%)
  local copies, waits for them, and re-layouts  37.9 us (14%)
  blocking collectives  30.4 us (11%)
  starting transfers between devices  29.8 us (11%)
  waiting for transfers between devices  21 us (8%)
  other arithmetic  16.7 us (6%)
  between operations  9.92 us (4%)
    pallas_call x1, Pallas kernels, denoise(): pl.pallas_call(functools.partial(denoise_kernel, group), in_specs=[pl.Blo...  48.9 us
    pallas_call x1, Pallas kernels, second_call(): pl.pallas_call(second_kernel, grid=(x_count, maps.shape[1]), in_specs=[ma...  28.5 us
    pallas_call x1, Pallas kernels, first_call(): pl.pallas_call(first_kernel, grid=(x_count, maps.shape[1]), in_specs=[map...  28 us
    all_to_all x5, starting transfers between devices, exchange(): return lax.all_to_all(blocks, axis, split_axis=0, concat_axis=0, tiled=True)  24.8 us
    all_to_all x1, blocking collectives, exchange(): return lax.all_to_all(blocks, axis, split_axis=0, concat_axis=0, tiled=True)  24.8 us
    all_to_all x5, waiting for transfers between devices, exchange(): return lax.all_to_all(blocks, axis, split_axis=0, concat_axis=0, tiled=True)  20.9 us
    unnamed x46, local copies, waits for them, and re-layouts  16.8 us
    pallas_call x1, Pallas kernels, adjoint_call(): pl.pallas_call(adjoint_kernel, grid=(x_count, coils), in_specs=[spectra_s...  14.4 us
  transfers between devices with their start and end apart: 7, of which 2 were waited for; matrix products, arithmetic and copies ran while one was open for 15% of the time, Pallas kernels for 35%

profile of v2, /device:TPU:0, one launch (start us, length us, event | category | flops | bytes accessed | tf_op | source)
XLA Modules:
  0.0 265.4 jit_solution(7706890394549299812)
XLA Ops:
  0.6 3.3 %copy.46 = bf16[1,64,128,128]{2,1,3,0:T(8,128)(2,1)S(1)} copy(bf16[1,64,128,128]{3,2,1,0:T(8,128)(2,1)} %param.19) | data formatting | bytes 4194304 | tf_op args[1]
  3.9 1.7 copy.47
  5.6 7.3 %all-to-all-start = ((bf16[32,2,2,64,128]{4,3,2,1,0:T(8,128)(2,1)}), bf16[32,2,2,64,128]{4,3,2,1,0:T(8,128)(2,1)S(1)}, u32[]{:S(2)}, u32[]{:S(2)}) async-start(bf16[32,2,2,64,128]{4,3,2,1,0:T(8,128)(2,1)} %copy.47), calls=%async_computation | async-start | bytes 4194304 | tf_op jit(solution)/shard_map/all_to_all | solution.py:548
  13.7 3.7 %collective-permute-start = (bf16[3,128,128]{2,1,0:T(8,128)(2,1)}, bf16[3,128,128]{2,1,0:T(8,128)(2,1)S(1)}, u32[]{:S(2)}, u32[]{:S(2)}) collective-permute-start(bf16[3,128,128]{2,1,0:T(8,128)(2,1)} %get-tuple-element.18), channel_id=1, source_target_pairs={{0,1},{1,2},{2,3},{3,4},{4,5},{5,6},{6,7},{7,8},{8,9},{9,10},{10,1... | collective-permute-start | bytes 294920 | tf_op jit(solution)/shard_map/ppermute | solution.py:28
  17.4 1.3 collective-permute-start.1
  30.5 4.6 %copy.48 = bf16[1,32,256,128]{2,1,3,0:T(8,128)(2,1)} copy(bf16[1,32,256,128]{3,2,1,0:T(8,128)(2,1)} %param.20) | data formatting | bytes 4194304 | tf_op args[2]
  35.1 3.2 %copy.49 = bf16[32,2,2,32,256]{4,3,2,1,0:T(8,128)(2,1)} copy(bf16[32,2,2,32,256]{4,3,2,0,1:T(8,128)(2,1)} %bitcast.60) | data formatting | bytes 4194304 | tf_op jit(solution)/shard_map/transpose | solution.py:554
  38.5 2.0 select_select_fusion.2
  40.9 4.1 %select_select_fusion.1 = bf16[18,64,2048]{2,1,0:T(8,128)(2,1)} fusion(pred[64,2048]{1,0:T(8,128)(4,1)S(1)} %get-tuple-element.33, pred[64,2048]{1,0:T(8,128)(4,1)S(1)} %get-tuple-element.34, pred[64,2048]{1,0:T(8,128)(4,1)S(1)} %get-tuple-element.32, bf16[18,2048]{1,0:T(8,128)(2,1)S(1)} %copy-done.11, bf16[18,2048]{1,0:T(8,128)(2,1)S(1)} %copy-done.10, ...), kind=kLoop, calls=%fused_computation.1 | loop fusion | flops 7077888 | bytes 5332992 | tf_op jit(solution)/shard_map/jit(_where)/select_n | solution.py:150
  45.0 4.2 %select_select_fusion = bf16[64,32,1152]{2,1,0:T(8,128)(2,1)} fusion(pred[64,1152]{1,0:T(8,128)(4,1)S(1)} %get-tuple-element.30, pred[64,1152]{1,0:T(8,128)(4,1)S(1)} %get-tuple-element.31, pred[64,1152]{1,0:T(8,128)(4,1)S(1)} %get-tuple-element.29, bf16[32,1152]{1,0:T(8,128)(2,1)S(1)} %copy-done.14, bf16[32,1152]{1,0:T(8,128)(2,1)S(1)} %copy-done.13, ...), kind=kLoop, calls=%fused_computation | loop fusion | flops 7077888 | bytes 5160960 | tf_op jit(solution)/shard_map/jit(_where)/select_n | solution.py:150
  49.9 14.2 %all-to-all-done = bf16[32,2,2,64,128]{4,3,2,1,0:T(8,128)(2,1)S(1)} async-done(((bf16[32,2,2,64,128]{4,3,2,1,0:T(8,128)(2,1)}), bf16[32,2,2,64,128]{4,3,2,1,0:T(8,128)(2,1)S(1)}, u32[]{:S(2)}, u32[]{:S(2)}) %all-to-all-start) | async-done | bytes 2097184 | tf_op jit(solution)/shard_map/all_to_all | solution.py:548
  64.0 3.7 %all-to-all-start.1 = ((bf16[32,2,2,32,256]{4,3,2,1,0:T(8,128)(2,1)}), bf16[32,2,2,32,256]{4,3,2,1,0:T(8,128)(2,1)}, u32[]{:S(2)}, u32[]{:S(2)}) async-start(bf16[32,2,2,32,256]{4,3,2,1,0:T(8,128)(2,1)} %copy.49), calls=%async_computation.1 | async-start | bytes 4194304 | tf_op jit(solution)/shard_map/all_to_all | solution.py:548
  68.9 2.3 fusion.2.features_ref
  71.2 48.9 %denoise.1 = f32[8,128,128]{2,1,0:T(8,128)} custom-call(s32[2]{0:T(128)} %pad_add_fusion.first_ref, bf16[14,128,384]{2,1,0:T(8,128)(2,1)} %fusion.2.features_ref, f32[8,128,128]{2,1,0:T(8,128)} %prior_ref.1, bf16[1152,2048]{1,0:T(8,128)(2,1)} %bitcast.62, f32[1,2048]{1,0:T(1,128)} %broadcast_in_dim_tile.8.bias_first_ref, bf16[1536,768]{1,0:T(8,128)(2,1)} %bitcast.63, ...), custom_call_target="tpu_custom_call" | custom-call | flops 37446746112 | bytes 16777216 | tf_op jit(solution)/shard_map/denoise/pallas_call | solution.py:215
  120.1 1.3 copy.57
  122.4 5.6 %all-to-all-start.2 = ((f32[32,2,2,8,128]{4,3,2,1,0:T(8,128)}), f32[32,2,2,8,128]{4,3,2,1,0:T(8,128)S(1)}, u32[]{:S(2)}, u32[]{:S(2)}) async-start(f32[32,2,2,8,128]{4,3,2,1,0:T(8,128)} %bitcast.64), calls=%async_computation.2 | async-start | bytes 1048576 | tf_op jit(solution)/shard_map/all_to_all | solution.py:548
  128.7 5.6 %all_gather.3 = bf16[128,256]{1,0:T(8,128)(2,1)S(1)} all-gather(bf16[32,256]{1,0:T(8,128)(2,1)S(1)} %convert_element_type.11), channel_id=1, replica_groups=mesh['slab'=4,'coil'=8] {'slab'}, dimensions={0}, use_global_device_ids=true | all-gather | bytes 81920 | tf_op jit(solution)/shard_map/all_gather | solution.py:603
  136.9 14.4 %adjoint.1.adjoint_ref = f32[32,2,2,8,128]{4,3,2,1,0:T(8,128)S(1)} custom-call(bf16[4,8,2,2,32,256]{5,4,3,2,1,0:T(8,128)(2,1)} %bitcast.5.kspace_ref, bf16[4,8,2,2,64,128]{5,4,3,2,1,0:T(8,128)(2,1)S(1)} %bitcast.56, f32[256,128]{1,0:T(8,128)S(1)} %convert_bitcast_fusion.mask_ref, bf16[512,768]{1,0:T(8,128)(2,1)S(1)} %copy-done, bf16[768,256]{1,0:T(8,128)(2,1)S(1)} %copy-done.1), custom_call_target="tpu_custom_call" | custom-call | flops 4831838208 | bytes 2097152 | tf_op jit(solution)/shard_map/adjoint/pallas_call | solution.py:481
  155.1 28.0 %first_product.1 = (f32[32,2,2,8,128]{4,3,2,1,0:T(8,128)}, f32[32,2,2,8,128]{4,3,2,1,0:T(8,128)}) custom-call(bf16[4,8,2,2,64,128]{5,4,3,2,1,0:T(8,128)(2,1)S(1)} %bitcast.57, f32[32,2,2,8,128]{4,3,2,1,0:T(8,128)S(1)} %copy-done.7, f32[32,2,2,8,128]{4,3,2,1,0:T(8,128)S(1)} %all-to-all-done.2.denoised_ref, f32[256,128]{1,0:T(8,128)S(1)} %convert_bitcast_fusion.mask_ref, ...), custom_call_target="tpu_custom_call" | custom-call | flops 9663676416 | bytes 2097152 | tf_op jit(solution)/shard_map/first_product/pallas_call | solution.py:498
  183.1 5.6 %all-to-all-start.4 = ((f32[32,2,2,8,128]{4,3,2,1,0:T(8,128)}), f32[32,2,2,8,128]{4,3,2,1,0:T(8,128)S(1)}, u32[]{:S(2)}, u32[]{:S(2)}) async-start(f32[32,2,2,8,128]{4,3,2,1,0:T(8,128)} %get-tuple-element.6.right_ref), calls=%async_computation.4 | async-start | bytes 1048576 | tf_op jit(solution)/shard_map/all_to_all | solution.py:548
  190.8 28.5 %second_product.1 = (f32[32,4,8,128]{3,2,1,0:T(8,128)S(1)}, f32[8,128]{1,0:T(8,128)S(1)}) custom-call(bf16[4,8,2,2,64,128]{5,4,3,2,1,0:T(8,128)(2,1)S(1)} %bitcast.58, f32[32,2,2,8,128]{4,3,2,1,0:T(8,128)} %get-tuple-element.6.right_ref, f32[32,2,2,8,128]{4,3,2,1,0:T(8,128)} %get-tuple-element.7.field_ref, f32[256,128]{1,0:T(8,128)S(1)} %convert_bitcast_fusion.mask_ref, ...), custom_call_target="tpu_custom_call" | custom-call | flops 9663676416 | bytes 2097152 | tf_op jit(solution)/shard_map/second_product/pallas_call | solution.py:524
  219.3 24.8 %all_to_all.30 = f32[32,5,8,128]{3,2,1,0:T(8,128)S(1)} all-to-all(f32[32,5,8,128]{3,2,1,0:T(8,128)S(1)} %pad_maximum_fusion), channel_id=1, replica_groups=mesh['slab'=4,'coil'=8] {'slab','coil'}, dimensions={0} | all-to-all | bytes 1310720 | tf_op jit(solution)/shard_map/all_to_all | solution.py:548
  244.1 2.6 all-to-all-start.5
  256.3 6.8 %all-to-all-done.5 = f32[32,2,2,8,128]{4,3,2,1,0:T(8,128)S(1)} async-done(((f32[32,2,2,8,128]{4,3,2,1,0:T(8,128)}), f32[32,2,2,8,128]{4,3,2,1,0:T(8,128)S(1)}, u32[]{:S(2)}, u32[]{:S(2)}) %all-to-all-start.5) | async-done | bytes 524320 | tf_op jit(solution)/shard_map/all_to_all | solution.py:548
  (115 shorter events, 27.9 us)
Async XLA Ops:
  5.6 7.3 %copy-start.8 = (f32[8,128,128]{2,1,0:T(8,128)S(1)}, f32[8,128,128]{2,1,0:T(8,128)}, u32[]{:S(2)}) copy-start(f32[8,128,128]{2,1,0:T(8,128)} %prior_ref.1) | copy-start | bytes 1572868
  5.6 13.1 %copy-start.16 = (bf16[3,3,3,32,2]{3,4,2,1,0:T(2,128)(2,1)S(1)}, bf16[3,3,3,32,2]{3,4,2,1,0:T(2,128)(2,1)}, u32[]{:S(2)}) copy-start(bf16[3,3,3,32,2]{3,4,2,1,0:T(2,128)(2,1)} %param.22) | copy-start | bytes 10372
  5.6 58.4 %all-to-all-start = ((bf16[32,2,2,64,128]{4,3,2,1,0:T(8,128)(2,1)}), bf16[32,2,2,64,128]{4,3,2,1,0:T(8,128)(2,1)S(1)}, u32[]{:S(2)}, u32[]{:S(2)}) async-start(bf16[32,2,2,64,128]{4,3,2,1,0:T(8,128)(2,1)} %copy.47), calls=%async_computation | async-start | bytes 4194304 | tf_op jit(solution)/shard_map/all_to_all | solution.py:548
  12.9 8.8 %copy-start.17 = (bf16[3,3,3,2,32]{4,3,2,1,0:T(2,128)(2,1)S(1)}, bf16[3,3,3,2,32]{4,3,2,1,0:T(2,128)(2,1)}, u32[]{:S(2)}) copy-start(bf16[3,3,3,2,32]{4,3,2,1,0:T(2,128)(2,1)} %param.26) | copy-start | bytes 10372
  12.9 12.2 %copy-start.15 = (bf16[3,3,3,32,32]{4,3,2,1,0:T(8,128)(2,1)S(1)}, bf16[3,3,3,32,32]{4,3,2,1,0:T(8,128)(2,1)}, u32[]{:S(2)}) copy-start(bf16[3,3,3,32,32]{4,3,2,1,0:T(8,128)(2,1)} %param.24) | copy-start | bytes 165892
  13.7 54.1 %collective-permute-start = (bf16[3,128,128]{2,1,0:T(8,128)(2,1)}, bf16[3,128,128]{2,1,0:T(8,128)(2,1)S(1)}, u32[]{:S(2)}, u32[]{:S(2)}) collective-permute-start(bf16[3,128,128]{2,1,0:T(8,128)(2,1)} %get-tuple-element.18), channel_id=1, source_target_pairs={{0,1},{1,2},{2,3},{3,4},{4,5},{5,6},{6,7},{7,8},{8,9},{9,10},{10,1... | collective-permute-start | bytes 294920 | tf_op jit(solution)/shard_map/ppermute | solution.py:28
  17.4 50.4 %collective-permute-start.1 = (bf16[3,128,128]{2,1,0:T(8,128)(2,1)}, bf16[3,128,128]{2,1,0:T(8,128)(2,1)}, u32[]{:S(2)}, u32[]{:S(2)}) collective-permute-start(bf16[3,128,128]{2,1,0:T(8,128)(2,1)} %get-tuple-element.19), channel_id=1, source_target_pairs={{1,0},{2,1},{3,2},{4,3},{5,4},{6,5},{7,6},{8,7},{9,8},{10,9},{11,1... | collective-permute-start | bytes 294920 | tf_op jit(solution)/shard_map/ppermute | solution.py:29
  25.9 2.6 copy-start.18
  25.9 3.3 %copy-start.19 = (f32[32]{0:T(128)S(1)}, f32[32]{0:T(128)}, u32[]{:S(2)}) copy-start(f32[32]{0:T(128)} %param.25) | copy-start | bytes 388
  25.9 4.0 %copy-start.20 = (f32[2]{0:T(128)S(1)}, f32[2]{0:T(128)}, u32[]{:S(2)}) copy-start(f32[2]{0:T(128)} %param.27) | copy-start | bytes 28
  38.3 2.5 copy-start.9
  38.3 2.5 copy-start.10
  38.3 2.5 copy-start.11
  40.9 4.1 %copy-start.12 = (bf16[32,1152]{1,0:T(8,128)(2,1)S(1)}, bf16[32,1152]{1,0:T(8,128)(2,1)}, u32[]{:S(2)}) copy-start(bf16[32,1152]{1,0:T(8,128)(2,1)} %broadcast_in_dim.204) | copy-start | bytes 221188
  40.9 4.1 %copy-start.13 = (bf16[32,1152]{1,0:T(8,128)(2,1)S(1)}, bf16[32,1152]{1,0:T(8,128)(2,1)}, u32[]{:S(2)}) copy-start(bf16[32,1152]{1,0:T(8,128)(2,1)} %broadcast_in_dim.208) | copy-start | bytes 221188
  40.9 4.1 %copy-start.14 = (bf16[32,1152]{1,0:T(8,128)(2,1)S(1)}, bf16[32,1152]{1,0:T(8,128)(2,1)}, u32[]{:S(2)}) copy-start(bf16[32,1152]{1,0:T(8,128)(2,1)} %broadcast_in_dim.212) | copy-start | bytes 221188
  64.0 58.3 %all-to-all-start.1 = ((bf16[32,2,2,32,256]{4,3,2,1,0:T(8,128)(2,1)}), bf16[32,2,2,32,256]{4,3,2,1,0:T(8,128)(2,1)}, u32[]{:S(2)}, u32[]{:S(2)}) async-start(bf16[32,2,2,32,256]{4,3,2,1,0:T(8,128)(2,1)} %copy.49), calls=%async_computation.1 | async-start | bytes 4194304 | tf_op jit(solution)/shard_map/all_to_all | solution.py:548
  120.1 15.7 %copy-start = (bf16[512,768]{1,0:T(8,128)(2,1)S(1)}, bf16[512,768]{1,0:T(8,128)(2,1)}, u32[]{:S(2)}) copy-start(bf16[512,768]{1,0:T(8,128)(2,1)} %constant.71.clone.rows_ref) | copy-start | bytes 2359300
  122.4 29.7 %all-to-all-start.2 = ((f32[32,2,2,8,128]{4,3,2,1,0:T(8,128)}), f32[32,2,2,8,128]{4,3,2,1,0:T(8,128)S(1)}, u32[]{:S(2)}, u32[]{:S(2)}) async-start(f32[32,2,2,8,128]{4,3,2,1,0:T(8,128)} %bitcast.64), calls=%async_computation.2 | async-start | bytes 1048576 | tf_op jit(solution)/shard_map/all_to_all | solution.py:548
  135.9 1.0 copy-start.1
  154.1 1.0 copy-start.7
  183.1 36.2 %all-to-all-start.4 = ((f32[32,2,2,8,128]{4,3,2,1,0:T(8,128)}), f32[32,2,2,8,128]{4,3,2,1,0:T(8,128)S(1)}, u32[]{:S(2)}, u32[]{:S(2)}) async-start(f32[32,2,2,8,128]{4,3,2,1,0:T(8,128)} %get-tuple-element.6.right_ref), calls=%async_computation.4 | async-start | bytes 1048576 | tf_op jit(solution)/shard_map/all_to_all | solution.py:548
  188.8 1.0 copy-start.3
  244.1 19.0 %all-to-all-start.5 = ((f32[32,2,2,8,128]{4,3,2,1,0:T(8,128)}), f32[32,2,2,8,128]{4,3,2,1,0:T(8,128)S(1)}, u32[]{:S(2)}, u32[]{:S(2)}) async-start(f32[32,2,2,8,128]{4,3,2,1,0:T(8,128)} %get-tuple-element.7.field_ref), calls=%async_computation.5 | async-start | bytes 1048576 | tf_op jit(solution)/shard_map/all_to_all | solution.py:548
  (4 other events, 3.8 us)

commit v3 on v2

--- a/solution.py
+++ b/solution.py
@@ -253,25 +253,23 @@
     return np.cos(angles) * scale, np.sin(angles) * scale
 
 
-def row_table(length):
+def turn_block(length):
     cos_part, sin_part = dft_parts(length)
-    high, low = table_parts(np.concatenate([cos_part, sin_part], axis=0))
-    return np.concatenate([high, low, high], axis=1)
-
-
-def plane_table(length, inverse):
-    cos_part, sin_part = dft_parts(length)
-    if inverse:
-        sin_part = -sin_part
-    table = np.concatenate(
+    return np.concatenate(
         [
-            np.concatenate([cos_part, -sin_part], axis=1),
-            np.concatenate([sin_part, cos_part], axis=1),
+            np.concatenate([cos_part, sin_part], axis=1),
+            np.concatenate([-sin_part, cos_part], axis=1),
         ],
         axis=0,
     )
-    high, low = table_parts(table)
-    return np.concatenate([high, low, high], axis=0)
+
+
+def dft_table(rows, planes):
+    rows_high, rows_low = table_parts(turn_block(rows))
+    planes_parts = np.concatenate(table_parts(turn_block(planes).T), axis=0)
+    short = max(2 * rows - planes_parts.shape[0], 0)
+    planes_parts = np.pad(planes_parts, ((0, short), (0, 0)))
+    return np.concatenate([rows_high, rows_low, planes_parts], axis=1)
 
 
 def value_parts(value):
@@ -280,28 +278,54 @@
     return high, low
 
 
-def along_planes(value, table):
-    high, low = value_parts(value)
-    return jnp.dot(
+def tables_of(ref, rows, planes):
+    high, low = ref[:, : 2 * rows], ref[:, 2 * rows : 4 * rows]
+    row_table = jnp.concatenate([high, low, high], axis=1)
+    high, low = ref[: 2 * planes, 4 * rows :], ref[2 * planes : 4 * planes, 4 * rows :]
+    return row_table, jnp.concatenate([high, low, high], axis=0)
+
+
+def along_planes(fields, table):
+    rows, planes = fields[0][0].shape
+    stacked = jnp.concatenate([jnp.concatenate(field, axis=1) for field in fields], axis=0)
+    high, low = value_parts(stacked)
+    moved = jnp.dot(
         jnp.concatenate([high, high, low], axis=1), table, preferred_element_type=jnp.float32
     )
-
-
-def along_rows(table, value):
-    high, low = value_parts(value)
-    return jnp.dot(
+    return [
+        (
+            moved[index * rows : (index + 1) * rows, :planes],
+            moved[index * rows : (index + 1) * rows, planes:],
+        )
+        for index in range(len(fields))
+    ]
+
+
+def side_by_side(fields):
+    return jnp.concatenate(
+        [jnp.concatenate([field[part] for field in fields], axis=1) for part in range(2)], axis=0
+    )
+
+
+def along_rows(table, fields):
+    rows, planes = fields[0][0].shape
+    high, low = value_parts(side_by_side(fields))
+    moved = jnp.dot(
         table, jnp.concatenate([high, high, low], axis=0), preferred_element_type=jnp.float32
     )
-
-
-def rows_combined(stacked, inverse):
-    rows = stacked.shape[0] // 2
-    half = stacked.shape[1] // 2
-    cos_real, cos_imag = stacked[:rows, :half], stacked[:rows, half:]
-    sin_real, sin_imag = stacked[rows:, :half], stacked[rows:, half:]
-    if inverse:
-        return cos_real - sin_imag, cos_imag + sin_real
-    return cos_real + sin_imag, cos_imag - sin_real
+    return apart(moved, len(fields))
+
+
+def apart(moved, count):
+    rows = moved.shape[0] // 2
+    planes = moved.shape[1] // count
+    return [
+        (
+            moved[:rows, index * planes : (index + 1) * planes],
+            moved[rows:, index * planes : (index + 1) * planes],
+        )
+        for index in range(count)
+    ]
 
 
 def plane_of(ref, part):
@@ -309,43 +333,91 @@
     return value.reshape(value.shape[0] * value.shape[1], value.shape[2])
 
 
-def map_of(ref, part):
-    value = ref[:, 0, part, 0]
-    return value.reshape(value.shape[0] * value.shape[1], value.shape[2]).astype(jnp.float32)
-
-
-def normal_product(map_real, map_imag, real, imag, mask, rows, planes, inverse_planes):
-    half = real.shape[1]
-    coil_real = map_real * real - map_imag * imag
-    coil_imag = map_real * imag + map_imag * real
-    field = along_planes(jnp.concatenate([coil_real, coil_imag], axis=1), planes)
-    real, imag = rows_combined(along_rows(rows, field), False)
-    spectrum = jnp.concatenate([real * mask, imag * mask], axis=1)
-    real, imag = rows_combined(along_rows(rows, spectrum), True)
-    field = along_planes(jnp.concatenate([real, imag], axis=1), inverse_planes)
-    real, imag = field[:, :half], field[:, half:]
-    return map_real * real + map_imag * imag, map_real * imag - map_imag * real
-
-
-def adjoint_kernel(kspace_ref, maps_ref, mask_ref, rows_ref, inverse_ref, out_ref):
+def coil_plane(ref, coil, part):
+    value = ref[:, coil, part, 0]
+    return value.reshape(value.shape[0] * value.shape[1], value.shape[2])
+
+
+def map_of(ref, coil):
+    return [coil_plane(ref, coil, part).astype(jnp.float32) for part in range(2)]
+
+
+def image_sums(maps, fields):
+    sums = None
+    for (map_real, map_imag), (real, imag) in zip(maps, fields):
+        terms = (map_real * real - map_imag * imag, -(map_real * imag + map_imag * real))
+        sums = terms if sums is None else (sums[0] + terms[0], sums[1] + terms[1])
+    return sums
+
+
+def units_of(ref):
+    count = ref.shape[1]
+    held = 2 if count % 2 == 0 else 1
+    return [tuple(range(first, first + held)) for first in range(0, count, held)]
+
+
+def normal_sums(maps_ref, real, imag, mask, tables):
+    row_table, plane_table = tables
+    total = None
+    for unit in units_of(maps_ref):
+        maps = [map_of(maps_ref, coil) for coil in unit]
+        fields = [
+            (map_real * real - map_imag * imag, map_real * imag + map_imag * real)
+            for map_real, map_imag in maps
+        ]
+        fields = along_rows(row_table, along_planes(fields, plane_table))
+        fields = [(real_part * mask, imag_part * -mask) for real_part, imag_part in fields]
+        fields = along_planes(along_rows(row_table, fields), plane_table)
+        sums = image_sums(maps, fields)
+        total = sums if total is None else (total[0] + sums[0], total[1] + sums[1])
+    return total
+
+
+def adjoint_kernel(kspace_ref, maps_ref, mask_ref, table_ref, out_ref):
     mask = mask_ref[...]
-    parts = []
-    for part in range(2):
-        parts.append((jnp.transpose(map_of(kspace_ref, part)) * mask).astype(jnp.bfloat16))
-    spectrum = jnp.concatenate(parts, axis=1)
-    length = spectrum.shape[0]
-    stacked = jnp.dot(
-        rows_ref[:, : 2 * length],
-        jnp.concatenate([spectrum, spectrum], axis=0),
-        preferred_element_type=jnp.float32,
-    )
-    real, imag = rows_combined(stacked, True)
-    half = real.shape[1]
-    field = along_planes(jnp.concatenate([real, imag], axis=1), inverse_ref[...])
-    real, imag = field[:, :half], field[:, half:]
-    map_real, map_imag = map_of(maps_ref, 0), map_of(maps_ref, 1)
+    rows, planes = mask.shape
+    row_table, plane_table = tables_of(table_ref, rows, planes)
+    total = None
+    for unit in units_of(maps_ref):
+        spectra = []
+        for coil in unit:
+            real, imag = (
+                jnp.transpose(coil_plane(kspace_ref, coil, part).astype(jnp.float32))
+                for part in range(2)
+            )
+            spectra.append((real * mask, imag * -mask))
+        spectrum = side_by_side(spectra).astype(jnp.bfloat16)
+        moved = jnp.dot(
+            row_table[:, : 4 * rows],
+            jnp.concatenate([spectrum, spectrum], axis=0),
+            preferred_element_type=jnp.float32,
+        )
+        fields = along_planes(apart(moved, len(unit)), plane_table)
+        sums = image_sums([map_of(maps_ref, coil) for coil in unit], fields)
+        total = sums if total is None else (total[0] + sums[0], total[1] + sums[1])
     shape = out_ref.shape[0], out_ref.shape[3], out_ref.shape[4]
-    sums = (map_real * real + map_imag * imag, map_real * imag - map_imag * real)
+
+    @pl.when(pl.program_id(1) == 0)
+    def _():
+        for part in range(2):
+            out_ref[:, part, 0] = total[part].reshape(shape)
+
+    @pl.when(pl.program_id(1) > 0)
+    def _():
+        for part in range(2):
+            out_ref[:, part, 0] += total[part].reshape(shape)
+
+
+def first_kernel(maps_ref, field_ref, mask_ref, table_ref, out_ref):
+    mask = mask_ref[...]
+    sums = normal_sums(
+        maps_ref,
+        plane_of(field_ref, 0),
+        plane_of(field_ref, 1),
+        mask,
+        tables_of(table_ref, *mask.shape),
+    )
+    shape = out_ref.shape[0], out_ref.shape[3], out_ref.shape[4]
 
     @pl.when(pl.program_id(1) == 0)
     def _():
@@ -358,55 +430,29 @@
             out_ref[:, part, 0] += sums[part].reshape(shape)
 
 
-def first_kernel(
-    maps_ref, adjoint_ref, denoised_ref, mask_ref, rows_ref, planes_ref, inverse_ref, right_ref, out_ref
-):
-    @pl.when(pl.program_id(1) == 0)
-    def _():
-        right = adjoint_ref[...] + penalty * denoised_ref[...]
-        right_ref[...] = right
-        out_ref[...] = jnp.zeros_like(out_ref)
-
-    sums = normal_product(
-        map_of(maps_ref, 0),
-        map_of(maps_ref, 1),
-        plane_of(right_ref, 0),
-        plane_of(right_ref, 1),
-        mask_ref[...],
-        rows_ref[...],
-        planes_ref[...],
-        inverse_ref[...],
-    )
-    shape = out_ref.shape[0], out_ref.shape[3], out_ref.shape[4]
-    for part in range(2):
-        out_ref[:, part, 0] += sums[part].reshape(shape)
-
-
-def second_kernel(
-    maps_ref, right_ref, field_ref, mask_ref, rows_ref, planes_ref, inverse_ref, out_ref, total_ref
-):
+def second_kernel(maps_ref, right_ref, field_ref, mask_ref, table_ref, out_ref, total_ref):
     x_index = pl.program_id(0)
     x_count = pl.num_programs(0)
     blocks, block_rows, planes = out_ref.shape[0], out_ref.shape[2], out_ref.shape[3]
     shape = blocks, block_rows, planes
+    mask = mask_ref[...]
+    sums = normal_sums(
+        maps_ref,
+        plane_of(field_ref, 0),
+        plane_of(field_ref, 1),
+        mask,
+        tables_of(table_ref, *mask.shape),
+    )
 
     @pl.when(pl.program_id(1) == 0)
     def _():
         for part in range(2):
-            out_ref[:, part * x_count + x_index] = jnp.zeros(shape, jnp.float32)
-
-    sums = normal_product(
-        map_of(maps_ref, 0),
-        map_of(maps_ref, 1),
-        plane_of(field_ref, 0),
-        plane_of(field_ref, 1),
-        mask_ref[...],
-        rows_ref[...],
-        planes_ref[...],
-        inverse_ref[...],
-    )
-    for part in range(2):
-        out_ref[:, part * x_count + x_index] += sums[part].reshape(shape)
+            out_ref[:, part * x_count + x_index] = sums[part].reshape(shape)
+
+    @pl.when(pl.program_id(1) > 0)
+    def _():
+        for part in range(2):
+            out_ref[:, part * x_count + x_index] += sums[part].reshape(shape)
 
     @pl.when(pl.program_id(1) == pl.num_programs(1) - 1)
     def _():
@@ -438,21 +484,27 @@
             total_ref[...] += totals
 
 
-def plan_specs(maps, blocks, block_rows, mask):
-    slabs, coils, _, x_count, slab_rows, planes = maps.shape
-    row_count = slabs * slab_rows
-    maps_spec = pl.BlockSpec(
-        (slabs, 1, 2, 1, slab_rows, planes), lambda x, c: (0, c, 0, x, 0, 0)
-    )
-    field_spec = pl.BlockSpec((blocks, 2, 1, block_rows, planes), lambda x, c: (0, 0, x, 0, 0))
-
-    def whole(shape):
-        return pl.BlockSpec(shape, lambda x, c: (0,) * len(shape))
-
-    rows = row_table(row_count)
-    forward = plane_table(planes, False)
-    inverse = plane_table(planes, True)
-    return maps_spec, field_spec, whole, rows, forward, inverse
+def held_coils(count):
+    return max(size for size in (1, 2, 4) if count % size == 0)
+
+
+def whole(shape):
+    return pl.BlockSpec(shape, lambda x, c: (0,) * len(shape))
+
+
+def maps_spec(maps):
+    slabs, coils, _, _, slab_rows, planes = maps.shape
+    return pl.BlockSpec(
+        (slabs, held_coils(coils), 2, 1, slab_rows, planes), lambda x, c: (0, c, 0, x, 0, 0)
+    )
+
+
+def field_spec(shape):
+    return pl.BlockSpec((shape[0], 2, 1) + shape[3:], lambda x, c: (0, 0, x, 0, 0))
+
+
+def grid_of(maps):
+    return maps.shape[3], maps.shape[1] // held_coils(maps.shape[1])
 
 
 def compute_params():
@@ -466,72 +518,52 @@
     rows = slabs * slab_rows
     per_plane = 2 * 2 * rows * planes * (2 * rows + 2 * planes)
     return pl.CostEstimate(
-        flops=int(coils * x_count * per_plane * passes), bytes_accessed=int(2 * maps.size), transcendentals=0
-    )
-
-
-def adjoint_call(spectra, maps, mask, blocks):
-    slabs, coils, _, x_count, slab_planes, row_count = spectra.shape
-    planes = slabs * slab_planes
-    block_rows = row_count // blocks
-    maps_spec, field_spec, whole, rows, _, inverse = plan_specs(maps, blocks, block_rows, mask)
-    spectra_spec = pl.BlockSpec(
-        (slabs, 1, 2, 1, slab_planes, row_count), lambda x, c: (0, c, 0, x, 0, 0)
-    )
+        flops=int(coils * x_count * per_plane * passes),
+        bytes_accessed=int(2 * maps.size),
+        transcendentals=0,
+    )
+
+
+def adjoint_call(spectra, maps, mask, table, blocks):
+    rows, planes = mask.shape
+    shape = (blocks, 2, maps.shape[3], rows // blocks, planes)
     return pl.pallas_call(
         adjoint_kernel,
-        grid=(x_count, coils),
-        in_specs=[spectra_spec, maps_spec, whole(mask.shape), whole(rows.shape), whole(inverse.shape)],
-        out_specs=field_spec,
-        out_shape=jax.ShapeDtypeStruct((blocks, 2, x_count, block_rows, planes), jnp.float32),
+        grid=grid_of(maps),
+        in_specs=[maps_spec(spectra), maps_spec(maps), whole(mask.shape), whole(table.shape)],
+        out_specs=field_spec(shape),
+        out_shape=jax.ShapeDtypeStruct(shape, jnp.float32),
         compiler_params=compute_params(),
         cost_estimate=product_cost(maps, 3),
         name="adjoint",
-    )(spectra, maps, mask, rows, inverse)
-
-
-def first_call(maps, adjoint, denoised, mask):
-    blocks, _, x_count, block_rows, planes = adjoint.shape
-    maps_spec, field_spec, whole, rows, forward, inverse = plan_specs(
-        maps, blocks, block_rows, mask
-    )
+    )(spectra, maps, mask, table)
+
+
+def first_call(maps, field, mask, table):
     return pl.pallas_call(
         first_kernel,
-        grid=(x_count, maps.shape[1]),
-        in_specs=[
-            maps_spec,
-            field_spec,
-            field_spec,
-            whole(mask.shape),
-            whole(rows.shape),
-            whole(forward.shape),
-            whole(inverse.shape),
-        ],
-        out_specs=[field_spec, field_spec],
-        out_shape=[jax.ShapeDtypeStruct(adjoint.shape, jnp.float32)] * 2,
+        grid=grid_of(maps),
+        in_specs=[maps_spec(maps), field_spec(field.shape), whole(mask.shape), whole(table.shape)],
+        out_specs=field_spec(field.shape),
+        out_shape=jax.ShapeDtypeStruct(field.shape, jnp.float32),
         compiler_params=compute_params(),
         cost_estimate=product_cost(maps, 6),
         name="first_product",
-    )(maps, adjoint, denoised, mask, rows, forward, inverse)
-
-
-def second_call(maps, right, field, mask):
+    )(maps, field, mask, table)
+
+
+def second_call(maps, right, field, mask, table):
     blocks, _, x_count, block_rows, planes = field.shape
-    maps_spec, field_spec, whole, rows, forward, inverse = plan_specs(
-        maps, blocks, block_rows, mask
-    )
     out_shape = (blocks, 2 * x_count, block_rows, planes)
     return pl.pallas_call(
         second_kernel,
-        grid=(x_count, maps.shape[1]),
+        grid=grid_of(maps),
         in_specs=[
-            maps_spec,
-            field_spec,
-            field_spec,
+            maps_spec(maps),
+            field_spec(field.shape),
+            field_spec(field.shape),
             whole(mask.shape),
-            whole(rows.shape),
-            whole(forward.shape),
-            whole(inverse.shape),
+            whole(table.shape),
         ],
         out_specs=[whole(out_shape), whole((8, planes))],
         out_shape=[
@@ -541,7 +573,7 @@
         compiler_params=compute_params(),
         cost_estimate=product_cost(maps, 6),
         name="second_product",
-    )(maps, right, field, mask, rows, forward, inverse)
+    )(maps, right, field, mask, table)
 
 
 def exchange(blocks, axis):
@@ -613,19 +645,21 @@
         blocks = exchange(blocks, "coil").reshape((slabs, coils // slabs) + tail)
         return exchange(blocks, "slab")
 
-    spectra = coils_to_x(kspace[0])
     maps = coils_to_x(coil_maps[0])
+    measured, mask = lax.optimization_barrier((kspace[0], mask))
+    spectra = coils_to_x(measured)
+    table = jnp.asarray(dft_table(sampling.shape[1], planes))
     denoised = denoise(
         prior_image, weight_first, bias_first, weight_middle, bias_middle, weight_last, bias_last
     )
     blocks = x_first(denoised, parts)
     if spread:
         denoised = exchange(blocks, axes)
-        adjoint = adjoint_call(spectra, maps, mask, devices)
-        right, field = first_call(maps, adjoint, denoised, mask)
+        right = adjoint_call(spectra, maps, mask, table, devices) + penalty * denoised
         right_rows = x_last(exchange(right, axes))
+        field = first_call(maps, right, mask, table)
         field_rows = x_last(exchange(field, axes))
-        image, totals = second_call(maps, right, field, mask)
+        image, totals = second_call(maps, right, field, mask, table)
         payload = jnp.concatenate(
             [image, jnp.broadcast_to(totals[None, None], (devices, 1) + totals.shape)], axis=1
         )
@@ -646,11 +680,10 @@
         split = jnp.transpose(mine.reshape(tail + (coils, own_rows, planes)), (2, 0, 1, 3, 4))
         return x_last(exchange(split, "coil"))
 
-    adjoint = lax.psum(adjoint_call(spectra, maps, mask, 1), "slab")
+    adjoint = lax.psum(adjoint_call(spectra, maps, mask, table, 1), "slab")
     right = adjoint + penalty * whole_rows(blocks)
-    _, field = first_call(maps, right, jnp.zeros_like(right), mask)
-    field = lax.psum(field, "slab")
-    image, _ = second_call(maps, right, field, mask)
+    field = lax.psum(first_call(maps, right, mask, table), "slab")
+    image, _ = second_call(maps, right, field, mask, table)
     image = lax.psum(image.reshape(field.shape), "slab")
     squares = lax.psum(
         jnp.stack(

time: 267 us -> 248 us (0.929)
  Pallas kernels: 120 us -> 103 us
  local copies, waits for them, and re-layouts: 37.9 us -> 34.4 us
  waiting for transfers between devices: 21 us -> 24.5 us
    pallas_call x3, Pallas kernels: 70.9 us -> 53.7 us  [the longest x1 21.9 us: first_call(): pl.pallas_call(first_kernel, grid=grid_of(maps), in_specs=[maps_spec(maps...]
    all_to_all x5, waiting for transfers between devices: 20.9 us -> 24.5 us  [exchange(): return lax.all_to_all(blocks, axis, split_axis=0, concat_axis=0, tiled=True)]
    all_to_all x5, starting transfers between devices: 24.8 us -> 21.7 us  [exchange(): return lax.all_to_all(blocks, axis, split_axis=0, concat_axis=0, tiled=True)]
    unnamed x46 -> x36, local copies, waits for them, and re-layouts: 16.8 us -> 14 us
  transfers between devices with their start and end apart: 7 -> 7, of which waited for: 2 -> 3; matrix products, arithmetic and copies ran while one was open for 15% -> 17% of each run, Pallas kernels for 35% -> 33%
where the time goes in v3:
time: 248 us; the launch traced here: 247 us
  Pallas kernels  103 us (42%)
  local copies, waits for them, and re-layouts  34.4 us (14%)
  blocking collectives  30 us (12%)
  starting transfers between devices  27.8 us (11%)
  waiting for transfers between devices  24.5 us (10%)
  other arithmetic  17 us (7%)
  between operations  10.2 us (4%)
    pallas_call x1, Pallas kernels, denoise(): pl.pallas_call(functools.partial(denoise_kernel, group), in_specs=[pl.Blo...  48.9 us
    all_to_all x1, blocking collectives, exchange(): return lax.all_to_all(blocks, axis, split_axis=0, concat_axis=0, tiled=True)  24.6 us
    all_to_all x5, waiting for transfers between devices, exchange(): return lax.all_to_all(blocks, axis, split_axis=0, concat_axis=0, tiled=True)  24.5 us
    pallas_call x1, Pallas kernels, first_call(): pl.pallas_call(first_kernel, grid=grid_of(maps), in_specs=[maps_spec(maps...  21.9 us
    all_to_all x5, starting transfers between devices, exchange(): return lax.all_to_all(blocks, axis, split_axis=0, concat_axis=0, tiled=True)  21.7 us
    pallas_call x1, Pallas kernels, second_call(): pl.pallas_call(second_kernel, grid=grid_of(maps), in_specs=[maps_spec(map...  21.5 us
    unnamed x36, local copies, waits for them, and re-layouts  14 us
    select_n x3, other arithmetic, banded(): result = jnp.where(inner - outer + offset == tap, tiles[tap], result)  10.3 us
  transfers between devices with their start and end apart: 7, of which 3 were waited for; matrix products, arithmetic and copies ran while one was open for 17% of the time, Pallas kernels for 33%

profile of v3, /device:TPU:0, one launch (start us, length us, event | category | flops | bytes accessed | tf_op | source)
XLA Modules:
  0.0 246.6 jit_solution(4824753515822617021)
XLA Ops:
  2.4 4.9 %collective-permute-start = (bf16[3,128,128]{2,1,0:T(8,128)(2,1)}, bf16[3,128,128]{2,1,0:T(8,128)(2,1)S(1)}, u32[]{:S(2)}, u32[]{:S(2)}) collective-permute-start(bf16[3,128,128]{2,1,0:T(8,128)(2,1)} %get-tuple-element.18), channel_id=1, source_target_pairs={{0,1},{1,2},{2,3},{3,4},{4,5},{5,6},{6,7},{7,8},{8,9},{9,10},{10,1... | collective-permute-start | bytes 294920 | tf_op jit(solution)/shard_map/ppermute | solution.py:28
  8.6 3.3 %copy.39 = bf16[1,64,128,128]{2,1,3,0:T(8,128)(2,1)S(1)} copy(bf16[1,64,128,128]{3,2,1,0:T(8,128)(2,1)} %param.12) | data formatting | bytes 4194304 | tf_op args[1]
  11.9 1.7 copy.40
  13.6 7.0 %all-to-all-start = ((bf16[32,2,2,64,128]{4,3,2,1,0:T(8,128)(2,1)}), bf16[32,2,2,64,128]{4,3,2,1,0:T(8,128)(2,1)S(1)}, u32[]{:S(2)}, u32[]{:S(2)}) async-start(bf16[32,2,2,64,128]{4,3,2,1,0:T(8,128)(2,1)} %copy.40), calls=%async_computation | async-start | bytes 4194304 | tf_op jit(solution)/shard_map/all_to_all | solution.py:580
  32.5 4.6 %copy.41 = bf16[1,32,256,128]{2,1,3,0:T(8,128)(2,1)} copy(bf16[1,32,256,128]{3,2,1,0:T(8,128)(2,1)} %param.13) | data formatting | bytes 4194304 | tf_op args[2]
  37.1 5.4 %all_gather.3 = bf16[128,256]{1,0:T(8,128)(2,1)S(1)} all-gather(bf16[32,256]{1,0:T(8,128)(2,1)S(1)} %convert_element_type.12), channel_id=1, replica_groups=mesh['slab'=4,'coil'=8] {'slab'}, dimensions={0}, use_global_device_ids=true | all-gather | bytes 81920 | tf_op jit(solution)/shard_map/all_gather | solution.py:635
  42.7 3.2 %copy.43 = bf16[32,2,2,32,256]{4,3,2,1,0:T(8,128)(2,1)} copy(bf16[32,2,2,32,256]{4,3,2,0,1:T(8,128)(2,1)} %bitcast.60) | data formatting | bytes 4194304 | tf_op jit(solution)/shard_map/transpose | solution.py:586
  46.0 2.0 select_select_fusion.2
  48.4 4.1 %select_select_fusion.1 = bf16[18,64,2048]{2,1,0:T(8,128)(2,1)} fusion(pred[64,2048]{1,0:T(8,128)(4,1)S(1)} %get-tuple-element.33, pred[64,2048]{1,0:T(8,128)(4,1)S(1)} %get-tuple-element.34, pred[64,2048]{1,0:T(8,128)(4,1)S(1)} %get-tuple-element.32, bf16[18,2048]{1,0:T(8,128)(2,1)S(1)} %copy-done.5, bf16[18,2048]{1,0:T(8,128)(2,1)S(1)} %copy-done.4, ...), kind=kLoop, calls=%fused_computation.1 | loop fusion | flops 7077888 | bytes 5332992 | tf_op jit(solution)/shard_map/jit(_where)/select_n | solution.py:150
  52.5 4.2 %select_select_fusion = bf16[64,32,1152]{2,1,0:T(8,128)(2,1)} fusion(pred[64,1152]{1,0:T(8,128)(4,1)S(1)} %get-tuple-element.30, pred[64,1152]{1,0:T(8,128)(4,1)S(1)} %get-tuple-element.31, pred[64,1152]{1,0:T(8,128)(4,1)S(1)} %get-tuple-element.29, bf16[32,1152]{1,0:T(8,128)(2,1)S(1)} %copy-done.8, bf16[32,1152]{1,0:T(8,128)(2,1)S(1)} %copy-done.7, ...), kind=kLoop, calls=%fused_computation | loop fusion | flops 7077888 | bytes 5160960 | tf_op jit(solution)/shard_map/jit(_where)/select_n | solution.py:150
  57.3 13.3 %all-to-all-done = bf16[32,2,2,64,128]{4,3,2,1,0:T(8,128)(2,1)S(1)} async-done(((bf16[32,2,2,64,128]{4,3,2,1,0:T(8,128)(2,1)}), bf16[32,2,2,64,128]{4,3,2,1,0:T(8,128)(2,1)S(1)}, u32[]{:S(2)}, u32[]{:S(2)}) %all-to-all-start) | async-done | bytes 2097184 | tf_op jit(solution)/shard_map/all_to_all | solution.py:580
  70.6 3.7 %all-to-all-start.1 = ((bf16[32,2,2,32,256]{4,3,2,1,0:T(8,128)(2,1)}), bf16[32,2,2,32,256]{4,3,2,1,0:T(8,128)(2,1)}, u32[]{:S(2)}, u32[]{:S(2)}) async-start(bf16[32,2,2,32,256]{4,3,2,1,0:T(8,128)(2,1)} %copy.43), calls=%async_computation.1 | async-start | bytes 4194304 | tf_op jit(solution)/shard_map/all_to_all | solution.py:580
  75.5 2.3 fusion.2.features_ref
  77.8 48.9 %denoise.1 = f32[8,128,128]{2,1,0:T(8,128)} custom-call(s32[2]{0:T(128)} %pad_add_fusion.first_ref, bf16[14,128,384]{2,1,0:T(8,128)(2,1)} %fusion.2.features_ref, f32[8,128,128]{2,1,0:T(8,128)} %prior_ref.1, bf16[1152,2048]{1,0:T(8,128)(2,1)} %bitcast.63, f32[1,2048]{1,0:T(1,128)} %broadcast_in_dim_tile.8.bias_first_ref, bf16[1536,768]{1,0:T(8,128)(2,1)} %bitcast.64, ...), custom_call_target="tpu_custom_call" | custom-call | flops 37446746112 | bytes 16777216 | tf_op jit(solution)/shard_map/denoise/pallas_call | solution.py:215
  128.9 5.6 %all-to-all-start.2 = ((f32[32,2,2,8,128]{4,3,2,1,0:T(8,128)}), f32[32,2,2,8,128]{4,3,2,1,0:T(8,128)S(1)}, u32[]{:S(2)}, u32[]{:S(2)}) async-start(f32[32,2,2,8,128]{4,3,2,1,0:T(8,128)} %bitcast.56), calls=%async_computation.2 | async-start | bytes 1048576 | tf_op jit(solution)/shard_map/all_to_all | solution.py:580
  135.8 10.3 %adjoint.1 = f32[32,2,2,8,128]{4,3,2,1,0:T(8,128)S(1)} custom-call(bf16[4,8,2,2,32,256]{5,4,3,2,1,0:T(8,128)(2,1)} %bitcast.7.kspace_ref, bf16[4,8,2,2,64,128]{5,4,3,2,1,0:T(8,128)(2,1)S(1)} %bitcast.57, f32[256,128]{1,0:T(8,128)S(1)} %convert_bitcast_fusion.mask_ref, bf16[512,1280]{1,0:T(8,128)(2,1)S(1)} %copy-done), custom_call_target="tpu_custom_call" | custom-call | flops 4831838208 | bytes 2097152 | tf_op jit(solution)/shard_map/adjoint/pallas_call | solution.py:530
  146.1 4.7 %all-to-all-done.2 = f32[32,2,2,8,128]{4,3,2,1,0:T(8,128)S(1)} async-done(((f32[32,2,2,8,128]{4,3,2,1,0:T(8,128)}), f32[32,2,2,8,128]{4,3,2,1,0:T(8,128)S(1)}, u32[]{:S(2)}, u32[]{:S(2)}) %all-to-all-start.2) | async-done | bytes 524320 | tf_op jit(solution)/shard_map/all_to_all | solution.py:580
  151.7 1.3 copy-done.1
  153.0 21.9 %first_product.1.field_ref = f32[32,2,2,8,128]{4,3,2,1,0:T(8,128)} custom-call(bf16[4,8,2,2,64,128]{5,4,3,2,1,0:T(8,128)(2,1)S(1)} %bitcast.58, f32[32,2,2,8,128]{4,3,2,1,0:T(8,128)} %multiply_add_fusion.field_ref.right_ref, f32[256,128]{1,0:T(8,128)S(1)} %convert_bitcast_fusion.mask_ref, bf16[512,1280]{1,0:T(8,128)(2,1)S(1)} %copy-done.1), custom_call_target="tpu_custom_call" | custom-call | flops 9663676416 | bytes 2097152 | tf_op jit(solution)/shard_map/first_product/pallas_call | solution.py:543
  174.9 2.8 %all-to-all-start.5 = ((f32[32,2,2,8,128]{4,3,2,1,0:T(8,128)}), f32[32,2,2,8,128]{4,3,2,1,0:T(8,128)S(1)}, u32[]{:S(2)}, u32[]{:S(2)}) async-start(f32[32,2,2,8,128]{4,3,2,1,0:T(8,128)} %first_product.1.field_ref), calls=%async_computation.5 | async-start | bytes 1048576 | tf_op jit(solution)/shard_map/all_to_all | solution.py:580
  179.1 21.5 %second_product.1 = (f32[32,4,8,128]{3,2,1,0:T(8,128)S(1)}, f32[8,128]{1,0:T(8,128)S(1)}) custom-call(bf16[4,8,2,2,64,128]{5,4,3,2,1,0:T(8,128)(2,1)S(1)} %bitcast.59, f32[32,2,2,8,128]{4,3,2,1,0:T(8,128)} %multiply_add_fusion.field_ref.right_ref, f32[32,2,2,8,128]{4,3,2,1,0:T(8,128)} %first_product.1.field_ref, ...), custom_call_target="tpu_custom_call" | custom-call | flops 9663676416 | bytes 2097152 | tf_op jit(solution)/shard_map/second_product/pallas_call | solution.py:558
  200.7 24.6 %all_to_all.30 = f32[32,5,8,128]{3,2,1,0:T(8,128)S(1)} all-to-all(f32[32,5,8,128]{3,2,1,0:T(8,128)S(1)} %pad_maximum_fusion), channel_id=1, replica_groups=mesh['slab'=4,'coil'=8] {'slab','coil'}, dimensions={0} | all-to-all | bytes 1310720 | tf_op jit(solution)/shard_map/all_to_all | solution.py:580
  225.3 2.6 %all-to-all-start.4 = ((f32[32,2,2,8,128]{4,3,2,1,0:T(8,128)}), f32[32,2,2,8,128]{4,3,2,1,0:T(8,128)S(1)}, u32[]{:S(2)}, u32[]{:S(2)}) async-start(f32[32,2,2,8,128]{4,3,2,1,0:T(8,128)} %multiply_add_fusion.field_ref.right_ref), calls=%async_computation.4 | async-start | bytes 1048576 | tf_op jit(solution)/shard_map/all_to_all | solution.py:580
  237.8 6.5 %all-to-all-done.4 = f32[32,2,2,8,128]{4,3,2,1,0:T(8,128)S(1)} async-done(((f32[32,2,2,8,128]{4,3,2,1,0:T(8,128)}), f32[32,2,2,8,128]{4,3,2,1,0:T(8,128)S(1)}, u32[]{:S(2)}, u32[]{:S(2)}) %all-to-all-start.4) | async-done | bytes 524320 | tf_op jit(solution)/shard_map/all_to_all | solution.py:580
  (106 shorter events, 26.1 us)
Async XLA Ops:
  2.4 71.9 %collective-permute-start = (bf16[3,128,128]{2,1,0:T(8,128)(2,1)}, bf16[3,128,128]{2,1,0:T(8,128)(2,1)S(1)}, u32[]{:S(2)}, u32[]{:S(2)}) collective-permute-start(bf16[3,128,128]{2,1,0:T(8,128)(2,1)} %get-tuple-element.18), channel_id=1, source_target_pairs={{0,1},{1,2},{2,3},{3,4},{4,5},{5,6},{6,7},{7,8},{8,9},{9,10},{10,1... | collective-permute-start | bytes 294920 | tf_op jit(solution)/shard_map/ppermute | solution.py:28
  7.3 67.0 %collective-permute-start.1 = (bf16[3,128,128]{2,1,0:T(8,128)(2,1)}, bf16[3,128,128]{2,1,0:T(8,128)(2,1)}, u32[]{:S(2)}, u32[]{:S(2)}) collective-permute-start(bf16[3,128,128]{2,1,0:T(8,128)(2,1)} %get-tuple-element.19), channel_id=1, source_target_pairs={{1,0},{2,1},{3,2},{4,3},{5,4},{6,5},{7,6},{8,7},{9,8},{10,9},{11,1... | collective-permute-start | bytes 294920 | tf_op jit(solution)/shard_map/ppermute | solution.py:29
  13.6 7.0 %copy-start.11 = (bf16[3,3,3,32,2]{3,4,2,1,0:T(2,128)(2,1)S(1)}, bf16[3,3,3,32,2]{3,4,2,1,0:T(2,128)(2,1)}, u32[]{:S(2)}) copy-start(bf16[3,3,3,32,2]{3,4,2,1,0:T(2,128)(2,1)} %param.15) | copy-start | bytes 10372
  13.6 10.1 %copy-start.12 = (bf16[3,3,3,2,32]{4,3,2,1,0:T(2,128)(2,1)S(1)}, bf16[3,3,3,2,32]{4,3,2,1,0:T(2,128)(2,1)}, u32[]{:S(2)}) copy-start(bf16[3,3,3,2,32]{4,3,2,1,0:T(2,128)(2,1)} %param.19) | copy-start | bytes 10372
  13.6 57.1 %all-to-all-start = ((bf16[32,2,2,64,128]{4,3,2,1,0:T(8,128)(2,1)}), bf16[32,2,2,64,128]{4,3,2,1,0:T(8,128)(2,1)S(1)}, u32[]{:S(2)}, u32[]{:S(2)}) async-start(bf16[32,2,2,64,128]{4,3,2,1,0:T(8,128)(2,1)} %copy.40), calls=%async_computation | async-start | bytes 4194304 | tf_op jit(solution)/shard_map/all_to_all | solution.py:580
  20.6 6.5 %copy-start.9 = (bf16[3,3,3,32,32]{4,3,2,1,0:T(8,128)(2,1)S(1)}, bf16[3,3,3,32,32]{4,3,2,1,0:T(8,128)(2,1)}, u32[]{:S(2)}) copy-start(bf16[3,3,3,32,32]{4,3,2,1,0:T(8,128)(2,1)} %param.17) | copy-start | bytes 165892
  27.8 2.6 %copy-start.13 = (f32[32]{0:T(128)S(1)}, f32[32]{0:T(128)}, u32[]{:S(2)}) copy-start(f32[32]{0:T(128)} %param.16) | copy-start | bytes 388
  27.8 3.3 %copy-start.14 = (f32[32]{0:T(128)S(1)}, f32[32]{0:T(128)}, u32[]{:S(2)}) copy-start(f32[32]{0:T(128)} %param.18) | copy-start | bytes 388
  27.8 4.0 %copy-start.15 = (f32[2]{0:T(128)S(1)}, f32[2]{0:T(128)}, u32[]{:S(2)}) copy-start(f32[2]{0:T(128)} %param.20) | copy-start | bytes 28
  30.4 6.8 %copy-start.10 = (s32[32,256]{1,0:T(8,128)S(1)}, s32[32,256]{1,0:T(8,128)}, u32[]{:S(2)}) copy-start(s32[32,256]{1,0:T(8,128)} %param.14) | copy-start | bytes 98308
  45.9 2.5 %copy-start.3 = (bf16[18,2048]{1,0:T(8,128)(2,1)S(1)}, bf16[18,2048]{1,0:T(8,128)(2,1)}, u32[]{:S(2)}) copy-start(bf16[18,2048]{1,0:T(8,128)(2,1)} %broadcast_in_dim.178) | copy-start | bytes 221188
  45.9 2.5 %copy-start.4 = (bf16[18,2048]{1,0:T(8,128)(2,1)S(1)}, bf16[18,2048]{1,0:T(8,128)(2,1)}, u32[]{:S(2)}) copy-start(bf16[18,2048]{1,0:T(8,128)(2,1)} %broadcast_in_dim.182) | copy-start | bytes 221188
  45.9 2.5 %copy-start.5 = (bf16[18,2048]{1,0:T(8,128)(2,1)S(1)}, bf16[18,2048]{1,0:T(8,128)(2,1)}, u32[]{:S(2)}) copy-start(bf16[18,2048]{1,0:T(8,128)(2,1)} %broadcast_in_dim.186) | copy-start | bytes 221188
  48.4 4.1 %copy-start.6 = (bf16[32,1152]{1,0:T(8,128)(2,1)S(1)}, bf16[32,1152]{1,0:T(8,128)(2,1)}, u32[]{:S(2)}) copy-start(bf16[32,1152]{1,0:T(8,128)(2,1)} %broadcast_in_dim.204) | copy-start | bytes 221188
  48.4 4.1 %copy-start.7 = (bf16[32,1152]{1,0:T(8,128)(2,1)S(1)}, bf16[32,1152]{1,0:T(8,128)(2,1)}, u32[]{:S(2)}) copy-start(bf16[32,1152]{1,0:T(8,128)(2,1)} %broadcast_in_dim.208) | copy-start | bytes 221188
  48.4 4.1 %copy-start.8 = (bf16[32,1152]{1,0:T(8,128)(2,1)S(1)}, bf16[32,1152]{1,0:T(8,128)(2,1)}, u32[]{:S(2)}) copy-start(bf16[32,1152]{1,0:T(8,128)(2,1)} %broadcast_in_dim.212) | copy-start | bytes 221188
  70.6 58.2 %all-to-all-start.1 = ((bf16[32,2,2,32,256]{4,3,2,1,0:T(8,128)(2,1)}), bf16[32,2,2,32,256]{4,3,2,1,0:T(8,128)(2,1)}, u32[]{:S(2)}, u32[]{:S(2)}) async-start(bf16[32,2,2,32,256]{4,3,2,1,0:T(8,128)(2,1)} %copy.43), calls=%async_computation.1 | async-start | bytes 4194304 | tf_op jit(solution)/shard_map/all_to_all | solution.py:580
  128.9 21.9 %all-to-all-start.2 = ((f32[32,2,2,8,128]{4,3,2,1,0:T(8,128)}), f32[32,2,2,8,128]{4,3,2,1,0:T(8,128)S(1)}, u32[]{:S(2)}, u32[]{:S(2)}) async-start(f32[32,2,2,8,128]{4,3,2,1,0:T(8,128)} %bitcast.56), calls=%async_computation.2 | async-start | bytes 1048576 | tf_op jit(solution)/shard_map/all_to_all | solution.py:580
  134.5 1.3 copy-start
  151.7 1.3 copy-start.1
  174.9 25.8 %all-to-all-start.5 = ((f32[32,2,2,8,128]{4,3,2,1,0:T(8,128)}), f32[32,2,2,8,128]{4,3,2,1,0:T(8,128)S(1)}, u32[]{:S(2)}, u32[]{:S(2)}) async-start(f32[32,2,2,8,128]{4,3,2,1,0:T(8,128)} %first_product.1.field_ref), calls=%async_computation.5 | async-start | bytes 1048576 | tf_op jit(solution)/shard_map/all_to_all | solution.py:580
  177.7 1.3 copy-start.2
  225.3 19.0 %all-to-all-start.4 = ((f32[32,2,2,8,128]{4,3,2,1,0:T(8,128)}), f32[32,2,2,8,128]{4,3,2,1,0:T(8,128)S(1)}, u32[]{:S(2)}, u32[]{:S(2)}) async-start(f32[32,2,2,8,128]{4,3,2,1,0:T(8,128)} %multiply_add_fusion.field_ref.right_ref), calls=%async_computation.4 | async-start | bytes 1048576 | tf_op jit(solution)/shard_map/all_to_all | solution.py:580

commit v4 on v3

--- a/solution.py
+++ b/solution.py
@@ -152,7 +152,7 @@
 
 
 def denoise(
-    prior_image, weight_first, bias_first, weight_middle, bias_middle, weight_last, bias_last
+    features, prior_image, weight_first, bias_first, weight_middle, bias_middle, weight_last, bias_last
 ):
     own_rows, planes, width = prior_image.shape
     readout = width // 2
@@ -195,7 +195,7 @@
         1,
     ).reshape(span, 18 * readout)
 
-    features = with_halo(prior_image.astype(jnp.bfloat16), 3)
+    features = with_halo(features, 3)
     rim = jnp.zeros_like(features[:, :1])
     features = jnp.concatenate(
         [
@@ -358,17 +358,26 @@
 
 def normal_sums(maps_ref, real, imag, mask, tables):
     row_table, plane_table = tables
+    units = units_of(maps_ref)
+    fields = []
+    for unit in units:
+        products = []
+        for coil in unit:
+            map_real, map_imag = map_of(maps_ref, coil)
+            products.append(
+                (map_real * real - map_imag * imag, map_real * imag + map_imag * real)
+            )
+        fields.append(along_planes(products, plane_table))
+    fields = [along_rows(row_table, field) for field in fields]
+    spectra = [
+        [(real_part * mask, imag_part * -mask) for real_part, imag_part in field]
+        for field in fields
+    ]
+    fields = [along_rows(row_table, spectrum) for spectrum in spectra]
+    fields = [along_planes(field, plane_table) for field in fields]
     total = None
-    for unit in units_of(maps_ref):
-        maps = [map_of(maps_ref, coil) for coil in unit]
-        fields = [
-            (map_real * real - map_imag * imag, map_real * imag + map_imag * real)
-            for map_real, map_imag in maps
-        ]
-        fields = along_rows(row_table, along_planes(fields, plane_table))
-        fields = [(real_part * mask, imag_part * -mask) for real_part, imag_part in fields]
-        fields = along_planes(along_rows(row_table, fields), plane_table)
-        sums = image_sums(maps, fields)
+    for unit, field in zip(units, fields):
+        sums = image_sums([map_of(maps_ref, coil) for coil in unit], field)
         total = sums if total is None else (total[0] + sums[0], total[1] + sums[1])
     return total
 
@@ -377,8 +386,9 @@
     mask = mask_ref[...]
     rows, planes = mask.shape
     row_table, plane_table = tables_of(table_ref, rows, planes)
-    total = None
-    for unit in units_of(maps_ref):
+    units = units_of(maps_ref)
+    images = []
+    for unit in units:
         spectra = []
         for coil in unit:
             real, imag = (
@@ -392,8 +402,11 @@
             jnp.concatenate([spectrum, spectrum], axis=0),
             preferred_element_type=jnp.float32,
         )
-        fields = along_planes(apart(moved, len(unit)), plane_table)
-        sums = image_sums([map_of(maps_ref, coil) for coil in unit], fields)
+        images.append(apart(moved, len(unit)))
+    images = [along_planes(image, plane_table) for image in images]
+    total = None
+    for unit, image in zip(units, images):
+        sums = image_sums([map_of(maps_ref, coil) for coil in unit], image)
         total = sums if total is None else (total[0] + sums[0], total[1] + sums[1])
     shape = out_ref.shape[0], out_ref.shape[3], out_ref.shape[4]
 
@@ -485,7 +498,7 @@
 
 
 def held_coils(count):
-    return max(size for size in (1, 2, 4) if count % size == 0)
+    return max(size for size in (1, 2, 4, 8) if count % size == 0)
 
 
 def whole(shape):
@@ -637,27 +650,33 @@
     spread = readout % devices == 0
     parts = devices if spread else coils
 
-    def coils_to_x(values):
-        blocks = x_first(values, parts)
+    def coils_to_x(blocks):
         tail = blocks.shape[1:]
         if spread:
             return exchange(blocks, axes).reshape((slabs, coils) + tail)
         blocks = exchange(blocks, "coil").reshape((slabs, coils // slabs) + tail)
         return exchange(blocks, "slab")
 
-    maps = coils_to_x(coil_maps[0])
-    measured, mask = lax.optimization_barrier((kspace[0], mask))
-    spectra = coils_to_x(measured)
+    map_blocks, measured = lax.optimization_barrier(
+        (x_first(coil_maps[0], parts), kspace[0])
+    )
+    maps = coils_to_x(map_blocks)
+    blocks, features, mask = lax.optimization_barrier(
+        (x_first(measured, parts), prior_image.astype(jnp.bfloat16), mask)
+    )
+    spectra = coils_to_x(blocks)
     table = jnp.asarray(dft_table(sampling.shape[1], planes))
     denoised = denoise(
-        prior_image, weight_first, bias_first, weight_middle, bias_middle, weight_last, bias_last
+        features, prior_image, weight_first, bias_first, weight_middle, bias_middle, weight_last, bias_last
     )
     blocks = x_first(denoised, parts)
     if spread:
         denoised = exchange(blocks, axes)
         right = adjoint_call(spectra, maps, mask, table, devices) + penalty * denoised
-        right_rows = x_last(exchange(right, axes))
-        field = first_call(maps, right, mask, table)
+        field, right_back = lax.optimization_barrier(
+            (first_call(maps, right, mask, table), exchange(right, axes))
+        )
+        right_rows = x_last(right_back)
         field_rows = x_last(exchange(field, axes))
         image, totals = second_call(maps, right, field, mask, table)
         payload = jnp.concatenate(

time: 248 us -> 231 us (0.931)
  Pallas kernels: 103 us -> 79.6 us
  waiting for transfers between devices: 24.5 us -> 37.2 us
  local copies, waits for them, and re-layouts: 34.4 us -> 31.7 us
  blocking collectives: 30 us -> 27.3 us
    all_to_all x5, waiting for transfers between devices: 24.5 us -> 37.2 us  [exchange(): return lax.all_to_all(blocks, axis, split_axis=0, concat_axis=0, tiled=True)]
    pallas_call x1, Pallas kernels: 21.5 us -> 12.1 us  [second_call(): pl.pallas_call(second_kernel, grid=grid_of(maps), in_specs=[maps_spec(map...]
    pallas_call x1, Pallas kernels: 21.9 us -> 12.6 us  [first_call(): pl.pallas_call(first_kernel, grid=grid_of(maps), in_specs=[maps_spec(maps...]
    transpose x2 -> x0, local copies, waits for them, and re-layouts: 4.9 us -> none  [x_first(): return jnp.transpose(split, (3, 2, 4, 0, 1))]
    optimization_barrier x0 -> x2, local copies, waits for them, and re-layouts: none -> 4.8 us  [the longest x1 3.23 us: body(): lax.optimization_barrier((x_first(coil_maps[0], parts), kspace[0]))]
    pallas_call x1, Pallas kernels: 10.3 us -> 6 us  [adjoint_call(): pl.pallas_call(adjoint_kernel, grid=grid_of(maps), in_specs=[maps_spec(sp...]
    all_to_all x1, blocking collectives: 24.6 us -> 21.1 us  [exchange(): return lax.all_to_all(blocks, axis, split_axis=0, concat_axis=0, tiled=True)]
    unnamed x36 -> x34, local copies, waits for them, and re-layouts: 14 us -> 11.9 us
  transfers between devices with their start and end apart: 7 -> 7, of which waited for: 3 -> 4; matrix products, arithmetic and copies ran while one was open for 17% -> 14% of each run, Pallas kernels for 33% -> 29%
where the time goes in v4:
time: 231 us; the launch traced here: 230 us
  Pallas kernels  79.6 us (34%)
  waiting for transfers between devices  37.2 us (16%)
  local copies, waits for them, and re-layouts  31.7 us (14%)
  starting transfers between devices  27.9 us (12%)
  blocking collectives  27.3 us (12%)
  other arithmetic  16 us (7%)
  between operations  9.84 us (4%)
    pallas_call x1, Pallas kernels, denoise(): pl.pallas_call(functools.partial(denoise_kernel, group), in_specs=[pl.Blo...  48.9 us
    all_to_all x5, waiting for transfers between devices, exchange(): return lax.all_to_all(blocks, axis, split_axis=0, concat_axis=0, tiled=True)  37.2 us
    all_to_all x5, starting transfers between devices, exchange(): return lax.all_to_all(blocks, axis, split_axis=0, concat_axis=0, tiled=True)  21.4 us
    all_to_all x1, blocking collectives, exchange(): return lax.all_to_all(blocks, axis, split_axis=0, concat_axis=0, tiled=True)  21.1 us
    pallas_call x1, Pallas kernels, first_call(): pl.pallas_call(first_kernel, grid=grid_of(maps), in_specs=[maps_spec(maps...  12.6 us
    pallas_call x1, Pallas kernels, second_call(): pl.pallas_call(second_kernel, grid=grid_of(maps), in_specs=[maps_spec(map...  12.1 us
    unnamed x34, local copies, waits for them, and re-layouts  11.9 us
    select_n x3, other arithmetic, banded(): result = jnp.where(inner - outer + offset == tap, tiles[tap], result)  10.4 us
  transfers between devices with their start and end apart: 7, of which 4 were waited for; matrix products, arithmetic and copies ran while one was open for 14% of the time, Pallas kernels for 29%

profile of v4, /device:TPU:0, one launch (start us, length us, event | category | flops | bytes accessed | tf_op | source)
XLA Modules:
  0.0 229.5 jit_solution(2828109446053418543)
XLA Ops:
  1.4 6.1 %all_gather.3 = bf16[128,256]{1,0:T(8,128)(2,1)S(1)} all-gather(bf16[32,256]{1,0:T(8,128)(2,1)S(1)} %convert_element_type.13), channel_id=1, replica_groups=mesh['slab'=4,'coil'=8] {'slab'}, dimensions={0}, use_global_device_ids=true | all-gather | bytes 81920 | tf_op jit(solution)/shard_map/all_gather | solution.py:648
  8.8 4.2 %copy.39 = bf16[1,64,128,128]{2,1,3,0:T(8,128)(2,1)} copy(bf16[1,64,128,128]{3,2,1,0:T(8,128)(2,1)} %param.12) | data formatting | bytes 4194304 | tf_op args[1]
  12.9 3.4 %copy.40 = bf16[1,32,256,128]{2,1,3,0:T(8,128)(2,1)S(1)} copy(bf16[1,32,256,128]{3,2,1,0:T(8,128)(2,1)} %param.13) | data formatting | bytes 4194304 | tf_op args[2]
  16.3 1.6 copy.43
  17.9 6.4 %all-to-all-start.1 = ((bf16[32,2,2,32,256]{4,3,2,1,0:T(8,128)(2,1)}), bf16[32,2,2,32,256]{4,3,2,1,0:T(8,128)(2,1)S(1)}, u32[]{:S(2)}, u32[]{:S(2)}) async-start(bf16[32,2,2,32,256]{4,3,2,1,0:T(8,128)(2,1)} %copy.43), calls=%async_computation.1 | async-start | bytes 4194304 | tf_op jit(solution)/shard_map/all_to_all | solution.py:593
  26.3 5.2 %collective-permute-start = (bf16[3,128,128]{2,1,0:T(8,128)(2,1)}, bf16[3,128,128]{2,1,0:T(8,128)(2,1)}, u32[]{:S(2)}, u32[]{:S(2)}) collective-permute-start(bf16[3,128,128]{2,1,0:T(8,128)(2,1)} %get-tuple-element.29), channel_id=1, source_target_pairs={{0,1},{1,2},{2,3},{3,4},{4,5},{5,6},{6,7},{7,8},{8,9},{9,10},{10,1... | collective-permute-start | bytes 294920 | tf_op jit(solution)/shard_map/ppermute | solution.py:28
  41.9 3.2 %copy.41 = bf16[32,2,2,64,128]{4,3,2,1,0:T(8,128)(2,1)} copy(bf16[32,2,2,64,128]{4,3,2,0,1:T(8,128)(2,1)} %bitcast.58) | data formatting | bytes 4194304 | tf_op jit(solution)/shard_map/optimization_barrier | solution.py:660
  45.2 2.0 select_select_fusion.2
  47.6 4.1 %select_select_fusion.1 = bf16[18,64,2048]{2,1,0:T(8,128)(2,1)} fusion(pred[64,2048]{1,0:T(8,128)(4,1)S(1)} %get-tuple-element.43, pred[64,2048]{1,0:T(8,128)(4,1)S(1)} %get-tuple-element.44, pred[64,2048]{1,0:T(8,128)(4,1)S(1)} %get-tuple-element.42, bf16[18,2048]{1,0:T(8,128)(2,1)S(1)} %copy-done.3, bf16[18,2048]{1,0:T(8,128)(2,1)S(1)} %copy-done.2, ...), kind=kLoop, calls=%fused_computation.1 | loop fusion | flops 7077888 | bytes 5332992 | tf_op jit(solution)/shard_map/jit(_where)/select_n | solution.py:150
  51.8 4.3 %select_select_fusion = bf16[64,32,1152]{2,1,0:T(8,128)(2,1)} fusion(pred[64,1152]{1,0:T(8,128)(4,1)S(1)} %get-tuple-element.40, pred[64,1152]{1,0:T(8,128)(4,1)S(1)} %get-tuple-element.41, pred[64,1152]{1,0:T(8,128)(4,1)S(1)} %get-tuple-element.39, bf16[32,1152]{1,0:T(8,128)(2,1)S(1)} %copy-done.6, bf16[32,1152]{1,0:T(8,128)(2,1)S(1)} %copy-done.5, ...), kind=kLoop, calls=%fused_computation | loop fusion | flops 7077888 | bytes 5160960 | tf_op jit(solution)/shard_map/jit(_where)/select_n | solution.py:150
  57.6 17.9 %all-to-all-done.1 = bf16[32,2,2,32,256]{4,3,2,1,0:T(8,128)(2,1)S(1)} async-done(((bf16[32,2,2,32,256]{4,3,2,1,0:T(8,128)(2,1)}), bf16[32,2,2,32,256]{4,3,2,1,0:T(8,128)(2,1)S(1)}, u32[]{:S(2)}, u32[]{:S(2)}) %all-to-all-start.1) | async-done | bytes 2097184 | tf_op jit(solution)/shard_map/all_to_all | solution.py:593
  75.5 4.0 %all-to-all-start = ((bf16[32,2,2,64,128]{4,3,2,1,0:T(8,128)(2,1)}), bf16[32,2,2,64,128]{4,3,2,1,0:T(8,128)(2,1)}, u32[]{:S(2)}, u32[]{:S(2)}) async-start(bf16[32,2,2,64,128]{4,3,2,1,0:T(8,128)(2,1)} %copy.41), calls=%async_computation | async-start | bytes 4194304 | tf_op jit(solution)/shard_map/all_to_all | solution.py:593
  80.6 1.4 fusion.2.features_ref
  82.0 48.9 %denoise.1 = f32[8,128,128]{2,1,0:T(8,128)} custom-call(s32[2]{0:T(128)} %pad_add_fusion.first_ref, bf16[14,128,384]{2,1,0:T(8,128)(2,1)} %fusion.2.features_ref, f32[8,128,128]{2,1,0:T(8,128)} %prior_ref.1, bf16[1152,2048]{1,0:T(8,128)(2,1)} %bitcast.61, f32[1,2048]{1,0:T(1,128)} %broadcast_in_dim_tile.8.bias_first_ref, bf16[1536,768]{1,0:T(8,128)(2,1)} %bitcast.62, ...), custom_call_target="tpu_custom_call" | custom-call | flops 37446746112 | bytes 16777216 | tf_op jit(solution)/shard_map/denoise/pallas_call | solution.py:215
  133.0 5.6 %all-to-all-start.2 = ((f32[32,2,2,8,128]{4,3,2,1,0:T(8,128)}), f32[32,2,2,8,128]{4,3,2,1,0:T(8,128)S(1)}, u32[]{:S(2)}, u32[]{:S(2)}) async-start(f32[32,2,2,8,128]{4,3,2,1,0:T(8,128)} %bitcast.56), calls=%async_computation.2 | async-start | bytes 1048576 | tf_op jit(solution)/shard_map/all_to_all | solution.py:593
  140.0 6.0 %adjoint.1 = f32[32,2,2,8,128]{4,3,2,1,0:T(8,128)S(1)} custom-call(bf16[4,8,2,2,32,256]{5,4,3,2,1,0:T(8,128)(2,1)S(1)} %bitcast.57, bf16[4,8,2,2,64,128]{5,4,3,2,1,0:T(8,128)(2,1)} %bitcast.3.maps_ref, f32[256,128]{1,0:T(8,128)S(1)} %convert_bitcast_fusion.mask_ref, bf16[512,1280]{1,0:T(8,128)(2,1)S(1)} %copy-done), custom_call_target="tpu_custom_call" | custom-call | flops 4831838208 | bytes 2097152 | tf_op jit(solution)/shard_map/adjoint/pallas_call | solution.py:543
  146.0 9.0 %all-to-all-done.2 = f32[32,2,2,8,128]{4,3,2,1,0:T(8,128)S(1)} async-done(((f32[32,2,2,8,128]{4,3,2,1,0:T(8,128)}), f32[32,2,2,8,128]{4,3,2,1,0:T(8,128)S(1)}, u32[]{:S(2)}, u32[]{:S(2)}) %all-to-all-start.2) | async-done | bytes 524320 | tf_op jit(solution)/shard_map/all_to_all | solution.py:593
  155.9 2.8 %all-to-all-start.3 = ((f32[32,2,2,8,128]{4,3,2,1,0:T(8,128)}), f32[32,2,2,8,128]{4,3,2,1,0:T(8,128)S(1)}, u32[]{:S(2)}, u32[]{:S(2)}) async-start(f32[32,2,2,8,128]{4,3,2,1,0:T(8,128)} %multiply_add_fusion.field_ref.right_ref), calls=%async_computation.3 | async-start | bytes 1048576 | tf_op jit(solution)/shard_map/all_to_all | solution.py:593
  158.7 12.6 %first_product.1.field_ref = f32[32,2,2,8,128]{4,3,2,1,0:T(8,128)} custom-call(bf16[4,8,2,2,64,128]{5,4,3,2,1,0:T(8,128)(2,1)} %bitcast.3.maps_ref, f32[32,2,2,8,128]{4,3,2,1,0:T(8,128)} %multiply_add_fusion.field_ref.right_ref, f32[256,128]{1,0:T(8,128)S(1)} %convert_bitcast_fusion.mask_ref, bf16[512,1280]{1,0:T(8,128)(2,1)S(1)} %copy-done.1), custom_call_target="tpu_custom_call" | custom-call | flops 9663676416 | bytes 2097152 | tf_op jit(solution)/shard_map/first_product/pallas_call | solution.py:556
  171.3 3.5 %all-to-all-done.3 = f32[32,2,2,8,128]{4,3,2,1,0:T(8,128)S(1)} async-done(((f32[32,2,2,8,128]{4,3,2,1,0:T(8,128)}), f32[32,2,2,8,128]{4,3,2,1,0:T(8,128)S(1)}, u32[]{:S(2)}, u32[]{:S(2)}) %all-to-all-start.3) | async-done | bytes 524320 | tf_op jit(solution)/shard_map/all_to_all | solution.py:593
  174.8 12.1 %second_product.1 = (f32[32,4,8,128]{3,2,1,0:T(8,128)S(1)}, f32[8,128]{1,0:T(8,128)S(1)}) custom-call(bf16[4,8,2,2,64,128]{5,4,3,2,1,0:T(8,128)(2,1)} %bitcast.3.maps_ref, f32[32,2,2,8,128]{4,3,2,1,0:T(8,128)} %multiply_add_fusion.field_ref.right_ref, f32[32,2,2,8,128]{4,3,2,1,0:T(8,128)} %first_product.1.field_ref, ...), custom_call_target="tpu_custom_call" | custom-call | flops 9663676416 | bytes 2097152 | tf_op jit(solution)/shard_map/second_product/pallas_call | solution.py:571
  187.0 21.1 %all_to_all.30 = f32[32,5,8,128]{3,2,1,0:T(8,128)S(1)} all-to-all(f32[32,5,8,128]{3,2,1,0:T(8,128)S(1)} %pad_maximum_fusion), channel_id=1, replica_groups=mesh['slab'=4,'coil'=8] {'slab','coil'}, dimensions={0} | all-to-all | bytes 1310720 | tf_op jit(solution)/shard_map/all_to_all | solution.py:593
  208.2 2.6 %all-to-all-start.5 = ((f32[32,2,2,8,128]{4,3,2,1,0:T(8,128)}), f32[32,2,2,8,128]{4,3,2,1,0:T(8,128)S(1)}, u32[]{:S(2)}, u32[]{:S(2)}) async-start(f32[32,2,2,8,128]{4,3,2,1,0:T(8,128)} %first_product.1.field_ref), calls=%async_computation.5 | async-start | bytes 1048576 | tf_op jit(solution)/shard_map/all_to_all | solution.py:593
  220.4 6.8 %all-to-all-done.5 = f32[32,2,2,8,128]{4,3,2,1,0:T(8,128)S(1)} async-done(((f32[32,2,2,8,128]{4,3,2,1,0:T(8,128)}), f32[32,2,2,8,128]{4,3,2,1,0:T(8,128)S(1)}, u32[]{:S(2)}, u32[]{:S(2)}) %all-to-all-start.5) | async-done | bytes 524320 | tf_op jit(solution)/shard_map/all_to_all | solution.py:593
  (104 shorter events, 24.9 us)
Async XLA Ops:
  17.9 13.6 %copy-start.13 = (f32[2]{0:T(128)S(1)}, f32[2]{0:T(128)}, u32[]{:S(2)}) copy-start(f32[2]{0:T(128)} %param.20) | copy-start | bytes 28
  17.9 14.4 %copy-start.9 = (bf16[3,3,3,32,2]{3,4,2,1,0:T(2,128)(2,1)S(1)}, bf16[3,3,3,32,2]{3,4,2,1,0:T(2,128)(2,1)}, u32[]{:S(2)}) copy-start(bf16[3,3,3,32,2]{3,4,2,1,0:T(2,128)(2,1)} %param.15) | copy-start | bytes 10372
  17.9 14.5 %copy-start.10 = (bf16[3,3,3,2,32]{4,3,2,1,0:T(2,128)(2,1)S(1)}, bf16[3,3,3,2,32]{4,3,2,1,0:T(2,128)(2,1)}, u32[]{:S(2)}) copy-start(bf16[3,3,3,2,32]{4,3,2,1,0:T(2,128)(2,1)} %param.19) | copy-start | bytes 10372
  17.9 14.9 %copy-start.11 = (f32[32]{0:T(128)S(1)}, f32[32]{0:T(128)}, u32[]{:S(2)}) copy-start(f32[32]{0:T(128)} %param.16) | copy-start | bytes 388
  17.9 15.6 %copy-start.12 = (f32[32]{0:T(128)S(1)}, f32[32]{0:T(128)}, u32[]{:S(2)}) copy-start(f32[32]{0:T(128)} %param.18) | copy-start | bytes 388
  17.9 19.1 %copy-start.8 = (bf16[3,3,3,32,32]{4,3,2,1,0:T(8,128)(2,1)S(1)}, bf16[3,3,3,32,32]{4,3,2,1,0:T(8,128)(2,1)}, u32[]{:S(2)}) copy-start(bf16[3,3,3,32,32]{4,3,2,1,0:T(8,128)(2,1)} %param.17) | copy-start | bytes 165892
  17.9 57.5 %all-to-all-start.1 = ((bf16[32,2,2,32,256]{4,3,2,1,0:T(8,128)(2,1)}), bf16[32,2,2,32,256]{4,3,2,1,0:T(8,128)(2,1)S(1)}, u32[]{:S(2)}, u32[]{:S(2)}) async-start(bf16[32,2,2,32,256]{4,3,2,1,0:T(8,128)(2,1)} %copy.43), calls=%async_computation.1 | async-start | bytes 4194304 | tf_op jit(solution)/shard_map/all_to_all | solution.py:593
  25.0 54.4 %collective-permute-start.1 = (bf16[3,128,128]{2,1,0:T(8,128)(2,1)}, bf16[3,128,128]{2,1,0:T(8,128)(2,1)}, u32[]{:S(2)}, u32[]{:S(2)}) collective-permute-start(bf16[3,128,128]{2,1,0:T(8,128)(2,1)} %get-tuple-element.28), channel_id=1, source_target_pairs={{1,0},{2,1},{3,2},{4,3},{5,4},{6,5},{7,6},{8,7},{9,8},{10,9},{11,1... | collective-permute-start | bytes 294920 | tf_op jit(solution)/shard_map/ppermute | solution.py:29
  26.3 30.3 %collective-permute-start = (bf16[3,128,128]{2,1,0:T(8,128)(2,1)}, bf16[3,128,128]{2,1,0:T(8,128)(2,1)}, u32[]{:S(2)}, u32[]{:S(2)}) collective-permute-start(bf16[3,128,128]{2,1,0:T(8,128)(2,1)} %get-tuple-element.29), channel_id=1, source_target_pairs={{0,1},{1,2},{2,3},{3,4},{4,5},{5,6},{6,7},{7,8},{8,9},{9,10},{10,1... | collective-permute-start | bytes 294920 | tf_op jit(solution)/shard_map/ppermute | solution.py:28
  45.1 2.5 %copy-start.2 = (bf16[18,2048]{1,0:T(8,128)(2,1)S(1)}, bf16[18,2048]{1,0:T(8,128)(2,1)}, u32[]{:S(2)}) copy-start(bf16[18,2048]{1,0:T(8,128)(2,1)} %broadcast_in_dim.182) | copy-start | bytes 221188
  45.1 2.5 %copy-start.3 = (bf16[18,2048]{1,0:T(8,128)(2,1)S(1)}, bf16[18,2048]{1,0:T(8,128)(2,1)}, u32[]{:S(2)}) copy-start(bf16[18,2048]{1,0:T(8,128)(2,1)} %broadcast_in_dim.186) | copy-start | bytes 221188
  45.1 2.5 %copy-start.4 = (bf16[18,2048]{1,0:T(8,128)(2,1)S(1)}, bf16[18,2048]{1,0:T(8,128)(2,1)}, u32[]{:S(2)}) copy-start(bf16[18,2048]{1,0:T(8,128)(2,1)} %broadcast_in_dim.178) | copy-start | bytes 221188
  47.6 4.1 %copy-start.5 = (bf16[32,1152]{1,0:T(8,128)(2,1)S(1)}, bf16[32,1152]{1,0:T(8,128)(2,1)}, u32[]{:S(2)}) copy-start(bf16[32,1152]{1,0:T(8,128)(2,1)} %broadcast_in_dim.208) | copy-start | bytes 221188
  47.6 4.1 %copy-start.6 = (bf16[32,1152]{1,0:T(8,128)(2,1)S(1)}, bf16[32,1152]{1,0:T(8,128)(2,1)}, u32[]{:S(2)}) copy-start(bf16[32,1152]{1,0:T(8,128)(2,1)} %broadcast_in_dim.212) | copy-start | bytes 221188
  47.6 4.1 %copy-start.7 = (bf16[32,1152]{1,0:T(8,128)(2,1)S(1)}, bf16[32,1152]{1,0:T(8,128)(2,1)}, u32[]{:S(2)}) copy-start(bf16[32,1152]{1,0:T(8,128)(2,1)} %broadcast_in_dim.204) | copy-start | bytes 221188
  75.5 57.6 %all-to-all-start = ((bf16[32,2,2,64,128]{4,3,2,1,0:T(8,128)(2,1)}), bf16[32,2,2,64,128]{4,3,2,1,0:T(8,128)(2,1)}, u32[]{:S(2)}, u32[]{:S(2)}) async-start(bf16[32,2,2,64,128]{4,3,2,1,0:T(8,128)(2,1)} %copy.41), calls=%async_computation | async-start | bytes 4194304 | tf_op jit(solution)/shard_map/all_to_all | solution.py:593
  133.0 21.9 %all-to-all-start.2 = ((f32[32,2,2,8,128]{4,3,2,1,0:T(8,128)}), f32[32,2,2,8,128]{4,3,2,1,0:T(8,128)S(1)}, u32[]{:S(2)}, u32[]{:S(2)}) async-start(f32[32,2,2,8,128]{4,3,2,1,0:T(8,128)} %bitcast.56), calls=%async_computation.2 | async-start | bytes 1048576 | tf_op jit(solution)/shard_map/all_to_all | solution.py:593
  138.6 1.3 copy-start
  146.0 12.7 %copy-start.1 = (bf16[512,1280]{1,0:T(8,128)(2,1)S(1)}, bf16[512,1280]{1,0:T(8,128)(2,1)}, u32[]{:S(2)}) copy-start(bf16[512,1280]{1,0:T(8,128)(2,1)} %constant.68.clone.table_ref) | copy-start | bytes 3932164
  155.9 19.0 %all-to-all-start.3 = ((f32[32,2,2,8,128]{4,3,2,1,0:T(8,128)}), f32[32,2,2,8,128]{4,3,2,1,0:T(8,128)S(1)}, u32[]{:S(2)}, u32[]{:S(2)}) async-start(f32[32,2,2,8,128]{4,3,2,1,0:T(8,128)} %multiply_add_fusion.field_ref.right_ref), calls=%async_computation.3 | async-start | bytes 1048576 | tf_op jit(solution)/shard_map/all_to_all | solution.py:593
  208.2 19.0 %all-to-all-start.5 = ((f32[32,2,2,8,128]{4,3,2,1,0:T(8,128)}), f32[32,2,2,8,128]{4,3,2,1,0:T(8,128)S(1)}, u32[]{:S(2)}, u32[]{:S(2)}) async-start(f32[32,2,2,8,128]{4,3,2,1,0:T(8,128)} %first_product.1.field_ref), calls=%async_computation.5 | async-start | bytes 1048576 | tf_op jit(solution)/shard_map/all_to_all | solution.py:593

commit v5 on v4

--- a/solution.py
+++ b/solution.py
@@ -152,7 +152,7 @@
 
 
 def denoise(
-    features, prior_image, weight_first, bias_first, weight_middle, bias_middle, weight_last, bias_last
+    prior_image, weight_first, bias_first, weight_middle, bias_middle, weight_last, bias_last
 ):
     own_rows, planes, width = prior_image.shape
     readout = width // 2
@@ -195,7 +195,7 @@
         1,
     ).reshape(span, 18 * readout)
 
-    features = with_halo(features, 3)
+    features = with_halo(prior_image.astype(jnp.bfloat16), 3)
     rim = jnp.zeros_like(features[:, :1])
     features = jnp.concatenate(
         [
@@ -443,7 +443,7 @@
             out_ref[:, part, 0] += sums[part].reshape(shape)
 
 
-def second_kernel(maps_ref, right_ref, field_ref, mask_ref, table_ref, out_ref, total_ref):
+def second_kernel(maps_ref, right_ref, field_ref, mask_ref, table_ref, out_ref):
     x_index = pl.program_id(0)
     x_count = pl.num_programs(0)
     blocks, block_rows, planes = out_ref.shape[0], out_ref.shape[2], out_ref.shape[3]
@@ -472,6 +472,8 @@
         rights = [right_ref[:, part, 0] for part in range(2)]
         fields = [field_ref[:, part, 0] for part in range(2)]
         images = [out_ref[:, part * x_count + x_index] for part in range(2)]
+        for part in range(2):
+            out_ref[:, (2 + part) * x_count + x_index] = fields[part]
 
         def lane_sums(left, other):
             product = left[0] * other[0] + left[1] * other[1]
@@ -483,18 +485,19 @@
                 lane_sums(rights, fields),
                 lane_sums(fields, fields),
                 lane_sums(fields, images),
-                jnp.zeros((4, planes), jnp.float32),
+                jnp.zeros((block_rows - 4, planes), jnp.float32),
             ],
             axis=0,
         )
+        totals = jnp.broadcast_to(totals[None], shape)
 
         @pl.when(x_index == 0)
         def _():
-            total_ref[...] = totals
+            out_ref[:, 4 * x_count] = totals
 
         @pl.when(x_index > 0)
         def _():
-            total_ref[...] += totals
+            out_ref[:, 4 * x_count] += totals
 
 
 def held_coils(count):
@@ -567,7 +570,7 @@
 
 def second_call(maps, right, field, mask, table):
     blocks, _, x_count, block_rows, planes = field.shape
-    out_shape = (blocks, 2 * x_count, block_rows, planes)
+    out_shape = (blocks, 4 * x_count + 1, block_rows, planes)
     return pl.pallas_call(
         second_kernel,
         grid=grid_of(maps),
@@ -578,11 +581,8 @@
             whole(mask.shape),
             whole(table.shape),
         ],
-        out_specs=[whole(out_shape), whole((8, planes))],
-        out_shape=[
-            jax.ShapeDtypeStruct(out_shape, jnp.float32),
-            jax.ShapeDtypeStruct((8, planes), jnp.float32),
-        ],
+        out_specs=whole(out_shape),
+        out_shape=jax.ShapeDtypeStruct(out_shape, jnp.float32),
         compiler_params=compute_params(),
         cost_estimate=product_cost(maps, 6),
         name="second_product",
@@ -657,34 +657,27 @@
         blocks = exchange(blocks, "coil").reshape((slabs, coils // slabs) + tail)
         return exchange(blocks, "slab")
 
-    map_blocks, measured = lax.optimization_barrier(
-        (x_first(coil_maps[0], parts), kspace[0])
-    )
-    maps = coils_to_x(map_blocks)
-    blocks, features, mask = lax.optimization_barrier(
-        (x_first(measured, parts), prior_image.astype(jnp.bfloat16), mask)
-    )
-    spectra = coils_to_x(blocks)
+    maps = coils_to_x(x_first(coil_maps[0], parts))
+    spectra = coils_to_x(x_first(kspace[0], parts))
     table = jnp.asarray(dft_table(sampling.shape[1], planes))
     denoised = denoise(
-        features, prior_image, weight_first, bias_first, weight_middle, bias_middle, weight_last, bias_last
+        prior_image, weight_first, bias_first, weight_middle, bias_middle, weight_last, bias_last
     )
     blocks = x_first(denoised, parts)
     if spread:
+        x_count = blocks.shape[2]
         denoised = exchange(blocks, axes)
         right = adjoint_call(spectra, maps, mask, table, devices) + penalty * denoised
         field, right_back = lax.optimization_barrier(
             (first_call(maps, right, mask, table), exchange(right, axes))
         )
         right_rows = x_last(right_back)
-        field_rows = x_last(exchange(field, axes))
-        image, totals = second_call(maps, right, field, mask, table)
-        payload = jnp.concatenate(
-            [image, jnp.broadcast_to(totals[None, None], (devices, 1) + totals.shape)], axis=1
+        payload = exchange(second_call(maps, right, field, mask, table), axes)
+        squares = jnp.sum(payload[:, -1], axis=(0, 2))
+        image_rows, field_rows = (
+            x_last(payload[:, first : first + 2 * x_count].reshape(blocks.shape))
+            for first in (0, 2 * x_count)
         )
-        payload = exchange(payload, axes)
-        squares = jnp.sum(payload[:, -1], axis=(0, 2))
-        image_rows = x_last(payload[:, :-1].reshape(blocks.shape))
         return combined(right_rows, field_rows, image_rows, squares)
 
     tail = blocks.shape[1:3]
@@ -702,8 +695,7 @@
     adjoint = lax.psum(adjoint_call(spectra, maps, mask, table, 1), "slab")
     right = adjoint + penalty * whole_rows(blocks)
     field = lax.psum(first_call(maps, right, mask, table), "slab")
-    image, _ = second_call(maps, right, field, mask, table)
-    image = lax.psum(image.reshape(field.shape), "slab")
+    image = lax.psum(first_call(maps, field, mask, table), "slab")
     squares = lax.psum(
         jnp.stack(
             [

time: 231 us -> 223 us (0.965)
  waiting for transfers between devices: 37.2 us -> 20 us
  blocking collectives: 27.3 us -> 38.9 us
  starting transfers between devices: 27.9 us -> 24.7 us
  local copies, waits for them, and re-layouts: 31.7 us -> 34.2 us
    all_to_all x5 -> x4, waiting for transfers between devices: 37.2 us -> 20 us  [exchange(): return lax.all_to_all(blocks, axis, split_axis=0, concat_axis=0, tiled=True)]
    all_to_all x1, blocking collectives: 21.1 us -> 32.7 us  [exchange(): return lax.all_to_all(blocks, axis, split_axis=0, concat_axis=0, tiled=True)]
    optimization_barrier x2 -> x0, local copies, waits for them, and re-layouts: 4.8 us -> none  [the longest x1 3.23 us: body(): lax.optimization_barrier((x_first(coil_maps[0], parts), kspace[0]))]
    transpose x0 -> x2, local copies, waits for them, and re-layouts: none -> 4.79 us  [x_first(): return jnp.transpose(split, (3, 2, 4, 0, 1))]
    unnamed x34 -> x38, local copies, waits for them, and re-layouts: 11.9 us -> 14 us
    all_to_all x5 -> x4, starting transfers between devices: 21.4 us -> 19.8 us  [exchange(): return lax.all_to_all(blocks, axis, split_axis=0, concat_axis=0, tiled=True)]
  transfers between devices with their start and end apart: 7 -> 6, of which waited for: 4 -> 3; matrix products, arithmetic and copies ran while one was open for 14% -> 17% of each run, Pallas kernels for 29% -> 30%
where the time goes in v5:
time: 223 us; the launch traced here: 222 us
  Pallas kernels  78.3 us (35%)
  blocking collectives  38.9 us (17%)
  local copies, waits for them, and re-layouts  34.2 us (15%)
  starting transfers between devices  24.7 us (11%)
  waiting for transfers between devices  20 us (9%)
  other arithmetic  16.2 us (7%)
  between operations  10 us (4%)
    pallas_call x1, Pallas kernels, denoise(): pl.pallas_call(functools.partial(denoise_kernel, group), in_specs=[pl.Blo...  48.9 us
    all_to_all x1, blocking collectives, exchange(): return lax.all_to_all(blocks, axis, split_axis=0, concat_axis=0, tiled=True)  32.7 us
    all_to_all x4, waiting for transfers between devices, exchange(): return lax.all_to_all(blocks, axis, split_axis=0, concat_axis=0, tiled=True)  20 us
    all_to_all x4, starting transfers between devices, exchange(): return lax.all_to_all(blocks, axis, split_axis=0, concat_axis=0, tiled=True)  19.8 us
    unnamed x38, local copies, waits for them, and re-layouts  14 us
    pallas_call x1, Pallas kernels, second_call(): pl.pallas_call(second_kernel, grid=grid_of(maps), in_specs=[maps_spec(map...  11.8 us
    pallas_call x1, Pallas kernels, first_call(): pl.pallas_call(first_kernel, grid=grid_of(maps), in_specs=[maps_spec(maps...  11.7 us
    select_n x3, other arithmetic, banded(): result = jnp.where(inner - outer + offset == tap, tiles[tap], result)  10.3 us
  transfers between devices with their start and end apart: 6, of which 3 were waited for; matrix products, arithmetic and copies ran while one was open for 17% of the time, Pallas kernels for 30%

profile of v5, /device:TPU:0, one launch (start us, length us, event | category | flops | bytes accessed | tf_op | source)
XLA Modules:
  0.0 222.4 jit_solution(9622618805434810034)
XLA Ops:
  0.6 3.3 %copy.39 = bf16[1,64,128,128]{2,1,3,0:T(8,128)(2,1)S(1)} copy(bf16[1,64,128,128]{3,2,1,0:T(8,128)(2,1)} %param.12) | data formatting | bytes 4194304 | tf_op args[1]
  3.9 1.6 copy.40
  5.5 7.3 %all-to-all-start = ((bf16[32,2,2,64,128]{4,3,2,1,0:T(8,128)(2,1)}), bf16[32,2,2,64,128]{4,3,2,1,0:T(8,128)(2,1)S(1)}, u32[]{:S(2)}, u32[]{:S(2)}) async-start(bf16[32,2,2,64,128]{4,3,2,1,0:T(8,128)(2,1)} %copy.40), calls=%async_computation | async-start | bytes 4194304 | tf_op jit(solution)/shard_map/all_to_all | solution.py:593
  13.6 3.7 %collective-permute-start = (bf16[3,128,128]{2,1,0:T(8,128)(2,1)}, bf16[3,128,128]{2,1,0:T(8,128)(2,1)S(1)}, u32[]{:S(2)}, u32[]{:S(2)}) collective-permute-start(bf16[3,128,128]{2,1,0:T(8,128)(2,1)} %get-tuple-element.17), channel_id=1, source_target_pairs={{0,1},{1,2},{2,3},{3,4},{4,5},{5,6},{6,7},{7,8},{8,9},{9,10},{10,1... | collective-permute-start | bytes 294920 | tf_op jit(solution)/shard_map/ppermute | solution.py:28
  30.5 4.6 %copy.41 = bf16[1,32,256,128]{2,1,3,0:T(8,128)(2,1)} copy(bf16[1,32,256,128]{3,2,1,0:T(8,128)(2,1)} %param.13) | data formatting | bytes 4194304 | tf_op args[2]
  35.1 3.2 %copy.42 = bf16[32,2,2,32,256]{4,3,2,1,0:T(8,128)(2,1)} copy(bf16[32,2,2,32,256]{4,3,2,0,1:T(8,128)(2,1)} %bitcast.62) | data formatting | bytes 4194304 | tf_op jit(solution)/shard_map/transpose | solution.py:599
  38.4 2.0 select_select_fusion.2
  40.8 4.1 %select_select_fusion.1 = bf16[18,64,2048]{2,1,0:T(8,128)(2,1)} fusion(pred[64,2048]{1,0:T(8,128)(4,1)S(1)} %get-tuple-element.32, pred[64,2048]{1,0:T(8,128)(4,1)S(1)} %get-tuple-element.33, pred[64,2048]{1,0:T(8,128)(4,1)S(1)} %get-tuple-element.31, bf16[18,2048]{1,0:T(8,128)(2,1)S(1)} %copy-done.6, bf16[18,2048]{1,0:T(8,128)(2,1)S(1)} %copy-done.5, ...), kind=kLoop, calls=%fused_computation.1 | loop fusion | flops 7077888 | bytes 5332992 | tf_op jit(solution)/shard_map/jit(_where)/select_n | solution.py:150
  44.9 4.2 %select_select_fusion = bf16[64,32,1152]{2,1,0:T(8,128)(2,1)} fusion(pred[64,1152]{1,0:T(8,128)(4,1)S(1)} %get-tuple-element.29, pred[64,1152]{1,0:T(8,128)(4,1)S(1)} %get-tuple-element.30, pred[64,1152]{1,0:T(8,128)(4,1)S(1)} %get-tuple-element.28, bf16[32,1152]{1,0:T(8,128)(2,1)S(1)} %copy-done.9, bf16[32,1152]{1,0:T(8,128)(2,1)S(1)} %copy-done.8, ...), kind=kLoop, calls=%fused_computation | loop fusion | flops 7077888 | bytes 5160960 | tf_op jit(solution)/shard_map/jit(_where)/select_n | solution.py:150
  49.8 14.1 %all-to-all-done = bf16[32,2,2,64,128]{4,3,2,1,0:T(8,128)(2,1)S(1)} async-done(((bf16[32,2,2,64,128]{4,3,2,1,0:T(8,128)(2,1)}), bf16[32,2,2,64,128]{4,3,2,1,0:T(8,128)(2,1)S(1)}, u32[]{:S(2)}, u32[]{:S(2)}) %all-to-all-start) | async-done | bytes 2097184 | tf_op jit(solution)/shard_map/all_to_all | solution.py:593
  63.9 3.7 %all-to-all-start.1 = ((bf16[32,2,2,32,256]{4,3,2,1,0:T(8,128)(2,1)}), bf16[32,2,2,32,256]{4,3,2,1,0:T(8,128)(2,1)}, u32[]{:S(2)}, u32[]{:S(2)}) async-start(bf16[32,2,2,32,256]{4,3,2,1,0:T(8,128)(2,1)} %copy.42), calls=%async_computation.1 | async-start | bytes 4194304 | tf_op jit(solution)/shard_map/all_to_all | solution.py:593
  68.8 2.3 %fusion.2.features_ref = bf16[14,128,384]{2,1,0:T(8,128)(2,1)} fusion(bf16[14,127,128]{2,1,0:T(8,128)(2,1)S(1)} %get-tuple-element.16, bf16[14,127,128]{2,1,0:T(8,128)(2,1)S(1)} %get-tuple-element.15, bf16[3,128,128]{2,1,0:T(8,128)(2,1)} %collective-permute-done.1, bf16[8,128,128]{2,1,0:T(8,128)(2,1)S(1)} %convert_element_type.14, ...), kind=kLoop, calls=%fused_computation.7 | loop fusion | flops 9633792 | bytes 2745344 | tf_op jit(solution)/shard_map/concatenate | solution.py:200
  71.1 48.9 %denoise.1 = f32[8,128,128]{2,1,0:T(8,128)} custom-call(s32[2]{0:T(128)} %pad_add_fusion.first_ref, bf16[14,128,384]{2,1,0:T(8,128)(2,1)} %fusion.2.features_ref, f32[8,128,128]{2,1,0:T(8,128)} %prior_ref.1, bf16[1152,2048]{1,0:T(8,128)(2,1)} %bitcast.64, f32[1,2048]{1,0:T(1,128)} %broadcast_in_dim_tile.8.bias_first_ref, bf16[1536,768]{1,0:T(8,128)(2,1)} %bitcast.65, ...), custom_call_target="tpu_custom_call" | custom-call | flops 37446746112 | bytes 16777216 | tf_op jit(solution)/shard_map/denoise/pallas_call | solution.py:215
  122.1 5.6 %all-to-all-start.2 = ((f32[32,2,2,8,128]{4,3,2,1,0:T(8,128)}), f32[32,2,2,8,128]{4,3,2,1,0:T(8,128)S(1)}, u32[]{:S(2)}, u32[]{:S(2)}) async-start(f32[32,2,2,8,128]{4,3,2,1,0:T(8,128)} %bitcast.57), calls=%async_computation.2 | async-start | bytes 1048576 | tf_op jit(solution)/shard_map/all_to_all | solution.py:593
  127.8 6.2 %all_gather.3 = bf16[128,256]{1,0:T(8,128)(2,1)S(1)} all-gather(bf16[32,256]{1,0:T(8,128)(2,1)S(1)} %convert_element_type.11), channel_id=1, replica_groups=mesh['slab'=4,'coil'=8] {'slab'}, dimensions={0}, use_global_device_ids=true | all-gather | bytes 81920 | tf_op jit(solution)/shard_map/all_gather | solution.py:648
  134.2 1.3 copy-done
  135.5 5.9 %adjoint.1 = f32[32,2,2,8,128]{4,3,2,1,0:T(8,128)S(1)} custom-call(bf16[4,8,2,2,32,256]{5,4,3,2,1,0:T(8,128)(2,1)} %bitcast.5.kspace_ref, bf16[4,8,2,2,64,128]{5,4,3,2,1,0:T(8,128)(2,1)S(1)} %bitcast.58, f32[256,128]{1,0:T(8,128)S(1)} %convert_bitcast_fusion.mask_ref, bf16[512,1280]{1,0:T(8,128)(2,1)S(1)} %copy-done), custom_call_target="tpu_custom_call" | custom-call | flops 4831838208 | bytes 2097152 | tf_op jit(solution)/shard_map/adjoint/pallas_call | solution.py:546
  141.4 2.7 %all-to-all-done.2 = f32[32,2,2,8,128]{4,3,2,1,0:T(8,128)S(1)} async-done(((f32[32,2,2,8,128]{4,3,2,1,0:T(8,128)}), f32[32,2,2,8,128]{4,3,2,1,0:T(8,128)S(1)}, u32[]{:S(2)}, u32[]{:S(2)}) %all-to-all-start.2) | async-done | bytes 524320 | tf_op jit(solution)/shard_map/all_to_all | solution.py:593
  145.0 3.2 %all-to-all-start.3 = ((f32[32,2,2,8,128]{4,3,2,1,0:T(8,128)}), f32[32,2,2,8,128]{4,3,2,1,0:T(8,128)S(1)}, u32[]{:S(2)}, u32[]{:S(2)}) async-start(f32[32,2,2,8,128]{4,3,2,1,0:T(8,128)} %multiply_add_fusion.field_ref.right_ref), calls=%async_computation.3 | async-start | bytes 1048576 | tf_op jit(solution)/shard_map/all_to_all | solution.py:593
  149.5 11.7 %first_product.1.field_ref = f32[32,2,2,8,128]{4,3,2,1,0:T(8,128)S(1)} custom-call(bf16[4,8,2,2,64,128]{5,4,3,2,1,0:T(8,128)(2,1)S(1)} %bitcast.59, f32[32,2,2,8,128]{4,3,2,1,0:T(8,128)} %multiply_add_fusion.field_ref.right_ref, f32[256,128]{1,0:T(8,128)S(1)} %convert_bitcast_fusion.mask_ref, bf16[512,1280]{1,0:T(8,128)(2,1)S(1)} %copy-done.1), custom_call_target="tpu_custom_call" | custom-call | flops 9663676416 | bytes 2097152 | tf_op jit(solution)/shard_map/first_product/pallas_call | solution.py:559
  161.2 3.2 %all-to-all-done.3 = f32[32,2,2,8,128]{4,3,2,1,0:T(8,128)S(1)} async-done(((f32[32,2,2,8,128]{4,3,2,1,0:T(8,128)}), f32[32,2,2,8,128]{4,3,2,1,0:T(8,128)S(1)}, u32[]{:S(2)}, u32[]{:S(2)}) %all-to-all-start.3) | async-done | bytes 524320 | tf_op jit(solution)/shard_map/all_to_all | solution.py:593
  164.3 1.3 copy-done.2
  165.7 11.8 %second_product.1 = f32[32,9,8,128]{3,2,1,0:T(8,128)S(1)} custom-call(bf16[4,8,2,2,64,128]{5,4,3,2,1,0:T(8,128)(2,1)S(1)} %bitcast.60, f32[32,2,2,8,128]{4,3,2,1,0:T(8,128)} %multiply_add_fusion.field_ref.right_ref, f32[32,2,2,8,128]{4,3,2,1,0:T(8,128)S(1)} %first_product.1.field_ref, f32[256,128]{1,0:T(8,128)S(1)} %convert_bitcast_fusion.mask_ref, ...), custom_call_target="tpu_custom_call" | custom-call | flops 9663676416 | bytes 2097152 | tf_op jit(solution)/shard_map/second_product/pallas_call | solution.py:574
  177.5 32.7 %all_to_all.25 = f32[32,9,8,128]{3,2,1,0:T(8,128)S(1)} all-to-all(f32[32,9,8,128]{3,2,1,0:T(8,128)S(1)} %second_product.1), channel_id=1, replica_groups=mesh['slab'=4,'coil'=8] {'slab','coil'}, dimensions={0} | all-to-all | bytes 2359296 | tf_op jit(solution)/shard_map/all_to_all | solution.py:593
  (104 shorter events, 23.8 us)
Async XLA Ops:
  5.5 7.3 %copy-start.3 = (f32[8,128,128]{2,1,0:T(8,128)S(1)}, f32[8,128,128]{2,1,0:T(8,128)}, u32[]{:S(2)}) copy-start(f32[8,128,128]{2,1,0:T(8,128)} %prior_ref.1) | copy-start | bytes 1572868
  5.5 13.1 %copy-start.12 = (bf16[3,3,3,32,2]{3,4,2,1,0:T(2,128)(2,1)S(1)}, bf16[3,3,3,32,2]{3,4,2,1,0:T(2,128)(2,1)}, u32[]{:S(2)}) copy-start(bf16[3,3,3,32,2]{3,4,2,1,0:T(2,128)(2,1)} %param.15) | copy-start | bytes 10372
  5.5 58.4 %all-to-all-start = ((bf16[32,2,2,64,128]{4,3,2,1,0:T(8,128)(2,1)}), bf16[32,2,2,64,128]{4,3,2,1,0:T(8,128)(2,1)S(1)}, u32[]{:S(2)}, u32[]{:S(2)}) async-start(bf16[32,2,2,64,128]{4,3,2,1,0:T(8,128)(2,1)} %copy.40), calls=%async_computation | async-start | bytes 4194304 | tf_op jit(solution)/shard_map/all_to_all | solution.py:593
  12.8 8.8 %copy-start.13 = (bf16[3,3,3,2,32]{4,3,2,1,0:T(2,128)(2,1)S(1)}, bf16[3,3,3,2,32]{4,3,2,1,0:T(2,128)(2,1)}, u32[]{:S(2)}) copy-start(bf16[3,3,3,2,32]{4,3,2,1,0:T(2,128)(2,1)} %param.19) | copy-start | bytes 10372
  12.8 12.2 %copy-start.10 = (bf16[3,3,3,32,32]{4,3,2,1,0:T(8,128)(2,1)S(1)}, bf16[3,3,3,32,32]{4,3,2,1,0:T(8,128)(2,1)}, u32[]{:S(2)}) copy-start(bf16[3,3,3,32,32]{4,3,2,1,0:T(8,128)(2,1)} %param.17) | copy-start | bytes 165892
  13.6 54.0 %collective-permute-start = (bf16[3,128,128]{2,1,0:T(8,128)(2,1)}, bf16[3,128,128]{2,1,0:T(8,128)(2,1)S(1)}, u32[]{:S(2)}, u32[]{:S(2)}) collective-permute-start(bf16[3,128,128]{2,1,0:T(8,128)(2,1)} %get-tuple-element.17), channel_id=1, source_target_pairs={{0,1},{1,2},{2,3},{3,4},{4,5},{5,6},{6,7},{7,8},{8,9},{9,10},{10,1... | collective-permute-start | bytes 294920 | tf_op jit(solution)/shard_map/ppermute | solution.py:28
  17.3 50.4 %collective-permute-start.1 = (bf16[3,128,128]{2,1,0:T(8,128)(2,1)}, bf16[3,128,128]{2,1,0:T(8,128)(2,1)}, u32[]{:S(2)}, u32[]{:S(2)}) collective-permute-start(bf16[3,128,128]{2,1,0:T(8,128)(2,1)} %get-tuple-element.18), channel_id=1, source_target_pairs={{1,0},{2,1},{3,2},{4,3},{5,4},{6,5},{7,6},{8,7},{9,8},{10,9},{11,1... | collective-permute-start | bytes 294920 | tf_op jit(solution)/shard_map/ppermute | solution.py:29
  25.8 2.6 %copy-start.14 = (f32[32]{0:T(128)S(1)}, f32[32]{0:T(128)}, u32[]{:S(2)}) copy-start(f32[32]{0:T(128)} %param.16) | copy-start | bytes 388
  25.8 3.3 %copy-start.15 = (f32[32]{0:T(128)S(1)}, f32[32]{0:T(128)}, u32[]{:S(2)}) copy-start(f32[32]{0:T(128)} %param.18) | copy-start | bytes 388
  25.8 4.0 %copy-start.16 = (f32[2]{0:T(128)S(1)}, f32[2]{0:T(128)}, u32[]{:S(2)}) copy-start(f32[2]{0:T(128)} %param.20) | copy-start | bytes 28
  38.3 2.5 %copy-start.4 = (bf16[18,2048]{1,0:T(8,128)(2,1)S(1)}, bf16[18,2048]{1,0:T(8,128)(2,1)}, u32[]{:S(2)}) copy-start(bf16[18,2048]{1,0:T(8,128)(2,1)} %broadcast_in_dim.172) | copy-start | bytes 221188
  38.3 2.5 %copy-start.5 = (bf16[18,2048]{1,0:T(8,128)(2,1)S(1)}, bf16[18,2048]{1,0:T(8,128)(2,1)}, u32[]{:S(2)}) copy-start(bf16[18,2048]{1,0:T(8,128)(2,1)} %broadcast_in_dim.176) | copy-start | bytes 221188
  38.3 2.5 %copy-start.6 = (bf16[18,2048]{1,0:T(8,128)(2,1)S(1)}, bf16[18,2048]{1,0:T(8,128)(2,1)}, u32[]{:S(2)}) copy-start(bf16[18,2048]{1,0:T(8,128)(2,1)} %broadcast_in_dim.180) | copy-start | bytes 221188
  40.8 4.1 %copy-start.7 = (bf16[32,1152]{1,0:T(8,128)(2,1)S(1)}, bf16[32,1152]{1,0:T(8,128)(2,1)}, u32[]{:S(2)}) copy-start(bf16[32,1152]{1,0:T(8,128)(2,1)} %broadcast_in_dim.198) | copy-start | bytes 221188
  40.8 4.1 %copy-start.8 = (bf16[32,1152]{1,0:T(8,128)(2,1)S(1)}, bf16[32,1152]{1,0:T(8,128)(2,1)}, u32[]{:S(2)}) copy-start(bf16[32,1152]{1,0:T(8,128)(2,1)} %broadcast_in_dim.202) | copy-start | bytes 221188
  40.8 4.1 %copy-start.9 = (bf16[32,1152]{1,0:T(8,128)(2,1)S(1)}, bf16[32,1152]{1,0:T(8,128)(2,1)}, u32[]{:S(2)}) copy-start(bf16[32,1152]{1,0:T(8,128)(2,1)} %broadcast_in_dim.206) | copy-start | bytes 221188
  63.9 58.2 %all-to-all-start.1 = ((bf16[32,2,2,32,256]{4,3,2,1,0:T(8,128)(2,1)}), bf16[32,2,2,32,256]{4,3,2,1,0:T(8,128)(2,1)}, u32[]{:S(2)}, u32[]{:S(2)}) async-start(bf16[32,2,2,32,256]{4,3,2,1,0:T(8,128)(2,1)} %copy.42), calls=%async_computation.1 | async-start | bytes 4194304 | tf_op jit(solution)/shard_map/all_to_all | solution.py:593
  120.0 7.8 %copy-start.11 = (s32[32,256]{1,0:T(8,128)S(1)}, s32[32,256]{1,0:T(8,128)}, u32[]{:S(2)}) copy-start(s32[32,256]{1,0:T(8,128)} %param.14) | copy-start | bytes 98308
  122.1 22.0 %all-to-all-start.2 = ((f32[32,2,2,8,128]{4,3,2,1,0:T(8,128)}), f32[32,2,2,8,128]{4,3,2,1,0:T(8,128)S(1)}, u32[]{:S(2)}, u32[]{:S(2)}) async-start(f32[32,2,2,8,128]{4,3,2,1,0:T(8,128)} %bitcast.57), calls=%async_computation.2 | async-start | bytes 1048576 | tf_op jit(solution)/shard_map/all_to_all | solution.py:593
  134.1 1.3 copy-start
  145.0 19.4 %all-to-all-start.3 = ((f32[32,2,2,8,128]{4,3,2,1,0:T(8,128)}), f32[32,2,2,8,128]{4,3,2,1,0:T(8,128)S(1)}, u32[]{:S(2)}, u32[]{:S(2)}) async-start(f32[32,2,2,8,128]{4,3,2,1,0:T(8,128)} %multiply_add_fusion.field_ref.right_ref), calls=%async_computation.3 | async-start | bytes 1048576 | tf_op jit(solution)/shard_map/all_to_all | solution.py:593
  148.2 1.3 copy-start.1
  164.3 1.3 copy-start.2

commit v6 on v5

--- a/solution.py
+++ b/solution.py
@@ -55,9 +55,9 @@
     one_ref,
     two_ref,
     taps_ref,
+    *turned_refs,
 ):
-    planes = out_ref.shape[1]
-    width = out_ref.shape[2]
+    own_rows, planes, width = prior_ref.shape
     edge = (one_ref.shape[2] - two_ref.shape[2]) // 2
     groups = two_ref.shape[2] // group
     first = first_ref[0]
@@ -127,7 +127,7 @@
     lax.fori_loop(0, two_ref.shape[0] // count, last_layer, 0)
     plane = plane_index(1, width)
 
-    def last_sum(row, carry):
+    def last_sum(row):
         sums = []
         for plane_tap in range(3):
             running = None
@@ -137,10 +137,22 @@
                 running = value if running is None else running + value
             sums.append(running)
         value = sums[1] + shifted(sums[0], plane, 1) + shifted(sums[2], plane, -1)
-        out_ref[row] = prior_ref[row] + (value + bias_last_ref[...])
-        return carry
-
-    lax.fori_loop(0, out_ref.shape[0], last_sum, 0)
+        return prior_ref[row] + (value + bias_last_ref[...])
+
+    if not turned_refs:
+        for row in range(own_rows):
+            out_ref[row] = last_sum(row)
+        return
+
+    turned_ref = turned_refs[0]
+    for row in range(own_rows):
+        turned_ref[pl.ds(row, width, stride=own_rows), :] = jnp.transpose(last_sum(row))
+    blocks, _, x_count = out_ref.shape[:3]
+    for block in range(blocks):
+        for part in range(2):
+            for inner in range(x_count):
+                place = part * (width // 2) + block * x_count + inner
+                out_ref[block, part, inner] = turned_ref[place * own_rows : (place + 1) * own_rows]
 
 
 def banded(tiles, inner, outer, offset):
@@ -152,9 +164,11 @@
 
 
 def denoise(
-    prior_image, weight_first, bias_first, weight_middle, bias_middle, weight_last, bias_last
+    parts, prior_image, weight_first, bias_first, weight_middle, bias_middle, weight_last, bias_last
 ):
     own_rows, planes, width = prior_image.shape
+    turned = own_rows % 8 == 0
+    out_shape = (parts, 2, width // (2 * parts), own_rows, planes) if turned else prior_image.shape
     readout = width // 2
     channels = weight_first.shape[3]
     span = readout * channels
@@ -216,12 +230,13 @@
         functools.partial(denoise_kernel, group),
         in_specs=[pl.BlockSpec(memory_space=pltpu.SMEM)] + [vmem] * 8,
         out_specs=vmem,
-        out_shape=jax.ShapeDtypeStruct(prior_image.shape, jnp.float32),
+        out_shape=jax.ShapeDtypeStruct(out_shape, jnp.float32),
         scratch_shapes=[
             pltpu.VMEM((own_rows + 4, planes, span + 2 * edge), jnp.bfloat16),
             pltpu.VMEM((own_rows + 2, planes, span), jnp.bfloat16),
             pltpu.VMEM((own_rows + 2, planes, 18 * readout), jnp.float32),
-        ],
+        ]
+        + [pltpu.VMEM((width * own_rows, planes), jnp.float32)] * turned,
         compiler_params=pltpu.CompilerParams(vmem_limit_bytes=56 * 1024 * 1024),
         cost_estimate=pl.CostEstimate(
             flops=int(flops), bytes_accessed=16 * 1024 * 1024, transcendentals=0
@@ -472,8 +487,6 @@
         rights = [right_ref[:, part, 0] for part in range(2)]
         fields = [field_ref[:, part, 0] for part in range(2)]
         images = [out_ref[:, part * x_count + x_index] for part in range(2)]
-        for part in range(2):
-            out_ref[:, (2 + part) * x_count + x_index] = fields[part]
 
         def lane_sums(left, other):
             product = left[0] * other[0] + left[1] * other[1]
@@ -493,11 +506,11 @@
 
         @pl.when(x_index == 0)
         def _():
-            out_ref[:, 4 * x_count] = totals
+            out_ref[:, 2 * x_count] = totals
 
         @pl.when(x_index > 0)
         def _():
-            out_ref[:, 4 * x_count] += totals
+            out_ref[:, 2 * x_count] += totals
 
 
 def held_coils(count):
@@ -570,7 +583,7 @@
 
 def second_call(maps, right, field, mask, table):
     blocks, _, x_count, block_rows, planes = field.shape
-    out_shape = (blocks, 4 * x_count + 1, block_rows, planes)
+    out_shape = (blocks, 2 * x_count + 1, block_rows, planes)
     return pl.pallas_call(
         second_kernel,
         grid=grid_of(maps),
@@ -604,8 +617,7 @@
     return jnp.transpose(blocks, (3, 4, 1, 0, 2)).reshape(rows, planes, 2 * parts * x_count)
 
 
-def combined(right, field, image, squares):
-    right_right, right_field, field_field, field_image = (squares[i] for i in range(4))
+def factors(right_right, right_field, field_field, field_image):
     ratio = right_field / right_right
     alpha = right_right / (right_field + penalty * right_right)
     fresh = alpha * alpha * (field_field - ratio * right_field)
@@ -617,13 +629,46 @@
         weight * weight * right_right - 2.0 * mixed * right_field + alpha * alpha * field_field
     )
     second = fresh / curvature
-    solution = (alpha + second * weight) * right - (second * alpha) * field
-    residual = (
-        (alpha * ratio - penalty * second * weight) * right
-        - (alpha + second * weight - penalty * second * alpha) * field
-        + (second * alpha) * image
-    )
-    return solution, residual
+    moved = alpha + second * weight
+    bent = second * alpha
+    return (moved, -bent), (alpha * ratio - penalty * second * weight, penalty * bent - moved, bent)
+
+
+def finish_kernel(right_ref, field_ref, image_ref, solution_ref, residual_ref, rows_ref):
+    blocks, _, x_count, rows, planes = right_ref.shape
+    readout = blocks * x_count
+    totals = jnp.sum(jnp.sum(image_ref[:, 2 * x_count], axis=0), axis=1, keepdims=True)
+    found = factors(*(totals[index : index + 1] for index in range(4)))
+    for out_ref, scales in zip((solution_ref, residual_ref), found):
+        scales = [jnp.broadcast_to(scale, (rows, planes))[None] for scale in scales]
+        for part in range(2):
+            for inner in range(x_count):
+                value = scales[0] * right_ref[:, part, inner] + scales[1] * field_ref[:, part, inner]
+                if len(scales) > 2:
+                    value = value + scales[2] * image_ref[:, part * x_count + inner]
+                for block in range(blocks):
+                    place = part * readout + block * x_count + inner
+                    rows_ref[place * rows : (place + 1) * rows] = value[block]
+        for row in range(rows):
+            out_ref[row] = jnp.transpose(rows_ref[pl.ds(row, 2 * readout, stride=rows), :])
+
+
+def finish_call(right, field, image):
+    blocks, _, x_count, rows, planes = right.shape
+    shape = (rows, planes, 2 * blocks * x_count)
+    vmem = pl.BlockSpec(memory_space=pltpu.VMEM)
+    return pl.pallas_call(
+        finish_kernel,
+        in_specs=[vmem] * 3,
+        out_specs=[vmem] * 2,
+        out_shape=[jax.ShapeDtypeStruct(shape, jnp.float32)] * 2,
+        scratch_shapes=[pltpu.VMEM((2 * blocks * x_count * rows, planes), jnp.float32)],
+        compiler_params=pltpu.CompilerParams(vmem_limit_bytes=32 * 1024 * 1024),
+        cost_estimate=pl.CostEstimate(
+            flops=8 * right.size, bytes_accessed=20 * right.size, transcendentals=0
+        ),
+        name="finish",
+    )(right, field, image)
 
 
 def body(
@@ -647,7 +692,7 @@
     mask = jnp.transpose(
         lax.all_gather(sampling.astype(jnp.bfloat16), "slab", axis=0, tiled=True)
     ).astype(jnp.float32)
-    spread = readout % devices == 0
+    spread = readout % devices == 0 and own_rows % 8 == 0
     parts = devices if spread else coils
 
     def coils_to_x(blocks):
@@ -660,25 +705,28 @@
     maps = coils_to_x(x_first(coil_maps[0], parts))
     spectra = coils_to_x(x_first(kspace[0], parts))
     table = jnp.asarray(dft_table(sampling.shape[1], planes))
-    denoised = denoise(
-        prior_image, weight_first, bias_first, weight_middle, bias_middle, weight_last, bias_last
-    )
-    blocks = x_first(denoised, parts)
+    blocks = denoise(
+        parts,
+        prior_image,
+        weight_first,
+        bias_first,
+        weight_middle,
+        bias_middle,
+        weight_last,
+        bias_last,
+    )
+    if blocks.ndim == 3:
+        blocks = x_first(blocks, parts)
     if spread:
-        x_count = blocks.shape[2]
         denoised = exchange(blocks, axes)
         right = adjoint_call(spectra, maps, mask, table, devices) + penalty * denoised
         field, right_back = lax.optimization_barrier(
             (first_call(maps, right, mask, table), exchange(right, axes))
         )
-        right_rows = x_last(right_back)
-        payload = exchange(second_call(maps, right, field, mask, table), axes)
-        squares = jnp.sum(payload[:, -1], axis=(0, 2))
-        image_rows, field_rows = (
-            x_last(payload[:, first : first + 2 * x_count].reshape(blocks.shape))
-            for first in (0, 2 * x_count)
+        payload, field_back = lax.optimization_barrier(
+            (second_call(maps, right, field, mask, table), exchange(field, axes))
         )
-        return combined(right_rows, field_rows, image_rows, squares)
+        return tuple(finish_call(right_back, field_back, exchange(payload, axes)))
 
     tail = blocks.shape[1:3]
 
@@ -707,7 +755,12 @@
         ),
         "coil",
     )
-    return combined(own_part(right), own_part(field), own_part(image), squares)
+    scales, others = factors(*(squares[index] for index in range(4)))
+    right, field, image = own_part(right), own_part(field), own_part(image)
+    return (
+        scales[0] * right + scales[1] * field,
+        others[0] * right + others[1] * field + others[2] * image,
+    )
 
 
 def solution(mesh):

time: 223 us -> 208 us (0.933)
  blocking collectives: 38.9 us -> 29.9 us
  between operations: 10 us -> 1.14 us
  starting transfers between devices: 24.7 us -> 28 us
    all_to_all x1, blocking collectives: 32.7 us -> 23.7 us  [exchange(): return lax.all_to_all(blocks, axis, split_axis=0, concat_axis=0, tiled=True)]
    all_to_all x4 -> x5, starting transfers between devices: 19.8 us -> 23 us  [exchange(): return lax.all_to_all(blocks, axis, split_axis=0, concat_axis=0, tiled=True)]
    unnamed x38 -> x42, local copies, waits for them, and re-layouts: 14 us -> 14.6 us
    all_to_all x4 -> x5, waiting for transfers between devices: 20 us -> 20.5 us  [exchange(): return lax.all_to_all(blocks, axis, split_axis=0, concat_axis=0, tiled=True)]
  transfers between devices with their start and end apart: 6 -> 7, of which waited for: 3 -> 4; matrix products, arithmetic and copies ran while one was open for 17% -> 17% of each run, Pallas kernels for 30% -> 38%
where the time goes in v6:
time: 208 us; the launch traced here: 207 us
  Pallas kernels  79.8 us (38%)
  local copies, waits for them, and re-layouts  32.2 us (15%)
  blocking collectives  29.9 us (14%)
  starting transfers between devices  28 us (13%)
  waiting for transfers between devices  20.5 us (10%)
  other arithmetic  15.6 us (8%)
    pallas_call x1, Pallas kernels, denoise(): pl.pallas_call(functools.partial(denoise_kernel, group), in_specs=[pl.Blo...  49 us
    all_to_all x1, blocking collectives, exchange(): return lax.all_to_all(blocks, axis, split_axis=0, concat_axis=0, tiled=True)  23.7 us
    all_to_all x5, starting transfers between devices, exchange(): return lax.all_to_all(blocks, axis, split_axis=0, concat_axis=0, tiled=True)  23 us
    all_to_all x5, waiting for transfers between devices, exchange(): return lax.all_to_all(blocks, axis, split_axis=0, concat_axis=0, tiled=True)  20.5 us
    unnamed x42, local copies, waits for them, and re-layouts  14.6 us
    pallas_call x1, Pallas kernels, second_call(): pl.pallas_call(second_kernel, grid=grid_of(maps), in_specs=[maps_spec(map...  11.8 us
    pallas_call x1, Pallas kernels, first_call(): pl.pallas_call(first_kernel, grid=grid_of(maps), in_specs=[maps_spec(maps...  11.7 us
    select_n x3, other arithmetic, banded(): result = jnp.where(inner - outer + offset == tap, tiles[tap], result)  10.3 us
  transfers between devices with their start and end apart: 7, of which 4 were waited for; matrix products, arithmetic and copies ran while one was open for 17% of the time, Pallas kernels for 38%

profile of v6, /device:TPU:0, one launch (start us, length us, event | category | flops | bytes accessed | tf_op | source)
XLA Modules:
  0.0 207.1 jit_solution(1308607931414234327)
XLA Ops:
  0.6 3.3 %copy.33 = bf16[1,64,128,128]{2,1,3,0:T(8,128)(2,1)S(1)} copy(bf16[1,64,128,128]{3,2,1,0:T(8,128)(2,1)} %param.12) | data formatting | bytes 4194304 | tf_op args[1]
  3.9 1.7 copy.34
  5.6 7.3 %all-to-all-start = ((bf16[32,2,2,64,128]{4,3,2,1,0:T(8,128)(2,1)}), bf16[32,2,2,64,128]{4,3,2,1,0:T(8,128)(2,1)S(1)}, u32[]{:S(2)}, u32[]{:S(2)}) async-start(bf16[32,2,2,64,128]{4,3,2,1,0:T(8,128)(2,1)} %copy.34), calls=%async_computation | async-start | bytes 4194304 | tf_op jit(solution)/shard_map/all_to_all | solution.py:606
  13.7 3.7 %collective-permute-start = (bf16[3,128,128]{2,1,0:T(8,128)(2,1)}, bf16[3,128,128]{2,1,0:T(8,128)(2,1)S(1)}, u32[]{:S(2)}, u32[]{:S(2)}) collective-permute-start(bf16[3,128,128]{2,1,0:T(8,128)(2,1)} %get-tuple-element.12), channel_id=1, source_target_pairs={{0,1},{1,2},{2,3},{3,4},{4,5},{5,6},{6,7},{7,8},{8,9},{9,10},{10,1... | collective-permute-start | bytes 294920 | tf_op jit(solution)/shard_map/ppermute | solution.py:28
  30.6 4.6 %copy.35 = bf16[1,32,256,128]{2,1,3,0:T(8,128)(2,1)} copy(bf16[1,32,256,128]{3,2,1,0:T(8,128)(2,1)} %param.13) | data formatting | bytes 4194304 | tf_op args[2]
  35.2 3.2 %copy.36 = bf16[32,2,2,32,256]{4,3,2,1,0:T(8,128)(2,1)} copy(bf16[32,2,2,32,256]{4,3,2,0,1:T(8,128)(2,1)} %bitcast.45) | data formatting | bytes 4194304 | tf_op jit(solution)/shard_map/transpose | solution.py:612
  38.5 2.0 select_select_fusion.2
  41.0 4.1 %select_select_fusion.1 = bf16[18,64,2048]{2,1,0:T(8,128)(2,1)} fusion(pred[64,2048]{1,0:T(8,128)(4,1)S(1)} %get-tuple-element.27, pred[64,2048]{1,0:T(8,128)(4,1)S(1)} %get-tuple-element.28, pred[64,2048]{1,0:T(8,128)(4,1)S(1)} %get-tuple-element.26, bf16[18,2048]{1,0:T(8,128)(2,1)S(1)} %copy-done.9, bf16[18,2048]{1,0:T(8,128)(2,1)S(1)} %copy-done.8, ...), kind=kLoop, calls=%fused_computation.1 | loop fusion | flops 7077888 | bytes 5332992 | tf_op jit(solution)/shard_map/jit(_where)/select_n | solution.py:162
  45.1 4.2 %select_select_fusion = bf16[64,32,1152]{2,1,0:T(8,128)(2,1)} fusion(pred[64,1152]{1,0:T(8,128)(4,1)S(1)} %get-tuple-element.24, pred[64,1152]{1,0:T(8,128)(4,1)S(1)} %get-tuple-element.25, pred[64,1152]{1,0:T(8,128)(4,1)S(1)} %get-tuple-element.23, bf16[32,1152]{1,0:T(8,128)(2,1)S(1)} %copy-done.12, bf16[32,1152]{1,0:T(8,128)(2,1)S(1)} %copy-done.11, ...), kind=kLoop, calls=%fused_computation | loop fusion | flops 7077888 | bytes 5160960 | tf_op jit(solution)/shard_map/jit(_where)/select_n | solution.py:162
  49.9 14.1 %all-to-all-done = bf16[32,2,2,64,128]{4,3,2,1,0:T(8,128)(2,1)S(1)} async-done(((bf16[32,2,2,64,128]{4,3,2,1,0:T(8,128)(2,1)}), bf16[32,2,2,64,128]{4,3,2,1,0:T(8,128)(2,1)S(1)}, u32[]{:S(2)}, u32[]{:S(2)}) %all-to-all-start) | async-done | bytes 2097184 | tf_op jit(solution)/shard_map/all_to_all | solution.py:606
  64.0 3.7 %all-to-all-start.1 = ((bf16[32,2,2,32,256]{4,3,2,1,0:T(8,128)(2,1)}), bf16[32,2,2,32,256]{4,3,2,1,0:T(8,128)(2,1)}, u32[]{:S(2)}, u32[]{:S(2)}) async-start(bf16[32,2,2,32,256]{4,3,2,1,0:T(8,128)(2,1)} %copy.36), calls=%async_computation.1 | async-start | bytes 4194304 | tf_op jit(solution)/shard_map/all_to_all | solution.py:606
  68.9 2.3 %fusion.2.features_ref = bf16[14,128,384]{2,1,0:T(8,128)(2,1)} fusion(bf16[14,127,128]{2,1,0:T(8,128)(2,1)S(1)} %get-tuple-element.11, bf16[14,127,128]{2,1,0:T(8,128)(2,1)S(1)} %get-tuple-element.10, bf16[3,128,128]{2,1,0:T(8,128)(2,1)} %collective-permute-done.1, bf16[8,128,128]{2,1,0:T(8,128)(2,1)S(1)} %convert_element_type.14, ...), kind=kLoop, calls=%fused_computation.7 | loop fusion | flops 9633792 | bytes 2745344 | tf_op jit(solution)/shard_map/concatenate | solution.py:214
  71.2 49.0 %denoise.1 = f32[32,2,2,8,128]{4,3,2,1,0:T(8,128)} custom-call(s32[2]{0:T(128)} %pad_add_fusion.first_ref, bf16[14,128,384]{2,1,0:T(8,128)(2,1)} %fusion.2.features_ref, f32[8,128,128]{2,1,0:T(8,128)} %prior_ref.1, bf16[1152,2048]{1,0:T(8,128)(2,1)} %bitcast.47, f32[1,2048]{1,0:T(1,128)} %broadcast_in_dim_tile.8.bias_first_ref, bf16[1536,768]{1,0:T(8,128)(2,1)} %bitcast.48, ...), custom_call_target="tpu_custom_call" | custom-call | flops 37446746112 | bytes 16777216 | tf_op jit(solution)/shard_map/denoise/pallas_call | solution.py:229
  120.2 5.6 %all-to-all-start.2 = ((f32[32,2,2,8,128]{4,3,2,1,0:T(8,128)}), f32[32,2,2,8,128]{4,3,2,1,0:T(8,128)S(1)}, u32[]{:S(2)}, u32[]{:S(2)}) async-start(f32[32,2,2,8,128]{4,3,2,1,0:T(8,128)} %denoise.1), calls=%async_computation.2 | async-start | bytes 1048576 | tf_op jit(solution)/shard_map/all_to_all | solution.py:606
  125.8 6.2 %all_gather.3 = bf16[128,256]{1,0:T(8,128)(2,1)S(1)} all-gather(bf16[32,256]{1,0:T(8,128)(2,1)S(1)} %convert_element_type.11), channel_id=1, replica_groups=mesh['slab'=4,'coil'=8] {'slab'}, dimensions={0}, use_global_device_ids=true | all-gather | bytes 81920 | tf_op jit(solution)/shard_map/all_gather | solution.py:693
  133.5 5.9 %adjoint.1 = f32[32,2,2,8,128]{4,3,2,1,0:T(8,128)S(1)} custom-call(bf16[4,8,2,2,32,256]{5,4,3,2,1,0:T(8,128)(2,1)} %bitcast.5.kspace_ref, bf16[4,8,2,2,64,128]{5,4,3,2,1,0:T(8,128)(2,1)S(1)} %bitcast.41, f32[256,128]{1,0:T(8,128)S(1)} %convert_bitcast_fusion.mask_ref, bf16[512,1280]{1,0:T(8,128)(2,1)S(1)} %copy-done.3), custom_call_target="tpu_custom_call" | custom-call | flops 4831838208 | bytes 2097152 | tf_op jit(solution)/shard_map/adjoint/pallas_call | solution.py:559
  139.4 2.7 %all-to-all-done.2 = f32[32,2,2,8,128]{4,3,2,1,0:T(8,128)S(1)} async-done(((f32[32,2,2,8,128]{4,3,2,1,0:T(8,128)}), f32[32,2,2,8,128]{4,3,2,1,0:T(8,128)S(1)}, u32[]{:S(2)}, u32[]{:S(2)}) %all-to-all-start.2) | async-done | bytes 524320 | tf_op jit(solution)/shard_map/all_to_all | solution.py:606
  143.0 3.2 %all-to-all-start.3 = ((f32[32,2,2,8,128]{4,3,2,1,0:T(8,128)}), f32[32,2,2,8,128]{4,3,2,1,0:T(8,128)S(1)}, u32[]{:S(2)}, u32[]{:S(2)}) async-start(f32[32,2,2,8,128]{4,3,2,1,0:T(8,128)} %multiply_add_fusion.field_ref.right_ref), calls=%async_computation.3 | async-start | bytes 1048576 | tf_op jit(solution)/shard_map/all_to_all | solution.py:606
  147.5 11.7 %first_product.1.field_ref = f32[32,2,2,8,128]{4,3,2,1,0:T(8,128)S(1)} custom-call(bf16[4,8,2,2,64,128]{5,4,3,2,1,0:T(8,128)(2,1)S(1)} %bitcast.42, f32[32,2,2,8,128]{4,3,2,1,0:T(8,128)} %multiply_add_fusion.field_ref.right_ref, f32[256,128]{1,0:T(8,128)S(1)} %convert_bitcast_fusion.mask_ref, bf16[512,1280]{1,0:T(8,128)(2,1)S(1)} %copy-done.4), custom_call_target="tpu_custom_call" | custom-call | flops 9663676416 | bytes 2097152 | tf_op jit(solution)/shard_map/first_product/pallas_call | solution.py:572
  160.0 2.4 %all-to-all-done.3.right_ref = f32[32,2,2,8,128]{4,3,2,1,0:T(8,128)S(1)} async-done(((f32[32,2,2,8,128]{4,3,2,1,0:T(8,128)}), f32[32,2,2,8,128]{4,3,2,1,0:T(8,128)S(1)}, u32[]{:S(2)}, u32[]{:S(2)}) %all-to-all-start.3) | async-done | bytes 524320 | tf_op jit(solution)/shard_map/all_to_all | solution.py:606
  162.4 3.3 %all-to-all-start.4 = ((f32[32,2,2,8,128]{4,3,2,1,0:T(8,128)}), f32[32,2,2,8,128]{4,3,2,1,0:T(8,128)S(1)}, u32[]{:S(2)}, u32[]{:S(2)}) async-start(f32[32,2,2,8,128]{4,3,2,1,0:T(8,128)} %copy-done.1), calls=%async_computation.4 | async-start | bytes 1048576 | tf_op jit(solution)/shard_map/all_to_all | solution.py:606
  168.0 11.8 %second_product.1 = f32[32,5,8,128]{3,2,1,0:T(8,128)S(1)} custom-call(bf16[4,8,2,2,64,128]{5,4,3,2,1,0:T(8,128)(2,1)S(1)} %bitcast.43, f32[32,2,2,8,128]{4,3,2,1,0:T(8,128)} %multiply_add_fusion.field_ref.right_ref, f32[32,2,2,8,128]{4,3,2,1,0:T(8,128)S(1)} %copy-done.2, f32[256,128]{1,0:T(8,128)S(1)} %convert_bitcast_fusion.mask_ref, ...), custom_call_target="tpu_custom_call" | custom-call | flops 9663676416 | bytes 2097152 | tf_op jit(solution)/shard_map/second_product/pallas_call | solution.py:587
  182.0 23.7 %all_to_all.30.image_ref = f32[32,5,8,128]{3,2,1,0:T(8,128)S(1)} all-to-all(f32[32,5,8,128]{3,2,1,0:T(8,128)} %copy-done), channel_id=1, replica_groups=mesh['slab'=4,'coil'=8] {'slab','coil'}, dimensions={0} | all-to-all | bytes 1310720 | tf_op jit(solution)/shard_map/all_to_all | solution.py:606
  205.7 1.5 finish.1
  (103 shorter events, 25.0 us)
Async XLA Ops:
  5.6 7.3 %copy-start.6 = (f32[8,128,128]{2,1,0:T(8,128)S(1)}, f32[8,128,128]{2,1,0:T(8,128)}, u32[]{:S(2)}) copy-start(f32[8,128,128]{2,1,0:T(8,128)} %prior_ref.1) | copy-start | bytes 1572868
  5.6 13.1 %copy-start.15 = (bf16[3,3,3,32,2]{3,4,2,1,0:T(2,128)(2,1)S(1)}, bf16[3,3,3,32,2]{3,4,2,1,0:T(2,128)(2,1)}, u32[]{:S(2)}) copy-start(bf16[3,3,3,32,2]{3,4,2,1,0:T(2,128)(2,1)} %param.15) | copy-start | bytes 10372
  5.6 58.4 %all-to-all-start = ((bf16[32,2,2,64,128]{4,3,2,1,0:T(8,128)(2,1)}), bf16[32,2,2,64,128]{4,3,2,1,0:T(8,128)(2,1)S(1)}, u32[]{:S(2)}, u32[]{:S(2)}) async-start(bf16[32,2,2,64,128]{4,3,2,1,0:T(8,128)(2,1)} %copy.34), calls=%async_computation | async-start | bytes 4194304 | tf_op jit(solution)/shard_map/all_to_all | solution.py:606
  12.9 8.8 %copy-start.16 = (bf16[3,3,3,2,32]{4,3,2,1,0:T(2,128)(2,1)S(1)}, bf16[3,3,3,2,32]{4,3,2,1,0:T(2,128)(2,1)}, u32[]{:S(2)}) copy-start(bf16[3,3,3,2,32]{4,3,2,1,0:T(2,128)(2,1)} %param.19) | copy-start | bytes 10372
  12.9 12.2 %copy-start.13 = (bf16[3,3,3,32,32]{4,3,2,1,0:T(8,128)(2,1)S(1)}, bf16[3,3,3,32,32]{4,3,2,1,0:T(8,128)(2,1)}, u32[]{:S(2)}) copy-start(bf16[3,3,3,32,32]{4,3,2,1,0:T(8,128)(2,1)} %param.17) | copy-start | bytes 165892
  13.7 54.0 %collective-permute-start = (bf16[3,128,128]{2,1,0:T(8,128)(2,1)}, bf16[3,128,128]{2,1,0:T(8,128)(2,1)S(1)}, u32[]{:S(2)}, u32[]{:S(2)}) collective-permute-start(bf16[3,128,128]{2,1,0:T(8,128)(2,1)} %get-tuple-element.12), channel_id=1, source_target_pairs={{0,1},{1,2},{2,3},{3,4},{4,5},{5,6},{6,7},{7,8},{8,9},{9,10},{10,1... | collective-permute-start | bytes 294920 | tf_op jit(solution)/shard_map/ppermute | solution.py:28
  17.4 50.4 %collective-permute-start.1 = (bf16[3,128,128]{2,1,0:T(8,128)(2,1)}, bf16[3,128,128]{2,1,0:T(8,128)(2,1)}, u32[]{:S(2)}, u32[]{:S(2)}) collective-permute-start(bf16[3,128,128]{2,1,0:T(8,128)(2,1)} %get-tuple-element.13), channel_id=1, source_target_pairs={{1,0},{2,1},{3,2},{4,3},{5,4},{6,5},{7,6},{8,7},{9,8},{10,9},{11,1... | collective-permute-start | bytes 294920 | tf_op jit(solution)/shard_map/ppermute | solution.py:29
  25.9 2.6 %copy-start.17 = (f32[32]{0:T(128)S(1)}, f32[32]{0:T(128)}, u32[]{:S(2)}) copy-start(f32[32]{0:T(128)} %param.16) | copy-start | bytes 388
  25.9 3.3 %copy-start.18 = (f32[32]{0:T(128)S(1)}, f32[32]{0:T(128)}, u32[]{:S(2)}) copy-start(f32[32]{0:T(128)} %param.18) | copy-start | bytes 388
  25.9 4.0 %copy-start.19 = (f32[2]{0:T(128)S(1)}, f32[2]{0:T(128)}, u32[]{:S(2)}) copy-start(f32[2]{0:T(128)} %param.20) | copy-start | bytes 28
  38.4 2.5 %copy-start.7 = (bf16[18,2048]{1,0:T(8,128)(2,1)S(1)}, bf16[18,2048]{1,0:T(8,128)(2,1)}, u32[]{:S(2)}) copy-start(bf16[18,2048]{1,0:T(8,128)(2,1)} %broadcast_in_dim.172) | copy-start | bytes 221188
  38.4 2.5 %copy-start.8 = (bf16[18,2048]{1,0:T(8,128)(2,1)S(1)}, bf16[18,2048]{1,0:T(8,128)(2,1)}, u32[]{:S(2)}) copy-start(bf16[18,2048]{1,0:T(8,128)(2,1)} %broadcast_in_dim.176) | copy-start | bytes 221188
  38.4 2.5 %copy-start.9 = (bf16[18,2048]{1,0:T(8,128)(2,1)S(1)}, bf16[18,2048]{1,0:T(8,128)(2,1)}, u32[]{:S(2)}) copy-start(bf16[18,2048]{1,0:T(8,128)(2,1)} %broadcast_in_dim.180) | copy-start | bytes 221188
  40.9 4.1 %copy-start.10 = (bf16[32,1152]{1,0:T(8,128)(2,1)S(1)}, bf16[32,1152]{1,0:T(8,128)(2,1)}, u32[]{:S(2)}) copy-start(bf16[32,1152]{1,0:T(8,128)(2,1)} %broadcast_in_dim.198) | copy-start | bytes 221188
  41.0 4.1 %copy-start.11 = (bf16[32,1152]{1,0:T(8,128)(2,1)S(1)}, bf16[32,1152]{1,0:T(8,128)(2,1)}, u32[]{:S(2)}) copy-start(bf16[32,1152]{1,0:T(8,128)(2,1)} %broadcast_in_dim.202) | copy-start | bytes 221188
  41.0 4.1 %copy-start.12 = (bf16[32,1152]{1,0:T(8,128)(2,1)S(1)}, bf16[32,1152]{1,0:T(8,128)(2,1)}, u32[]{:S(2)}) copy-start(bf16[32,1152]{1,0:T(8,128)(2,1)} %broadcast_in_dim.206) | copy-start | bytes 221188
  64.0 56.1 %all-to-all-start.1 = ((bf16[32,2,2,32,256]{4,3,2,1,0:T(8,128)(2,1)}), bf16[32,2,2,32,256]{4,3,2,1,0:T(8,128)(2,1)}, u32[]{:S(2)}, u32[]{:S(2)}) async-start(bf16[32,2,2,32,256]{4,3,2,1,0:T(8,128)(2,1)} %copy.36), calls=%async_computation.1 | async-start | bytes 4194304 | tf_op jit(solution)/shard_map/all_to_all | solution.py:606
  71.2 54.6 %copy-start.14 = (s32[32,256]{1,0:T(8,128)S(1)}, s32[32,256]{1,0:T(8,128)}, u32[]{:S(2)}) copy-start(s32[32,256]{1,0:T(8,128)} %param.14) | copy-start | bytes 98308
  120.2 21.9 %all-to-all-start.2 = ((f32[32,2,2,8,128]{4,3,2,1,0:T(8,128)}), f32[32,2,2,8,128]{4,3,2,1,0:T(8,128)S(1)}, u32[]{:S(2)}, u32[]{:S(2)}) async-start(f32[32,2,2,8,128]{4,3,2,1,0:T(8,128)} %denoise.1), calls=%async_computation.2 | async-start | bytes 1048576 | tf_op jit(solution)/shard_map/all_to_all | solution.py:606
  132.2 1.3 copy-start.3
  143.0 19.4 %all-to-all-start.3 = ((f32[32,2,2,8,128]{4,3,2,1,0:T(8,128)}), f32[32,2,2,8,128]{4,3,2,1,0:T(8,128)S(1)}, u32[]{:S(2)}, u32[]{:S(2)}) async-start(f32[32,2,2,8,128]{4,3,2,1,0:T(8,128)} %multiply_add_fusion.field_ref.right_ref), calls=%async_computation.3 | async-start | bytes 1048576 | tf_op jit(solution)/shard_map/all_to_all | solution.py:606
  146.2 1.3 copy-start.4
  162.4 19.6 %all-to-all-start.4 = ((f32[32,2,2,8,128]{4,3,2,1,0:T(8,128)}), f32[32,2,2,8,128]{4,3,2,1,0:T(8,128)S(1)}, u32[]{:S(2)}, u32[]{:S(2)}) async-start(f32[32,2,2,8,128]{4,3,2,1,0:T(8,128)} %copy-done.1), calls=%async_computation.4 | async-start | bytes 1048576 | tf_op jit(solution)/shard_map/all_to_all | solution.py:606
  166.7 1.3 copy-start.5
  (3 other events, 2.7 us)

commit v7 on v6

--- a/solution.py
+++ b/solution.py
@@ -164,7 +164,15 @@
 
 
 def denoise(
-    parts, prior_image, weight_first, bias_first, weight_middle, bias_middle, weight_last, bias_last
+    parts,
+    features,
+    prior_image,
+    weight_first,
+    bias_first,
+    weight_middle,
+    bias_middle,
+    weight_last,
+    bias_last,
 ):
     own_rows, planes, width = prior_image.shape
     turned = own_rows % 8 == 0
@@ -209,7 +217,6 @@
         1,
     ).reshape(span, 18 * readout)
 
-    features = with_halo(prior_image.astype(jnp.bfloat16), 3)
     rim = jnp.zeros_like(features[:, :1])
     features = jnp.concatenate(
         [
@@ -348,13 +355,24 @@
     return value.reshape(value.shape[0] * value.shape[1], value.shape[2])
 
 
-def coil_plane(ref, coil, part):
-    value = ref[:, coil, part, 0]
+def coil_plane(ref, coil):
+    value = ref[:, coil, 0]
     return value.reshape(value.shape[0] * value.shape[1], value.shape[2])
 
 
-def map_of(ref, coil):
-    return [coil_plane(ref, coil, part).astype(jnp.float32) for part in range(2)]
+def map_of(refs, coil):
+    return [coil_plane(ref, coil).astype(jnp.float32) for ref in refs]
+
+
+def spectrum_plane(ref, coil, rows):
+    value = ref[:, coil, 0]
+    slabs, held, lanes = value.shape
+    planes = held * lanes // rows
+    pieces = [
+        value[:, first : first + planes].reshape(slabs * planes, lanes)
+        for first in range(0, held, planes)
+    ]
+    return jnp.concatenate(pieces, axis=1)
 
 
 def image_sums(maps, fields):
@@ -365,20 +383,20 @@
     return sums
 
 
-def units_of(ref):
-    count = ref.shape[1]
+def units_of(refs):
+    count = refs[0].shape[1]
     held = 2 if count % 2 == 0 else 1
     return [tuple(range(first, first + held)) for first in range(0, count, held)]
 
 
-def normal_sums(maps_ref, real, imag, mask, tables):
+def normal_sums(maps_refs, real, imag, mask, tables):
     row_table, plane_table = tables
-    units = units_of(maps_ref)
+    units = units_of(maps_refs)
     fields = []
     for unit in units:
         products = []
         for coil in unit:
-            map_real, map_imag = map_of(maps_ref, coil)
+            map_real, map_imag = map_of(maps_refs, coil)
             products.append(
                 (map_real * real - map_imag * imag, map_real * imag + map_imag * real)
             )
@@ -392,23 +410,40 @@
     fields = [along_planes(field, plane_table) for field in fields]
     total = None
     for unit, field in zip(units, fields):
-        sums = image_sums([map_of(maps_ref, coil) for coil in unit], field)
+        sums = image_sums([map_of(maps_refs, coil) for coil in unit], field)
         total = sums if total is None else (total[0] + sums[0], total[1] + sums[1])
     return total
 
 
-def adjoint_kernel(kspace_ref, maps_ref, mask_ref, table_ref, out_ref):
+def accumulate(out_ref, values, places):
+    shape = out_ref.shape[0], out_ref.shape[-2], out_ref.shape[-1]
+
+    @pl.when(pl.program_id(1) == 0)
+    def _():
+        for value, place in zip(values, places):
+            out_ref[(slice(None),) + place] = value.reshape(shape)
+
+    @pl.when(pl.program_id(1) > 0)
+    def _():
+        for value, place in zip(values, places):
+            out_ref[(slice(None),) + place] += value.reshape(shape)
+
+
+def adjoint_kernel(
+    spectra_real_ref, spectra_imag_ref, maps_real_ref, maps_imag_ref, mask_ref, table_ref, out_ref
+):
+    maps_refs = maps_real_ref, maps_imag_ref
     mask = mask_ref[...]
     rows, planes = mask.shape
     row_table, plane_table = tables_of(table_ref, rows, planes)
-    units = units_of(maps_ref)
+    units = units_of(maps_refs)
     images = []
     for unit in units:
         spectra = []
         for coil in unit:
             real, imag = (
-                jnp.transpose(coil_plane(kspace_ref, coil, part).astype(jnp.float32))
-                for part in range(2)
+                jnp.transpose(spectrum_plane(ref, coil, rows).astype(jnp.float32))
+                for ref in (spectra_real_ref, spectra_imag_ref)
             )
             spectra.append((real * mask, imag * -mask))
         spectrum = side_by_side(spectra).astype(jnp.bfloat16)
@@ -421,96 +456,91 @@
     images = [along_planes(image, plane_table) for image in images]
     total = None
     for unit, image in zip(units, images):
-        sums = image_sums([map_of(maps_ref, coil) for coil in unit], image)
+        sums = image_sums([map_of(maps_refs, coil) for coil in unit], image)
         total = sums if total is None else (total[0] + sums[0], total[1] + sums[1])
-    shape = out_ref.shape[0], out_ref.shape[3], out_ref.shape[4]
-
-    @pl.when(pl.program_id(1) == 0)
+    accumulate(out_ref, total, ((0, 0), (1, 0)))
+
+
+def lane_sums(left, other):
+    product = left[0] * other[0] + left[1] * other[1]
+    return jnp.sum(jnp.sum(product, axis=0), axis=0, keepdims=True)
+
+
+def first_kernel(
+    maps_real_ref, maps_imag_ref, adjoint_ref, denoised_ref, mask_ref, table_ref, out_ref, total_ref
+):
+    mask = mask_ref[...]
+    rights = [
+        plane_of(adjoint_ref, part) + penalty * plane_of(denoised_ref, part) for part in range(2)
+    ]
+    sums = normal_sums(
+        (maps_real_ref, maps_imag_ref), *rights, mask, tables_of(table_ref, *mask.shape)
+    )
+    accumulate(out_ref, sums, ((0, 0), (1, 0)))
+
+    @pl.when(pl.program_id(1) == pl.num_programs(1) - 1)
     def _():
-        for part in range(2):
-            out_ref[:, part, 0] = total[part].reshape(shape)
-
-    @pl.when(pl.program_id(1) > 0)
-    def _():
-        for part in range(2):
-            out_ref[:, part, 0] += total[part].reshape(shape)
-
-
-def first_kernel(maps_ref, field_ref, mask_ref, table_ref, out_ref):
+        shape = out_ref.shape[0], out_ref.shape[3], out_ref.shape[4]
+        sides = [right.reshape(shape) for right in rights]
+        fields = [out_ref[:, part, 0] for part in range(2)]
+        totals = jnp.concatenate(
+            [
+                lane_sums(sides, sides),
+                lane_sums(sides, fields),
+                lane_sums(fields, fields),
+                jnp.zeros((total_ref.shape[0] - 3, total_ref.shape[1]), jnp.float32),
+            ],
+            axis=0,
+        )
+
+        @pl.when(pl.program_id(0) == 0)
+        def _():
+            total_ref[...] = totals
+
+        @pl.when(pl.program_id(0) > 0)
+        def _():
+            total_ref[...] += totals
+
+
+def second_kernel(
+    maps_real_ref, maps_imag_ref, field_ref, total_ref, mask_ref, table_ref, out_ref
+):
+    x_index = pl.program_id(0)
+    x_count = pl.num_programs(0)
+    blocks, block_rows, planes = out_ref.shape[0], out_ref.shape[2], out_ref.shape[3]
     mask = mask_ref[...]
     sums = normal_sums(
-        maps_ref,
+        (maps_real_ref, maps_imag_ref),
         plane_of(field_ref, 0),
         plane_of(field_ref, 1),
         mask,
         tables_of(table_ref, *mask.shape),
     )
-    shape = out_ref.shape[0], out_ref.shape[3], out_ref.shape[4]
-
-    @pl.when(pl.program_id(1) == 0)
-    def _():
-        for part in range(2):
-            out_ref[:, part, 0] = sums[part].reshape(shape)
-
-    @pl.when(pl.program_id(1) > 0)
-    def _():
-        for part in range(2):
-            out_ref[:, part, 0] += sums[part].reshape(shape)
-
-
-def second_kernel(maps_ref, right_ref, field_ref, mask_ref, table_ref, out_ref):
-    x_index = pl.program_id(0)
-    x_count = pl.num_programs(0)
-    blocks, block_rows, planes = out_ref.shape[0], out_ref.shape[2], out_ref.shape[3]
-    shape = blocks, block_rows, planes
-    mask = mask_ref[...]
-    sums = normal_sums(
-        maps_ref,
-        plane_of(field_ref, 0),
-        plane_of(field_ref, 1),
-        mask,
-        tables_of(table_ref, *mask.shape),
-    )
-
-    @pl.when(pl.program_id(1) == 0)
-    def _():
-        for part in range(2):
-            out_ref[:, part * x_count + x_index] = sums[part].reshape(shape)
-
-    @pl.when(pl.program_id(1) > 0)
-    def _():
-        for part in range(2):
-            out_ref[:, part * x_count + x_index] += sums[part].reshape(shape)
+    places = [(part * x_count + x_index,) for part in range(2)]
+    accumulate(out_ref, sums, places)
 
     @pl.when(pl.program_id(1) == pl.num_programs(1) - 1)
     def _():
-        rights = [right_ref[:, part, 0] for part in range(2)]
         fields = [field_ref[:, part, 0] for part in range(2)]
-        images = [out_ref[:, part * x_count + x_index] for part in range(2)]
-
-        def lane_sums(left, other):
-            product = left[0] * other[0] + left[1] * other[1]
-            return jnp.sum(jnp.sum(product, axis=0), axis=0, keepdims=True)
-
+        images = [out_ref[(slice(None),) + place] for place in places]
         totals = jnp.concatenate(
             [
-                lane_sums(rights, rights),
-                lane_sums(rights, fields),
-                lane_sums(fields, fields),
+                jnp.zeros((3, planes), jnp.float32),
                 lane_sums(fields, images),
                 jnp.zeros((block_rows - 4, planes), jnp.float32),
             ],
             axis=0,
         )
-        totals = jnp.broadcast_to(totals[None], shape)
 
         @pl.when(x_index == 0)
         def _():
-            out_ref[:, 2 * x_count] = totals
+            out_ref[:, 2 * x_count] = jnp.broadcast_to(
+                (total_ref[...] + totals)[None], (blocks, block_rows, planes)
+            )
 
         @pl.when(x_index > 0)
         def _():
-            out_ref[:, 2 * x_count] += totals
+            out_ref[:, 2 * x_count] += totals[None]
 
 
 def held_coils(count):
@@ -521,19 +551,16 @@
     return pl.BlockSpec(shape, lambda x, c: (0,) * len(shape))
 
 
-def maps_spec(maps):
-    slabs, coils, _, _, slab_rows, planes = maps.shape
+def coils_spec(planes):
+    values, first = planes
+    slabs, coils, _, rows, lanes = values.shape
     return pl.BlockSpec(
-        (slabs, held_coils(coils), 2, 1, slab_rows, planes), lambda x, c: (0, c, 0, x, 0, 0)
+        (slabs, held_coils(coils), 1, rows, lanes), lambda x, c: (0, c, first + x, 0, 0)
     )
 
 
 def field_spec(shape):
     return pl.BlockSpec((shape[0], 2, 1) + shape[3:], lambda x, c: (0, 0, x, 0, 0))
-
-
-def grid_of(maps):
-    return maps.shape[3], maps.shape[1] // held_coils(maps.shape[1])
 
 
 def compute_params():
@@ -542,73 +569,62 @@
     )
 
 
-def product_cost(maps, passes):
-    slabs, coils, _, x_count, slab_rows, planes = maps.shape
-    rows = slabs * slab_rows
-    per_plane = 2 * 2 * rows * planes * (2 * rows + 2 * planes)
-    return pl.CostEstimate(
-        flops=int(coils * x_count * per_plane * passes),
-        bytes_accessed=int(2 * maps.size),
-        transcendentals=0,
-    )
-
-
-def adjoint_call(spectra, maps, mask, table, blocks):
+def product_call(kernel, name, x_count, coil_planes, fields, extras, constants, outs, passes):
+    coils = coil_planes[0][0].shape[1]
+    mask = constants[0]
     rows, planes = mask.shape
-    shape = (blocks, 2, maps.shape[3], rows // blocks, planes)
+    flops = 2 * 2 * rows * planes * (2 * rows + 2 * planes) * coils * x_count * passes
+    values = [planes_of[0] for planes_of in coil_planes] + fields + extras + constants
     return pl.pallas_call(
-        adjoint_kernel,
-        grid=grid_of(maps),
-        in_specs=[maps_spec(spectra), maps_spec(maps), whole(mask.shape), whole(table.shape)],
-        out_specs=field_spec(shape),
-        out_shape=jax.ShapeDtypeStruct(shape, jnp.float32),
+        kernel,
+        grid=(x_count, coils // held_coils(coils)),
+        in_specs=[coils_spec(planes_of) for planes_of in coil_planes]
+        + [field_spec(field.shape) for field in fields]
+        + [whole(value.shape) for value in extras + constants],
+        out_specs=[spec for spec, _ in outs],
+        out_shape=[jax.ShapeDtypeStruct(shape, jnp.float32) for _, shape in outs],
         compiler_params=compute_params(),
-        cost_estimate=product_cost(maps, 3),
-        name="adjoint",
-    )(spectra, maps, mask, table)
-
-
-def first_call(maps, field, mask, table):
-    return pl.pallas_call(
-        first_kernel,
-        grid=grid_of(maps),
-        in_specs=[maps_spec(maps), field_spec(field.shape), whole(mask.shape), whole(table.shape)],
-        out_specs=field_spec(field.shape),
-        out_shape=jax.ShapeDtypeStruct(field.shape, jnp.float32),
-        compiler_params=compute_params(),
-        cost_estimate=product_cost(maps, 6),
-        name="first_product",
-    )(maps, field, mask, table)
-
-
-def second_call(maps, right, field, mask, table):
+        cost_estimate=pl.CostEstimate(
+            flops=int(flops), bytes_accessed=8 * 1024 * 1024, transcendentals=0
+        ),
+        name=name,
+    )(*values)
+
+
+def adjoint_call(spectra, maps, constants, x_count, blocks):
+    rows, planes = constants[0].shape
+    shape = (blocks, 2, x_count, rows // blocks, planes)
+    outs = [(field_spec(shape), shape)]
+    return product_call(
+        adjoint_kernel, "adjoint", x_count, spectra + maps, [], [], constants, outs, 3
+    )[0]
+
+
+def first_call(maps, adjoint, denoised, constants):
+    shape = adjoint.shape
+    totals = (8, shape[4])
+    outs = [(field_spec(shape), shape), (whole(totals), totals)]
+    return product_call(
+        first_kernel, "first_product", shape[2], maps, [adjoint, denoised], [], constants, outs, 6
+    )
+
+
+def second_call(maps, field, totals, constants):
     blocks, _, x_count, block_rows, planes = field.shape
-    out_shape = (blocks, 2 * x_count + 1, block_rows, planes)
-    return pl.pallas_call(
-        second_kernel,
-        grid=grid_of(maps),
-        in_specs=[
-            maps_spec(maps),
-            field_spec(field.shape),
-            field_spec(field.shape),
-            whole(mask.shape),
-            whole(table.shape),
-        ],
-        out_specs=whole(out_shape),
-        out_shape=jax.ShapeDtypeStruct(out_shape, jnp.float32),
-        compiler_params=compute_params(),
-        cost_estimate=product_cost(maps, 6),
-        name="second_product",
-    )(maps, right, field, mask, table)
+    shape = (blocks, 2 * x_count + 1, block_rows, planes)
+    outs = [(whole(shape), shape)]
+    return product_call(
+        second_kernel, "second_product", x_count, maps, [field], [totals], constants, outs, 6
+    )[0]
 
 
 def exchange(blocks, axis):
     return lax.all_to_all(blocks, axis, split_axis=0, concat_axis=0, tiled=True)
 
 
-def x_first(cells, parts):
+def x_first(cells, parts, count=2):
     rows, planes, width = cells.shape
-    split = cells.reshape(rows, planes, 2, parts, width // (2 * parts))
+    split = cells.reshape(rows, planes, count, parts, width // (count * parts))
     return jnp.transpose(split, (3, 2, 4, 0, 1))
 
 
@@ -634,8 +650,10 @@
     return (moved, -bent), (alpha * ratio - penalty * second * weight, penalty * bent - moved, bent)
 
 
-def finish_kernel(right_ref, field_ref, image_ref, solution_ref, residual_ref, rows_ref):
-    blocks, _, x_count, rows, planes = right_ref.shape
+def finish_kernel(
+    adjoint_ref, denoised_ref, field_ref, image_ref, solution_ref, residual_ref, rows_ref
+):
+    blocks, _, x_count, rows, planes = adjoint_ref.shape
     readout = blocks * x_count
     totals = jnp.sum(jnp.sum(image_ref[:, 2 * x_count], axis=0), axis=1, keepdims=True)
     found = factors(*(totals[index : index + 1] for index in range(4)))
@@ -643,7 +661,8 @@
         scales = [jnp.broadcast_to(scale, (rows, planes))[None] for scale in scales]
         for part in range(2):
             for inner in range(x_count):
-                value = scales[0] * right_ref[:, part, inner] + scales[1] * field_ref[:, part, inner]
+                right = adjoint_ref[:, part, inner] + penalty * denoised_ref[:, part, inner]
+                value = scales[0] * right + scales[1] * field_ref[:, part, inner]
                 if len(scales) > 2:
                     value = value + scales[2] * image_ref[:, part * x_count + inner]
                 for block in range(blocks):
@@ -653,22 +672,22 @@
             out_ref[row] = jnp.transpose(rows_ref[pl.ds(row, 2 * readout, stride=rows), :])
 
 
-def finish_call(right, field, image):
-    blocks, _, x_count, rows, planes = right.shape
+def finish_call(adjoint, denoised, field, image):
+    blocks, _, x_count, rows, planes = adjoint.shape
     shape = (rows, planes, 2 * blocks * x_count)
     vmem = pl.BlockSpec(memory_space=pltpu.VMEM)
     return pl.pallas_call(
         finish_kernel,
-        in_specs=[vmem] * 3,
+        in_specs=[vmem] * 4,
         out_specs=[vmem] * 2,
         out_shape=[jax.ShapeDtypeStruct(shape, jnp.float32)] * 2,
         scratch_shapes=[pltpu.VMEM((2 * blocks * x_count * rows, planes), jnp.float32)],
         compiler_params=pltpu.CompilerParams(vmem_limit_bytes=32 * 1024 * 1024),
         cost_estimate=pl.CostEstimate(
-            flops=8 * right.size, bytes_accessed=20 * right.size, transcendentals=0
+            flops=8 * adjoint.size, bytes_accessed=24 * adjoint.size, transcendentals=0
         ),
         name="finish",
-    )(right, field, image)
+    )(adjoint, denoised, field, image)
 
 
 def body(
@@ -689,24 +708,54 @@
     slabs = lax.axis_size("slab")
     coils = lax.axis_size("coil")
     devices = slabs * coils
-    mask = jnp.transpose(
-        lax.all_gather(sampling.astype(jnp.bfloat16), "slab", axis=0, tiled=True)
-    ).astype(jnp.float32)
-    spread = readout % devices == 0 and own_rows % 8 == 0
+    spread = readout % devices == 0 and own_rows % 8 == 0 and coil_maps.shape[1] % 16 == 0
     parts = devices if spread else coils
-
-    def coils_to_x(blocks):
-        tail = blocks.shape[1:]
-        if spread:
-            return exchange(blocks, axes).reshape((slabs, coils) + tail)
-        blocks = exchange(blocks, "coil").reshape((slabs, coils // slabs) + tail)
-        return exchange(blocks, "slab")
-
-    maps = coils_to_x(x_first(coil_maps[0], parts))
-    spectra = coils_to_x(x_first(kspace[0], parts))
-    table = jnp.asarray(dft_table(sampling.shape[1], planes))
+    x_count = readout // parts
+    mask = lax.all_gather(sampling.astype(jnp.bfloat16), "slab", axis=0, tiled=True)
+    features, mask = lax.optimization_barrier(
+        (with_halo(prior_image.astype(jnp.bfloat16), 3), mask)
+    )
+    constants = [
+        jnp.transpose(mask).astype(jnp.float32),
+        jnp.asarray(dft_table(sampling.shape[1], planes)),
+    ]
+
+    if spread:
+        own_maps, measured = coil_maps[0], kspace[0]
+        real = x_first(own_maps[..., :readout], parts, 1)
+        imag = x_first(own_maps[..., readout:], parts, 1)
+        slab_rows = own_maps.shape[0]
+        slab_planes, row_count = measured.shape[:2]
+        measured = measured.reshape(
+            slab_planes, row_count // planes, planes, 2, parts, x_count
+        )
+        measured = jnp.transpose(measured, (4, 3, 5, 1, 0, 2)).reshape(
+            parts, 2 * x_count, slab_rows, planes
+        )
+        real = exchange(real.reshape(parts, x_count, slab_rows, planes), axes)
+        rest = exchange(
+            jnp.concatenate([imag.reshape(parts, x_count, slab_rows, planes), measured], axis=1),
+            axes,
+        )
+        real = real.reshape((slabs, coils) + real.shape[1:])
+        rest = rest.reshape((slabs, coils) + rest.shape[1:])
+        maps = [(real, 0), (rest, 0)]
+        spectra = [(rest, x_count), (rest, 2 * x_count)]
+    else:
+
+        def coils_to_x(values):
+            blocks = x_first(values, parts)
+            tail = blocks.shape[1:]
+            blocks = exchange(blocks, "coil").reshape((slabs, coils // slabs) + tail)
+            blocks = exchange(blocks, "slab")
+            return [(blocks[:, :, part], 0) for part in range(2)]
+
+        maps = coils_to_x(coil_maps[0])
+        spectra = coils_to_x(kspace[0])
+
     blocks = denoise(
         parts,
+        features,
         prior_image,
         weight_first,
         bias_first,
@@ -718,15 +767,13 @@
     if blocks.ndim == 3:
         blocks = x_first(blocks, parts)
     if spread:
-        denoised = exchange(blocks, axes)
-        right = adjoint_call(spectra, maps, mask, table, devices) + penalty * denoised
-        field, right_back = lax.optimization_barrier(
-            (first_call(maps, right, mask, table), exchange(right, axes))
-        )
+        adjoint = adjoint_call(spectra, maps, constants, x_count, devices)
+        field, totals = first_call(maps, adjoint, exchange(blocks, axes), constants)
+        field, adjoint_back = lax.optimization_barrier((field, exchange(adjoint, axes)))
         payload, field_back = lax.optimization_barrier(
-            (second_call(maps, right, field, mask, table), exchange(field, axes))
-        )
-        return tuple(finish_call(right_back, field_back, exchange(payload, axes)))
+            (second_call(maps, field, totals, constants), exchange(field, axes))
+        )
+        return tuple(finish_call(adjoint_back, blocks, field_back, exchange(payload, axes)))
 
     tail = blocks.shape[1:3]
 
@@ -740,10 +787,11 @@
         split = jnp.transpose(mine.reshape(tail + (coils, own_rows, planes)), (2, 0, 1, 3, 4))
         return x_last(exchange(split, "coil"))
 
-    adjoint = lax.psum(adjoint_call(spectra, maps, mask, table, 1), "slab")
-    right = adjoint + penalty * whole_rows(blocks)
-    field = lax.psum(first_call(maps, right, mask, table), "slab")
-    image = lax.psum(first_call(maps, field, mask, table), "slab")
+    adjoint = lax.psum(adjoint_call(spectra, maps, constants, x_count, 1), "slab")
+    denoised = whole_rows(blocks)
+    right = adjoint + penalty * denoised
+    field = lax.psum(first_call(maps, adjoint, denoised, constants)[0], "slab")
+    image = lax.psum(first_call(maps, field, jnp.zeros_like(field), constants)[0], "slab")
     squares = lax.psum(
         jnp.stack(
             [

time: 208 us -> 246 us (1.18)
  local copies, waits for them, and re-layouts: 32.2 us -> 70.8 us
  waiting for transfers between devices: 20.5 us -> 14.5 us
  other arithmetic: 15.6 us -> 19.1 us
    slice x15, local copies, waits for them, and re-layouts: 2.32 us -> 13.5 us  [banded(): result = jnp.where(inner - outer + offset == tap, tiles[tap], result)]
    broadcast_in_dim x6, local copies, waits for them, and re-layouts: 2.99 us -> 10.2 us  [denoise(): jnp.broadcast_to(tiles, (3, 18, 1, readout, channels))]
    broadcast_in_dim x6, local copies, waits for them, and re-layouts: 2.87 us -> 9.78 us  [denoise(): jnp.broadcast_to(tiles, (3, 1, channels, 18, readout))]
    all_to_all x5, waiting for transfers between devices: 20.5 us -> 14.5 us  [exchange(): return lax.all_to_all(blocks, axis, split_axis=0, concat_axis=0, tiled=True)]
    another operation x0 -> x1, local copies, waits for them, and re-layouts: none -> 2.54 us  [body(): measured.reshape(slab_planes, row_count // planes, planes, 2, parts, x_co...]
    transpose x2 -> x1, local copies, waits for them, and re-layouts: 4.9 us -> 2.43 us  [body(): jnp.transpose(measured, (4, 3, 5, 1, 0, 2))]
    unnamed x42 -> x48, local copies, waits for them, and re-layouts: 14.6 us -> 16.6 us
  transfers between devices with their start and end apart: 7 -> 7, of which waited for: 4 -> 4; matrix products, arithmetic and copies ran while one was open for 17% -> 31% of each run, Pallas kernels for 38% -> 32%
where the time goes in v7:
time: 246 us; the launch traced here: 244 us
  Pallas kernels  80.1 us (33%)
  local copies, waits for them, and re-layouts  70.8 us (29%)
  starting transfers between devices  30.3 us (12%)
  blocking collectives  27.7 us (11%)
  other arithmetic  19.1 us (8%)
  waiting for transfers between devices  14.5 us (6%)
    pallas_call x1, Pallas kernels, denoise(): pl.pallas_call(functools.partial(denoise_kernel, group), in_specs=[pl.Blo...  49 us
    pallas_call x3, Pallas kernels, product_call(): pl.pallas_call(kernel, grid=(x_count, coils // held_coils(coils)), in_spe...  29.6 us
    all_to_all x5, starting transfers between devices, exchange(): return lax.all_to_all(blocks, axis, split_axis=0, concat_axis=0, tiled=True)  24.7 us
    all_to_all x1, blocking collectives, exchange(): return lax.all_to_all(blocks, axis, split_axis=0, concat_axis=0, tiled=True)  21.7 us
    unnamed x48, local copies, waits for them, and re-layouts  16.6 us
    all_to_all x5, waiting for transfers between devices, exchange(): return lax.all_to_all(blocks, axis, split_axis=0, concat_axis=0, tiled=True)  14.5 us
    slice x15, local copies, waits for them, and re-layouts, banded(): result = jnp.where(inner - outer + offset == tap, tiles[tap], result)  13.5 us
    select_n x3, other arithmetic, banded(): result = jnp.where(inner - outer + offset == tap, tiles[tap], result)  11.5 us
  transfers between devices with their start and end apart: 7, of which 4 were waited for; matrix products, arithmetic and copies ran while one was open for 31% of the time, Pallas kernels for 32%

profile of v7, /device:TPU:0, one launch (start us, length us, event | category | flops | bytes accessed | tf_op | source)
XLA Modules:
  0.0 243.5 jit_solution(2905566299805906092)
XLA Ops:
  0.6 3.3 %copy.42 = bf16[1,64,128,128]{2,1,3,0:T(8,128)(2,1)S(1)} copy(bf16[1,64,128,128]{3,2,1,0:T(8,128)(2,1)} %param.12) | data formatting | bytes 4194304 | tf_op args[1]
  5.4 7.3 %all-to-all-start = ((bf16[32,2,64,128]{3,2,1,0:T(8,128)(2,1)}), bf16[32,2,64,128]{3,2,1,0:T(8,128)(2,1)S(1)}, u32[]{:S(2)}, u32[]{:S(2)}) async-start(bf16[32,2,64,128]{3,2,1,0:T(8,128)(2,1)} %bitcast.3), calls=%async_computation | async-start | bytes 2097152 | tf_op jit(solution)/shard_map/all_to_all | solution.py:622
  13.5 4.3 %collective-permute-start = (bf16[3,128,128]{2,1,0:T(8,128)(2,1)}, bf16[3,128,128]{2,1,0:T(8,128)(2,1)}, u32[]{:S(2)}, u32[]{:S(2)}) collective-permute-start(bf16[3,128,128]{2,1,0:T(8,128)(2,1)} %get-tuple-element.22), channel_id=1, source_target_pairs={{0,1},{1,2},{2,3},{3,4},{4,5},{5,6},{6,7},{7,8},{8,9},{9,10},{10,1... | collective-permute-start | bytes 294920 | tf_op jit(solution)/shard_map/ppermute | solution.py:28
  22.8 4.1 %copy.43 = bf16[1,32,256,128]{2,3,1,0:T(8,128)(2,1)} copy(bf16[1,32,256,128]{3,2,1,0:T(8,128)(2,1)} %param.13) | data formatting | bytes 4194304 | tf_op args[2]
  26.9 2.5 %reshape_squeeze.3 = bf16[32,2,128,2,32,2]{2,1,5,4,3,0:T(2,128)(2,1)S(1)} reshape(bf16[1,32,256,128]{2,3,1,0:T(8,128)(2,1)} %copy.43) | data formatting | bytes 4194304 | tf_op jit(solution)/shard_map/reshape;squeeze | solution.py:729
  29.5 2.4 copy.44
  32.0 2.0 pad_maximum_fusion
  34.7 2.0 select_select_fusion.2
  37.6 3.7 %all-to-all-done = bf16[32,2,64,128]{3,2,1,0:T(8,128)(2,1)S(1)} async-done(((bf16[32,2,64,128]{3,2,1,0:T(8,128)(2,1)}), bf16[32,2,64,128]{3,2,1,0:T(8,128)(2,1)S(1)}, u32[]{:S(2)}, u32[]{:S(2)}) %all-to-all-start) | async-done | bytes 1048608 | tf_op jit(solution)/shard_map/all_to_all | solution.py:622
  42.4 2.8 %all-to-all-start.1 = ((bf16[32,6,64,128]{3,2,1,0:T(8,128)(2,1)}), bf16[32,6,64,128]{3,2,1,0:T(8,128)(2,1)S(1)}, u32[]{:S(2)}, u32[]{:S(2)}) async-start(bf16[32,6,64,128]{3,2,1,0:T(8,128)(2,1)} %pad_maximum_fusion), calls=%async_computation.1 | async-start | bytes 6291456 | tf_op jit(solution)/shard_map/all_to_all | solution.py:622
  58.7 2.0 broadcast_in_dim.180
  88.3 6.0 %all_gather.3 = bf16[128,256]{1,0:T(8,128)(2,1)} all-gather(bf16[32,256]{1,0:T(8,128)(2,1)S(1)} %convert_element_type.12), channel_id=1, replica_groups=mesh['slab'=4,'coil'=8] {'slab'}, dimensions={0}, use_global_device_ids=true | all-gather | bytes 81920 | tf_op jit(solution)/shard_map/all_gather | solution.py:714
  95.2 5.3 %select_select_fusion.1 = bf16[18,64,2048]{2,1,0:T(8,128)(2,1)} fusion(pred[64,2048]{1,0:T(8,128)(4,1)} %get-tuple-element.37, pred[64,2048]{1,0:T(8,128)(4,1)} %get-tuple-element.38, pred[64,2048]{1,0:T(8,128)(4,1)S(1)} %get-tuple-element.36, bf16[18,2048]{1,0:T(8,128)(2,1)} %broadcast_in_dim.180, bf16[18,2048]{1,0:T(8,128)(2,1)} %broadcast_in_dim.176, ...), kind=kLoop, calls=%fused_computation.1 | loop fusion | flops 7077888 | bytes 5332992 | tf_op jit(solution)/shard_map/jit(_where)/select_n | solution.py:162
  100.5 4.2 %select_select_fusion = bf16[64,32,1152]{2,1,0:T(8,128)(2,1)} fusion(pred[64,1152]{1,0:T(8,128)(4,1)S(1)} %get-tuple-element.34, pred[64,1152]{1,0:T(8,128)(4,1)S(1)} %get-tuple-element.35, pred[64,1152]{1,0:T(8,128)(4,1)S(1)} %get-tuple-element.33, bf16[32,1152]{1,0:T(8,128)(2,1)S(1)} %copy-done.17, bf16[32,1152]{1,0:T(8,128)(2,1)S(1)} %copy-done.16, ...), kind=kLoop, calls=%fused_computation | loop fusion | flops 7077888 | bytes 5160960 | tf_op jit(solution)/shard_map/jit(_where)/select_n | solution.py:162
  108.0 49.0 %denoise.1.denoised_ref = f32[32,2,2,8,128]{4,3,2,1,0:T(8,128)} custom-call(s32[2]{0:T(128)} %pad_add_fusion.first_ref, bf16[14,128,384]{2,1,0:T(8,128)(2,1)} %fusion.2.features_ref, f32[8,128,128]{2,1,0:T(8,128)} %prior_ref.1, bf16[1152,2048]{1,0:T(8,128)(2,1)} %bitcast.64, f32[1,2048]{1,0:T(1,128)} %broadcast_in_dim_tile.8.bias_first_ref, ...), custom_call_target="tpu_custom_call" | custom-call | flops 37446746112 | bytes 16777216 | tf_op jit(solution)/shard_map/denoise/pallas_call | solution.py:236
  157.0 6.2 %all-to-all-start.2 = ((f32[32,2,2,8,128]{4,3,2,1,0:T(8,128)}), f32[32,2,2,8,128]{4,3,2,1,0:T(8,128)}, u32[]{:S(2)}, u32[]{:S(2)}) async-start(f32[32,2,2,8,128]{4,3,2,1,0:T(8,128)} %denoise.1.denoised_ref), calls=%async_computation.2 | async-start | bytes 1048576 | tf_op jit(solution)/shard_map/all_to_all | solution.py:622
  165.8 5.0 %adjoint.1.adjoint_ref = f32[32,2,2,8,128]{4,3,2,1,0:T(8,128)S(1)} custom-call(bf16[4,8,6,64,128]{4,3,2,1,0:T(8,128)(2,1)S(1)} %bitcast.52, bf16[4,8,6,64,128]{4,3,2,1,0:T(8,128)(2,1)S(1)} %bitcast.53, bf16[4,8,2,64,128]{4,3,2,1,0:T(8,128)(2,1)S(1)} %bitcast.57, bf16[4,8,6,64,128]{4,3,2,1,0:T(8,128)(2,1)S(1)} %bitcast.54, ...), custom_call_target="tpu_custom_call" | custom-call | flops 4831838208 | bytes 8388608 | tf_op jit(solution)/shard_map/adjoint/pallas_call | solution.py:578
  171.7 7.6 %all-to-all-done.2.denoised_ref = f32[32,2,2,8,128]{4,3,2,1,0:T(8,128)} async-done(((f32[32,2,2,8,128]{4,3,2,1,0:T(8,128)}), f32[32,2,2,8,128]{4,3,2,1,0:T(8,128)}, u32[]{:S(2)}, u32[]{:S(2)}) %all-to-all-start.2) | async-done | bytes 524320 | tf_op jit(solution)/shard_map/all_to_all | solution.py:622
  179.3 2.6 %all-to-all-start.3 = ((f32[32,2,2,8,128]{4,3,2,1,0:T(8,128)}), f32[32,2,2,8,128]{4,3,2,1,0:T(8,128)S(1)}, u32[]{:S(2)}, u32[]{:S(2)}) async-start(f32[32,2,2,8,128]{4,3,2,1,0:T(8,128)} %copy-done.6), calls=%async_computation.3 | async-start | bytes 1048576 | tf_op jit(solution)/shard_map/all_to_all | solution.py:622
  185.5 12.7 %first_product.1 = (f32[32,2,2,8,128]{4,3,2,1,0:T(8,128)}, f32[8,128]{1,0:T(8,128)S(1)}) custom-call(bf16[4,8,2,64,128]{4,3,2,1,0:T(8,128)(2,1)S(1)} %bitcast.58, bf16[4,8,6,64,128]{4,3,2,1,0:T(8,128)(2,1)} %bitcast.55, f32[32,2,2,8,128]{4,3,2,1,0:T(8,128)S(1)} %copy-done.7, f32[32,2,2,8,128]{4,3,2,1,0:T(8,128)} %all-to-all-done.2.denoised_ref, ...), custom_call_target="tpu_custom_call" | custom-call | flops 9663676416 | bytes 8388608 | tf_op jit(solution)/shard_map/first_product/pallas_call | solution.py:578
  198.2 5.8 %all-to-all-start.4 = ((f32[32,2,2,8,128]{4,3,2,1,0:T(8,128)}), f32[32,2,2,8,128]{4,3,2,1,0:T(8,128)S(1)}, u32[]{:S(2)}, u32[]{:S(2)}) async-start(f32[32,2,2,8,128]{4,3,2,1,0:T(8,128)} %get-tuple-element.14.field_ref), calls=%async_computation.4 | async-start | bytes 1048576 | tf_op jit(solution)/shard_map/all_to_all | solution.py:622
  205.3 11.9 %second_product.1 = f32[32,5,8,128]{3,2,1,0:T(8,128)S(1)} custom-call(bf16[4,8,2,64,128]{4,3,2,1,0:T(8,128)(2,1)S(1)} %bitcast.59, bf16[4,8,6,64,128]{4,3,2,1,0:T(8,128)(2,1)} %bitcast.56, f32[32,2,2,8,128]{4,3,2,1,0:T(8,128)} %get-tuple-element.14.field_ref, f32[8,128]{1,0:T(8,128)S(1)} %get-tuple-element.15.total_ref, ...), custom_call_target="tpu_custom_call" | custom-call | flops 9663676416 | bytes 8388608 | tf_op jit(solution)/shard_map/second_product/pallas_call | solution.py:578
  217.3 3.1 %all-to-all-done.4.field_ref = f32[32,2,2,8,128]{4,3,2,1,0:T(8,128)S(1)} async-done(((f32[32,2,2,8,128]{4,3,2,1,0:T(8,128)}), f32[32,2,2,8,128]{4,3,2,1,0:T(8,128)S(1)}, u32[]{:S(2)}, u32[]{:S(2)}) %all-to-all-start.4) | async-done | bytes 524320 | tf_op jit(solution)/shard_map/all_to_all | solution.py:622
  220.4 21.7 %all_to_all.30.image_ref = f32[32,5,8,128]{3,2,1,0:T(8,128)S(1)} all-to-all(f32[32,5,8,128]{3,2,1,0:T(8,128)S(1)} %second_product.1), channel_id=1, replica_groups=mesh['slab'=4,'coil'=8] {'slab','coil'}, dimensions={0} | all-to-all | bytes 1310720 | tf_op jit(solution)/shard_map/all_to_all | solution.py:622
  (110 shorter events, 65.0 us)
Async XLA Ops:
  3.9 8.8 %copy-start.14 = (f32[8,128,128]{2,1,0:T(8,128)S(1)}, f32[8,128,128]{2,1,0:T(8,128)}, u32[]{:S(2)}) copy-start(f32[8,128,128]{2,1,0:T(8,128)} %prior_ref.1) | copy-start | bytes 1572868
  5.4 13.6 %copy-start.19 = (bf16[3,3,3,32,32]{4,3,2,1,0:T(8,128)(2,1)S(1)}, bf16[3,3,3,32,32]{4,3,2,1,0:T(8,128)(2,1)}, u32[]{:S(2)}) copy-start(bf16[3,3,3,32,32]{4,3,2,1,0:T(8,128)(2,1)} %param.17) | copy-start | bytes 165892
  5.4 35.9 %all-to-all-start = ((bf16[32,2,64,128]{3,2,1,0:T(8,128)(2,1)}), bf16[32,2,64,128]{3,2,1,0:T(8,128)(2,1)S(1)}, u32[]{:S(2)}, u32[]{:S(2)}) async-start(bf16[32,2,64,128]{3,2,1,0:T(8,128)(2,1)} %bitcast.3), calls=%async_computation | async-start | bytes 2097152 | tf_op jit(solution)/shard_map/all_to_all | solution.py:622
  13.5 91.8 %collective-permute-start = (bf16[3,128,128]{2,1,0:T(8,128)(2,1)}, bf16[3,128,128]{2,1,0:T(8,128)(2,1)}, u32[]{:S(2)}, u32[]{:S(2)}) collective-permute-start(bf16[3,128,128]{2,1,0:T(8,128)(2,1)} %get-tuple-element.22), channel_id=1, source_target_pairs={{0,1},{1,2},{2,3},{3,4},{4,5},{5,6},{6,7},{7,8},{8,9},{9,10},{10,1... | collective-permute-start | bytes 294920 | tf_op jit(solution)/shard_map/ppermute | solution.py:28
  17.8 87.5 %collective-permute-start.1 = (bf16[3,128,128]{2,1,0:T(8,128)(2,1)}, bf16[3,128,128]{2,1,0:T(8,128)(2,1)}, u32[]{:S(2)}, u32[]{:S(2)}) collective-permute-start(bf16[3,128,128]{2,1,0:T(8,128)(2,1)} %get-tuple-element.23), channel_id=1, source_target_pairs={{1,0},{2,1},{3,2},{4,3},{5,4},{6,5},{7,6},{8,7},{9,8},{10,9},{11,1... | collective-permute-start | bytes 294920 | tf_op jit(solution)/shard_map/ppermute | solution.py:29
  29.5 2.5 %copy-start.11 = (bf16[64,128,64]{1,0,2:T(8,128)(2,1)S(1)}, bf16[64,128,64]{1,0,2:T(8,128)(2,1)}, u32[]{:S(2)}) copy-start(bf16[64,128,64]{1,0,2:T(8,128)(2,1)} %get-tuple-element.18) | copy-start | bytes 3145732
  31.9 2.0 copy-start.21
  32.0 2.6 %copy-start.20 = (s32[768]{0:T(1024)S(1)}, s32[768]{0:T(1024)}, u32[]{:S(2)}) copy-start(s32[768]{0:T(1024)} %sub.196) | copy-start | bytes 9220
  32.0 2.7 %copy-start.12 = (bf16[3,32,768]{2,1,0:T(8,128)(2,1)S(1)}, bf16[3,32,768]{2,1,0:T(8,128)(2,1)}, u32[]{:S(2)}) copy-start(bf16[3,32,768]{2,1,0:T(8,128)(2,1)} %broadcast_in_dim.189) | copy-start | bytes 442372
  32.0 2.7 %copy-start.13 = (bf16[3,32,768]{2,1,0:T(8,128)(2,1)S(1)}, bf16[3,32,768]{2,1,0:T(8,128)(2,1)}, u32[]{:S(2)}) copy-start(bf16[3,32,768]{2,1,0:T(8,128)(2,1)} %broadcast_in_dim.193) | copy-start | bytes 442372
  37.6 7.5 %copy-start.22 = (bf16[3,3,3,2,32]{4,3,2,1,0:T(2,128)(2,1)S(1)}, bf16[3,3,3,2,32]{4,3,2,1,0:T(2,128)(2,1)}, u32[]{:S(2)}) copy-start(bf16[3,3,3,2,32]{4,3,2,1,0:T(2,128)(2,1)} %param.19) | copy-start | bytes 10372
  42.4 114.6 %all-to-all-start.1 = ((bf16[32,6,64,128]{3,2,1,0:T(8,128)(2,1)}), bf16[32,6,64,128]{3,2,1,0:T(8,128)(2,1)S(1)}, u32[]{:S(2)}, u32[]{:S(2)}) async-start(bf16[32,6,64,128]{3,2,1,0:T(8,128)(2,1)} %pad_maximum_fusion), calls=%async_computation.1 | async-start | bytes 6291456 | tf_op jit(solution)/shard_map/all_to_all | solution.py:622
  95.2 5.3 %copy-start.15 = (bf16[32,1152]{1,0:T(8,128)(2,1)S(1)}, bf16[32,1152]{1,0:T(8,128)(2,1)}, u32[]{:S(2)}) copy-start(bf16[32,1152]{1,0:T(8,128)(2,1)} %broadcast_in_dim.198) | copy-start | bytes 221188
  95.2 5.3 %copy-start.16 = (bf16[32,1152]{1,0:T(8,128)(2,1)S(1)}, bf16[32,1152]{1,0:T(8,128)(2,1)}, u32[]{:S(2)}) copy-start(bf16[32,1152]{1,0:T(8,128)(2,1)} %broadcast_in_dim.202) | copy-start | bytes 221188
  95.2 5.3 %copy-start.17 = (bf16[32,1152]{1,0:T(8,128)(2,1)S(1)}, bf16[32,1152]{1,0:T(8,128)(2,1)}, u32[]{:S(2)}) copy-start(bf16[32,1152]{1,0:T(8,128)(2,1)} %broadcast_in_dim.206) | copy-start | bytes 221188
  108.0 55.2 %copy-start.18 = (bf16[128,256]{1,0:T(8,128)(2,1)S(1)}, bf16[128,256]{1,0:T(8,128)(2,1)}, u32[]{:S(2)}) copy-start(bf16[128,256]{1,0:T(8,128)(2,1)} %all_gather.3) | copy-start | bytes 196612
  157.0 13.9 %copy-start = (bf16[32,6,64,128]{3,2,1,0:T(8,128)(2,1)}, bf16[32,6,64,128]{3,2,1,0:T(8,128)(2,1)S(1)}, u32[]{:S(2)}) copy-start(bf16[32,6,64,128]{3,2,1,0:T(8,128)(2,1)S(1)} %all-to-all-done.1) | copy-start | bytes 9437188
  157.0 22.3 %all-to-all-start.2 = ((f32[32,2,2,8,128]{4,3,2,1,0:T(8,128)}), f32[32,2,2,8,128]{4,3,2,1,0:T(8,128)}, u32[]{:S(2)}, u32[]{:S(2)}) async-start(f32[32,2,2,8,128]{4,3,2,1,0:T(8,128)} %denoise.1.denoised_ref), calls=%async_computation.2 | async-start | bytes 1048576 | tf_op jit(solution)/shard_map/all_to_all | solution.py:622
  164.5 1.3 copy-start.8
  179.3 19.0 %all-to-all-start.3 = ((f32[32,2,2,8,128]{4,3,2,1,0:T(8,128)}), f32[32,2,2,8,128]{4,3,2,1,0:T(8,128)S(1)}, u32[]{:S(2)}, u32[]{:S(2)}) async-start(f32[32,2,2,8,128]{4,3,2,1,0:T(8,128)} %copy-done.6), calls=%async_computation.3 | async-start | bytes 1048576 | tf_op jit(solution)/shard_map/all_to_all | solution.py:622
  185.5 18.6 %copy-start.5 = (bf16[32,2,64,128]{3,2,1,0:T(8,128)(2,1)S(1)}, bf16[32,2,64,128]{3,2,1,0:T(8,128)(2,1)}, u32[]{:S(2)}) copy-start(bf16[32,2,64,128]{3,2,1,0:T(8,128)(2,1)} %copy-done.2) | copy-start | bytes 3145732
  198.2 22.1 %all-to-all-start.4 = ((f32[32,2,2,8,128]{4,3,2,1,0:T(8,128)}), f32[32,2,2,8,128]{4,3,2,1,0:T(8,128)S(1)}, u32[]{:S(2)}, u32[]{:S(2)}) async-start(f32[32,2,2,8,128]{4,3,2,1,0:T(8,128)} %get-tuple-element.14.field_ref), calls=%async_computation.4 | async-start | bytes 1048576 | tf_op jit(solution)/shard_map/all_to_all | solution.py:622
  204.0 1.3 copy-start.10
  205.3 36.7 %copy-start.1 = (f32[32,2,2,8,128]{4,3,2,1,0:T(8,128)S(1)}, f32[32,2,2,8,128]{4,3,2,1,0:T(8,128)}, u32[]{:S(2)}) copy-start(f32[32,2,2,8,128]{4,3,2,1,0:T(8,128)} %denoise.1.denoised_ref) | copy-start | bytes 1572868
  (6 other events, 6.6 us)

commit v8 on v7

--- a/solution.py
+++ b/solution.py
@@ -294,6 +294,15 @@
     return np.concatenate([rows_high, rows_low, planes_parts], axis=1)
 
 
+def half_tables(rows, planes):
+    rows_parts = np.concatenate(table_parts(turn_block(rows // 2) * math.sqrt(0.5)), axis=1)
+    planes_parts = np.concatenate(table_parts(turn_block(planes).T), axis=0)
+    angles = np.arange(rows // 2) * (2.0 * math.pi / rows)
+    turns = np.stack([np.cos(angles), np.sin(angles)])[:, :, None]
+    turns = np.broadcast_to(turns, (2, rows // 2, planes)).astype(np.float32)
+    return [rows_parts, planes_parts, turns]
+
+
 def value_parts(value):
     high = value.astype(jnp.bfloat16)
     low = (value - high.astype(jnp.float32)).astype(jnp.bfloat16)
@@ -364,17 +373,6 @@
     return [coil_plane(ref, coil).astype(jnp.float32) for ref in refs]
 
 
-def spectrum_plane(ref, coil, rows):
-    value = ref[:, coil, 0]
-    slabs, held, lanes = value.shape
-    planes = held * lanes // rows
-    pieces = [
-        value[:, first : first + planes].reshape(slabs * planes, lanes)
-        for first in range(0, held, planes)
-    ]
-    return jnp.concatenate(pieces, axis=1)
-
-
 def image_sums(maps, fields):
     sums = None
     for (map_real, map_imag), (real, imag) in zip(maps, fields):
@@ -389,28 +387,68 @@
     return [tuple(range(first, first + held)) for first in range(0, count, held)]
 
 
-def normal_sums(maps_refs, real, imag, mask, tables):
-    row_table, plane_table = tables
-    units = units_of(maps_refs)
+def halved(fields, turns):
+    evens, odds = [], []
+    rows = fields[0][0].shape[0] // 2
+    for real, imag in fields:
+        evens.append((real[:rows] + real[rows:], imag[:rows] + imag[rows:]))
+        real, imag = real[:rows] - real[rows:], imag[:rows] - imag[rows:]
+        odds.append((real * turns[0] + imag * turns[1], imag * turns[0] - real * turns[1]))
+    return evens, odds
+
+
+def rejoined(evens, odds, turns):
     fields = []
-    for unit in units:
+    for (even_real, even_imag), (real, imag) in zip(evens, odds):
+        real, imag = real * turns[0] + imag * turns[1], imag * turns[0] - real * turns[1]
+        fields.append(
+            (
+                jnp.concatenate([even_real + real, even_real - real], axis=0),
+                jnp.concatenate([even_imag + imag, even_imag - imag], axis=0),
+            )
+        )
+    return fields
+
+
+def masked(fields, mask):
+    return [(real * mask, imag * -mask) for real, imag in fields]
+
+
+def in_groups(values, size):
+    return [values[first : first + size] for first in range(0, len(values), size)]
+
+
+def normal_sums(maps_refs, real, imag, mask_ref, rows_ref, planes_ref, turns_ref):
+    half = rows_ref.shape[1] // 2
+    row_table = jnp.concatenate([rows_ref[:, :half], rows_ref[:, half:], rows_ref[:, :half]], axis=1)
+    half = planes_ref.shape[0] // 2
+    plane_table = jnp.concatenate([planes_ref[:half], planes_ref[half:], planes_ref[:half]], axis=0)
+    turns = turns_ref[0], turns_ref[1]
+    half = turns[0].shape[0]
+    masks = mask_ref[:half], mask_ref[half:]
+    coils = list(range(maps_refs[0].shape[1]))
+    fields = []
+    for group in in_groups(coils, 4):
         products = []
-        for coil in unit:
+        for coil in group:
             map_real, map_imag = map_of(maps_refs, coil)
             products.append(
                 (map_real * real - map_imag * imag, map_real * imag + map_imag * real)
             )
-        fields.append(along_planes(products, plane_table))
-    fields = [along_rows(row_table, field) for field in fields]
-    spectra = [
-        [(real_part * mask, imag_part * -mask) for real_part, imag_part in field]
-        for field in fields
-    ]
-    fields = [along_rows(row_table, spectrum) for spectrum in spectra]
-    fields = [along_planes(field, plane_table) for field in fields]
+        fields += along_planes(products, plane_table)
+    units = [halved(unit, turns) for unit in in_groups(fields, 2)]
+    units = [[along_rows(row_table, part) for part in unit] for unit in units]
+    units = [[masked(part, mask) for part, mask in zip(unit, masks)] for unit in units]
+    units = [[along_rows(row_table, part) for part in unit] for unit in units]
+    fields = sum((rejoined(*unit, turns) for unit in units), [])
+    images = []
+    for group in in_groups(fields, 4):
+        images += along_planes(group, plane_table)
     total = None
-    for unit, field in zip(units, fields):
-        sums = image_sums([map_of(maps_refs, coil) for coil in unit], field)
+    for group in in_groups(coils, 2):
+        sums = image_sums(
+            [map_of(maps_refs, coil) for coil in group], [images[coil] for coil in group]
+        )
         total = sums if total is None else (total[0] + sums[0], total[1] + sums[1])
     return total
 
@@ -442,7 +480,7 @@
         spectra = []
         for coil in unit:
             real, imag = (
-                jnp.transpose(spectrum_plane(ref, coil, rows).astype(jnp.float32))
+                jnp.transpose(coil_plane(ref, coil).astype(jnp.float32))
                 for ref in (spectra_real_ref, spectra_imag_ref)
             )
             spectra.append((real * mask, imag * -mask))
@@ -467,15 +505,13 @@
 
 
 def first_kernel(
-    maps_real_ref, maps_imag_ref, adjoint_ref, denoised_ref, mask_ref, table_ref, out_ref, total_ref
+    maps_real_ref, maps_imag_ref, adjoint_ref, denoised_ref, *refs
 ):
-    mask = mask_ref[...]
+    constants, (out_ref, total_ref) = refs[:-2], refs[-2:]
     rights = [
         plane_of(adjoint_ref, part) + penalty * plane_of(denoised_ref, part) for part in range(2)
     ]
-    sums = normal_sums(
-        (maps_real_ref, maps_imag_ref), *rights, mask, tables_of(table_ref, *mask.shape)
-    )
+    sums = normal_sums((maps_real_ref, maps_imag_ref), *rights, *constants)
     accumulate(out_ref, sums, ((0, 0), (1, 0)))
 
     @pl.when(pl.program_id(1) == pl.num_programs(1) - 1)
@@ -502,19 +538,13 @@
             total_ref[...] += totals
 
 
-def second_kernel(
-    maps_real_ref, maps_imag_ref, field_ref, total_ref, mask_ref, table_ref, out_ref
-):
+def second_kernel(maps_real_ref, maps_imag_ref, field_ref, total_ref, *refs):
+    constants, out_ref = refs[:-1], refs[-1]
     x_index = pl.program_id(0)
     x_count = pl.num_programs(0)
     blocks, block_rows, planes = out_ref.shape[0], out_ref.shape[2], out_ref.shape[3]
-    mask = mask_ref[...]
     sums = normal_sums(
-        (maps_real_ref, maps_imag_ref),
-        plane_of(field_ref, 0),
-        plane_of(field_ref, 1),
-        mask,
-        tables_of(table_ref, *mask.shape),
+        (maps_real_ref, maps_imag_ref), plane_of(field_ref, 0), plane_of(field_ref, 1), *constants
     )
     places = [(part * x_count + x_index,) for part in range(2)]
     accumulate(out_ref, sums, places)
@@ -523,6 +553,8 @@
     def _():
         fields = [field_ref[:, part, 0] for part in range(2)]
         images = [out_ref[(slice(None),) + place] for place in places]
+        for part in range(2):
+            out_ref[:, (2 + part) * x_count + x_index] = fields[part]
         totals = jnp.concatenate(
             [
                 jnp.zeros((3, planes), jnp.float32),
@@ -534,13 +566,13 @@
 
         @pl.when(x_index == 0)
         def _():
-            out_ref[:, 2 * x_count] = jnp.broadcast_to(
+            out_ref[:, 4 * x_count] = jnp.broadcast_to(
                 (total_ref[...] + totals)[None], (blocks, block_rows, planes)
             )
 
         @pl.when(x_index > 0)
         def _():
-            out_ref[:, 2 * x_count] += totals[None]
+            out_ref[:, 4 * x_count] += totals[None]
 
 
 def held_coils(count):
@@ -611,7 +643,7 @@
 
 def second_call(maps, field, totals, constants):
     blocks, _, x_count, block_rows, planes = field.shape
-    shape = (blocks, 2 * x_count + 1, block_rows, planes)
+    shape = (blocks, 4 * x_count + 1, block_rows, planes)
     outs = [(whole(shape), shape)]
     return product_call(
         second_kernel, "second_product", x_count, maps, [field], [totals], constants, outs, 6
@@ -622,9 +654,9 @@
     return lax.all_to_all(blocks, axis, split_axis=0, concat_axis=0, tiled=True)
 
 
-def x_first(cells, parts, count=2):
+def x_first(cells, parts):
     rows, planes, width = cells.shape
-    split = cells.reshape(rows, planes, count, parts, width // (count * parts))
+    split = cells.reshape(rows, planes, 2, parts, width // (2 * parts))
     return jnp.transpose(split, (3, 2, 4, 0, 1))
 
 
@@ -651,20 +683,23 @@
 
 
 def finish_kernel(
-    adjoint_ref, denoised_ref, field_ref, image_ref, solution_ref, residual_ref, rows_ref
+    adjoint_ref, denoised_ref, moved_ref, solution_ref, residual_ref, rows_ref
 ):
     blocks, _, x_count, rows, planes = adjoint_ref.shape
     readout = blocks * x_count
-    totals = jnp.sum(jnp.sum(image_ref[:, 2 * x_count], axis=0), axis=1, keepdims=True)
+    totals = jnp.sum(jnp.sum(moved_ref[:, 4 * x_count], axis=0), axis=1, keepdims=True)
     found = factors(*(totals[index : index + 1] for index in range(4)))
     for out_ref, scales in zip((solution_ref, residual_ref), found):
         scales = [jnp.broadcast_to(scale, (rows, planes))[None] for scale in scales]
         for part in range(2):
             for inner in range(x_count):
                 right = adjoint_ref[:, part, inner] + penalty * denoised_ref[:, part, inner]
-                value = scales[0] * right + scales[1] * field_ref[:, part, inner]
+                value = (
+                    scales[0] * right
+                    + scales[1] * moved_ref[:, (2 + part) * x_count + inner]
+                )
                 if len(scales) > 2:
-                    value = value + scales[2] * image_ref[:, part * x_count + inner]
+                    value = value + scales[2] * moved_ref[:, part * x_count + inner]
                 for block in range(blocks):
                     place = part * readout + block * x_count + inner
                     rows_ref[place * rows : (place + 1) * rows] = value[block]
@@ -672,13 +707,13 @@
             out_ref[row] = jnp.transpose(rows_ref[pl.ds(row, 2 * readout, stride=rows), :])
 
 
-def finish_call(adjoint, denoised, field, image):
+def finish_call(adjoint, denoised, moved):
     blocks, _, x_count, rows, planes = adjoint.shape
     shape = (rows, planes, 2 * blocks * x_count)
     vmem = pl.BlockSpec(memory_space=pltpu.VMEM)
     return pl.pallas_call(
         finish_kernel,
-        in_specs=[vmem] * 4,
+        in_specs=[vmem] * 3,
         out_specs=[vmem] * 2,
         out_shape=[jax.ShapeDtypeStruct(shape, jnp.float32)] * 2,
         scratch_shapes=[pltpu.VMEM((2 * blocks * x_count * rows, planes), jnp.float32)],
@@ -687,7 +722,7 @@
             flops=8 * adjoint.size, bytes_accessed=24 * adjoint.size, transcendentals=0
         ),
         name="finish",
-    )(adjoint, denoised, field, image)
+    )(adjoint, denoised, moved)
 
 
 def body(
@@ -708,51 +743,32 @@
     slabs = lax.axis_size("slab")
     coils = lax.axis_size("coil")
     devices = slabs * coils
-    spread = readout % devices == 0 and own_rows % 8 == 0 and coil_maps.shape[1] % 16 == 0
+    spread = readout % devices == 0 and own_rows % 8 == 0
     parts = devices if spread else coils
     x_count = readout // parts
     mask = lax.all_gather(sampling.astype(jnp.bfloat16), "slab", axis=0, tiled=True)
     features, mask = lax.optimization_barrier(
         (with_halo(prior_image.astype(jnp.bfloat16), 3), mask)
     )
-    constants = [
-        jnp.transpose(mask).astype(jnp.float32),
-        jnp.asarray(dft_table(sampling.shape[1], planes)),
-    ]
-
-    if spread:
-        own_maps, measured = coil_maps[0], kspace[0]
-        real = x_first(own_maps[..., :readout], parts, 1)
-        imag = x_first(own_maps[..., readout:], parts, 1)
-        slab_rows = own_maps.shape[0]
-        slab_planes, row_count = measured.shape[:2]
-        measured = measured.reshape(
-            slab_planes, row_count // planes, planes, 2, parts, x_count
-        )
-        measured = jnp.transpose(measured, (4, 3, 5, 1, 0, 2)).reshape(
-            parts, 2 * x_count, slab_rows, planes
-        )
-        real = exchange(real.reshape(parts, x_count, slab_rows, planes), axes)
-        rest = exchange(
-            jnp.concatenate([imag.reshape(parts, x_count, slab_rows, planes), measured], axis=1),
-            axes,
-        )
-        real = real.reshape((slabs, coils) + real.shape[1:])
-        rest = rest.reshape((slabs, coils) + rest.shape[1:])
-        maps = [(real, 0), (rest, 0)]
-        spectra = [(rest, x_count), (rest, 2 * x_count)]
-    else:
-
-        def coils_to_x(values):
-            blocks = x_first(values, parts)
-            tail = blocks.shape[1:]
+    mask = jnp.transpose(mask).astype(jnp.float32)
+    row_count = mask.shape[0]
+    half_mask = jnp.concatenate([mask[::2], mask[1::2]], axis=0)
+    constants = [half_mask] + half_tables(row_count, planes)
+    constants = [jnp.asarray(value) for value in constants]
+    adjoint_constants = [mask, jnp.asarray(dft_table(row_count, planes))]
+
+    def coils_to_x(values):
+        blocks = x_first(values, parts)
+        tail = (2 * x_count,) + blocks.shape[3:]
+        if spread:
+            blocks = exchange(blocks, axes).reshape((slabs, coils) + tail)
+        else:
             blocks = exchange(blocks, "coil").reshape((slabs, coils // slabs) + tail)
             blocks = exchange(blocks, "slab")
-            return [(blocks[:, :, part], 0) for part in range(2)]
-
-        maps = coils_to_x(coil_maps[0])
-        spectra = coils_to_x(kspace[0])
-
+        return [(blocks, 0), (blocks, x_count)]
+
+    maps = coils_to_x(coil_maps[0])
+    spectra = coils_to_x(kspace[0])
     blocks = denoise(
         parts,
         features,
@@ -767,13 +783,11 @@
     if blocks.ndim == 3:
         blocks = x_first(blocks, parts)
     if spread:
-        adjoint = adjoint_call(spectra, maps, constants, x_count, devices)
+        adjoint = adjoint_call(spectra, maps, adjoint_constants, x_count, devices)
         field, totals = first_call(maps, adjoint, exchange(blocks, axes), constants)
         field, adjoint_back = lax.optimization_barrier((field, exchange(adjoint, axes)))
-        payload, field_back = lax.optimization_barrier(
-            (second_call(maps, field, totals, constants), exchange(field, axes))
-        )
-        return tuple(finish_call(adjoint_back, blocks, field_back, exchange(payload, axes)))
+        payload = exchange(second_call(maps, field, totals, constants), axes)
+        return tuple(finish_call(adjoint_back, blocks, payload))
 
     tail = blocks.shape[1:3]
 
@@ -787,7 +801,7 @@
         split = jnp.transpose(mine.reshape(tail + (coils, own_rows, planes)), (2, 0, 1, 3, 4))
         return x_last(exchange(split, "coil"))
 
-    adjoint = lax.psum(adjoint_call(spectra, maps, constants, x_count, 1), "slab")
+    adjoint = lax.psum(adjoint_call(spectra, maps, adjoint_constants, x_count, 1), "slab")
     denoised = whole_rows(blocks)
     right = adjoint + penalty * denoised
     field = lax.psum(first_call(maps, adjoint, denoised, constants)[0], "slab")

time: 246 us -> 207 us (0.84)
  local copies, waits for them, and re-layouts: 70.8 us -> 35.6 us
  blocking collectives: 27.7 us -> 41.8 us
  Pallas kernels: 80.1 us -> 73.9 us
  starting transfers between devices: 30.3 us -> 25 us
  other arithmetic: 19.1 us -> 15.4 us
    all_to_all x1, blocking collectives: 21.7 us -> 33.1 us  [exchange(): return lax.all_to_all(blocks, axis, split_axis=0, concat_axis=0, tiled=True)]
    slice x15, local copies, waits for them, and re-layouts: 13.5 us -> 2.31 us  [banded(): result = jnp.where(inner - outer + offset == tap, tiles[tap], result)]
    broadcast_in_dim x6, local copies, waits for them, and re-layouts: 10.2 us -> 2.34 us  [denoise(): jnp.broadcast_to(tiles, (3, 18, 1, readout, channels))]
    broadcast_in_dim x6, local copies, waits for them, and re-layouts: 9.78 us -> 2.91 us  [denoise(): jnp.broadcast_to(tiles, (3, 1, channels, 18, readout))]
    pallas_call x3, Pallas kernels: 29.6 us -> 23.4 us  [product_call(): pl.pallas_call(kernel, grid=(x_count, coils // held_coils(coils)), in_spe...]
    all_to_all x5 -> x4, starting transfers between devices: 24.7 us -> 19.4 us  [exchange(): return lax.all_to_all(blocks, axis, split_axis=0, concat_axis=0, tiled=True)]
    all_gather x1, blocking collectives: 6.03 us -> 8.74 us  [body(): lax.all_gather(sampling.astype(jnp.bfloat16), 'slab', axis=0, tiled=True)]
    another operation x1 -> x0, local copies, waits for them, and re-layouts: 2.54 us -> none  [body(): measured.reshape(slab_planes, row_count // planes, planes, 2, parts, x_co...]
  transfers between devices with their start and end apart: 7 -> 6, of which waited for: 4 -> 3; matrix products, arithmetic and copies ran while one was open for 31% -> 18% of each run, Pallas kernels for 32% -> 31%
where the time goes in v8:
time: 207 us; the launch traced here: 206 us
  Pallas kernels  73.9 us (36%)
  blocking collectives  41.8 us (20%)
  local copies, waits for them, and re-layouts  35.6 us (17%)
  starting transfers between devices  25 us (12%)
  other arithmetic  15.4 us (7%)
  waiting for transfers between devices  13.7 us (7%)
    pallas_call x1, Pallas kernels, denoise(): pl.pallas_call(functools.partial(denoise_kernel, group), in_specs=[pl.Blo...  49 us
    all_to_all x1, blocking collectives, exchange(): return lax.all_to_all(blocks, axis, split_axis=0, concat_axis=0, tiled=True)  33.1 us
    pallas_call x3, Pallas kernels, product_call(): pl.pallas_call(kernel, grid=(x_count, coils // held_coils(coils)), in_spe...  23.4 us
    all_to_all x4, starting transfers between devices, exchange(): return lax.all_to_all(blocks, axis, split_axis=0, concat_axis=0, tiled=True)  19.4 us
    unnamed x54, local copies, waits for them, and re-layouts  16.7 us
    all_to_all x4, waiting for transfers between devices, exchange(): return lax.all_to_all(blocks, axis, split_axis=0, concat_axis=0, tiled=True)  13.7 us
    select_n x3, other arithmetic, banded(): result = jnp.where(inner - outer + offset == tap, tiles[tap], result)  10.3 us
    all_gather x1, blocking collectives, body(): lax.all_gather(sampling.astype(jnp.bfloat16), 'slab', axis=0, tiled=True)  8.74 us
  transfers between devices with their start and end apart: 6, of which 3 were waited for; matrix products, arithmetic and copies ran while one was open for 18% of the time, Pallas kernels for 31%

profile of v8, /device:TPU:0, one launch (start us, length us, event | category | flops | bytes accessed | tf_op | source)
XLA Modules:
  0.0 206.4 jit_solution(12120619677925236943)
XLA Ops:
  0.6 3.3 %copy.36 = bf16[1,64,128,128]{2,1,3,0:T(8,128)(2,1)S(1)} copy(bf16[1,64,128,128]{3,2,1,0:T(8,128)(2,1)} %param.15) | data formatting | bytes 4194304 | tf_op args[1]
  3.9 1.7 copy.37
  5.6 7.3 %all-to-all-start = ((bf16[32,2,2,64,128]{4,3,2,1,0:T(8,128)(2,1)}), bf16[32,2,2,64,128]{4,3,2,1,0:T(8,128)(2,1)S(1)}, u32[]{:S(2)}, u32[]{:S(2)}) async-start(bf16[32,2,2,64,128]{4,3,2,1,0:T(8,128)(2,1)} %copy.37), calls=%async_computation | async-start | bytes 4194304 | tf_op jit(solution)/shard_map/all_to_all | solution.py:654
  13.7 4.3 %collective-permute-start = (bf16[3,128,128]{2,1,0:T(8,128)(2,1)}, bf16[3,128,128]{2,1,0:T(8,128)(2,1)}, u32[]{:S(2)}, u32[]{:S(2)}) collective-permute-start(bf16[3,128,128]{2,1,0:T(8,128)(2,1)} %get-tuple-element.16), channel_id=1, source_target_pairs={{0,1},{1,2},{2,3},{3,4},{4,5},{5,6},{6,7},{7,8},{8,9},{9,10},{10,1... | collective-permute-start | bytes 294920 | tf_op jit(solution)/shard_map/ppermute | solution.py:28
  31.8 4.6 %copy.38 = bf16[1,32,256,128]{2,1,3,0:T(8,128)(2,1)} copy(bf16[1,32,256,128]{3,2,1,0:T(8,128)(2,1)} %param.16) | data formatting | bytes 4194304 | tf_op args[2]
  36.4 3.3 %copy.39 = bf16[32,2,2,32,256]{4,3,2,1,0:T(8,128)(2,1)} copy(bf16[32,2,2,32,256]{4,3,2,0,1:T(8,128)(2,1)} %bitcast.48) | data formatting | bytes 4194304 | tf_op jit(solution)/shard_map/transpose | solution.py:660
  39.7 8.7 %all_gather.3 = bf16[128,256]{1,0:T(8,128)(2,1)S(1)} all-gather(bf16[32,256]{1,0:T(8,128)(2,1)S(1)} %copy-done.18), channel_id=1, replica_groups=mesh['slab'=4,'coil'=8] {'slab'}, dimensions={0}, use_global_device_ids=true | all-gather | bytes 81920 | tf_op jit(solution)/shard_map/all_gather | solution.py:749
  48.5 2.0 select_select_fusion.2
  50.9 4.1 %select_select_fusion.1 = bf16[18,64,2048]{2,1,0:T(8,128)(2,1)} fusion(pred[64,2048]{1,0:T(8,128)(4,1)S(1)} %get-tuple-element.31, pred[64,2048]{1,0:T(8,128)(4,1)S(1)} %get-tuple-element.32, pred[64,2048]{1,0:T(8,128)(4,1)S(1)} %get-tuple-element.30, bf16[18,2048]{1,0:T(8,128)(2,1)S(1)} %copy-done.13, bf16[18,2048]{1,0:T(8,128)(2,1)S(1)} %copy-done.12, ...), kind=kLoop, calls=%fused_computation.1 | loop fusion | flops 7077888 | bytes 5332992 | tf_op jit(solution)/shard_map/jit(_where)/select_n | solution.py:162
  55.1 4.2 %select_select_fusion = bf16[64,32,1152]{2,1,0:T(8,128)(2,1)} fusion(pred[64,1152]{1,0:T(8,128)(4,1)S(1)} %get-tuple-element.28, pred[64,1152]{1,0:T(8,128)(4,1)S(1)} %get-tuple-element.29, pred[64,1152]{1,0:T(8,128)(4,1)S(1)} %get-tuple-element.27, bf16[32,1152]{1,0:T(8,128)(2,1)S(1)} %copy-done.16, bf16[32,1152]{1,0:T(8,128)(2,1)S(1)} %copy-done.15, ...), kind=kLoop, calls=%fused_computation | loop fusion | flops 7077888 | bytes 5160960 | tf_op jit(solution)/shard_map/jit(_where)/select_n | solution.py:162
  59.9 4.1 %all-to-all-done = bf16[32,2,2,64,128]{4,3,2,1,0:T(8,128)(2,1)S(1)} async-done(((bf16[32,2,2,64,128]{4,3,2,1,0:T(8,128)(2,1)}), bf16[32,2,2,64,128]{4,3,2,1,0:T(8,128)(2,1)S(1)}, u32[]{:S(2)}, u32[]{:S(2)}) %all-to-all-start) | async-done | bytes 2097184 | tf_op jit(solution)/shard_map/all_to_all | solution.py:654
  64.0 3.7 %all-to-all-start.1 = ((bf16[32,2,2,32,256]{4,3,2,1,0:T(8,128)(2,1)}), bf16[32,2,2,32,256]{4,3,2,1,0:T(8,128)(2,1)}, u32[]{:S(2)}, u32[]{:S(2)}) async-start(bf16[32,2,2,32,256]{4,3,2,1,0:T(8,128)(2,1)} %copy.39), calls=%async_computation.1 | async-start | bytes 4194304 | tf_op jit(solution)/shard_map/all_to_all | solution.py:654
  69.0 1.4 fusion.2.features_ref
  70.4 49.0 %denoise.1.denoised_ref = f32[32,2,2,8,128]{4,3,2,1,0:T(8,128)} custom-call(s32[2]{0:T(128)} %pad_add_fusion.first_ref, bf16[14,128,384]{2,1,0:T(8,128)(2,1)} %fusion.2.features_ref, f32[8,128,128]{2,1,0:T(8,128)} %prior_ref.1, bf16[1152,2048]{1,0:T(8,128)(2,1)} %bitcast.50, f32[1,2048]{1,0:T(1,128)} %broadcast_in_dim_tile.8.bias_first_ref, ...), custom_call_target="tpu_custom_call" | custom-call | flops 37446746112 | bytes 16777216 | tf_op jit(solution)/shard_map/denoise/pallas_call | solution.py:236
  119.3 5.6 %all-to-all-start.2 = ((f32[32,2,2,8,128]{4,3,2,1,0:T(8,128)}), f32[32,2,2,8,128]{4,3,2,1,0:T(8,128)S(1)}, u32[]{:S(2)}, u32[]{:S(2)}) async-start(f32[32,2,2,8,128]{4,3,2,1,0:T(8,128)} %denoise.1.denoised_ref), calls=%async_computation.2 | async-start | bytes 1048576 | tf_op jit(solution)/shard_map/all_to_all | solution.py:654
  126.4 1.3 copy-done.3
  127.7 6.0 %adjoint.1.adjoint_ref = f32[32,2,2,8,128]{4,3,2,1,0:T(8,128)S(1)} custom-call(bf16[4,8,4,32,256]{4,3,2,1,0:T(8,128)(2,1)} %bitcast.5.spectra_real_ref.spectra_imag_ref, bf16[4,8,4,32,256]{4,3,2,1,0:T(8,128)(2,1)} %bitcast.5.spectra_real_ref.spectra_imag_ref, bf16[4,8,4,64,128]{4,3,2,1,0:T(8,128)(2,1)S(1)} %bitcast.41, ...), custom_call_target="tpu_custom_call" | custom-call | flops 4831838208 | bytes 8388608 | tf_op jit(solution)/shard_map/adjoint/pallas_call | solution.py:610
  134.4 6.8 %all-to-all-done.2.denoised_ref = f32[32,2,2,8,128]{4,3,2,1,0:T(8,128)S(1)} async-done(((f32[32,2,2,8,128]{4,3,2,1,0:T(8,128)}), f32[32,2,2,8,128]{4,3,2,1,0:T(8,128)S(1)}, u32[]{:S(2)}, u32[]{:S(2)}) %all-to-all-start.2) | async-done | bytes 524320 | tf_op jit(solution)/shard_map/all_to_all | solution.py:654
  141.3 2.8 %all-to-all-start.3 = ((f32[32,2,2,8,128]{4,3,2,1,0:T(8,128)}), f32[32,2,2,8,128]{4,3,2,1,0:T(8,128)S(1)}, u32[]{:S(2)}, u32[]{:S(2)}) async-start(f32[32,2,2,8,128]{4,3,2,1,0:T(8,128)} %copy-done.1), calls=%async_computation.3 | async-start | bytes 1048576 | tf_op jit(solution)/shard_map/all_to_all | solution.py:654
  147.9 8.8 %first_product.1 = (f32[32,2,2,8,128]{4,3,2,1,0:T(8,128)S(1)}, f32[8,128]{1,0:T(8,128)S(1)}) custom-call(bf16[4,8,4,64,128]{4,3,2,1,0:T(8,128)(2,1)S(1)} %bitcast.43, bf16[4,8,4,64,128]{4,3,2,1,0:T(8,128)(2,1)S(1)} %bitcast.44, f32[32,2,2,8,128]{4,3,2,1,0:T(8,128)S(1)} %copy-done.2, f32[32,2,2,8,128]{4,3,2,1,0:T(8,128)S(1)} %all-to-all-done.2.denoised_ref, ...), custom_call_target="tpu_custom_call" | custom-call | flops 9663676416 | bytes 8388608 | tf_op jit(solution)/shard_map/first_product/pallas_call | solution.py:610
  157.5 2.8 %all-to-all-done.3.adjoint_ref = f32[32,2,2,8,128]{4,3,2,1,0:T(8,128)S(1)} async-done(((f32[32,2,2,8,128]{4,3,2,1,0:T(8,128)}), f32[32,2,2,8,128]{4,3,2,1,0:T(8,128)S(1)}, u32[]{:S(2)}, u32[]{:S(2)}) %all-to-all-start.3) | async-done | bytes 524320 | tf_op jit(solution)/shard_map/all_to_all | solution.py:654
  163.1 8.7 %second_product.1 = f32[32,9,8,128]{3,2,1,0:T(8,128)S(1)} custom-call(bf16[4,8,4,64,128]{4,3,2,1,0:T(8,128)(2,1)S(1)} %bitcast.45, bf16[4,8,4,64,128]{4,3,2,1,0:T(8,128)(2,1)S(1)} %bitcast.46, f32[32,2,2,8,128]{4,3,2,1,0:T(8,128)S(1)} %copy-done.10, f32[8,128]{1,0:T(8,128)S(1)} %get-tuple-element.13.total_ref, f32[256,128]{1,0:T(8,128)S(1)} %pad_maximum_fusion.1.refs_0_, ...), custom_call_target="tpu_custom_call" | custom-call | flops 9663676416 | bytes 8388608 | tf_op jit(solution)/shard_map/second_product/pallas_call | solution.py:610
  171.9 33.1 %all_to_all.25.moved_ref = f32[32,9,8,128]{3,2,1,0:T(8,128)S(1)} all-to-all(f32[32,9,8,128]{3,2,1,0:T(8,128)S(1)} %second_product.1), channel_id=1, replica_groups=mesh['slab'=4,'coil'=8] {'slab','coil'}, dimensions={0} | all-to-all | bytes 2359296 | tf_op jit(solution)/shard_map/all_to_all | solution.py:654
  204.9 1.5 finish.1
  (115 shorter events, 26.4 us)
Async XLA Ops:
  5.6 7.3 %copy-start.11 = (f32[8,128,128]{2,1,0:T(8,128)S(1)}, f32[8,128,128]{2,1,0:T(8,128)}, u32[]{:S(2)}) copy-start(f32[8,128,128]{2,1,0:T(8,128)} %prior_ref.1) | copy-start | bytes 1572868
  5.6 13.7 %copy-start.20 = (s32[32,256]{1,0:T(8,128)S(1)}, s32[32,256]{1,0:T(8,128)}, u32[]{:S(2)}) copy-start(s32[32,256]{1,0:T(8,128)} %param.17) | copy-start | bytes 98308
  5.6 14.3 %copy-start.21 = (bf16[3,3,3,32,2]{3,4,2,1,0:T(2,128)(2,1)S(1)}, bf16[3,3,3,32,2]{3,4,2,1,0:T(2,128)(2,1)}, u32[]{:S(2)}) copy-start(bf16[3,3,3,32,2]{3,4,2,1,0:T(2,128)(2,1)} %param.18) | copy-start | bytes 10372
  5.6 58.4 %all-to-all-start = ((bf16[32,2,2,64,128]{4,3,2,1,0:T(8,128)(2,1)}), bf16[32,2,2,64,128]{4,3,2,1,0:T(8,128)(2,1)S(1)}, u32[]{:S(2)}, u32[]{:S(2)}) async-start(bf16[32,2,2,64,128]{4,3,2,1,0:T(8,128)(2,1)} %copy.37), calls=%async_computation | async-start | bytes 4194304 | tf_op jit(solution)/shard_map/all_to_all | solution.py:654
  12.9 9.4 %copy-start.22 = (bf16[3,3,3,2,32]{4,3,2,1,0:T(2,128)(2,1)S(1)}, bf16[3,3,3,2,32]{4,3,2,1,0:T(2,128)(2,1)}, u32[]{:S(2)}) copy-start(bf16[3,3,3,2,32]{4,3,2,1,0:T(2,128)(2,1)} %param.22) | copy-start | bytes 10372
  12.9 13.4 %copy-start.17 = (bf16[3,3,3,32,32]{4,3,2,1,0:T(8,128)(2,1)S(1)}, bf16[3,3,3,32,32]{4,3,2,1,0:T(8,128)(2,1)}, u32[]{:S(2)}) copy-start(bf16[3,3,3,32,32]{4,3,2,1,0:T(8,128)(2,1)} %param.20) | copy-start | bytes 165892
  13.7 54.0 %collective-permute-start = (bf16[3,128,128]{2,1,0:T(8,128)(2,1)}, bf16[3,128,128]{2,1,0:T(8,128)(2,1)}, u32[]{:S(2)}, u32[]{:S(2)}) collective-permute-start(bf16[3,128,128]{2,1,0:T(8,128)(2,1)} %get-tuple-element.16), channel_id=1, source_target_pairs={{0,1},{1,2},{2,3},{3,4},{4,5},{5,6},{6,7},{7,8},{8,9},{9,10},{10,1... | collective-permute-start | bytes 294920 | tf_op jit(solution)/shard_map/ppermute | solution.py:28
  18.0 49.7 %collective-permute-start.1 = (bf16[3,128,128]{2,1,0:T(8,128)(2,1)}, bf16[3,128,128]{2,1,0:T(8,128)(2,1)}, u32[]{:S(2)}, u32[]{:S(2)}) collective-permute-start(bf16[3,128,128]{2,1,0:T(8,128)(2,1)} %get-tuple-element.17), channel_id=1, source_target_pairs={{1,0},{2,1},{3,2},{4,3},{5,4},{6,5},{7,6},{8,7},{9,8},{10,9},{11,1... | collective-permute-start | bytes 294920 | tf_op jit(solution)/shard_map/ppermute | solution.py:29
  27.1 2.6 %copy-start.23 = (f32[32]{0:T(128)S(1)}, f32[32]{0:T(128)}, u32[]{:S(2)}) copy-start(f32[32]{0:T(128)} %param.19) | copy-start | bytes 388
  27.1 3.3 %copy-start.24 = (f32[32]{0:T(128)S(1)}, f32[32]{0:T(128)}, u32[]{:S(2)}) copy-start(f32[32]{0:T(128)} %param.21) | copy-start | bytes 388
  27.1 4.0 %copy-start.25 = (f32[2]{0:T(128)S(1)}, f32[2]{0:T(128)}, u32[]{:S(2)}) copy-start(f32[2]{0:T(128)} %param.23) | copy-start | bytes 28
  36.4 3.3 %copy-start.18 = (bf16[32,256]{1,0:T(8,128)(2,1)S(1)}, bf16[32,256]{1,0:T(8,128)(2,1)}, u32[]{:S(2)}) copy-start(bf16[32,256]{1,0:T(8,128)(2,1)} %convert_element_type.12) | copy-start | bytes 49156
  39.7 11.1 %copy-start.19 = (s32[1152]{0:T(1024)S(1)}, s32[1152]{0:T(1024)}, u32[]{:S(2)}) copy-start(s32[1152]{0:T(1024)} %sub.200) | copy-start | bytes 13828
  39.7 11.2 %copy-start.12 = (bf16[18,2048]{1,0:T(8,128)(2,1)S(1)}, bf16[18,2048]{1,0:T(8,128)(2,1)}, u32[]{:S(2)}) copy-start(bf16[18,2048]{1,0:T(8,128)(2,1)} %broadcast_in_dim.176) | copy-start | bytes 221188
  39.7 11.2 %copy-start.13 = (bf16[18,2048]{1,0:T(8,128)(2,1)S(1)}, bf16[18,2048]{1,0:T(8,128)(2,1)}, u32[]{:S(2)}) copy-start(bf16[18,2048]{1,0:T(8,128)(2,1)} %broadcast_in_dim.180) | copy-start | bytes 221188
  50.9 4.2 %copy-start.14 = (bf16[32,1152]{1,0:T(8,128)(2,1)S(1)}, bf16[32,1152]{1,0:T(8,128)(2,1)}, u32[]{:S(2)}) copy-start(bf16[32,1152]{1,0:T(8,128)(2,1)} %broadcast_in_dim.198) | copy-start | bytes 221188
  50.9 4.1 %copy-start.15 = (bf16[32,1152]{1,0:T(8,128)(2,1)S(1)}, bf16[32,1152]{1,0:T(8,128)(2,1)}, u32[]{:S(2)}) copy-start(bf16[32,1152]{1,0:T(8,128)(2,1)} %broadcast_in_dim.202) | copy-start | bytes 221188
  50.9 4.1 %copy-start.16 = (bf16[32,1152]{1,0:T(8,128)(2,1)S(1)}, bf16[32,1152]{1,0:T(8,128)(2,1)}, u32[]{:S(2)}) copy-start(bf16[32,1152]{1,0:T(8,128)(2,1)} %broadcast_in_dim.206) | copy-start | bytes 221188
  64.0 55.3 %all-to-all-start.1 = ((bf16[32,2,2,32,256]{4,3,2,1,0:T(8,128)(2,1)}), bf16[32,2,2,32,256]{4,3,2,1,0:T(8,128)(2,1)}, u32[]{:S(2)}, u32[]{:S(2)}) async-start(bf16[32,2,2,32,256]{4,3,2,1,0:T(8,128)(2,1)} %copy.39), calls=%async_computation.1 | async-start | bytes 4194304 | tf_op jit(solution)/shard_map/all_to_all | solution.py:654
  119.3 21.9 %all-to-all-start.2 = ((f32[32,2,2,8,128]{4,3,2,1,0:T(8,128)}), f32[32,2,2,8,128]{4,3,2,1,0:T(8,128)S(1)}, u32[]{:S(2)}, u32[]{:S(2)}) async-start(f32[32,2,2,8,128]{4,3,2,1,0:T(8,128)} %denoise.1.denoised_ref), calls=%async_computation.2 | async-start | bytes 1048576 | tf_op jit(solution)/shard_map/all_to_all | solution.py:654
  126.4 1.3 copy-start.3
  127.7 17.3 %copy-start.4 = (bf16[256,512]{1,0:T(8,128)(2,1)S(1)}, bf16[256,512]{1,0:T(8,128)(2,1)}, u32[]{:S(2)}) copy-start(bf16[256,512]{1,0:T(8,128)(2,1)} %constant.67.clone.refs_1_) | copy-start | bytes 786436
  141.3 19.0 %all-to-all-start.3 = ((f32[32,2,2,8,128]{4,3,2,1,0:T(8,128)}), f32[32,2,2,8,128]{4,3,2,1,0:T(8,128)S(1)}, u32[]{:S(2)}, u32[]{:S(2)}) async-start(f32[32,2,2,8,128]{4,3,2,1,0:T(8,128)} %copy-done.1), calls=%async_computation.3 | async-start | bytes 1048576 | tf_op jit(solution)/shard_map/all_to_all | solution.py:654
  171.8 33.1 %copy-start = (f32[32,2,2,8,128]{4,3,2,1,0:T(8,128)S(1)}, f32[32,2,2,8,128]{4,3,2,1,0:T(8,128)}, u32[]{:S(2)}) copy-start(f32[32,2,2,8,128]{4,3,2,1,0:T(8,128)} %denoise.1.denoised_ref) | copy-start | bytes 1572868
  (8 other events, 7.4 us)

commit v9 on v8

--- a/solution.py
+++ b/solution.py
@@ -31,7 +31,7 @@
 
 
 def chunk_rows(rows):
-    return max(size for size in range(1, 7) if rows % size == 0)
+    return max(size for size in range(1, 13) if rows % size == 0)
 
 
 def chained(lhs_pieces):
@@ -244,7 +244,7 @@
             pltpu.VMEM((own_rows + 2, planes, 18 * readout), jnp.float32),
         ]
         + [pltpu.VMEM((width * own_rows, planes), jnp.float32)] * turned,
-        compiler_params=pltpu.CompilerParams(vmem_limit_bytes=56 * 1024 * 1024),
+        compiler_params=pltpu.CompilerParams(vmem_limit_bytes=40 * 1024 * 1024),
         cost_estimate=pl.CostEstimate(
             flops=int(flops), bytes_accessed=16 * 1024 * 1024, transcendentals=0
         ),
@@ -499,80 +499,53 @@
     accumulate(out_ref, total, ((0, 0), (1, 0)))
 
 
+def product_kernel(maps_real_ref, maps_imag_ref, field_ref, *refs):
+    constants, out_ref = refs[:-1], refs[-1]
+    fields = [plane_of(field_ref, part) for part in range(2)]
+    accumulate(
+        out_ref,
+        normal_sums((maps_real_ref, maps_imag_ref), *fields, *constants),
+        ((0, 0), (1, 0)),
+    )
+
+
 def lane_sums(left, other):
-    product = left[0] * other[0] + left[1] * other[1]
-    return jnp.sum(jnp.sum(product, axis=0), axis=0, keepdims=True)
-
-
-def first_kernel(
-    maps_real_ref, maps_imag_ref, adjoint_ref, denoised_ref, *refs
-):
-    constants, (out_ref, total_ref) = refs[:-2], refs[-2:]
+    return jnp.sum(left[0] * other[0] + left[1] * other[1], axis=0, keepdims=True)
+
+
+def twice_kernel(maps_real_ref, maps_imag_ref, adjoint_ref, denoised_ref, *refs):
+    constants, out_ref = refs[:-1], refs[-1]
+    maps_refs = maps_real_ref, maps_imag_ref
+    x_index = pl.program_id(0)
+    x_count = pl.num_programs(0)
+    blocks, block_rows, planes = out_ref.shape[0], out_ref.shape[2], out_ref.shape[3]
+    shape = blocks, block_rows, planes
     rights = [
         plane_of(adjoint_ref, part) + penalty * plane_of(denoised_ref, part) for part in range(2)
     ]
-    sums = normal_sums((maps_real_ref, maps_imag_ref), *rights, *constants)
-    accumulate(out_ref, sums, ((0, 0), (1, 0)))
-
-    @pl.when(pl.program_id(1) == pl.num_programs(1) - 1)
+    fields = normal_sums(maps_refs, *rights, *constants)
+    images = normal_sums(maps_refs, *fields, *constants)
+    for part in range(2):
+        out_ref[:, part * x_count + x_index] = images[part].reshape(shape)
+        out_ref[:, (2 + part) * x_count + x_index] = fields[part].reshape(shape)
+    totals = jnp.concatenate(
+        [
+            lane_sums(rights, rights),
+            lane_sums(rights, fields),
+            lane_sums(fields, fields),
+            lane_sums(fields, images),
+            jnp.zeros((block_rows - 4, planes), jnp.float32),
+        ],
+        axis=0,
+    )[None]
+
+    @pl.when(x_index == 0)
     def _():
-        shape = out_ref.shape[0], out_ref.shape[3], out_ref.shape[4]
-        sides = [right.reshape(shape) for right in rights]
-        fields = [out_ref[:, part, 0] for part in range(2)]
-        totals = jnp.concatenate(
-            [
-                lane_sums(sides, sides),
-                lane_sums(sides, fields),
-                lane_sums(fields, fields),
-                jnp.zeros((total_ref.shape[0] - 3, total_ref.shape[1]), jnp.float32),
-            ],
-            axis=0,
-        )
-
-        @pl.when(pl.program_id(0) == 0)
-        def _():
-            total_ref[...] = totals
-
-        @pl.when(pl.program_id(0) > 0)
-        def _():
-            total_ref[...] += totals
-
-
-def second_kernel(maps_real_ref, maps_imag_ref, field_ref, total_ref, *refs):
-    constants, out_ref = refs[:-1], refs[-1]
-    x_index = pl.program_id(0)
-    x_count = pl.num_programs(0)
-    blocks, block_rows, planes = out_ref.shape[0], out_ref.shape[2], out_ref.shape[3]
-    sums = normal_sums(
-        (maps_real_ref, maps_imag_ref), plane_of(field_ref, 0), plane_of(field_ref, 1), *constants
-    )
-    places = [(part * x_count + x_index,) for part in range(2)]
-    accumulate(out_ref, sums, places)
-
-    @pl.when(pl.program_id(1) == pl.num_programs(1) - 1)
+        out_ref[:, 4 * x_count] = jnp.broadcast_to(totals, shape)
+
+    @pl.when(x_index > 0)
     def _():
-        fields = [field_ref[:, part, 0] for part in range(2)]
-        images = [out_ref[(slice(None),) + place] for place in places]
-        for part in range(2):
-            out_ref[:, (2 + part) * x_count + x_index] = fields[part]
-        totals = jnp.concatenate(
-            [
-                jnp.zeros((3, planes), jnp.float32),
-                lane_sums(fields, images),
-                jnp.zeros((block_rows - 4, planes), jnp.float32),
-            ],
-            axis=0,
-        )
-
-        @pl.when(x_index == 0)
-        def _():
-            out_ref[:, 4 * x_count] = jnp.broadcast_to(
-                (total_ref[...] + totals)[None], (blocks, block_rows, planes)
-            )
-
-        @pl.when(x_index > 0)
-        def _():
-            out_ref[:, 4 * x_count] += totals[None]
+        out_ref[:, 4 * x_count] += totals
 
 
 def held_coils(count):
@@ -597,7 +570,7 @@
 
 def compute_params():
     return pltpu.CompilerParams(
-        dimension_semantics=("arbitrary", "arbitrary"), vmem_limit_bytes=48 * 1024 * 1024
+        dimension_semantics=("arbitrary", "arbitrary"), vmem_limit_bytes=22 * 1024 * 1024
     )
 
 
@@ -632,21 +605,20 @@
     )[0]
 
 
-def first_call(maps, adjoint, denoised, constants):
-    shape = adjoint.shape
-    totals = (8, shape[4])
-    outs = [(field_spec(shape), shape), (whole(totals), totals)]
+def once_call(maps, field, constants):
+    shape = field.shape
+    outs = [(field_spec(shape), shape)]
     return product_call(
-        first_kernel, "first_product", shape[2], maps, [adjoint, denoised], [], constants, outs, 6
-    )
-
-
-def second_call(maps, field, totals, constants):
-    blocks, _, x_count, block_rows, planes = field.shape
+        product_kernel, "product", shape[2], maps, [field], [], constants, outs, 6
+    )[0]
+
+
+def twice_call(maps, adjoint, denoised, constants):
+    blocks, _, x_count, block_rows, planes = adjoint.shape
     shape = (blocks, 4 * x_count + 1, block_rows, planes)
     outs = [(whole(shape), shape)]
     return product_call(
-        second_kernel, "second_product", x_count, maps, [field], [totals], constants, outs, 6
+        twice_kernel, "products", x_count, maps, [adjoint, denoised], [], constants, outs, 12
     )[0]
 
 
@@ -717,7 +689,7 @@
         out_specs=[vmem] * 2,
         out_shape=[jax.ShapeDtypeStruct(shape, jnp.float32)] * 2,
         scratch_shapes=[pltpu.VMEM((2 * blocks * x_count * rows, planes), jnp.float32)],
-        compiler_params=pltpu.CompilerParams(vmem_limit_bytes=32 * 1024 * 1024),
+        compiler_params=pltpu.CompilerParams(vmem_limit_bytes=12 * 1024 * 1024),
         cost_estimate=pl.CostEstimate(
             flops=8 * adjoint.size, bytes_accessed=24 * adjoint.size, transcendentals=0
         ),
@@ -743,16 +715,16 @@
     slabs = lax.axis_size("slab")
     coils = lax.axis_size("coil")
     devices = slabs * coils
-    spread = readout % devices == 0 and own_rows % 8 == 0
+    spread = readout % devices == 0 and own_rows % 8 == 0 and held_coils(coils) == coils
     parts = devices if spread else coils
     x_count = readout // parts
     mask = lax.all_gather(sampling.astype(jnp.bfloat16), "slab", axis=0, tiled=True)
-    features, mask = lax.optimization_barrier(
-        (with_halo(prior_image.astype(jnp.bfloat16), 3), mask)
-    )
     mask = jnp.transpose(mask).astype(jnp.float32)
+    half_mask = jnp.concatenate([mask[::2], mask[1::2]], axis=0)
+    features, mask, half_mask = lax.optimization_barrier(
+        (with_halo(prior_image.astype(jnp.bfloat16), 3), mask, half_mask)
+    )
     row_count = mask.shape[0]
-    half_mask = jnp.concatenate([mask[::2], mask[1::2]], axis=0)
     constants = [half_mask] + half_tables(row_count, planes)
     constants = [jnp.asarray(value) for value in constants]
     adjoint_constants = [mask, jnp.asarray(dft_table(row_count, planes))]
@@ -784,9 +756,13 @@
         blocks = x_first(blocks, parts)
     if spread:
         adjoint = adjoint_call(spectra, maps, adjoint_constants, x_count, devices)
-        field, totals = first_call(maps, adjoint, exchange(blocks, axes), constants)
-        field, adjoint_back = lax.optimization_barrier((field, exchange(adjoint, axes)))
-        payload = exchange(second_call(maps, field, totals, constants), axes)
+        payload, adjoint_back = lax.optimization_barrier(
+            (
+                twice_call(maps, adjoint, exchange(blocks, axes), constants),
+                exchange(adjoint, axes),
+            )
+        )
+        payload = exchange(payload, axes)
         return tuple(finish_call(adjoint_back, blocks, payload))
 
     tail = blocks.shape[1:3]
@@ -802,10 +778,9 @@
         return x_last(exchange(split, "coil"))
 
     adjoint = lax.psum(adjoint_call(spectra, maps, adjoint_constants, x_count, 1), "slab")
-    denoised = whole_rows(blocks)
-    right = adjoint + penalty * denoised
-    field = lax.psum(first_call(maps, adjoint, denoised, constants)[0], "slab")
-    image = lax.psum(first_call(maps, field, jnp.zeros_like(field), constants)[0], "slab")
+    right = adjoint + penalty * whole_rows(blocks)
+    field = lax.psum(once_call(maps, right, constants), "slab")
+    image = lax.psum(once_call(maps, field, constants), "slab")
     squares = lax.psum(
         jnp.stack(
             [

time: 207 us -> 205 us (level)
  local copies, waits for them, and re-layouts: 35.6 us -> 22.7 us
  blocking collectives: 41.8 us -> 50.5 us
  waiting for transfers between devices: 13.7 us -> 21.3 us
  other arithmetic: 15.4 us -> 12.1 us
  Pallas kernels: 73.9 us -> 71.5 us
    all_to_all x4, waiting for transfers between devices: 13.7 us -> 21.2 us  [exchange(): return lax.all_to_all(blocks, axis, split_axis=0, concat_axis=0, tiled=True)]
    all_gather x1, blocking collectives: 8.74 us -> 14.4 us  [body(): lax.all_gather(sampling.astype(jnp.bfloat16), 'slab', axis=0, tiled=True)]
    unnamed x54 -> x38, local copies, waits for them, and re-layouts: 16.7 us -> 11.5 us
    pallas_call x1, Pallas kernels: 49 us -> 44.8 us  [denoise(): pl.pallas_call(functools.partial(denoise_kernel, group), in_specs=[pl.Blo...]
    all_to_all x1, blocking collectives: 33.1 us -> 36 us  [exchange(): return lax.all_to_all(blocks, axis, split_axis=0, concat_axis=0, tiled=True)]
    pallas_call x3 -> x2, Pallas kernels: 23.4 us -> 24.3 us  [product_call(): pl.pallas_call(kernel, grid=(x_count, coils // held_coils(coils)), in_spe...]
  transfers between devices with their start and end apart: 6 -> 6, of which waited for: 3 -> 2; matrix products, arithmetic and copies ran while one was open for 18% -> 14% of each run, Pallas kernels for 31% -> 34%
where the time goes in v9:
time: 205 us
  Pallas kernels  71.5 us (35%)
  blocking collectives  50.5 us (25%)
  starting transfers between devices  25.3 us (12%)
  local copies, waits for them, and re-layouts  22.7 us (11%)
  waiting for transfers between devices  21.3 us (10%)
  other arithmetic  12.1 us (6%)
    pallas_call x1, Pallas kernels, denoise(): pl.pallas_call(functools.partial(denoise_kernel, group), in_specs=[pl.Blo...  44.8 us
    all_to_all x1, blocking collectives, exchange(): return lax.all_to_all(blocks, axis, split_axis=0, concat_axis=0, tiled=True)  36 us
    pallas_call x2, Pallas kernels, product_call(): pl.pallas_call(kernel, grid=(x_count, coils // held_coils(coils)), in_spe...  24.3 us
    all_to_all x4, waiting for transfers between devices, exchange(): return lax.all_to_all(blocks, axis, split_axis=0, concat_axis=0, tiled=True)  21.2 us
    all_to_all x4, starting transfers between devices, exchange(): return lax.all_to_all(blocks, axis, split_axis=0, concat_axis=0, tiled=True)  18.6 us
    all_gather x1, blocking collectives, body(): lax.all_gather(sampling.astype(jnp.bfloat16), 'slab', axis=0, tiled=True)  14.4 us
    unnamed x38, local copies, waits for them, and re-layouts  11.5 us
    select_n x3, other arithmetic, banded(): result = jnp.where(inner - outer + offset == tap, tiles[tap], result)  8.94 us
  transfers between devices with their start and end apart: 6, of which 2 were waited for; matrix products, arithmetic and copies ran while one was open for 14% of the time, Pallas kernels for 34%

profile of v9, /device:TPU:0, one launch (start us, length us, event | category | flops | bytes accessed | tf_op | source)
XLA Modules:
  0.0 204.6 jit_solution(16925792919573125160)
XLA Ops:
  0.6 1.1 convert_element_type.12
  2.4 5.5 %collective-permute-start = (bf16[3,128,128]{2,1,0:T(8,128)(2,1)}, bf16[3,128,128]{2,1,0:T(8,128)(2,1)}, u32[]{:S(2)}, u32[]{:S(2)}) collective-permute-start(bf16[3,128,128]{2,1,0:T(8,128)(2,1)} %get-tuple-element.14), channel_id=1, source_target_pairs={{0,1},{1,2},{2,3},{3,4},{4,5},{5,6},{6,7},{7,8},{8,9},{9,10},{10,1... | collective-permute-start | bytes 294920 | tf_op jit(solution)/shard_map/ppermute | solution.py:28
  7.9 1.3 collective-permute-start.1
  9.2 3.3 %copy.36 = bf16[1,64,128,128]{2,1,3,0:T(8,128)(2,1)S(1)} copy(bf16[1,64,128,128]{3,2,1,0:T(8,128)(2,1)} %param.15) | data formatting | bytes 4194304 | tf_op args[1]
  12.5 1.5 copy.37
  14.0 6.5 %all-to-all-start = ((bf16[32,2,2,64,128]{4,3,2,1,0:T(8,128)(2,1)}), bf16[32,2,2,64,128]{4,3,2,1,0:T(8,128)(2,1)}, u32[]{:S(2)}, u32[]{:S(2)}) async-start(bf16[32,2,2,64,128]{4,3,2,1,0:T(8,128)(2,1)} %copy.37), calls=%async_computation | async-start | bytes 4194304 | tf_op jit(solution)/shard_map/all_to_all | solution.py:626
  20.5 14.4 %all_gather.3 = bf16[128,256]{1,0:T(8,128)(2,1)S(1)} all-gather(bf16[32,256]{1,0:T(8,128)(2,1)S(1)} %convert_element_type.13), channel_id=1, replica_groups=mesh['slab'=4,'coil'=8] {'slab'}, dimensions={0}, use_global_device_ids=true | all-gather | bytes 81920 | tf_op jit(solution)/shard_map/all_gather | solution.py:721
  42.6 3.4 %copy.38 = bf16[1,32,256,128]{2,1,3,0:T(8,128)(2,1)S(1)} copy(bf16[1,32,256,128]{3,2,1,0:T(8,128)(2,1)} %param.16) | data formatting | bytes 4194304 | tf_op args[2]
  46.0 1.6 copy.39
  48.7 4.1 %select_select_fusion.1 = bf16[18,64,2048]{2,1,0:T(8,128)(2,1)} fusion(pred[64,2048]{1,0:T(8,128)(4,1)S(1)} %get-tuple-element.29, pred[64,2048]{1,0:T(8,128)(4,1)S(1)} %get-tuple-element.30, pred[64,2048]{1,0:T(8,128)(4,1)S(1)} %get-tuple-element.28, bf16[18,2048]{1,0:T(8,128)(2,1)S(1)} %copy-done.7, bf16[18,2048]{1,0:T(8,128)(2,1)S(1)} %broadcast_in_dim.176, ...), kind=kLoop, calls=%fused_computation.1 | loop fusion | flops 7077888 | bytes 5332992 | tf_op jit(solution)/shard_map/jit(_where)/select_n | solution.py:162
  52.8 4.2 %select_select_fusion = bf16[64,32,1152]{2,1,0:T(8,128)(2,1)} fusion(pred[64,1152]{1,0:T(8,128)(4,1)S(1)} %get-tuple-element.26, pred[64,1152]{1,0:T(8,128)(4,1)S(1)} %get-tuple-element.27, pred[64,1152]{1,0:T(8,128)(4,1)S(1)} %get-tuple-element.25, bf16[32,1152]{1,0:T(8,128)(2,1)S(1)} %copy-done.10, bf16[32,1152]{1,0:T(8,128)(2,1)S(1)} %copy-done.9, ...), kind=kLoop, calls=%fused_computation | loop fusion | flops 7077888 | bytes 5160960 | tf_op jit(solution)/shard_map/jit(_where)/select_n | solution.py:162
  57.1 13.4 %all-to-all-done = bf16[32,2,2,64,128]{4,3,2,1,0:T(8,128)(2,1)} async-done(((bf16[32,2,2,64,128]{4,3,2,1,0:T(8,128)(2,1)}), bf16[32,2,2,64,128]{4,3,2,1,0:T(8,128)(2,1)}, u32[]{:S(2)}, u32[]{:S(2)}) %all-to-all-start) | async-done | bytes 2097184 | tf_op jit(solution)/shard_map/all_to_all | solution.py:626
  70.6 3.7 %all-to-all-start.1 = ((bf16[32,2,2,32,256]{4,3,2,1,0:T(8,128)(2,1)}), bf16[32,2,2,32,256]{4,3,2,1,0:T(8,128)(2,1)}, u32[]{:S(2)}, u32[]{:S(2)}) async-start(bf16[32,2,2,32,256]{4,3,2,1,0:T(8,128)(2,1)} %copy.39), calls=%async_computation.1 | async-start | bytes 4194304 | tf_op jit(solution)/shard_map/all_to_all | solution.py:626
  74.3 1.1 pad_maximum_fusion
  77.0 2.3 %copy-done.1 = bf16[18,64,2048]{2,1,0:T(8,128)(2,1)S(1)} copy-done((bf16[18,64,2048]{2,1,0:T(8,128)(2,1)S(1)}, bf16[18,64,2048]{2,1,0:T(8,128)(2,1)}, u32[]{:S(2)}) %copy-start.1) | copy-done | bytes 4718616
  79.4 44.8 %denoise.1.denoised_ref = f32[32,2,2,8,128]{4,3,2,1,0:T(8,128)} custom-call(s32[2]{0:T(128)S(1)} %pad_add_fusion.first_ref, bf16[14,128,384]{2,1,0:T(8,128)(2,1)S(1)} %fusion.2.features_ref, f32[8,128,128]{2,1,0:T(8,128)S(1)} %copy-done.2, bf16[1152,2048]{1,0:T(8,128)(2,1)S(1)} %bitcast.42, f32[1,2048]{1,0:T(1,128)S(1)} %broadcast_in_dim_tile.8.bias_first_ref, ...), custom_call_target="tpu_custom_call" | custom-call | flops 37446746112 | bytes 16777216 | tf_op jit(solution)/shard_map/denoise/pallas_call | solution.py:236
  124.1 5.8 %all-to-all-start.2 = ((f32[32,2,2,8,128]{4,3,2,1,0:T(8,128)}), f32[32,2,2,8,128]{4,3,2,1,0:T(8,128)S(1)}, u32[]{:S(2)}, u32[]{:S(2)}) async-start(f32[32,2,2,8,128]{4,3,2,1,0:T(8,128)} %denoise.1.denoised_ref), calls=%async_computation.2 | async-start | bytes 1048576 | tf_op jit(solution)/shard_map/all_to_all | solution.py:626
  130.0 1.3 copy-done.3
  131.3 7.0 %adjoint.1.adjoint_ref = f32[32,2,2,8,128]{4,3,2,1,0:T(8,128)} custom-call(bf16[4,8,4,32,256]{4,3,2,1,0:T(8,128)(2,1)} %bitcast.5.spectra_real_ref.spectra_imag_ref, bf16[4,8,4,32,256]{4,3,2,1,0:T(8,128)(2,1)} %bitcast.5.spectra_real_ref.spectra_imag_ref, bf16[4,8,4,64,128]{4,3,2,1,0:T(8,128)(2,1)} %bitcast.2.maps_real_ref.maps_imag_ref, ...), custom_call_target="tpu_custom_call" | custom-call | flops 4831838208 | bytes 8388608 | tf_op jit(solution)/shard_map/adjoint/pallas_call | solution.py:583
  138.3 7.8 %all-to-all-done.2.denoised_ref = f32[32,2,2,8,128]{4,3,2,1,0:T(8,128)S(1)} async-done(((f32[32,2,2,8,128]{4,3,2,1,0:T(8,128)}), f32[32,2,2,8,128]{4,3,2,1,0:T(8,128)S(1)}, u32[]{:S(2)}, u32[]{:S(2)}) %all-to-all-start.2) | async-done | bytes 524320 | tf_op jit(solution)/shard_map/all_to_all | solution.py:626
  146.1 2.6 %all-to-all-start.3 = ((f32[32,2,2,8,128]{4,3,2,1,0:T(8,128)}), f32[32,2,2,8,128]{4,3,2,1,0:T(8,128)S(1)}, u32[]{:S(2)}, u32[]{:S(2)}) async-start(f32[32,2,2,8,128]{4,3,2,1,0:T(8,128)} %adjoint.1.adjoint_ref), calls=%async_computation.3 | async-start | bytes 1048576 | tf_op jit(solution)/shard_map/all_to_all | solution.py:626
  148.7 17.3 %products.1 = f32[32,9,8,128]{3,2,1,0:T(8,128)S(1)} custom-call(bf16[4,8,4,64,128]{4,3,2,1,0:T(8,128)(2,1)} %bitcast.2.maps_real_ref.maps_imag_ref, bf16[4,8,4,64,128]{4,3,2,1,0:T(8,128)(2,1)} %bitcast.2.maps_real_ref.maps_imag_ref, f32[32,2,2,8,128]{4,3,2,1,0:T(8,128)} %adjoint.1.adjoint_ref, f32[32,2,2,8,128]{4,3,2,1,0:T(8,128)S(1)} %all-to-all-done.2.denoised_ref, ...), custom_call_target="tpu_custom_call" | custom-call | flops 19327352832 | bytes 8388608 | tf_op jit(solution)/shard_map/products/pallas_call | solution.py:583
  166.0 36.0 %all_to_all.25.moved_ref = f32[32,9,8,128]{3,2,1,0:T(8,128)S(1)} all-to-all(f32[32,9,8,128]{3,2,1,0:T(8,128)S(1)} %products.1), channel_id=1, replica_groups=mesh['slab'=4,'coil'=8] {'slab','coil'}, dimensions={0} | all-to-all | bytes 2359296 | tf_op jit(solution)/shard_map/all_to_all | solution.py:626
  202.1 2.5 %finish.1 = (f32[8,128,128]{2,1,0:T(8,128)}, f32[8,128,128]{2,1,0:T(8,128)}) custom-call(f32[32,2,2,8,128]{4,3,2,1,0:T(8,128)S(1)} %all-to-all-done.3.adjoint_ref, f32[32,2,2,8,128]{4,3,2,1,0:T(8,128)} %denoise.1.denoised_ref, f32[32,9,8,128]{3,2,1,0:T(8,128)S(1)} %all_to_all.25.moved_ref), custom_call_target="tpu_custom_call" | custom-call | flops 1048576 | bytes 3145728 | tf_op jit(solution)/shard_map/finish/pallas_call | solution.py:686
  (98 shorter events, 10.8 us)
Async XLA Ops:
  2.4 71.8 %collective-permute-start = (bf16[3,128,128]{2,1,0:T(8,128)(2,1)}, bf16[3,128,128]{2,1,0:T(8,128)(2,1)}, u32[]{:S(2)}, u32[]{:S(2)}) collective-permute-start(bf16[3,128,128]{2,1,0:T(8,128)(2,1)} %get-tuple-element.14), channel_id=1, source_target_pairs={{0,1},{1,2},{2,3},{3,4},{4,5},{5,6},{6,7},{7,8},{8,9},{9,10},{10,1... | collective-permute-start | bytes 294920 | tf_op jit(solution)/shard_map/ppermute | solution.py:28
  7.9 66.3 %collective-permute-start.1 = (bf16[3,128,128]{2,1,0:T(8,128)(2,1)}, bf16[3,128,128]{2,1,0:T(8,128)(2,1)}, u32[]{:S(2)}, u32[]{:S(2)}) collective-permute-start(bf16[3,128,128]{2,1,0:T(8,128)(2,1)} %get-tuple-element.15), channel_id=1, source_target_pairs={{1,0},{2,1},{3,2},{4,3},{5,4},{6,5},{7,6},{8,7},{9,8},{10,9},{11,1... | collective-permute-start | bytes 294920 | tf_op jit(solution)/shard_map/ppermute | solution.py:29
  14.0 6.5 %copy-start.12 = (s32[32,256]{1,0:T(8,128)S(1)}, s32[32,256]{1,0:T(8,128)}, u32[]{:S(2)}) copy-start(s32[32,256]{1,0:T(8,128)} %param.17) | copy-start | bytes 98308
  14.0 21.2 %copy-start.13 = (bf16[3,3,3,32,2]{3,4,2,1,0:T(2,128)(2,1)S(1)}, bf16[3,3,3,32,2]{3,4,2,1,0:T(2,128)(2,1)}, u32[]{:S(2)}) copy-start(bf16[3,3,3,32,2]{3,4,2,1,0:T(2,128)(2,1)} %param.18) | copy-start | bytes 10372
  14.0 56.6 %all-to-all-start = ((bf16[32,2,2,64,128]{4,3,2,1,0:T(8,128)(2,1)}), bf16[32,2,2,64,128]{4,3,2,1,0:T(8,128)(2,1)}, u32[]{:S(2)}, u32[]{:S(2)}) async-start(bf16[32,2,2,64,128]{4,3,2,1,0:T(8,128)(2,1)} %copy.37), calls=%async_computation | async-start | bytes 4194304 | tf_op jit(solution)/shard_map/all_to_all | solution.py:626
  20.5 16.5 %copy-start.14 = (bf16[3,3,3,2,32]{4,3,2,1,0:T(2,128)(2,1)S(1)}, bf16[3,3,3,2,32]{4,3,2,1,0:T(2,128)(2,1)}, u32[]{:S(2)}) copy-start(bf16[3,3,3,2,32]{4,3,2,1,0:T(2,128)(2,1)} %param.22) | copy-start | bytes 10372
  20.5 19.8 %copy-start.11 = (bf16[3,3,3,32,32]{4,3,2,1,0:T(8,128)(2,1)S(1)}, bf16[3,3,3,32,32]{4,3,2,1,0:T(8,128)(2,1)}, u32[]{:S(2)}) copy-start(bf16[3,3,3,32,32]{4,3,2,1,0:T(8,128)(2,1)} %param.20) | copy-start | bytes 165892
  40.5 1.7 copy-start.15
  40.5 1.8 copy-start.16
  40.5 1.9 copy-start.17
  47.5 1.1 copy-start.7
  48.7 4.1 %copy-start.8 = (bf16[32,1152]{1,0:T(8,128)(2,1)S(1)}, bf16[32,1152]{1,0:T(8,128)(2,1)}, u32[]{:S(2)}) copy-start(bf16[32,1152]{1,0:T(8,128)(2,1)} %broadcast_in_dim.198) | copy-start | bytes 221188
  48.7 4.1 %copy-start.9 = (bf16[32,1152]{1,0:T(8,128)(2,1)S(1)}, bf16[32,1152]{1,0:T(8,128)(2,1)}, u32[]{:S(2)}) copy-start(bf16[32,1152]{1,0:T(8,128)(2,1)} %broadcast_in_dim.202) | copy-start | bytes 221188
  48.7 4.1 %copy-start.10 = (bf16[32,1152]{1,0:T(8,128)(2,1)S(1)}, bf16[32,1152]{1,0:T(8,128)(2,1)}, u32[]{:S(2)}) copy-start(bf16[32,1152]{1,0:T(8,128)(2,1)} %broadcast_in_dim.206) | copy-start | bytes 221188
  70.6 53.6 %all-to-all-start.1 = ((bf16[32,2,2,32,256]{4,3,2,1,0:T(8,128)(2,1)}), bf16[32,2,2,32,256]{4,3,2,1,0:T(8,128)(2,1)}, u32[]{:S(2)}, u32[]{:S(2)}) async-start(bf16[32,2,2,32,256]{4,3,2,1,0:T(8,128)(2,1)} %copy.39), calls=%async_computation.1 | async-start | bytes 4194304 | tf_op jit(solution)/shard_map/all_to_all | solution.py:626
  74.3 2.4 %copy-start = (bf16[64,32,1152]{2,1,0:T(8,128)(2,1)S(1)}, bf16[64,32,1152]{2,1,0:T(8,128)(2,1)}, u32[]{:S(2)}) copy-start(bf16[64,32,1152]{2,1,0:T(8,128)(2,1)} %select_select_fusion) | copy-start | bytes 14155780
  75.4 1.6 copy-start.2
  77.0 2.3 %copy-start.1 = (bf16[18,64,2048]{2,1,0:T(8,128)(2,1)S(1)}, bf16[18,64,2048]{2,1,0:T(8,128)(2,1)}, u32[]{:S(2)}) copy-start(bf16[18,64,2048]{2,1,0:T(8,128)(2,1)} %select_select_fusion.1) | copy-start | bytes 14155780
  124.1 22.0 %all-to-all-start.2 = ((f32[32,2,2,8,128]{4,3,2,1,0:T(8,128)}), f32[32,2,2,8,128]{4,3,2,1,0:T(8,128)S(1)}, u32[]{:S(2)}, u32[]{:S(2)}) async-start(f32[32,2,2,8,128]{4,3,2,1,0:T(8,128)} %denoise.1.denoised_ref), calls=%async_computation.2 | async-start | bytes 1048576 | tf_op jit(solution)/shard_map/all_to_all | solution.py:626
  130.0 1.3 copy-start.3
  131.3 17.4 %copy-start.4 = (bf16[256,512]{1,0:T(8,128)(2,1)S(1)}, bf16[256,512]{1,0:T(8,128)(2,1)}, u32[]{:S(2)}) copy-start(bf16[256,512]{1,0:T(8,128)(2,1)} %constant.67.clone.refs_1_) | copy-start | bytes 786436
  131.3 17.4 %copy-start.5 = (bf16[512,256]{1,0:T(8,128)(2,1)S(1)}, bf16[512,256]{1,0:T(8,128)(2,1)}, u32[]{:S(2)}) copy-start(bf16[512,256]{1,0:T(8,128)(2,1)} %constant.68.clone.refs_2_) | copy-start | bytes 786436
  131.3 17.4 %copy-start.6 = (f32[2,128,128]{2,1,0:T(8,128)S(1)}, f32[2,128,128]{2,1,0:T(8,128)}, u32[]{:S(2)}) copy-start(f32[2,128,128]{2,1,0:T(8,128)} %constant.69.clone.refs_3_) | copy-start | bytes 393220
  146.1 19.9 %all-to-all-start.3 = ((f32[32,2,2,8,128]{4,3,2,1,0:T(8,128)}), f32[32,2,2,8,128]{4,3,2,1,0:T(8,128)S(1)}, u32[]{:S(2)}, u32[]{:S(2)}) async-start(f32[32,2,2,8,128]{4,3,2,1,0:T(8,128)} %adjoint.1.adjoint_ref), calls=%async_computation.3 | async-start | bytes 1048576 | tf_op jit(solution)/shard_map/all_to_all | solution.py:626

commit v10 on v9

--- a/solution.py
+++ b/solution.py
@@ -425,7 +425,7 @@
     plane_table = jnp.concatenate([planes_ref[:half], planes_ref[half:], planes_ref[:half]], axis=0)
     turns = turns_ref[0], turns_ref[1]
     half = turns[0].shape[0]
-    masks = mask_ref[:half], mask_ref[half:]
+    masks = tuple(mask_ref[pl.ds(odd, half, stride=2), :] for odd in range(2))
     coils = list(range(maps_refs[0].shape[1]))
     fields = []
     for group in in_groups(coils, 4):
@@ -689,7 +689,7 @@
         out_specs=[vmem] * 2,
         out_shape=[jax.ShapeDtypeStruct(shape, jnp.float32)] * 2,
         scratch_shapes=[pltpu.VMEM((2 * blocks * x_count * rows, planes), jnp.float32)],
-        compiler_params=pltpu.CompilerParams(vmem_limit_bytes=12 * 1024 * 1024),
+        compiler_params=pltpu.CompilerParams(vmem_limit_bytes=32 * 1024 * 1024),
         cost_estimate=pl.CostEstimate(
             flops=8 * adjoint.size, bytes_accessed=24 * adjoint.size, transcendentals=0
         ),
@@ -719,13 +719,12 @@
     parts = devices if spread else coils
     x_count = readout // parts
     mask = lax.all_gather(sampling.astype(jnp.bfloat16), "slab", axis=0, tiled=True)
+    features, mask = lax.optimization_barrier(
+        (with_halo(prior_image.astype(jnp.bfloat16), 3), mask)
+    )
     mask = jnp.transpose(mask).astype(jnp.float32)
-    half_mask = jnp.concatenate([mask[::2], mask[1::2]], axis=0)
-    features, mask, half_mask = lax.optimization_barrier(
-        (with_halo(prior_image.astype(jnp.bfloat16), 3), mask, half_mask)
-    )
     row_count = mask.shape[0]
-    constants = [half_mask] + half_tables(row_count, planes)
+    constants = [mask] + half_tables(row_count, planes)
     constants = [jnp.asarray(value) for value in constants]
     adjoint_constants = [mask, jnp.asarray(dft_table(row_count, planes))]
 

time: 205 us -> 199 us (0.971)
  blocking collectives: 50.5 us -> 46.2 us
    all_gather x1, blocking collectives: 14.4 us -> 10.1 us  [body(): lax.all_gather(sampling.astype(jnp.bfloat16), 'slab', axis=0, tiled=True)]
    unnamed x38 -> x44, local copies, waits for them, and re-layouts: 11.5 us -> 11.2 us
  transfers between devices with their start and end apart: 6 -> 6, of which waited for: 2 -> 3; matrix products, arithmetic and copies ran while one was open for 14% -> 13% of each run, Pallas kernels for 34% -> 35%
where the time goes in v10:
time: 199 us; the launch traced here: 198 us
  Pallas kernels  71.6 us (36%)
  blocking collectives  46.2 us (23%)
  starting transfers between devices  24.7 us (12%)
  local copies, waits for them, and re-layouts  23.8 us (12%)
  waiting for transfers between devices  19.4 us (10%)
  other arithmetic  11.1 us (6%)
    pallas_call x1, Pallas kernels, denoise(): pl.pallas_call(functools.partial(denoise_kernel, group), in_specs=[pl.Blo...  44.8 us
    all_to_all x1, blocking collectives, exchange(): return lax.all_to_all(blocks, axis, split_axis=0, concat_axis=0, tiled=True)  36 us
    pallas_call x2, Pallas kernels, product_call(): pl.pallas_call(kernel, grid=(x_count, coils // held_coils(coils)), in_spe...  24.3 us
    all_to_all x4, waiting for transfers between devices, exchange(): return lax.all_to_all(blocks, axis, split_axis=0, concat_axis=0, tiled=True)  19.4 us
    all_to_all x4, starting transfers between devices, exchange(): return lax.all_to_all(blocks, axis, split_axis=0, concat_axis=0, tiled=True)  19.2 us
    unnamed x44, local copies, waits for them, and re-layouts  11.2 us
    all_gather x1, blocking collectives, body(): lax.all_gather(sampling.astype(jnp.bfloat16), 'slab', axis=0, tiled=True)  10.1 us
    select_n x3, other arithmetic, banded(): result = jnp.where(inner - outer + offset == tap, tiles[tap], result)  8.98 us
  transfers between devices with their start and end apart: 6, of which 3 were waited for; matrix products, arithmetic and copies ran while one was open for 13% of the time, Pallas kernels for 35%

profile of v10, /device:TPU:0, one launch (start us, length us, event | category | flops | bytes accessed | tf_op | source)
XLA Modules:
  0.0 197.8 jit_solution(2583126591130773598)
XLA Ops:
  0.6 3.3 %copy.36 = bf16[1,64,128,128]{2,1,3,0:T(8,128)(2,1)S(1)} copy(bf16[1,64,128,128]{3,2,1,0:T(8,128)(2,1)} %param.15) | data formatting | bytes 4194304 | tf_op args[1]
  3.9 1.6 copy.37
  5.5 7.4 %all-to-all-start = ((bf16[32,2,2,64,128]{4,3,2,1,0:T(8,128)(2,1)}), bf16[32,2,2,64,128]{4,3,2,1,0:T(8,128)(2,1)}, u32[]{:S(2)}, u32[]{:S(2)}) async-start(bf16[32,2,2,64,128]{4,3,2,1,0:T(8,128)(2,1)} %copy.37), calls=%async_computation | async-start | bytes 4194304 | tf_op jit(solution)/shard_map/all_to_all | solution.py:626
  13.7 4.2 %collective-permute-start = (bf16[3,128,128]{2,1,0:T(8,128)(2,1)}, bf16[3,128,128]{2,1,0:T(8,128)(2,1)}, u32[]{:S(2)}, u32[]{:S(2)}) collective-permute-start(bf16[3,128,128]{2,1,0:T(8,128)(2,1)} %get-tuple-element.12), channel_id=1, source_target_pairs={{0,1},{1,2},{2,3},{3,4},{4,5},{5,6},{6,7},{7,8},{8,9},{9,10},{10,1... | collective-permute-start | bytes 294920 | tf_op jit(solution)/shard_map/ppermute | solution.py:28
  18.0 1.3 collective-permute-start.1
  26.6 1.0 broadcast_in_dim.193
  28.0 3.4 %copy.38 = bf16[1,32,256,128]{2,1,3,0:T(8,128)(2,1)S(1)} copy(bf16[1,32,256,128]{3,2,1,0:T(8,128)(2,1)} %param.16) | data formatting | bytes 4194304 | tf_op args[2]
  31.4 1.5 copy.39
  32.9 10.1 %all_gather.3 = bf16[128,256]{1,0:T(8,128)(2,1)} all-gather(bf16[32,256]{1,0:T(8,128)(2,1)S(1)} %convert_element_type.12), channel_id=1, replica_groups=mesh['slab'=4,'coil'=8] {'slab'}, dimensions={0}, use_global_device_ids=true | all-gather | bytes 81920 | tf_op jit(solution)/shard_map/all_gather | solution.py:721
  44.2 4.1 %select_select_fusion.1 = bf16[18,64,2048]{2,1,0:T(8,128)(2,1)} fusion(pred[64,2048]{1,0:T(8,128)(4,1)S(1)} %get-tuple-element.27, pred[64,2048]{1,0:T(8,128)(4,1)S(1)} %get-tuple-element.28, pred[64,2048]{1,0:T(8,128)(4,1)S(1)} %get-tuple-element.26, bf16[18,2048]{1,0:T(8,128)(2,1)S(1)} %copy-done.10, bf16[18,2048]{1,0:T(8,128)(2,1)S(1)} %copy-done.9, ...), kind=kLoop, calls=%fused_computation.1 | loop fusion | flops 7077888 | bytes 5332992 | tf_op jit(solution)/shard_map/jit(_where)/select_n | solution.py:162
  48.3 4.3 %select_select_fusion = bf16[64,32,1152]{2,1,0:T(8,128)(2,1)} fusion(pred[64,1152]{1,0:T(8,128)(4,1)S(1)} %get-tuple-element.24, pred[64,1152]{1,0:T(8,128)(4,1)S(1)} %get-tuple-element.25, pred[64,1152]{1,0:T(8,128)(4,1)S(1)} %get-tuple-element.23, bf16[32,1152]{1,0:T(8,128)(2,1)S(1)} %copy-done.12, bf16[32,1152]{1,0:T(8,128)(2,1)S(1)} %copy-done.11, ...), kind=kLoop, calls=%fused_computation | loop fusion | flops 7077888 | bytes 5160960 | tf_op jit(solution)/shard_map/jit(_where)/select_n | solution.py:162
  52.7 11.4 %all-to-all-done = bf16[32,2,2,64,128]{4,3,2,1,0:T(8,128)(2,1)} async-done(((bf16[32,2,2,64,128]{4,3,2,1,0:T(8,128)(2,1)}), bf16[32,2,2,64,128]{4,3,2,1,0:T(8,128)(2,1)}, u32[]{:S(2)}, u32[]{:S(2)}) %all-to-all-start) | async-done | bytes 2097184 | tf_op jit(solution)/shard_map/all_to_all | solution.py:626
  64.0 3.7 %all-to-all-start.1 = ((bf16[32,2,2,32,256]{4,3,2,1,0:T(8,128)(2,1)}), bf16[32,2,2,32,256]{4,3,2,1,0:T(8,128)(2,1)}, u32[]{:S(2)}, u32[]{:S(2)}) async-start(bf16[32,2,2,32,256]{4,3,2,1,0:T(8,128)(2,1)} %copy.39), calls=%async_computation.1 | async-start | bytes 4194304 | tf_op jit(solution)/shard_map/all_to_all | solution.py:626
  67.8 1.1 pad_maximum_fusion
  70.2 2.3 %copy-done.1 = bf16[18,64,2048]{2,1,0:T(8,128)(2,1)S(1)} copy-done((bf16[18,64,2048]{2,1,0:T(8,128)(2,1)S(1)}, bf16[18,64,2048]{2,1,0:T(8,128)(2,1)}, u32[]{:S(2)}) %copy-start.1) | copy-done | bytes 4718616
  72.5 44.8 %denoise.1.denoised_ref = f32[32,2,2,8,128]{4,3,2,1,0:T(8,128)} custom-call(s32[2]{0:T(128)S(1)} %pad_add_fusion.first_ref, bf16[14,128,384]{2,1,0:T(8,128)(2,1)S(1)} %fusion.2.features_ref, f32[8,128,128]{2,1,0:T(8,128)S(1)} %copy-done.2, bf16[1152,2048]{1,0:T(8,128)(2,1)S(1)} %bitcast.42, f32[1,2048]{1,0:T(1,128)S(1)} %broadcast_in_dim_tile.8.bias_first_ref, ...), custom_call_target="tpu_custom_call" | custom-call | flops 37446746112 | bytes 16777216 | tf_op jit(solution)/shard_map/denoise/pallas_call | solution.py:236
  117.6 5.5 %all-to-all-start.2 = ((f32[32,2,2,8,128]{4,3,2,1,0:T(8,128)}), f32[32,2,2,8,128]{4,3,2,1,0:T(8,128)S(1)}, u32[]{:S(2)}, u32[]{:S(2)}) async-start(f32[32,2,2,8,128]{4,3,2,1,0:T(8,128)} %denoise.1.denoised_ref), calls=%async_computation.2 | async-start | bytes 1048576 | tf_op jit(solution)/shard_map/all_to_all | solution.py:626
  123.3 1.3 copy-done.3
  124.6 7.0 %adjoint.1.adjoint_ref = f32[32,2,2,8,128]{4,3,2,1,0:T(8,128)} custom-call(bf16[4,8,4,32,256]{4,3,2,1,0:T(8,128)(2,1)} %bitcast.5.spectra_real_ref.spectra_imag_ref, bf16[4,8,4,32,256]{4,3,2,1,0:T(8,128)(2,1)} %bitcast.5.spectra_real_ref.spectra_imag_ref, bf16[4,8,4,64,128]{4,3,2,1,0:T(8,128)(2,1)} %bitcast.2.maps_real_ref.maps_imag_ref, ...), custom_call_target="tpu_custom_call" | custom-call | flops 4831838208 | bytes 8388608 | tf_op jit(solution)/shard_map/adjoint/pallas_call | solution.py:583
  131.6 7.7 %all-to-all-done.2.denoised_ref = f32[32,2,2,8,128]{4,3,2,1,0:T(8,128)S(1)} async-done(((f32[32,2,2,8,128]{4,3,2,1,0:T(8,128)}), f32[32,2,2,8,128]{4,3,2,1,0:T(8,128)S(1)}, u32[]{:S(2)}, u32[]{:S(2)}) %all-to-all-start.2) | async-done | bytes 524320 | tf_op jit(solution)/shard_map/all_to_all | solution.py:626
  139.3 2.6 %all-to-all-start.3 = ((f32[32,2,2,8,128]{4,3,2,1,0:T(8,128)}), f32[32,2,2,8,128]{4,3,2,1,0:T(8,128)S(1)}, u32[]{:S(2)}, u32[]{:S(2)}) async-start(f32[32,2,2,8,128]{4,3,2,1,0:T(8,128)} %adjoint.1.adjoint_ref), calls=%async_computation.3 | async-start | bytes 1048576 | tf_op jit(solution)/shard_map/all_to_all | solution.py:626
  141.9 17.3 %products.1 = f32[32,9,8,128]{3,2,1,0:T(8,128)S(1)} custom-call(bf16[4,8,4,64,128]{4,3,2,1,0:T(8,128)(2,1)} %bitcast.2.maps_real_ref.maps_imag_ref, bf16[4,8,4,64,128]{4,3,2,1,0:T(8,128)(2,1)} %bitcast.2.maps_real_ref.maps_imag_ref, f32[32,2,2,8,128]{4,3,2,1,0:T(8,128)} %adjoint.1.adjoint_ref, f32[32,2,2,8,128]{4,3,2,1,0:T(8,128)S(1)} %all-to-all-done.2.denoised_ref, ...), custom_call_target="tpu_custom_call" | custom-call | flops 19327352832 | bytes 8388608 | tf_op jit(solution)/shard_map/products/pallas_call | solution.py:583
  159.2 36.0 %all_to_all.25.moved_ref = f32[32,9,8,128]{3,2,1,0:T(8,128)S(1)} all-to-all(f32[32,9,8,128]{3,2,1,0:T(8,128)S(1)} %products.1), channel_id=1, replica_groups=mesh['slab'=4,'coil'=8] {'slab','coil'}, dimensions={0} | all-to-all | bytes 2359296 | tf_op jit(solution)/shard_map/all_to_all | solution.py:626
  195.3 2.5 %finish.1 = (f32[8,128,128]{2,1,0:T(8,128)}, f32[8,128,128]{2,1,0:T(8,128)}) custom-call(f32[32,2,2,8,128]{4,3,2,1,0:T(8,128)S(1)} %all-to-all-done.3.adjoint_ref, f32[32,2,2,8,128]{4,3,2,1,0:T(8,128)} %denoise.1.denoised_ref, f32[32,9,8,128]{3,2,1,0:T(8,128)S(1)} %all_to_all.25.moved_ref), custom_call_target="tpu_custom_call" | custom-call | flops 1048576 | bytes 3145728 | tf_op jit(solution)/shard_map/finish/pallas_call | solution.py:686
  (101 shorter events, 11.2 us)
Async XLA Ops:
  5.5 7.4 %copy-start.2 = (f32[8,128,128]{2,1,0:T(8,128)S(1)}, f32[8,128,128]{2,1,0:T(8,128)}, u32[]{:S(2)}) copy-start(f32[8,128,128]{2,1,0:T(8,128)} %prior_ref.1) | copy-start | bytes 1572868
  5.5 13.7 %copy-start.15 = (s32[32,256]{1,0:T(8,128)S(1)}, s32[32,256]{1,0:T(8,128)}, u32[]{:S(2)}) copy-start(s32[32,256]{1,0:T(8,128)} %param.17) | copy-start | bytes 98308
  5.5 13.8 %copy-start.16 = (bf16[3,3,3,32,2]{3,4,2,1,0:T(2,128)(2,1)S(1)}, bf16[3,3,3,32,2]{3,4,2,1,0:T(2,128)(2,1)}, u32[]{:S(2)}) copy-start(bf16[3,3,3,32,2]{3,4,2,1,0:T(2,128)(2,1)} %param.18) | copy-start | bytes 10372
  5.5 58.5 %all-to-all-start = ((bf16[32,2,2,64,128]{4,3,2,1,0:T(8,128)(2,1)}), bf16[32,2,2,64,128]{4,3,2,1,0:T(8,128)(2,1)}, u32[]{:S(2)}, u32[]{:S(2)}) async-start(bf16[32,2,2,64,128]{4,3,2,1,0:T(8,128)(2,1)} %copy.37), calls=%async_computation | async-start | bytes 4194304 | tf_op jit(solution)/shard_map/all_to_all | solution.py:626
  13.0 9.4 %copy-start.17 = (bf16[3,3,3,2,32]{4,3,2,1,0:T(2,128)(2,1)S(1)}, bf16[3,3,3,2,32]{4,3,2,1,0:T(2,128)(2,1)}, u32[]{:S(2)}) copy-start(bf16[3,3,3,2,32]{4,3,2,1,0:T(2,128)(2,1)} %param.22) | copy-start | bytes 10372
  13.0 12.1 %copy-start.14 = (bf16[3,3,3,32,32]{4,3,2,1,0:T(8,128)(2,1)S(1)}, bf16[3,3,3,32,32]{4,3,2,1,0:T(8,128)(2,1)}, u32[]{:S(2)}) copy-start(bf16[3,3,3,32,32]{4,3,2,1,0:T(8,128)(2,1)} %param.20) | copy-start | bytes 165892
  13.7 54.0 %collective-permute-start = (bf16[3,128,128]{2,1,0:T(8,128)(2,1)}, bf16[3,128,128]{2,1,0:T(8,128)(2,1)}, u32[]{:S(2)}, u32[]{:S(2)}) collective-permute-start(bf16[3,128,128]{2,1,0:T(8,128)(2,1)} %get-tuple-element.12), channel_id=1, source_target_pairs={{0,1},{1,2},{2,3},{3,4},{4,5},{5,6},{6,7},{7,8},{8,9},{9,10},{10,1... | collective-permute-start | bytes 294920 | tf_op jit(solution)/shard_map/ppermute | solution.py:28
  18.0 49.8 %collective-permute-start.1 = (bf16[3,128,128]{2,1,0:T(8,128)(2,1)}, bf16[3,128,128]{2,1,0:T(8,128)(2,1)}, u32[]{:S(2)}, u32[]{:S(2)}) collective-permute-start(bf16[3,128,128]{2,1,0:T(8,128)(2,1)} %get-tuple-element.13), channel_id=1, source_target_pairs={{1,0},{2,1},{3,2},{4,3},{5,4},{6,5},{7,6},{8,7},{9,8},{10,9},{11,1... | collective-permute-start | bytes 294920 | tf_op jit(solution)/shard_map/ppermute | solution.py:29
  25.3 2.4 %copy-start.19 = (f32[32]{0:T(128)S(1)}, f32[32]{0:T(128)}, u32[]{:S(2)}) copy-start(f32[32]{0:T(128)} %param.21) | copy-start | bytes 388
  25.3 2.5 %copy-start.20 = (f32[2]{0:T(128)S(1)}, f32[2]{0:T(128)}, u32[]{:S(2)}) copy-start(f32[2]{0:T(128)} %param.23) | copy-start | bytes 28
  31.4 11.7 %copy-start.7 = (bf16[3,32,768]{2,1,0:T(8,128)(2,1)S(1)}, bf16[3,32,768]{2,1,0:T(8,128)(2,1)}, u32[]{:S(2)}) copy-start(bf16[3,32,768]{2,1,0:T(8,128)(2,1)} %broadcast_in_dim.193) | copy-start | bytes 442372
  32.9 11.3 %copy-start.8 = (bf16[18,2048]{1,0:T(8,128)(2,1)S(1)}, bf16[18,2048]{1,0:T(8,128)(2,1)}, u32[]{:S(2)}) copy-start(bf16[18,2048]{1,0:T(8,128)(2,1)} %broadcast_in_dim.172) | copy-start | bytes 221188
  32.9 11.3 %copy-start.9 = (bf16[18,2048]{1,0:T(8,128)(2,1)S(1)}, bf16[18,2048]{1,0:T(8,128)(2,1)}, u32[]{:S(2)}) copy-start(bf16[18,2048]{1,0:T(8,128)(2,1)} %broadcast_in_dim.176) | copy-start | bytes 221188
  32.9 11.3 %copy-start.10 = (bf16[18,2048]{1,0:T(8,128)(2,1)S(1)}, bf16[18,2048]{1,0:T(8,128)(2,1)}, u32[]{:S(2)}) copy-start(bf16[18,2048]{1,0:T(8,128)(2,1)} %broadcast_in_dim.180) | copy-start | bytes 221188
  44.2 4.2 %copy-start.11 = (bf16[32,1152]{1,0:T(8,128)(2,1)S(1)}, bf16[32,1152]{1,0:T(8,128)(2,1)}, u32[]{:S(2)}) copy-start(bf16[32,1152]{1,0:T(8,128)(2,1)} %broadcast_in_dim.202) | copy-start | bytes 221188
  44.2 4.1 %copy-start.12 = (bf16[32,1152]{1,0:T(8,128)(2,1)S(1)}, bf16[32,1152]{1,0:T(8,128)(2,1)}, u32[]{:S(2)}) copy-start(bf16[32,1152]{1,0:T(8,128)(2,1)} %broadcast_in_dim.206) | copy-start | bytes 221188
  64.0 53.6 %all-to-all-start.1 = ((bf16[32,2,2,32,256]{4,3,2,1,0:T(8,128)(2,1)}), bf16[32,2,2,32,256]{4,3,2,1,0:T(8,128)(2,1)}, u32[]{:S(2)}, u32[]{:S(2)}) async-start(bf16[32,2,2,32,256]{4,3,2,1,0:T(8,128)(2,1)} %copy.39), calls=%async_computation.1 | async-start | bytes 4194304 | tf_op jit(solution)/shard_map/all_to_all | solution.py:626
  67.8 2.4 %copy-start = (bf16[64,32,1152]{2,1,0:T(8,128)(2,1)S(1)}, bf16[64,32,1152]{2,1,0:T(8,128)(2,1)}, u32[]{:S(2)}) copy-start(bf16[64,32,1152]{2,1,0:T(8,128)(2,1)} %select_select_fusion) | copy-start | bytes 14155780
  72.5 50.6 %copy-start.13 = (bf16[128,256]{1,0:T(8,128)(2,1)S(1)}, bf16[128,256]{1,0:T(8,128)(2,1)}, u32[]{:S(2)}) copy-start(bf16[128,256]{1,0:T(8,128)(2,1)} %all_gather.3) | copy-start | bytes 196612
  117.6 21.6 %all-to-all-start.2 = ((f32[32,2,2,8,128]{4,3,2,1,0:T(8,128)}), f32[32,2,2,8,128]{4,3,2,1,0:T(8,128)S(1)}, u32[]{:S(2)}, u32[]{:S(2)}) async-start(f32[32,2,2,8,128]{4,3,2,1,0:T(8,128)} %denoise.1.denoised_ref), calls=%async_computation.2 | async-start | bytes 1048576 | tf_op jit(solution)/shard_map/all_to_all | solution.py:626
  124.6 17.3 %copy-start.4 = (bf16[256,512]{1,0:T(8,128)(2,1)S(1)}, bf16[256,512]{1,0:T(8,128)(2,1)}, u32[]{:S(2)}) copy-start(bf16[256,512]{1,0:T(8,128)(2,1)} %constant.67.clone.refs_1_) | copy-start | bytes 786436
  124.6 17.3 %copy-start.5 = (bf16[512,256]{1,0:T(8,128)(2,1)S(1)}, bf16[512,256]{1,0:T(8,128)(2,1)}, u32[]{:S(2)}) copy-start(bf16[512,256]{1,0:T(8,128)(2,1)} %constant.68.clone.refs_2_) | copy-start | bytes 786436
  124.6 17.3 %copy-start.6 = (f32[2,128,128]{2,1,0:T(8,128)S(1)}, f32[2,128,128]{2,1,0:T(8,128)}, u32[]{:S(2)}) copy-start(f32[2,128,128]{2,1,0:T(8,128)} %constant.69.clone.refs_3_) | copy-start | bytes 393220
  139.3 20.0 %all-to-all-start.3 = ((f32[32,2,2,8,128]{4,3,2,1,0:T(8,128)}), f32[32,2,2,8,128]{4,3,2,1,0:T(8,128)S(1)}, u32[]{:S(2)}, u32[]{:S(2)}) async-start(f32[32,2,2,8,128]{4,3,2,1,0:T(8,128)} %adjoint.1.adjoint_ref), calls=%async_computation.3 | async-start | bytes 1048576 | tf_op jit(solution)/shard_map/all_to_all | solution.py:626
  (3 other events, 6.0 us)

commit v11 on v10

--- a/solution.py
+++ b/solution.py
@@ -514,7 +514,7 @@
 
 
 def twice_kernel(maps_real_ref, maps_imag_ref, adjoint_ref, denoised_ref, *refs):
-    constants, out_ref = refs[:-1], refs[-1]
+    constants, (out_ref, total_ref) = refs[:-2], refs[-2:]
     maps_refs = maps_real_ref, maps_imag_ref
     x_index = pl.program_id(0)
     x_count = pl.num_programs(0)
@@ -534,18 +534,18 @@
             lane_sums(rights, fields),
             lane_sums(fields, fields),
             lane_sums(fields, images),
-            jnp.zeros((block_rows - 4, planes), jnp.float32),
+            jnp.zeros((total_ref.shape[0] - 4, planes), jnp.float32),
         ],
         axis=0,
-    )[None]
+    )
 
     @pl.when(x_index == 0)
     def _():
-        out_ref[:, 4 * x_count] = jnp.broadcast_to(totals, shape)
+        total_ref[...] = totals
 
     @pl.when(x_index > 0)
     def _():
-        out_ref[:, 4 * x_count] += totals
+        total_ref[...] += totals
 
 
 def held_coils(count):
@@ -615,11 +615,11 @@
 
 def twice_call(maps, adjoint, denoised, constants):
     blocks, _, x_count, block_rows, planes = adjoint.shape
-    shape = (blocks, 4 * x_count + 1, block_rows, planes)
-    outs = [(whole(shape), shape)]
+    shape = (blocks, 4 * x_count, block_rows, planes)
+    outs = [(whole(shape), shape), (whole((8, planes)), (8, planes))]
     return product_call(
         twice_kernel, "products", x_count, maps, [adjoint, denoised], [], constants, outs, 12
-    )[0]
+    )
 
 
 def exchange(blocks, axis):
@@ -655,11 +655,12 @@
 
 
 def finish_kernel(
-    adjoint_ref, denoised_ref, moved_ref, solution_ref, residual_ref, rows_ref
+    adjoint_ref, denoised_ref, moved_ref, totals_ref, solution_ref, residual_ref, rows_ref
 ):
     blocks, _, x_count, rows, planes = adjoint_ref.shape
     readout = blocks * x_count
-    totals = jnp.sum(jnp.sum(moved_ref[:, 4 * x_count], axis=0), axis=1, keepdims=True)
+    totals = totals_ref[...].reshape(-1, 8, planes)
+    totals = jnp.sum(jnp.sum(totals, axis=0), axis=1, keepdims=True)
     found = factors(*(totals[index : index + 1] for index in range(4)))
     for out_ref, scales in zip((solution_ref, residual_ref), found):
         scales = [jnp.broadcast_to(scale, (rows, planes))[None] for scale in scales]
@@ -679,13 +680,13 @@
             out_ref[row] = jnp.transpose(rows_ref[pl.ds(row, 2 * readout, stride=rows), :])
 
 
-def finish_call(adjoint, denoised, moved):
+def finish_call(adjoint, denoised, moved, totals):
     blocks, _, x_count, rows, planes = adjoint.shape
     shape = (rows, planes, 2 * blocks * x_count)
     vmem = pl.BlockSpec(memory_space=pltpu.VMEM)
     return pl.pallas_call(
         finish_kernel,
-        in_specs=[vmem] * 3,
+        in_specs=[vmem] * 4,
         out_specs=[vmem] * 2,
         out_shape=[jax.ShapeDtypeStruct(shape, jnp.float32)] * 2,
         scratch_shapes=[pltpu.VMEM((2 * blocks * x_count * rows, planes), jnp.float32)],
@@ -694,7 +695,7 @@
             flops=8 * adjoint.size, bytes_accessed=24 * adjoint.size, transcendentals=0
         ),
         name="finish",
-    )(adjoint, denoised, moved)
+    )(adjoint, denoised, moved, totals)
 
 
 def body(
@@ -755,14 +756,16 @@
         blocks = x_first(blocks, parts)
     if spread:
         adjoint = adjoint_call(spectra, maps, adjoint_constants, x_count, devices)
-        payload, adjoint_back = lax.optimization_barrier(
+        (payload, totals), adjoint_back = lax.optimization_barrier(
             (
                 twice_call(maps, adjoint, exchange(blocks, axes), constants),
                 exchange(adjoint, axes),
             )
         )
-        payload = exchange(payload, axes)
-        return tuple(finish_call(adjoint_back, blocks, payload))
+        moved = exchange(payload, axes)
+        for axis in axes:
+            totals = lax.all_gather(totals, axis, axis=0, tiled=True)
+        return tuple(finish_call(adjoint_back, blocks, moved, totals))
 
     tail = blocks.shape[1:3]
 

time: 199 us -> 216 us (1.085)
  blocking collectives: 46.2 us -> 56.6 us
  starting transfers between devices: 24.7 us -> 30.5 us
    all_gather x0 -> x2, blocking collectives: none -> 46.4 us  [body(): totals = lax.all_gather(totals, axis, axis=0, tiled=True)]
    all_to_all x1 -> x0, blocking collectives: 36 us -> none  [exchange(): return lax.all_to_all(blocks, axis, split_axis=0, concat_axis=0, tiled=True)]
    all_to_all x4 -> x5, starting transfers between devices: 19.2 us -> 25 us  [exchange(): return lax.all_to_all(blocks, axis, split_axis=0, concat_axis=0, tiled=True)]
    all_to_all x4 -> x5, waiting for transfers between devices: 19.4 us -> 19.4 us  [exchange(): return lax.all_to_all(blocks, axis, split_axis=0, concat_axis=0, tiled=True)]
  transfers between devices with their start and end apart: 6 -> 7, of which waited for: 3 -> 3; matrix products, arithmetic and copies ran while one was open for 13% -> 12% of each run, Pallas kernels for 35% -> 33%
where the time goes in v11:
time: 216 us
  Pallas kernels  73.3 us (34%)
  blocking collectives  56.6 us (26%)
  starting transfers between devices  30.5 us (14%)
  local copies, waits for them, and re-layouts  23.7 us (11%)
  waiting for transfers between devices  19.4 us (9%)
  other arithmetic  11 us (5%)
    all_gather x2, blocking collectives, body(): totals = lax.all_gather(totals, axis, axis=0, tiled=True)  46.4 us
    pallas_call x1, Pallas kernels, denoise(): pl.pallas_call(functools.partial(denoise_kernel, group), in_specs=[pl.Blo...  44.8 us
    pallas_call x2, Pallas kernels, product_call(): pl.pallas_call(kernel, grid=(x_count, coils // held_coils(coils)), in_spe...  25.9 us
    all_to_all x5, starting transfers between devices, exchange(): return lax.all_to_all(blocks, axis, split_axis=0, concat_axis=0, tiled=True)  25 us
    all_to_all x5, waiting for transfers between devices, exchange(): return lax.all_to_all(blocks, axis, split_axis=0, concat_axis=0, tiled=True)  19.4 us
    unnamed x44, local copies, waits for them, and re-layouts  11.2 us
    all_gather x1, blocking collectives, body(): lax.all_gather(sampling.astype(jnp.bfloat16), 'slab', axis=0, tiled=True)  10.2 us
    select_n x3, other arithmetic, banded(): result = jnp.where(inner - outer + offset == tap, tiles[tap], result)  8.95 us
  transfers between devices with their start and end apart: 7, of which 3 were waited for; matrix products, arithmetic and copies ran while one was open for 12% of the time, Pallas kernels for 33%

profile of v11, /device:TPU:0, one launch (start us, length us, event | category | flops | bytes accessed | tf_op | source)
XLA Modules:
  0.0 215.6 jit_solution(14003366465877223996)
XLA Ops:
  0.6 3.3 %copy.36 = bf16[1,64,128,128]{2,1,3,0:T(8,128)(2,1)S(1)} copy(bf16[1,64,128,128]{3,2,1,0:T(8,128)(2,1)} %param.15) | data formatting | bytes 4194304 | tf_op args[1]
  3.9 1.5 copy.37
  5.5 7.4 %all-to-all-start = ((bf16[32,2,2,64,128]{4,3,2,1,0:T(8,128)(2,1)}), bf16[32,2,2,64,128]{4,3,2,1,0:T(8,128)(2,1)}, u32[]{:S(2)}, u32[]{:S(2)}) async-start(bf16[32,2,2,64,128]{4,3,2,1,0:T(8,128)(2,1)} %copy.37), calls=%async_computation | async-start | bytes 4194304 | tf_op jit(solution)/shard_map/all_to_all | solution.py:626
  13.7 4.2 %collective-permute-start = (bf16[3,128,128]{2,1,0:T(8,128)(2,1)}, bf16[3,128,128]{2,1,0:T(8,128)(2,1)}, u32[]{:S(2)}, u32[]{:S(2)}) collective-permute-start(bf16[3,128,128]{2,1,0:T(8,128)(2,1)} %get-tuple-element.18), channel_id=1, source_target_pairs={{0,1},{1,2},{2,3},{3,4},{4,5},{5,6},{6,7},{7,8},{8,9},{9,10},{10,1... | collective-permute-start | bytes 294920 | tf_op jit(solution)/shard_map/ppermute | solution.py:28
  17.9 1.3 collective-permute-start.1
  27.9 3.4 %copy.38 = bf16[1,32,256,128]{2,1,3,0:T(8,128)(2,1)S(1)} copy(bf16[1,32,256,128]{3,2,1,0:T(8,128)(2,1)} %param.16) | data formatting | bytes 4194304 | tf_op args[2]
  31.3 1.5 copy.39
  32.8 10.2 %all_gather.9 = bf16[128,256]{1,0:T(8,128)(2,1)} all-gather(bf16[32,256]{1,0:T(8,128)(2,1)S(1)} %convert_element_type.12), channel_id=1, replica_groups=mesh['slab'=4,'coil'=8] {'slab'}, dimensions={0}, use_global_device_ids=true | all-gather | bytes 81920 | tf_op jit(solution)/shard_map/all_gather | solution.py:722
  44.2 4.1 %select_select_fusion.1 = bf16[18,64,2048]{2,1,0:T(8,128)(2,1)} fusion(pred[64,2048]{1,0:T(8,128)(4,1)S(1)} %get-tuple-element.33, pred[64,2048]{1,0:T(8,128)(4,1)S(1)} %get-tuple-element.34, pred[64,2048]{1,0:T(8,128)(4,1)S(1)} %get-tuple-element.32, bf16[18,2048]{1,0:T(8,128)(2,1)S(1)} %copy-done.10, bf16[18,2048]{1,0:T(8,128)(2,1)S(1)} %copy-done.9, ...), kind=kLoop, calls=%fused_computation.1 | loop fusion | flops 7077888 | bytes 5332992 | tf_op jit(solution)/shard_map/jit(_where)/select_n | solution.py:162
  48.3 4.2 %select_select_fusion = bf16[64,32,1152]{2,1,0:T(8,128)(2,1)} fusion(pred[64,1152]{1,0:T(8,128)(4,1)S(1)} %get-tuple-element.30, pred[64,1152]{1,0:T(8,128)(4,1)S(1)} %get-tuple-element.31, pred[64,1152]{1,0:T(8,128)(4,1)S(1)} %get-tuple-element.29, bf16[32,1152]{1,0:T(8,128)(2,1)S(1)} %copy-done.12, bf16[32,1152]{1,0:T(8,128)(2,1)S(1)} %copy-done.11, ...), kind=kLoop, calls=%fused_computation | loop fusion | flops 7077888 | bytes 5160960 | tf_op jit(solution)/shard_map/jit(_where)/select_n | solution.py:162
  52.7 11.3 %all-to-all-done = bf16[32,2,2,64,128]{4,3,2,1,0:T(8,128)(2,1)} async-done(((bf16[32,2,2,64,128]{4,3,2,1,0:T(8,128)(2,1)}), bf16[32,2,2,64,128]{4,3,2,1,0:T(8,128)(2,1)}, u32[]{:S(2)}, u32[]{:S(2)}) %all-to-all-start) | async-done | bytes 2097184 | tf_op jit(solution)/shard_map/all_to_all | solution.py:626
  64.0 3.7 %all-to-all-start.1 = ((bf16[32,2,2,32,256]{4,3,2,1,0:T(8,128)(2,1)}), bf16[32,2,2,32,256]{4,3,2,1,0:T(8,128)(2,1)}, u32[]{:S(2)}, u32[]{:S(2)}) async-start(bf16[32,2,2,32,256]{4,3,2,1,0:T(8,128)(2,1)} %copy.39), calls=%async_computation.1 | async-start | bytes 4194304 | tf_op jit(solution)/shard_map/all_to_all | solution.py:626
  70.1 2.3 %copy-done.1 = bf16[18,64,2048]{2,1,0:T(8,128)(2,1)S(1)} copy-done((bf16[18,64,2048]{2,1,0:T(8,128)(2,1)S(1)}, bf16[18,64,2048]{2,1,0:T(8,128)(2,1)}, u32[]{:S(2)}) %copy-start.1) | copy-done | bytes 4718616
  72.5 44.8 %denoise.1.denoised_ref = f32[32,2,2,8,128]{4,3,2,1,0:T(8,128)} custom-call(s32[2]{0:T(128)S(1)} %pad_add_fusion.first_ref, bf16[14,128,384]{2,1,0:T(8,128)(2,1)S(1)} %fusion.2.features_ref, f32[8,128,128]{2,1,0:T(8,128)S(1)} %copy-done.2, bf16[1152,2048]{1,0:T(8,128)(2,1)S(1)} %bitcast.42, f32[1,2048]{1,0:T(1,128)S(1)} %broadcast_in_dim_tile.8.bias_first_ref, ...), custom_call_target="tpu_custom_call" | custom-call | flops 37446746112 | bytes 16777216 | tf_op jit(solution)/shard_map/denoise/pallas_call | solution.py:236
  117.6 5.5 %all-to-all-start.2 = ((f32[32,2,2,8,128]{4,3,2,1,0:T(8,128)}), f32[32,2,2,8,128]{4,3,2,1,0:T(8,128)S(1)}, u32[]{:S(2)}, u32[]{:S(2)}) async-start(f32[32,2,2,8,128]{4,3,2,1,0:T(8,128)} %denoise.1.denoised_ref), calls=%async_computation.2 | async-start | bytes 1048576 | tf_op jit(solution)/shard_map/all_to_all | solution.py:626
  123.2 1.3 copy-done.3
  124.5 7.0 %adjoint.1.adjoint_ref = f32[32,2,2,8,128]{4,3,2,1,0:T(8,128)} custom-call(bf16[4,8,4,32,256]{4,3,2,1,0:T(8,128)(2,1)} %bitcast.5.spectra_real_ref.spectra_imag_ref, bf16[4,8,4,32,256]{4,3,2,1,0:T(8,128)(2,1)} %bitcast.5.spectra_real_ref.spectra_imag_ref, bf16[4,8,4,64,128]{4,3,2,1,0:T(8,128)(2,1)} %bitcast.2.maps_real_ref.maps_imag_ref, ...), custom_call_target="tpu_custom_call" | custom-call | flops 4831838208 | bytes 8388608 | tf_op jit(solution)/shard_map/adjoint/pallas_call | solution.py:583
  131.5 7.7 %all-to-all-done.2.denoised_ref = f32[32,2,2,8,128]{4,3,2,1,0:T(8,128)S(1)} async-done(((f32[32,2,2,8,128]{4,3,2,1,0:T(8,128)}), f32[32,2,2,8,128]{4,3,2,1,0:T(8,128)S(1)}, u32[]{:S(2)}, u32[]{:S(2)}) %all-to-all-start.2) | async-done | bytes 524320 | tf_op jit(solution)/shard_map/all_to_all | solution.py:626
  139.2 2.6 %all-to-all-start.3 = ((f32[32,2,2,8,128]{4,3,2,1,0:T(8,128)}), f32[32,2,2,8,128]{4,3,2,1,0:T(8,128)S(1)}, u32[]{:S(2)}, u32[]{:S(2)}) async-start(f32[32,2,2,8,128]{4,3,2,1,0:T(8,128)} %adjoint.1.adjoint_ref), calls=%async_computation.3 | async-start | bytes 1048576 | tf_op jit(solution)/shard_map/all_to_all | solution.py:626
  141.8 18.9 %products.1 = (f32[32,8,8,128]{3,2,1,0:T(8,128)}, f32[8,128]{1,0:T(8,128)S(1)}) custom-call(bf16[4,8,4,64,128]{4,3,2,1,0:T(8,128)(2,1)} %bitcast.2.maps_real_ref.maps_imag_ref, bf16[4,8,4,64,128]{4,3,2,1,0:T(8,128)(2,1)} %bitcast.2.maps_real_ref.maps_imag_ref, f32[32,2,2,8,128]{4,3,2,1,0:T(8,128)} %adjoint.1.adjoint_ref, ...), custom_call_target="tpu_custom_call" | custom-call | flops 19327352832 | bytes 8388608 | tf_op jit(solution)/shard_map/products/pallas_call | solution.py:583
  160.7 5.8 %all-to-all-start.4 = ((f32[32,8,8,128]{3,2,1,0:T(8,128)}), f32[32,8,8,128]{3,2,1,0:T(8,128)S(1)}, u32[]{:S(2)}, u32[]{:S(2)}) async-start(f32[32,8,8,128]{3,2,1,0:T(8,128)} %get-tuple-element.14), calls=%async_computation.4 | async-start | bytes 2097152 | tf_op jit(solution)/shard_map/all_to_all | solution.py:626
  166.6 8.6 %all_gather.10 = f32[32,128]{1,0:T(8,128)S(1)} all-gather(f32[8,128]{1,0:T(8,128)S(1)} %get-tuple-element.15), channel_id=1, replica_groups=mesh['slab'=4,'coil'=8] {'slab'}, dimensions={0}, use_global_device_ids=true | all-gather | bytes 20480 | tf_op jit(solution)/shard_map/all_gather | solution.py:767
  175.2 37.8 %all_gather.11.totals_ref = f32[256,128]{1,0:T(8,128)S(1)} all-gather(f32[32,128]{1,0:T(8,128)S(1)} %all_gather.10), channel_id=1, replica_groups=mesh['slab'=4,'coil'=8] {'coil'}, dimensions={0}, use_global_device_ids=true | all-gather | bytes 147456 | tf_op jit(solution)/shard_map/all_gather | solution.py:767
  213.0 2.6 %finish.1 = (f32[8,128,128]{2,1,0:T(8,128)}, f32[8,128,128]{2,1,0:T(8,128)}) custom-call(f32[32,2,2,8,128]{4,3,2,1,0:T(8,128)S(1)} %all-to-all-done.3.adjoint_ref, f32[32,2,2,8,128]{4,3,2,1,0:T(8,128)} %denoise.1.denoised_ref, f32[32,8,8,128]{3,2,1,0:T(8,128)S(1)} %all-to-all-done.4.moved_ref, f32[256,128]{1,0:T(8,128)S(1)} %all_gather.11.totals_ref), custom_call_target="tpu_custom_call" | custom-call | flops 1048576 | bytes 3145728 | tf_op jit(solution)/shard_map/finish/pallas_call | solution.py:687
  (104 shorter events, 13.3 us)
Async XLA Ops:
  5.5 7.4 %copy-start.2 = (f32[8,128,128]{2,1,0:T(8,128)S(1)}, f32[8,128,128]{2,1,0:T(8,128)}, u32[]{:S(2)}) copy-start(f32[8,128,128]{2,1,0:T(8,128)} %prior_ref.1) | copy-start | bytes 1572868
  5.5 13.7 %copy-start.15 = (s32[32,256]{1,0:T(8,128)S(1)}, s32[32,256]{1,0:T(8,128)}, u32[]{:S(2)}) copy-start(s32[32,256]{1,0:T(8,128)} %param.17) | copy-start | bytes 98308
  5.5 13.7 %copy-start.16 = (bf16[3,3,3,32,2]{3,4,2,1,0:T(2,128)(2,1)S(1)}, bf16[3,3,3,32,2]{3,4,2,1,0:T(2,128)(2,1)}, u32[]{:S(2)}) copy-start(bf16[3,3,3,32,2]{3,4,2,1,0:T(2,128)(2,1)} %param.18) | copy-start | bytes 10372
  5.5 58.5 %all-to-all-start = ((bf16[32,2,2,64,128]{4,3,2,1,0:T(8,128)(2,1)}), bf16[32,2,2,64,128]{4,3,2,1,0:T(8,128)(2,1)}, u32[]{:S(2)}, u32[]{:S(2)}) async-start(bf16[32,2,2,64,128]{4,3,2,1,0:T(8,128)(2,1)} %copy.37), calls=%async_computation | async-start | bytes 4194304 | tf_op jit(solution)/shard_map/all_to_all | solution.py:626
  12.9 9.4 %copy-start.17 = (bf16[3,3,3,2,32]{4,3,2,1,0:T(2,128)(2,1)S(1)}, bf16[3,3,3,2,32]{4,3,2,1,0:T(2,128)(2,1)}, u32[]{:S(2)}) copy-start(bf16[3,3,3,2,32]{4,3,2,1,0:T(2,128)(2,1)} %param.22) | copy-start | bytes 10372
  12.9 12.1 %copy-start.14 = (bf16[3,3,3,32,32]{4,3,2,1,0:T(8,128)(2,1)S(1)}, bf16[3,3,3,32,32]{4,3,2,1,0:T(8,128)(2,1)}, u32[]{:S(2)}) copy-start(bf16[3,3,3,32,32]{4,3,2,1,0:T(8,128)(2,1)} %param.20) | copy-start | bytes 165892
  13.7 54.0 %collective-permute-start = (bf16[3,128,128]{2,1,0:T(8,128)(2,1)}, bf16[3,128,128]{2,1,0:T(8,128)(2,1)}, u32[]{:S(2)}, u32[]{:S(2)}) collective-permute-start(bf16[3,128,128]{2,1,0:T(8,128)(2,1)} %get-tuple-element.18), channel_id=1, source_target_pairs={{0,1},{1,2},{2,3},{3,4},{4,5},{5,6},{6,7},{7,8},{8,9},{9,10},{10,1... | collective-permute-start | bytes 294920 | tf_op jit(solution)/shard_map/ppermute | solution.py:28
  17.9 49.8 %collective-permute-start.1 = (bf16[3,128,128]{2,1,0:T(8,128)(2,1)}, bf16[3,128,128]{2,1,0:T(8,128)(2,1)}, u32[]{:S(2)}, u32[]{:S(2)}) collective-permute-start(bf16[3,128,128]{2,1,0:T(8,128)(2,1)} %get-tuple-element.19), channel_id=1, source_target_pairs={{1,0},{2,1},{3,2},{4,3},{5,4},{6,5},{7,6},{8,7},{9,8},{10,9},{11,1... | collective-permute-start | bytes 294920 | tf_op jit(solution)/shard_map/ppermute | solution.py:29
  25.2 2.4 %copy-start.19 = (f32[32]{0:T(128)S(1)}, f32[32]{0:T(128)}, u32[]{:S(2)}) copy-start(f32[32]{0:T(128)} %param.21) | copy-start | bytes 388
  25.2 2.5 %copy-start.20 = (f32[2]{0:T(128)S(1)}, f32[2]{0:T(128)}, u32[]{:S(2)}) copy-start(f32[2]{0:T(128)} %param.23) | copy-start | bytes 28
  31.3 11.8 %copy-start.7 = (bf16[3,32,768]{2,1,0:T(8,128)(2,1)S(1)}, bf16[3,32,768]{2,1,0:T(8,128)(2,1)}, u32[]{:S(2)}) copy-start(bf16[3,32,768]{2,1,0:T(8,128)(2,1)} %broadcast_in_dim.193) | copy-start | bytes 442372
  32.8 11.4 %copy-start.8 = (bf16[18,2048]{1,0:T(8,128)(2,1)S(1)}, bf16[18,2048]{1,0:T(8,128)(2,1)}, u32[]{:S(2)}) copy-start(bf16[18,2048]{1,0:T(8,128)(2,1)} %broadcast_in_dim.172) | copy-start | bytes 221188
  32.8 11.4 %copy-start.9 = (bf16[18,2048]{1,0:T(8,128)(2,1)S(1)}, bf16[18,2048]{1,0:T(8,128)(2,1)}, u32[]{:S(2)}) copy-start(bf16[18,2048]{1,0:T(8,128)(2,1)} %broadcast_in_dim.176) | copy-start | bytes 221188
  32.8 11.4 %copy-start.10 = (bf16[18,2048]{1,0:T(8,128)(2,1)S(1)}, bf16[18,2048]{1,0:T(8,128)(2,1)}, u32[]{:S(2)}) copy-start(bf16[18,2048]{1,0:T(8,128)(2,1)} %broadcast_in_dim.180) | copy-start | bytes 221188
  44.2 4.1 %copy-start.11 = (bf16[32,1152]{1,0:T(8,128)(2,1)S(1)}, bf16[32,1152]{1,0:T(8,128)(2,1)}, u32[]{:S(2)}) copy-start(bf16[32,1152]{1,0:T(8,128)(2,1)} %broadcast_in_dim.202) | copy-start | bytes 221188
  44.2 4.1 %copy-start.12 = (bf16[32,1152]{1,0:T(8,128)(2,1)S(1)}, bf16[32,1152]{1,0:T(8,128)(2,1)}, u32[]{:S(2)}) copy-start(bf16[32,1152]{1,0:T(8,128)(2,1)} %broadcast_in_dim.206) | copy-start | bytes 221188
  64.0 53.6 %all-to-all-start.1 = ((bf16[32,2,2,32,256]{4,3,2,1,0:T(8,128)(2,1)}), bf16[32,2,2,32,256]{4,3,2,1,0:T(8,128)(2,1)}, u32[]{:S(2)}, u32[]{:S(2)}) async-start(bf16[32,2,2,32,256]{4,3,2,1,0:T(8,128)(2,1)} %copy.39), calls=%async_computation.1 | async-start | bytes 4194304 | tf_op jit(solution)/shard_map/all_to_all | solution.py:626
  72.5 50.6 %copy-start.13 = (bf16[128,256]{1,0:T(8,128)(2,1)S(1)}, bf16[128,256]{1,0:T(8,128)(2,1)}, u32[]{:S(2)}) copy-start(bf16[128,256]{1,0:T(8,128)(2,1)} %all_gather.9) | copy-start | bytes 196612
  117.6 21.6 %all-to-all-start.2 = ((f32[32,2,2,8,128]{4,3,2,1,0:T(8,128)}), f32[32,2,2,8,128]{4,3,2,1,0:T(8,128)S(1)}, u32[]{:S(2)}, u32[]{:S(2)}) async-start(f32[32,2,2,8,128]{4,3,2,1,0:T(8,128)} %denoise.1.denoised_ref), calls=%async_computation.2 | async-start | bytes 1048576 | tf_op jit(solution)/shard_map/all_to_all | solution.py:626
  124.5 17.3 %copy-start.4 = (bf16[256,512]{1,0:T(8,128)(2,1)S(1)}, bf16[256,512]{1,0:T(8,128)(2,1)}, u32[]{:S(2)}) copy-start(bf16[256,512]{1,0:T(8,128)(2,1)} %constant.67.clone.refs_1_) | copy-start | bytes 786436
  124.5 17.3 %copy-start.5 = (bf16[512,256]{1,0:T(8,128)(2,1)S(1)}, bf16[512,256]{1,0:T(8,128)(2,1)}, u32[]{:S(2)}) copy-start(bf16[512,256]{1,0:T(8,128)(2,1)} %constant.68.clone.refs_2_) | copy-start | bytes 786436
  124.5 17.3 %copy-start.6 = (f32[2,128,128]{2,1,0:T(8,128)S(1)}, f32[2,128,128]{2,1,0:T(8,128)}, u32[]{:S(2)}) copy-start(f32[2,128,128]{2,1,0:T(8,128)} %constant.69.clone.refs_3_) | copy-start | bytes 393220
  139.2 21.5 %all-to-all-start.3 = ((f32[32,2,2,8,128]{4,3,2,1,0:T(8,128)}), f32[32,2,2,8,128]{4,3,2,1,0:T(8,128)S(1)}, u32[]{:S(2)}, u32[]{:S(2)}) async-start(f32[32,2,2,8,128]{4,3,2,1,0:T(8,128)} %adjoint.1.adjoint_ref), calls=%async_computation.3 | async-start | bytes 1048576 | tf_op jit(solution)/shard_map/all_to_all | solution.py:626
  160.7 52.2 %all-to-all-start.4 = ((f32[32,8,8,128]{3,2,1,0:T(8,128)}), f32[32,8,8,128]{3,2,1,0:T(8,128)S(1)}, u32[]{:S(2)}, u32[]{:S(2)}) async-start(f32[32,8,8,128]{3,2,1,0:T(8,128)} %get-tuple-element.14), calls=%async_computation.4 | async-start | bytes 2097152 | tf_op jit(solution)/shard_map/all_to_all | solution.py:626
  (4 other events, 8.5 us)

commit v12 on v10

--- a/solution.py
+++ b/solution.py
@@ -371,6 +371,17 @@
 
 def map_of(refs, coil):
     return [coil_plane(ref, coil).astype(jnp.float32) for ref in refs]
+
+
+def spectrum_plane(ref, coil, rows):
+    value = ref[:, coil, 0]
+    slabs, held, lanes = value.shape
+    planes = held * lanes // rows
+    pieces = [
+        value[:, first : first + planes].reshape(slabs * planes, lanes)
+        for first in range(0, held, planes)
+    ]
+    return jnp.concatenate(pieces, axis=1)
 
 
 def image_sums(maps, fields):
@@ -480,7 +491,7 @@
         spectra = []
         for coil in unit:
             real, imag = (
-                jnp.transpose(coil_plane(ref, coil).astype(jnp.float32))
+                jnp.transpose(spectrum_plane(ref, coil, rows).astype(jnp.float32))
                 for ref in (spectra_real_ref, spectra_imag_ref)
             )
             spectra.append((real * mask, imag * -mask))
@@ -622,6 +633,66 @@
     )[0]
 
 
+def pack_kernel(maps_ref, kspace_ref, prior_ref, order_ref, out_ref, features_ref, *rows_refs):
+    rows, planes, width = maps_ref.shape[1:]
+    parts, held = out_ref.shape[:2]
+    held = held // 2
+    for kind, (ref, rows_ref) in enumerate(zip((maps_ref, kspace_ref), rows_refs)):
+        for row in range(0, rows, 2):
+            moved = lax.dot_general(
+                order_ref[...],
+                ref[0, row : row + 2].reshape(2 * planes, width),
+                (((1,), (1,)), ((), ())),
+                preferred_element_type=jnp.float32,
+            )
+            for odd in range(2):
+                lanes = slice(odd * planes, (odd + 1) * planes)
+                rows_ref[pl.ds(row + odd, width, stride=rows), :] = moved[:, lanes]
+        for part in range(parts):
+            for inner in range(held):
+                place = (part * held + inner) * rows
+                out_ref[part, kind * held + inner] = rows_ref[place : place + rows].astype(
+                    out_ref.dtype
+                )
+    features_ref[...] = prior_ref[...].astype(features_ref.dtype)
+
+
+def pack_call(maps, kspace, prior, parts):
+    _, slab_rows, planes, width = maps.shape
+    slab_planes = kspace.shape[1]
+    chunk = 16
+    count = slab_rows // chunk
+    inside = slab_planes // chunk
+    held = width // parts
+    lanes = np.arange(width).reshape(2, parts, held // 2).transpose(1, 0, 2).reshape(-1)
+    order = (lanes[:, None] == np.arange(width)[None, :]).astype(jnp.bfloat16)
+    shape = (parts, 2 * held, slab_rows, planes)
+    return pl.pallas_call(
+        pack_kernel,
+        grid=(count,),
+        in_specs=[
+            pl.BlockSpec((1, chunk, planes, width), lambda g: (0, g, 0, 0)),
+            pl.BlockSpec((1, chunk, planes, width), lambda g: (0, g % inside, g // inside, 0)),
+            pl.BlockSpec(prior.shape, lambda g: (0, 0, 0)),
+            pl.BlockSpec(order.shape, lambda g: (0, 0)),
+        ],
+        out_specs=[
+            pl.BlockSpec((parts, 2 * held, chunk, planes), lambda g: (0, 0, g, 0)),
+            pl.BlockSpec(prior.shape, lambda g: (0, 0, 0)),
+        ],
+        out_shape=[
+            jax.ShapeDtypeStruct(shape, jnp.bfloat16),
+            jax.ShapeDtypeStruct(prior.shape, jnp.bfloat16),
+        ],
+        scratch_shapes=[pltpu.VMEM((width * chunk, planes), jnp.float32)] * 2,
+        compiler_params=pltpu.CompilerParams(vmem_limit_bytes=24 * 1024 * 1024),
+        cost_estimate=pl.CostEstimate(
+            flops=4 * maps.size * width, bytes_accessed=8 * maps.size, transcendentals=0
+        ),
+        name="pack",
+    )(maps, kspace, prior, jnp.asarray(order))
+
+
 def exchange(blocks, axis):
     return lax.all_to_all(blocks, axis, split_axis=0, concat_axis=0, tiled=True)
 
@@ -716,12 +787,16 @@
     coils = lax.axis_size("coil")
     devices = slabs * coils
     spread = readout % devices == 0 and own_rows % 8 == 0 and held_coils(coils) == coils
+    spread = spread and coil_maps.shape[1] % 16 == 0
+    spread = spread and kspace.shape[1] % 16 == 0 and kspace.shape[2] % planes == 0
     parts = devices if spread else coils
     x_count = readout // parts
+    if spread:
+        packed, features = pack_call(coil_maps, kspace, prior_image, parts)
+    else:
+        features = prior_image.astype(jnp.bfloat16)
     mask = lax.all_gather(sampling.astype(jnp.bfloat16), "slab", axis=0, tiled=True)
-    features, mask = lax.optimization_barrier(
-        (with_halo(prior_image.astype(jnp.bfloat16), 3), mask)
-    )
+    features, mask = lax.optimization_barrier((with_halo(features, 3), mask))
     mask = jnp.transpose(mask).astype(jnp.float32)
     row_count = mask.shape[0]
     constants = [mask] + half_tables(row_count, planes)
@@ -731,15 +806,19 @@
     def coils_to_x(values):
         blocks = x_first(values, parts)
         tail = (2 * x_count,) + blocks.shape[3:]
-        if spread:
-            blocks = exchange(blocks, axes).reshape((slabs, coils) + tail)
-        else:
-            blocks = exchange(blocks, "coil").reshape((slabs, coils // slabs) + tail)
-            blocks = exchange(blocks, "slab")
+        blocks = exchange(blocks, "coil").reshape((slabs, coils // slabs) + tail)
+        blocks = exchange(blocks, "slab")
         return [(blocks, 0), (blocks, x_count)]
 
-    maps = coils_to_x(coil_maps[0])
-    spectra = coils_to_x(kspace[0])
+    if spread:
+        arrived = exchange(packed, axes)
+        arrived = arrived.reshape((slabs, coils) + arrived.shape[1:])
+        maps = [(arrived, 0), (arrived, x_count)]
+        spectra = [(arrived, 2 * x_count), (arrived, 3 * x_count)]
+    else:
+        maps = coils_to_x(coil_maps[0])
+        spectra = coils_to_x(kspace[0])
+
     blocks = denoise(
         parts,
         features,

time: 199 us -> 241 us (1.21)
  starting transfers between devices: 24.7 us -> 63.6 us
  local copies, waits for them, and re-layouts: 23.8 us -> 12.5 us
  waiting for transfers between devices: 19.4 us -> 29.6 us
  other arithmetic: 11.1 us -> 5.58 us
  blocking collectives: 46.2 us -> 51.1 us
  Pallas kernels: 71.6 us -> 76.3 us
    all_to_all x4 -> x3, starting transfers between devices: 19.2 us -> 58.6 us  [exchange(): return lax.all_to_all(blocks, axis, split_axis=0, concat_axis=0, tiled=True)]
    all_to_all x4 -> x3, waiting for transfers between devices: 19.4 us -> 29.6 us  [exchange(): return lax.all_to_all(blocks, axis, split_axis=0, concat_axis=0, tiled=True)]
    all_gather x1, blocking collectives: 10.1 us -> 15 us  [body(): lax.all_gather(sampling.astype(jnp.bfloat16), 'slab', axis=0, tiled=True)]
    pallas_call x0 -> x1, Pallas kernels: none -> 4.55 us  [pack_call(): pl.pallas_call(pack_kernel, grid=(count,), in_specs=[pl.BlockSpec((1, chu...]
    select_n x3, other arithmetic: 8.98 us -> 4.63 us  [banded(): result = jnp.where(inner - outer + offset == tap, tiles[tap], result)]
    unnamed x44 -> x34, local copies, waits for them, and re-layouts: 11.2 us -> 7.57 us
    transpose x2 -> x0, local copies, waits for them, and re-layouts: 3.07 us -> none  [x_first(): return jnp.transpose(split, (3, 2, 4, 0, 1))]
  transfers between devices with their start and end apart: 6 -> 5, of which waited for: 3 -> 2; matrix products, arithmetic and copies ran while one was open for 13% -> 4% of each run, Pallas kernels for 35% -> 29%
where the time goes in v12:
time: 241 us; the launch traced here: 240 us
  Pallas kernels  76.3 us (32%)
  starting transfers between devices  63.6 us (26%)
  blocking collectives  51.1 us (21%)
  waiting for transfers between devices  29.6 us (12%)
  local copies, waits for them, and re-layouts  12.5 us (5%)
  other arithmetic  5.58 us (2%)
    all_to_all x3, starting transfers between devices, exchange(): return lax.all_to_all(blocks, axis, split_axis=0, concat_axis=0, tiled=True)  58.6 us
    pallas_call x1, Pallas kernels, denoise(): pl.pallas_call(functools.partial(denoise_kernel, group), in_specs=[pl.Blo...  45 us
    all_to_all x1, blocking collectives, exchange(): return lax.all_to_all(blocks, axis, split_axis=0, concat_axis=0, tiled=True)  36 us
    all_to_all x3, waiting for transfers between devices, exchange(): return lax.all_to_all(blocks, axis, split_axis=0, concat_axis=0, tiled=True)  29.6 us
    pallas_call x2, Pallas kernels, product_call(): pl.pallas_call(kernel, grid=(x_count, coils // held_coils(coils)), in_spe...  24.3 us
    all_gather x1, blocking collectives, body(): lax.all_gather(sampling.astype(jnp.bfloat16), 'slab', axis=0, tiled=True)  15 us
    unnamed x34, local copies, waits for them, and re-layouts  7.57 us
  transfers between devices with their start and end apart: 5, of which 2 were waited for; matrix products, arithmetic and copies ran while one was open for 4% of the time, Pallas kernels for 29%

profile of v12, /device:TPU:0, one launch (start us, length us, event | category | flops | bytes accessed | tf_op | source)
XLA Modules:
  0.0 239.9 jit_solution(3127280467995342526)
XLA Ops:
  0.6 1.6 copy-done.1
  2.2 1.6 copy-done.2
  3.8 1.0 copy-done.4
  4.9 0.8 copy-done.6
  5.6 4.6 %pack.1 = (bf16[32,8,64,128]{3,2,1,0:T(8,128)(2,1)S(1)}, bf16[8,128,128]{2,1,0:T(8,128)(2,1)S(1)}) custom-call(bf16[1,64,128,128]{3,2,1,0:T(8,128)(2,1)S(1)} %copy-done.1, bf16[1,32,256,128]{3,2,1,0:T(8,128)(2,1)S(1)} %copy-done.2, f32[8,128,128]{2,1,0:T(8,128)S(1)} %copy-done.4, bf16[128,128]{1,0:T(8,128)(2,1)S(1)} %copy-done.6), custom_call_target="tpu_custom_call" | custom-call | flops 536870912 | bytes 8388608 | tf_op jit(solution)/shard_map/pack/pallas_call | solution.py:670
  10.2 2.0 copy-done
  12.2 7.4 %all-to-all-start = ((bf16[32,8,64,128]{3,2,1,0:T(8,128)(2,1)}), bf16[32,8,64,128]{3,2,1,0:T(8,128)(2,1)}, u32[]{:S(2)}, u32[]{:S(2)}) async-start(bf16[32,8,64,128]{3,2,1,0:T(8,128)(2,1)} %copy-done), calls=%async_computation | async-start | bytes 8388608 | tf_op jit(solution)/shard_map/all_to_all | solution.py:697
  19.7 3.7 %collective-permute-start = (bf16[3,128,128]{2,1,0:T(8,128)(2,1)S(1)}, bf16[3,128,128]{2,1,0:T(8,128)(2,1)S(1)}, u32[]{:S(2)}, u32[]{:S(2)}) collective-permute-start(bf16[3,128,128]{2,1,0:T(8,128)(2,1)S(1)} %get-tuple-element.16), channel_id=1, source_target_pairs={{0,1},{1,2},{2,3},{3,4},{4,5},{5,6},{6,7},{7,8},{8,9},{9,10},{10,1... | collective-permute-start | bytes 294920 | tf_op jit(solution)/shard_map/ppermute | solution.py:28
  23.4 1.3 collective-permute-start.1
  28.3 0.3 broadcast_in_dim.189
  29.7 15.0 %all_gather.3 = bf16[128,256]{1,0:T(8,128)(2,1)S(1)} all-gather(bf16[32,256]{1,0:T(8,128)(2,1)S(1)} %convert_element_type.8), channel_id=1, replica_groups=mesh['slab'=4,'coil'=8] {'slab'}, dimensions={0}, use_global_device_ids=true | all-gather | bytes 81920 | tf_op jit(solution)/shard_map/all_gather | solution.py:798
  44.8 0.6 select_select_fusion.2
  45.8 2.0 select_select_fusion.1
  47.8 2.1 select_select_fusion
  50.5 0.5 copy-done.5
  51.1 45.0 %denoise.1.denoised_ref = f32[32,2,2,8,128]{4,3,2,1,0:T(8,128)} custom-call(s32[2]{0:T(128)S(1)} %pad_add_fusion.first_ref, bf16[14,128,384]{2,1,0:T(8,128)(2,1)S(1)} %fusion.2.features_ref, f32[8,128,128]{2,1,0:T(8,128)S(1)} %copy-done.5, bf16[1152,2048]{1,0:T(8,128)(2,1)S(1)} %bitcast.35, f32[1,2048]{1,0:T(1,128)S(1)} %broadcast_in_dim_tile.8.bias_first_ref, ...), custom_call_target="tpu_custom_call" | custom-call | flops 37446746112 | bytes 16777216 | tf_op jit(solution)/shard_map/denoise/pallas_call | solution.py:236
  96.0 20.4 %all-to-all-done = bf16[32,8,64,128]{3,2,1,0:T(8,128)(2,1)} async-done(((bf16[32,8,64,128]{3,2,1,0:T(8,128)(2,1)}), bf16[32,8,64,128]{3,2,1,0:T(8,128)(2,1)}, u32[]{:S(2)}, u32[]{:S(2)}) %all-to-all-start) | async-done | bytes 4194336 | tf_op jit(solution)/shard_map/all_to_all | solution.py:697
  116.4 48.3 %all-to-all-start.1 = ((f32[32,2,2,8,128]{4,3,2,1,0:T(8,128)}), f32[32,2,2,8,128]{4,3,2,1,0:T(8,128)S(1)}, u32[]{:S(2)}, u32[]{:S(2)}) async-start(f32[32,2,2,8,128]{4,3,2,1,0:T(8,128)} %denoise.1.denoised_ref), calls=%async_computation.1 | async-start | bytes 1048576 | tf_op jit(solution)/shard_map/all_to_all | solution.py:697
  164.9 7.0 %adjoint.1.adjoint_ref = f32[32,2,2,8,128]{4,3,2,1,0:T(8,128)} custom-call(bf16[4,8,8,64,128]{4,3,2,1,0:T(8,128)(2,1)} %bitcast.spectra_real_ref.spectra_imag_ref.maps_real_ref.maps_imag_ref, bf16[4,8,8,64,128]{4,3,2,1,0:T(8,128)(2,1)} %bitcast.spectra_real_ref.spectra_imag_ref.maps_real_ref.maps_imag_ref, ...), custom_call_target="tpu_custom_call" | custom-call | flops 4831838208 | bytes 8388608 | tf_op jit(solution)/shard_map/adjoint/pallas_call | solution.py:594
  172.0 9.2 %all-to-all-done.1.denoised_ref = f32[32,2,2,8,128]{4,3,2,1,0:T(8,128)S(1)} async-done(((f32[32,2,2,8,128]{4,3,2,1,0:T(8,128)}), f32[32,2,2,8,128]{4,3,2,1,0:T(8,128)S(1)}, u32[]{:S(2)}, u32[]{:S(2)}) %all-to-all-start.1) | async-done | bytes 524320 | tf_op jit(solution)/shard_map/all_to_all | solution.py:697
  181.1 2.8 %all-to-all-start.2 = ((f32[32,2,2,8,128]{4,3,2,1,0:T(8,128)}), f32[32,2,2,8,128]{4,3,2,1,0:T(8,128)S(1)}, u32[]{:S(2)}, u32[]{:S(2)}) async-start(f32[32,2,2,8,128]{4,3,2,1,0:T(8,128)} %adjoint.1.adjoint_ref), calls=%async_computation.2 | async-start | bytes 1048576 | tf_op jit(solution)/shard_map/all_to_all | solution.py:697
  184.0 17.3 %products.1 = f32[32,9,8,128]{3,2,1,0:T(8,128)S(1)} custom-call(bf16[4,8,8,64,128]{4,3,2,1,0:T(8,128)(2,1)} %bitcast.spectra_real_ref.spectra_imag_ref.maps_real_ref.maps_imag_ref, bf16[4,8,8,64,128]{4,3,2,1,0:T(8,128)(2,1)} %bitcast.spectra_real_ref.spectra_imag_ref.maps_real_ref.maps_imag_ref, f32[32,2,2,8,128]{4,3,2,1,0:T(8,128)} %adjoint.1.adjoint_ref, ...), custom_call_target="tpu_custom_call" | custom-call | flops 19327352832 | bytes 8388608 | tf_op jit(solution)/shard_map/products/pallas_call | solution.py:594
  201.3 36.0 %all_to_all.20.moved_ref = f32[32,9,8,128]{3,2,1,0:T(8,128)S(1)} all-to-all(f32[32,9,8,128]{3,2,1,0:T(8,128)S(1)} %products.1), channel_id=1, replica_groups=mesh['slab'=4,'coil'=8] {'slab','coil'}, dimensions={0} | all-to-all | bytes 2359296 | tf_op jit(solution)/shard_map/all_to_all | solution.py:697
  237.3 2.5 %finish.1 = (f32[8,128,128]{2,1,0:T(8,128)}, f32[8,128,128]{2,1,0:T(8,128)}) custom-call(f32[32,2,2,8,128]{4,3,2,1,0:T(8,128)S(1)} %all-to-all-done.2.adjoint_ref, f32[32,2,2,8,128]{4,3,2,1,0:T(8,128)} %denoise.1.denoised_ref, f32[32,9,8,128]{3,2,1,0:T(8,128)S(1)} %all_to_all.20.moved_ref), custom_call_target="tpu_custom_call" | custom-call | flops 1048576 | bytes 3145728 | tf_op jit(solution)/shard_map/finish/pallas_call | solution.py:757
  (87 shorter events, 5.6 us)
Async XLA Ops:
  0.6 1.6 copy-start.1
  2.2 1.6 copy-start.2
  3.8 1.0 copy-start.4
  4.9 0.8 copy-start.6
  10.2 2.0 copy-start
  12.2 12.5 %copy-start.11 = (s32[32,256]{1,0:T(8,128)S(1)}, s32[32,256]{1,0:T(8,128)}, u32[]{:S(2)}) copy-start(s32[32,256]{1,0:T(8,128)} %param.18) | copy-start | bytes 98308
  12.2 12.6 %copy-start.12 = (bf16[3,3,3,32,2]{3,4,2,1,0:T(2,128)(2,1)S(1)}, bf16[3,3,3,32,2]{3,4,2,1,0:T(2,128)(2,1)}, u32[]{:S(2)}) copy-start(bf16[3,3,3,32,2]{3,4,2,1,0:T(2,128)(2,1)} %param.19) | copy-start | bytes 10372
  12.2 104.2 %all-to-all-start = ((bf16[32,8,64,128]{3,2,1,0:T(8,128)(2,1)}), bf16[32,8,64,128]{3,2,1,0:T(8,128)(2,1)}, u32[]{:S(2)}, u32[]{:S(2)}) async-start(bf16[32,8,64,128]{3,2,1,0:T(8,128)(2,1)} %copy-done), calls=%async_computation | async-start | bytes 8388608 | tf_op jit(solution)/shard_map/all_to_all | solution.py:697
  19.6 6.3 %copy-start.13 = (bf16[3,3,3,2,32]{4,3,2,1,0:T(2,128)(2,1)S(1)}, bf16[3,3,3,2,32]{4,3,2,1,0:T(2,128)(2,1)}, u32[]{:S(2)}) copy-start(bf16[3,3,3,2,32]{4,3,2,1,0:T(2,128)(2,1)} %param.23) | copy-start | bytes 10372
  19.7 7.8 %copy-start.10 = (bf16[3,3,3,32,32]{4,3,2,1,0:T(8,128)(2,1)S(1)}, bf16[3,3,3,32,32]{4,3,2,1,0:T(8,128)(2,1)}, u32[]{:S(2)}) copy-start(bf16[3,3,3,32,32]{4,3,2,1,0:T(8,128)(2,1)} %param.21) | copy-start | bytes 165892
  19.7 30.3 %collective-permute-start = (bf16[3,128,128]{2,1,0:T(8,128)(2,1)S(1)}, bf16[3,128,128]{2,1,0:T(8,128)(2,1)S(1)}, u32[]{:S(2)}, u32[]{:S(2)}) collective-permute-start(bf16[3,128,128]{2,1,0:T(8,128)(2,1)S(1)} %get-tuple-element.16), channel_id=1, source_target_pairs={{0,1},{1,2},{2,3},{3,4},{4,5},{5,6},{6,7},{7,8},{8,9},{9,10},{10,1... | collective-permute-start | bytes 294920 | tf_op jit(solution)/shard_map/ppermute | solution.py:28
  23.4 26.5 %collective-permute-start.1 = (bf16[3,128,128]{2,1,0:T(8,128)(2,1)S(1)}, bf16[3,128,128]{2,1,0:T(8,128)(2,1)S(1)}, u32[]{:S(2)}, u32[]{:S(2)}) collective-permute-start(bf16[3,128,128]{2,1,0:T(8,128)(2,1)S(1)} %get-tuple-element.17), channel_id=1, source_target_pairs={{1,0},{2,1},{3,2},{4,3},{5,4},{6,5},{7,6},{8,7},{9,8},{10,9},{11,1... | collective-permute-start | bytes 294920 | tf_op jit(solution)/shard_map/ppermute | solution.py:29
  27.6 1.7 copy-start.14
  27.6 1.8 copy-start.15
  27.6 1.9 copy-start.16
  50.0 1.0 copy-start.5
  51.1 113.8 %copy-start.3 = (bf16[512,1280]{1,0:T(8,128)(2,1)S(1)}, bf16[512,1280]{1,0:T(8,128)(2,1)}, u32[]{:S(2)}) copy-start(bf16[512,1280]{1,0:T(8,128)(2,1)} %constant.73.clone.table_ref) | copy-start | bytes 3932164
  116.4 64.7 %all-to-all-start.1 = ((f32[32,2,2,8,128]{4,3,2,1,0:T(8,128)}), f32[32,2,2,8,128]{4,3,2,1,0:T(8,128)S(1)}, u32[]{:S(2)}, u32[]{:S(2)}) async-start(f32[32,2,2,8,128]{4,3,2,1,0:T(8,128)} %denoise.1.denoised_ref), calls=%async_computation.1 | async-start | bytes 1048576 | tf_op jit(solution)/shard_map/all_to_all | solution.py:697
  164.9 19.0 %copy-start.7 = (bf16[256,512]{1,0:T(8,128)(2,1)S(1)}, bf16[256,512]{1,0:T(8,128)(2,1)}, u32[]{:S(2)}) copy-start(bf16[256,512]{1,0:T(8,128)(2,1)} %constant.70.clone.refs_1_) | copy-start | bytes 786436
  164.9 19.0 %copy-start.8 = (bf16[512,256]{1,0:T(8,128)(2,1)S(1)}, bf16[512,256]{1,0:T(8,128)(2,1)}, u32[]{:S(2)}) copy-start(bf16[512,256]{1,0:T(8,128)(2,1)} %constant.71.clone.refs_2_) | copy-start | bytes 786436
  164.9 19.0 %copy-start.9 = (f32[2,128,128]{2,1,0:T(8,128)S(1)}, f32[2,128,128]{2,1,0:T(8,128)}, u32[]{:S(2)}) copy-start(f32[2,128,128]{2,1,0:T(8,128)} %constant.72.clone.refs_3_) | copy-start | bytes 393220
  181.1 20.2 %all-to-all-start.2 = ((f32[32,2,2,8,128]{4,3,2,1,0:T(8,128)}), f32[32,2,2,8,128]{4,3,2,1,0:T(8,128)S(1)}, u32[]{:S(2)}, u32[]{:S(2)}) async-start(f32[32,2,2,8,128]{4,3,2,1,0:T(8,128)} %adjoint.1.adjoint_ref), calls=%async_computation.2 | async-start | bytes 1048576 | tf_op jit(solution)/shard_map/all_to_all | solution.py:697

commit v13 on v10

--- a/solution.py
+++ b/solution.py
@@ -622,6 +622,60 @@
     )[0]
 
 
+def pack_kernel(maps_ref, prior_ref, order_ref, out_ref, features_ref, rows_ref):
+    rows, planes, width = maps_ref.shape[1:]
+    parts, held = out_ref.shape[:2]
+    for row in range(0, rows, 2):
+        moved = lax.dot_general(
+            order_ref[...],
+            maps_ref[0, row : row + 2].reshape(2 * planes, width),
+            (((1,), (1,)), ((), ())),
+            preferred_element_type=jnp.float32,
+        )
+        for odd in range(2):
+            lanes = slice(odd * planes, (odd + 1) * planes)
+            rows_ref[pl.ds(row + odd, width, stride=rows), :] = moved[:, lanes]
+    for part in range(parts):
+        for inner in range(held):
+            place = (part * held + inner) * rows
+            out_ref[part, inner] = rows_ref[place : place + rows].astype(out_ref.dtype)
+    features_ref[...] = prior_ref[...].astype(features_ref.dtype)
+
+
+def pack_call(maps, prior, parts):
+    _, slab_rows, planes, width = maps.shape
+    chunk = 16
+    count = slab_rows // chunk
+    own_rows = prior.shape[0] // count
+    held = width // parts
+    lanes = np.arange(width).reshape(2, parts, held // 2).transpose(1, 0, 2).reshape(-1)
+    order = (lanes[:, None] == np.arange(width)[None, :]).astype(jnp.bfloat16)
+    prior_spec = pl.BlockSpec((own_rows,) + prior.shape[1:], lambda g: (g, 0, 0))
+    return pl.pallas_call(
+        pack_kernel,
+        grid=(count,),
+        in_specs=[
+            pl.BlockSpec((1, chunk, planes, width), lambda g: (0, g, 0, 0)),
+            prior_spec,
+            pl.BlockSpec(order.shape, lambda g: (0, 0)),
+        ],
+        out_specs=[
+            pl.BlockSpec((parts, held, chunk, planes), lambda g: (0, 0, g, 0)),
+            prior_spec,
+        ],
+        out_shape=[
+            jax.ShapeDtypeStruct((parts, held, slab_rows, planes), jnp.bfloat16),
+            jax.ShapeDtypeStruct(prior.shape, jnp.bfloat16),
+        ],
+        scratch_shapes=[pltpu.VMEM((width * chunk, planes), jnp.float32)],
+        compiler_params=pltpu.CompilerParams(vmem_limit_bytes=60 * 1024 * 1024),
+        cost_estimate=pl.CostEstimate(
+            flops=2 * maps.size * width, bytes_accessed=5 * maps.size, transcendentals=0
+        ),
+        name="pack",
+    )(maps, prior, jnp.asarray(order))
+
+
 def exchange(blocks, axis):
     return lax.all_to_all(blocks, axis, split_axis=0, concat_axis=0, tiled=True)
 
@@ -716,11 +770,17 @@
     coils = lax.axis_size("coil")
     devices = slabs * coils
     spread = readout % devices == 0 and own_rows % 8 == 0 and held_coils(coils) == coils
+    packs = spread and coil_maps.shape[1] % 16 == 0 and own_rows % (coil_maps.shape[1] // 16) == 0
     parts = devices if spread else coils
     x_count = readout // parts
+    if packs:
+        map_blocks, features = pack_call(coil_maps, prior_image, parts)
+    else:
+        map_blocks = x_first(coil_maps[0], parts)
+        features = prior_image.astype(jnp.bfloat16)
     mask = lax.all_gather(sampling.astype(jnp.bfloat16), "slab", axis=0, tiled=True)
     features, mask = lax.optimization_barrier(
-        (with_halo(prior_image.astype(jnp.bfloat16), 3), mask)
+        (with_halo(features, 3), mask)
     )
     mask = jnp.transpose(mask).astype(jnp.float32)
     row_count = mask.shape[0]
@@ -728,9 +788,8 @@
     constants = [jnp.asarray(value) for value in constants]
     adjoint_constants = [mask, jnp.asarray(dft_table(row_count, planes))]
 
-    def coils_to_x(values):
-        blocks = x_first(values, parts)
-        tail = (2 * x_count,) + blocks.shape[3:]
+    def coils_to_x(blocks):
+        tail = (2 * x_count,) + blocks.shape[-2:]
         if spread:
             blocks = exchange(blocks, axes).reshape((slabs, coils) + tail)
         else:
@@ -738,8 +797,8 @@
             blocks = exchange(blocks, "slab")
         return [(blocks, 0), (blocks, x_count)]
 
-    maps = coils_to_x(coil_maps[0])
-    spectra = coils_to_x(kspace[0])
+    maps = coils_to_x(map_blocks)
+    spectra = coils_to_x(x_first(kspace[0], parts))
     blocks = denoise(
         parts,
         features,

time: 199 us -> 199 us (level)
  local copies, waits for them, and re-layouts: 23.8 us -> 16 us
  Pallas kernels: 71.6 us -> 76.6 us
  waiting for transfers between devices: 19.4 us -> 23.3 us
    pallas_call x0 -> x1, Pallas kernels: none -> 5.05 us  [pack_call(): pl.pallas_call(pack_kernel, grid=(count,), in_specs=[pl.BlockSpec((1, chu...]
    all_to_all x4, waiting for transfers between devices: 19.4 us -> 23.3 us  [exchange(): return lax.all_to_all(blocks, axis, split_axis=0, concat_axis=0, tiled=True)]
    unnamed x44 -> x35, local copies, waits for them, and re-layouts: 11.2 us -> 8.18 us
  transfers between devices with their start and end apart: 6 -> 6, of which waited for: 3 -> 2; matrix products, arithmetic and copies ran while one was open for 13% -> 11% of each run, Pallas kernels for 35% -> 35%
where the time goes in v13:
time: 199 us; the launch traced here: 198 us
  Pallas kernels  76.6 us (38%)
  blocking collectives  45.2 us (23%)
  starting transfers between devices  25 us (13%)
  waiting for transfers between devices  23.3 us (12%)
  local copies, waits for them, and re-layouts  16 us (8%)
  other arithmetic  11 us (6%)
    pallas_call x1, Pallas kernels, denoise(): pl.pallas_call(functools.partial(denoise_kernel, group), in_specs=[pl.Blo...  44.8 us
    all_to_all x1, blocking collectives, exchange(): return lax.all_to_all(blocks, axis, split_axis=0, concat_axis=0, tiled=True)  36 us
    pallas_call x2, Pallas kernels, product_call(): pl.pallas_call(kernel, grid=(x_count, coils // held_coils(coils)), in_spe...  24.3 us
    all_to_all x4, waiting for transfers between devices, exchange(): return lax.all_to_all(blocks, axis, split_axis=0, concat_axis=0, tiled=True)  23.3 us
    all_to_all x4, starting transfers between devices, exchange(): return lax.all_to_all(blocks, axis, split_axis=0, concat_axis=0, tiled=True)  19.5 us
    all_gather x1, blocking collectives, body(): lax.all_gather(sampling.astype(jnp.bfloat16), 'slab', axis=0, tiled=True)  9.16 us
    select_n x3, other arithmetic, banded(): result = jnp.where(inner - outer + offset == tap, tiles[tap], result)  8.95 us
    unnamed x35, local copies, waits for them, and re-layouts  8.18 us
  transfers between devices with their start and end apart: 6, of which 2 were waited for; matrix products, arithmetic and copies ran while one was open for 11% of the time, Pallas kernels for 35%

profile of v13, /device:TPU:0, one launch (start us, length us, event | category | flops | bytes accessed | tf_op | source)
XLA Modules:
  0.0 198.3 jit_solution(11923677309392863591)
XLA Ops:
  0.6 5.1 %pack.1 = (bf16[32,4,64,128]{3,2,1,0:T(8,128)(2,1)}, bf16[8,128,128]{2,1,0:T(8,128)(2,1)}) custom-call(bf16[1,64,128,128]{3,2,1,0:T(8,128)(2,1)} %maps_ref.1, f32[8,128,128]{2,1,0:T(8,128)} %prior_ref.3, bf16[128,128]{1,0:T(8,128)(2,1)} %constant.69.clone.order_ref), custom_call_target="tpu_custom_call" | custom-call | flops 268435456 | bytes 5242880 | tf_op jit(solution)/shard_map/pack/pallas_call | solution.py:654
  5.7 7.4 %all-to-all-start = ((bf16[32,4,64,128]{3,2,1,0:T(8,128)(2,1)}), bf16[32,4,64,128]{3,2,1,0:T(8,128)(2,1)}, u32[]{:S(2)}, u32[]{:S(2)}) async-start(bf16[32,4,64,128]{3,2,1,0:T(8,128)(2,1)} %get-tuple-element.8), calls=%async_computation | async-start | bytes 4194304 | tf_op jit(solution)/shard_map/all_to_all | solution.py:680
  13.9 4.2 %collective-permute-start = (bf16[3,128,128]{2,1,0:T(8,128)(2,1)}, bf16[3,128,128]{2,1,0:T(8,128)(2,1)}, u32[]{:S(2)}, u32[]{:S(2)}) collective-permute-start(bf16[3,128,128]{2,1,0:T(8,128)(2,1)} %get-tuple-element.16), channel_id=1, source_target_pairs={{0,1},{1,2},{2,3},{3,4},{4,5},{5,6},{6,7},{7,8},{8,9},{9,10},{10,1... | collective-permute-start | bytes 294920 | tf_op jit(solution)/shard_map/ppermute | solution.py:28
  18.1 1.3 collective-permute-start.1
  21.8 0.8 broadcast_in_dim.206
  24.9 3.4 %copy.34 = bf16[1,32,256,128]{2,1,3,0:T(8,128)(2,1)S(1)} copy(bf16[1,32,256,128]{3,2,1,0:T(8,128)(2,1)} %param.17) | data formatting | bytes 4194304 | tf_op args[2]
  28.3 1.6 copy.35
  29.9 9.2 %all_gather.3 = bf16[128,256]{1,0:T(8,128)(2,1)} all-gather(bf16[32,256]{1,0:T(8,128)(2,1)S(1)} %convert_element_type.8), channel_id=1, replica_groups=mesh['slab'=4,'coil'=8] {'slab'}, dimensions={0}, use_global_device_ids=true | all-gather | bytes 81920 | tf_op jit(solution)/shard_map/all_gather | solution.py:781
  40.2 4.1 %select_select_fusion.1 = bf16[18,64,2048]{2,1,0:T(8,128)(2,1)} fusion(pred[64,2048]{1,0:T(8,128)(4,1)S(1)} %get-tuple-element.31, pred[64,2048]{1,0:T(8,128)(4,1)S(1)} %get-tuple-element.32, pred[64,2048]{1,0:T(8,128)(4,1)S(1)} %get-tuple-element.30, bf16[18,2048]{1,0:T(8,128)(2,1)S(1)} %broadcast_in_dim.180, bf16[18,2048]{1,0:T(8,128)(2,1)S(1)} %broadcast_in_dim.176, ...), kind=kLoop, calls=%fused_computation.1 | loop fusion | flops 7077888 | bytes 5332992 | tf_op jit(solution)/shard_map/jit(_where)/select_n | solution.py:162
  44.3 4.2 %select_select_fusion = bf16[64,32,1152]{2,1,0:T(8,128)(2,1)} fusion(pred[64,1152]{1,0:T(8,128)(4,1)S(1)} %get-tuple-element.28, pred[64,1152]{1,0:T(8,128)(4,1)S(1)} %get-tuple-element.29, pred[64,1152]{1,0:T(8,128)(4,1)S(1)} %get-tuple-element.27, bf16[32,1152]{1,0:T(8,128)(2,1)S(1)} %copy-done.8, bf16[32,1152]{1,0:T(8,128)(2,1)S(1)} %broadcast_in_dim.202, ...), kind=kLoop, calls=%fused_computation | loop fusion | flops 7077888 | bytes 5160960 | tf_op jit(solution)/shard_map/jit(_where)/select_n | solution.py:162
  48.6 15.6 %all-to-all-done = bf16[32,4,64,128]{3,2,1,0:T(8,128)(2,1)} async-done(((bf16[32,4,64,128]{3,2,1,0:T(8,128)(2,1)}), bf16[32,4,64,128]{3,2,1,0:T(8,128)(2,1)}, u32[]{:S(2)}, u32[]{:S(2)}) %all-to-all-start) | async-done | bytes 2097184 | tf_op jit(solution)/shard_map/all_to_all | solution.py:680
  64.2 3.7 %all-to-all-start.1 = ((bf16[32,2,2,32,256]{4,3,2,1,0:T(8,128)(2,1)}), bf16[32,2,2,32,256]{4,3,2,1,0:T(8,128)(2,1)}, u32[]{:S(2)}, u32[]{:S(2)}) async-start(bf16[32,2,2,32,256]{4,3,2,1,0:T(8,128)(2,1)} %copy.35), calls=%async_computation.1 | async-start | bytes 4194304 | tf_op jit(solution)/shard_map/all_to_all | solution.py:680
  67.9 1.1 pad_maximum_fusion
  69.7 0.7 copy-done
  70.7 2.3 %copy-done.1 = bf16[18,64,2048]{2,1,0:T(8,128)(2,1)S(1)} copy-done((bf16[18,64,2048]{2,1,0:T(8,128)(2,1)S(1)}, bf16[18,64,2048]{2,1,0:T(8,128)(2,1)}, u32[]{:S(2)}) %copy-start.1) | copy-done | bytes 4718616
  73.1 44.8 %denoise.1.denoised_ref = f32[32,2,2,8,128]{4,3,2,1,0:T(8,128)} custom-call(s32[2]{0:T(128)S(1)} %pad_add_fusion.first_ref, bf16[14,128,384]{2,1,0:T(8,128)(2,1)S(1)} %fusion.2.features_ref, f32[8,128,128]{2,1,0:T(8,128)S(1)} %copy-done.2, bf16[1152,2048]{1,0:T(8,128)(2,1)S(1)} %bitcast.39, f32[1,2048]{1,0:T(1,128)S(1)} %broadcast_in_dim_tile.8.bias_first_ref, ...), custom_call_target="tpu_custom_call" | custom-call | flops 37446746112 | bytes 16777216 | tf_op jit(solution)/shard_map/denoise/pallas_call | solution.py:236
  117.8 5.8 %all-to-all-start.2 = ((f32[32,2,2,8,128]{4,3,2,1,0:T(8,128)}), f32[32,2,2,8,128]{4,3,2,1,0:T(8,128)S(1)}, u32[]{:S(2)}, u32[]{:S(2)}) async-start(f32[32,2,2,8,128]{4,3,2,1,0:T(8,128)} %denoise.1.denoised_ref), calls=%async_computation.2 | async-start | bytes 1048576 | tf_op jit(solution)/shard_map/all_to_all | solution.py:680
  123.8 1.3 copy-done.3
  125.1 7.0 %adjoint.1.adjoint_ref = f32[32,2,2,8,128]{4,3,2,1,0:T(8,128)} custom-call(bf16[4,8,4,32,256]{4,3,2,1,0:T(8,128)(2,1)} %bitcast.3.spectra_real_ref.spectra_imag_ref, bf16[4,8,4,32,256]{4,3,2,1,0:T(8,128)(2,1)} %bitcast.3.spectra_real_ref.spectra_imag_ref, bf16[4,8,4,64,128]{4,3,2,1,0:T(8,128)(2,1)} %bitcast.maps_real_ref.maps_imag_ref, ...), custom_call_target="tpu_custom_call" | custom-call | flops 4831838208 | bytes 8388608 | tf_op jit(solution)/shard_map/adjoint/pallas_call | solution.py:583
  132.1 7.7 %all-to-all-done.2.denoised_ref = f32[32,2,2,8,128]{4,3,2,1,0:T(8,128)S(1)} async-done(((f32[32,2,2,8,128]{4,3,2,1,0:T(8,128)}), f32[32,2,2,8,128]{4,3,2,1,0:T(8,128)S(1)}, u32[]{:S(2)}, u32[]{:S(2)}) %all-to-all-start.2) | async-done | bytes 524320 | tf_op jit(solution)/shard_map/all_to_all | solution.py:680
  139.8 2.6 %all-to-all-start.3 = ((f32[32,2,2,8,128]{4,3,2,1,0:T(8,128)}), f32[32,2,2,8,128]{4,3,2,1,0:T(8,128)S(1)}, u32[]{:S(2)}, u32[]{:S(2)}) async-start(f32[32,2,2,8,128]{4,3,2,1,0:T(8,128)} %adjoint.1.adjoint_ref), calls=%async_computation.3 | async-start | bytes 1048576 | tf_op jit(solution)/shard_map/all_to_all | solution.py:680
  142.4 17.3 %products.1 = f32[32,9,8,128]{3,2,1,0:T(8,128)S(1)} custom-call(bf16[4,8,4,64,128]{4,3,2,1,0:T(8,128)(2,1)} %bitcast.maps_real_ref.maps_imag_ref, bf16[4,8,4,64,128]{4,3,2,1,0:T(8,128)(2,1)} %bitcast.maps_real_ref.maps_imag_ref, f32[32,2,2,8,128]{4,3,2,1,0:T(8,128)} %adjoint.1.adjoint_ref, f32[32,2,2,8,128]{4,3,2,1,0:T(8,128)S(1)} %all-to-all-done.2.denoised_ref, ...), custom_call_target="tpu_custom_call" | custom-call | flops 19327352832 | bytes 8388608 | tf_op jit(solution)/shard_map/products/pallas_call | solution.py:583
  159.7 36.0 %all_to_all.25.moved_ref = f32[32,9,8,128]{3,2,1,0:T(8,128)S(1)} all-to-all(f32[32,9,8,128]{3,2,1,0:T(8,128)S(1)} %products.1), channel_id=1, replica_groups=mesh['slab'=4,'coil'=8] {'slab','coil'}, dimensions={0} | all-to-all | bytes 2359296 | tf_op jit(solution)/shard_map/all_to_all | solution.py:680
  195.8 2.5 %finish.1 = (f32[8,128,128]{2,1,0:T(8,128)}, f32[8,128,128]{2,1,0:T(8,128)}) custom-call(f32[32,2,2,8,128]{4,3,2,1,0:T(8,128)S(1)} %all-to-all-done.3.adjoint_ref, f32[32,2,2,8,128]{4,3,2,1,0:T(8,128)} %denoise.1.denoised_ref, f32[32,9,8,128]{3,2,1,0:T(8,128)S(1)} %all_to_all.25.moved_ref), custom_call_target="tpu_custom_call" | custom-call | flops 1048576 | bytes 3145728 | tf_op jit(solution)/shard_map/finish/pallas_call | solution.py:740
  (91 shorter events, 7.4 us)
Async XLA Ops:
  5.7 7.5 %copy-start.7 = (bf16[8,128,128]{2,1,0:T(8,128)(2,1)S(1)}, bf16[8,128,128]{2,1,0:T(8,128)(2,1)}, u32[]{:S(2)}) copy-start(bf16[8,128,128]{2,1,0:T(8,128)(2,1)} %get-tuple-element.9) | copy-start | bytes 786436
  5.7 13.7 %copy-start.11 = (s32[32,256]{1,0:T(8,128)S(1)}, s32[32,256]{1,0:T(8,128)}, u32[]{:S(2)}) copy-start(s32[32,256]{1,0:T(8,128)} %param.18) | copy-start | bytes 98308
  5.7 13.7 %copy-start.12 = (bf16[3,3,3,32,2]{3,4,2,1,0:T(2,128)(2,1)S(1)}, bf16[3,3,3,32,2]{3,4,2,1,0:T(2,128)(2,1)}, u32[]{:S(2)}) copy-start(bf16[3,3,3,32,2]{3,4,2,1,0:T(2,128)(2,1)} %param.19) | copy-start | bytes 10372
  5.7 14.9 %copy-start.13 = (bf16[3,3,3,2,32]{4,3,2,1,0:T(2,128)(2,1)S(1)}, bf16[3,3,3,2,32]{4,3,2,1,0:T(2,128)(2,1)}, u32[]{:S(2)}) copy-start(bf16[3,3,3,2,32]{4,3,2,1,0:T(2,128)(2,1)} %param.23) | copy-start | bytes 10372
  5.7 58.5 %all-to-all-start = ((bf16[32,4,64,128]{3,2,1,0:T(8,128)(2,1)}), bf16[32,4,64,128]{3,2,1,0:T(8,128)(2,1)}, u32[]{:S(2)}, u32[]{:S(2)}) async-start(bf16[32,4,64,128]{3,2,1,0:T(8,128)(2,1)} %get-tuple-element.8), calls=%async_computation | async-start | bytes 4194304 | tf_op jit(solution)/shard_map/all_to_all | solution.py:680
  13.2 9.5 %copy-start.10 = (bf16[3,3,3,32,32]{4,3,2,1,0:T(8,128)(2,1)S(1)}, bf16[3,3,3,32,32]{4,3,2,1,0:T(8,128)(2,1)}, u32[]{:S(2)}) copy-start(bf16[3,3,3,32,32]{4,3,2,1,0:T(8,128)(2,1)} %param.21) | copy-start | bytes 165892
  13.9 54.1 %collective-permute-start = (bf16[3,128,128]{2,1,0:T(8,128)(2,1)}, bf16[3,128,128]{2,1,0:T(8,128)(2,1)}, u32[]{:S(2)}, u32[]{:S(2)}) collective-permute-start(bf16[3,128,128]{2,1,0:T(8,128)(2,1)} %get-tuple-element.16), channel_id=1, source_target_pairs={{0,1},{1,2},{2,3},{3,4},{4,5},{5,6},{6,7},{7,8},{8,9},{9,10},{10,1... | collective-permute-start | bytes 294920 | tf_op jit(solution)/shard_map/ppermute | solution.py:28
  18.1 49.8 %collective-permute-start.1 = (bf16[3,128,128]{2,1,0:T(8,128)(2,1)}, bf16[3,128,128]{2,1,0:T(8,128)(2,1)}, u32[]{:S(2)}, u32[]{:S(2)}) collective-permute-start(bf16[3,128,128]{2,1,0:T(8,128)(2,1)} %get-tuple-element.17), channel_id=1, source_target_pairs={{1,0},{2,1},{3,2},{4,3},{5,4},{6,5},{7,6},{8,7},{9,8},{10,9},{11,1... | collective-permute-start | bytes 294920 | tf_op jit(solution)/shard_map/ppermute | solution.py:29
  22.8 1.7 copy-start.14
  22.9 1.8 copy-start.15
  22.9 1.9 copy-start.16
  40.2 4.1 %copy-start.8 = (bf16[32,1152]{1,0:T(8,128)(2,1)S(1)}, bf16[32,1152]{1,0:T(8,128)(2,1)}, u32[]{:S(2)}) copy-start(bf16[32,1152]{1,0:T(8,128)(2,1)} %broadcast_in_dim.206) | copy-start | bytes 221188
  64.2 53.6 %all-to-all-start.1 = ((bf16[32,2,2,32,256]{4,3,2,1,0:T(8,128)(2,1)}), bf16[32,2,2,32,256]{4,3,2,1,0:T(8,128)(2,1)}, u32[]{:S(2)}, u32[]{:S(2)}) async-start(bf16[32,2,2,32,256]{4,3,2,1,0:T(8,128)(2,1)} %copy.35), calls=%async_computation.1 | async-start | bytes 4194304 | tf_op jit(solution)/shard_map/all_to_all | solution.py:680
  67.9 2.4 %copy-start = (bf16[64,32,1152]{2,1,0:T(8,128)(2,1)S(1)}, bf16[64,32,1152]{2,1,0:T(8,128)(2,1)}, u32[]{:S(2)}) copy-start(bf16[64,32,1152]{2,1,0:T(8,128)(2,1)} %select_select_fusion) | copy-start | bytes 14155780
  69.1 1.6 copy-start.2
  70.7 2.3 %copy-start.1 = (bf16[18,64,2048]{2,1,0:T(8,128)(2,1)S(1)}, bf16[18,64,2048]{2,1,0:T(8,128)(2,1)}, u32[]{:S(2)}) copy-start(bf16[18,64,2048]{2,1,0:T(8,128)(2,1)} %select_select_fusion.1) | copy-start | bytes 14155780
  73.0 50.6 %copy-start.9 = (bf16[128,256]{1,0:T(8,128)(2,1)S(1)}, bf16[128,256]{1,0:T(8,128)(2,1)}, u32[]{:S(2)}) copy-start(bf16[128,256]{1,0:T(8,128)(2,1)} %all_gather.3) | copy-start | bytes 196612
  117.8 21.9 %all-to-all-start.2 = ((f32[32,2,2,8,128]{4,3,2,1,0:T(8,128)}), f32[32,2,2,8,128]{4,3,2,1,0:T(8,128)S(1)}, u32[]{:S(2)}, u32[]{:S(2)}) async-start(f32[32,2,2,8,128]{4,3,2,1,0:T(8,128)} %denoise.1.denoised_ref), calls=%async_computation.2 | async-start | bytes 1048576 | tf_op jit(solution)/shard_map/all_to_all | solution.py:680
  123.8 1.3 copy-start.3
  125.1 17.3 %copy-start.4 = (bf16[256,512]{1,0:T(8,128)(2,1)S(1)}, bf16[256,512]{1,0:T(8,128)(2,1)}, u32[]{:S(2)}) copy-start(bf16[256,512]{1,0:T(8,128)(2,1)} %constant.70.clone.refs_1_) | copy-start | bytes 786436
  125.1 17.3 %copy-start.5 = (bf16[512,256]{1,0:T(8,128)(2,1)S(1)}, bf16[512,256]{1,0:T(8,128)(2,1)}, u32[]{:S(2)}) copy-start(bf16[512,256]{1,0:T(8,128)(2,1)} %constant.71.clone.refs_2_) | copy-start | bytes 786436
  125.1 17.3 %copy-start.6 = (f32[2,128,128]{2,1,0:T(8,128)S(1)}, f32[2,128,128]{2,1,0:T(8,128)}, u32[]{:S(2)}) copy-start(f32[2,128,128]{2,1,0:T(8,128)} %constant.72.clone.refs_3_) | copy-start | bytes 393220
  139.8 20.0 %all-to-all-start.3 = ((f32[32,2,2,8,128]{4,3,2,1,0:T(8,128)}), f32[32,2,2,8,128]{4,3,2,1,0:T(8,128)S(1)}, u32[]{:S(2)}, u32[]{:S(2)}) async-start(f32[32,2,2,8,128]{4,3,2,1,0:T(8,128)} %adjoint.1.adjoint_ref), calls=%async_computation.3 | async-start | bytes 1048576 | tf_op jit(solution)/shard_map/all_to_all | solution.py:680

commit v14 on v13

--- a/solution.py
+++ b/solution.py
@@ -625,6 +625,7 @@
 def pack_kernel(maps_ref, prior_ref, order_ref, out_ref, features_ref, rows_ref):
     rows, planes, width = maps_ref.shape[1:]
     parts, held = out_ref.shape[:2]
+    chunk = pl.ds(pl.multiple_of(pl.program_id(0) * rows, rows), rows)
     for row in range(0, rows, 2):
         moved = lax.dot_general(
             order_ref[...],
@@ -638,7 +639,7 @@
     for part in range(parts):
         for inner in range(held):
             place = (part * held + inner) * rows
-            out_ref[part, inner] = rows_ref[place : place + rows].astype(out_ref.dtype)
+            out_ref[part, inner, chunk, :] = rows_ref[place : place + rows].astype(out_ref.dtype)
     features_ref[...] = prior_ref[...].astype(features_ref.dtype)
 
 
@@ -660,7 +661,7 @@
             pl.BlockSpec(order.shape, lambda g: (0, 0)),
         ],
         out_specs=[
-            pl.BlockSpec((parts, held, chunk, planes), lambda g: (0, 0, g, 0)),
+            pl.BlockSpec((parts, held, slab_rows, planes), lambda g: (0, 0, 0, 0)),
             prior_spec,
         ],
         out_shape=[

time: 199 us -> 199 us (level)
  no operation moved by 1% of the time
where the time goes in v14:
time: 199 us; the launch traced here: 198 us
  Pallas kernels  76.8 us (39%)
  blocking collectives  45.2 us (23%)
  starting transfers between devices  25 us (13%)
  waiting for transfers between devices  23.3 us (12%)
  local copies, waits for them, and re-layouts  16 us (8%)
  other arithmetic  11 us (6%)
    pallas_call x1, Pallas kernels, denoise(): pl.pallas_call(functools.partial(denoise_kernel, group), in_specs=[pl.Blo...  44.8 us
    all_to_all x1, blocking collectives, exchange(): return lax.all_to_all(blocks, axis, split_axis=0, concat_axis=0, tiled=True)  36 us
    pallas_call x2, Pallas kernels, product_call(): pl.pallas_call(kernel, grid=(x_count, coils // held_coils(coils)), in_spe...  24.3 us
    all_to_all x4, waiting for transfers between devices, exchange(): return lax.all_to_all(blocks, axis, split_axis=0, concat_axis=0, tiled=True)  23.3 us
    all_to_all x4, starting transfers between devices, exchange(): return lax.all_to_all(blocks, axis, split_axis=0, concat_axis=0, tiled=True)  19.5 us
    all_gather x1, blocking collectives, body(): lax.all_gather(sampling.astype(jnp.bfloat16), 'slab', axis=0, tiled=True)  9.16 us
    select_n x3, other arithmetic, banded(): result = jnp.where(inner - outer + offset == tap, tiles[tap], result)  8.95 us
    unnamed x35, local copies, waits for them, and re-layouts  8.18 us
  transfers between devices with their start and end apart: 6, of which 2 were waited for; matrix products, arithmetic and copies ran while one was open for 11% of the time, Pallas kernels for 35%

profile of v14, /device:TPU:0, one launch (start us, length us, event | category | flops | bytes accessed | tf_op | source)
XLA Modules:
  0.0 198.5 jit_solution(10346254398597990484)
XLA Ops:
  0.6 5.3 %pack.1 = (bf16[32,4,64,128]{3,2,1,0:T(8,128)(2,1)}, bf16[8,128,128]{2,1,0:T(8,128)(2,1)}) custom-call(bf16[1,64,128,128]{3,2,1,0:T(8,128)(2,1)} %maps_ref.1, f32[8,128,128]{2,1,0:T(8,128)} %prior_ref.3, bf16[128,128]{1,0:T(8,128)(2,1)} %constant.69.clone.order_ref), custom_call_target="tpu_custom_call" | custom-call | flops 268435456 | bytes 5242880 | tf_op jit(solution)/shard_map/pack/pallas_call | solution.py:655
  5.9 7.4 %all-to-all-start = ((bf16[32,4,64,128]{3,2,1,0:T(8,128)(2,1)}), bf16[32,4,64,128]{3,2,1,0:T(8,128)(2,1)}, u32[]{:S(2)}, u32[]{:S(2)}) async-start(bf16[32,4,64,128]{3,2,1,0:T(8,128)(2,1)} %get-tuple-element.8), calls=%async_computation | async-start | bytes 4194304 | tf_op jit(solution)/shard_map/all_to_all | solution.py:681
  14.1 4.2 %collective-permute-start = (bf16[3,128,128]{2,1,0:T(8,128)(2,1)}, bf16[3,128,128]{2,1,0:T(8,128)(2,1)}, u32[]{:S(2)}, u32[]{:S(2)}) collective-permute-start(bf16[3,128,128]{2,1,0:T(8,128)(2,1)} %get-tuple-element.16), channel_id=1, source_target_pairs={{0,1},{1,2},{2,3},{3,4},{4,5},{5,6},{6,7},{7,8},{8,9},{9,10},{10,1... | collective-permute-start | bytes 294920 | tf_op jit(solution)/shard_map/ppermute | solution.py:28
  18.3 1.3 collective-permute-start.1
  22.0 0.8 broadcast_in_dim.206
  25.1 3.4 %copy.34 = bf16[1,32,256,128]{2,1,3,0:T(8,128)(2,1)S(1)} copy(bf16[1,32,256,128]{3,2,1,0:T(8,128)(2,1)} %param.17) | data formatting | bytes 4194304 | tf_op args[2]
  28.6 1.6 copy.35
  30.1 9.2 %all_gather.3 = bf16[128,256]{1,0:T(8,128)(2,1)} all-gather(bf16[32,256]{1,0:T(8,128)(2,1)S(1)} %convert_element_type.8), channel_id=1, replica_groups=mesh['slab'=4,'coil'=8] {'slab'}, dimensions={0}, use_global_device_ids=true | all-gather | bytes 81920 | tf_op jit(solution)/shard_map/all_gather | solution.py:782
  40.4 4.1 %select_select_fusion.1 = bf16[18,64,2048]{2,1,0:T(8,128)(2,1)} fusion(pred[64,2048]{1,0:T(8,128)(4,1)S(1)} %get-tuple-element.31, pred[64,2048]{1,0:T(8,128)(4,1)S(1)} %get-tuple-element.32, pred[64,2048]{1,0:T(8,128)(4,1)S(1)} %get-tuple-element.30, bf16[18,2048]{1,0:T(8,128)(2,1)S(1)} %broadcast_in_dim.180, bf16[18,2048]{1,0:T(8,128)(2,1)S(1)} %broadcast_in_dim.176, ...), kind=kLoop, calls=%fused_computation.1 | loop fusion | flops 7077888 | bytes 5332992 | tf_op jit(solution)/shard_map/jit(_where)/select_n | solution.py:162
  44.5 4.2 %select_select_fusion = bf16[64,32,1152]{2,1,0:T(8,128)(2,1)} fusion(pred[64,1152]{1,0:T(8,128)(4,1)S(1)} %get-tuple-element.28, pred[64,1152]{1,0:T(8,128)(4,1)S(1)} %get-tuple-element.29, pred[64,1152]{1,0:T(8,128)(4,1)S(1)} %get-tuple-element.27, bf16[32,1152]{1,0:T(8,128)(2,1)S(1)} %copy-done.8, bf16[32,1152]{1,0:T(8,128)(2,1)S(1)} %broadcast_in_dim.202, ...), kind=kLoop, calls=%fused_computation | loop fusion | flops 7077888 | bytes 5160960 | tf_op jit(solution)/shard_map/jit(_where)/select_n | solution.py:162
  48.8 15.6 %all-to-all-done = bf16[32,4,64,128]{3,2,1,0:T(8,128)(2,1)} async-done(((bf16[32,4,64,128]{3,2,1,0:T(8,128)(2,1)}), bf16[32,4,64,128]{3,2,1,0:T(8,128)(2,1)}, u32[]{:S(2)}, u32[]{:S(2)}) %all-to-all-start) | async-done | bytes 2097184 | tf_op jit(solution)/shard_map/all_to_all | solution.py:681
  64.5 3.7 %all-to-all-start.1 = ((bf16[32,2,2,32,256]{4,3,2,1,0:T(8,128)(2,1)}), bf16[32,2,2,32,256]{4,3,2,1,0:T(8,128)(2,1)}, u32[]{:S(2)}, u32[]{:S(2)}) async-start(bf16[32,2,2,32,256]{4,3,2,1,0:T(8,128)(2,1)} %copy.35), calls=%async_computation.1 | async-start | bytes 4194304 | tf_op jit(solution)/shard_map/all_to_all | solution.py:681
  68.2 1.1 pad_maximum_fusion
  69.9 0.7 copy-done
  70.9 2.3 %copy-done.1 = bf16[18,64,2048]{2,1,0:T(8,128)(2,1)S(1)} copy-done((bf16[18,64,2048]{2,1,0:T(8,128)(2,1)S(1)}, bf16[18,64,2048]{2,1,0:T(8,128)(2,1)}, u32[]{:S(2)}) %copy-start.1) | copy-done | bytes 4718616
  73.3 44.8 %denoise.1.denoised_ref = f32[32,2,2,8,128]{4,3,2,1,0:T(8,128)} custom-call(s32[2]{0:T(128)S(1)} %pad_add_fusion.first_ref, bf16[14,128,384]{2,1,0:T(8,128)(2,1)S(1)} %fusion.2.features_ref, f32[8,128,128]{2,1,0:T(8,128)S(1)} %copy-done.2, bf16[1152,2048]{1,0:T(8,128)(2,1)S(1)} %bitcast.39, f32[1,2048]{1,0:T(1,128)S(1)} %broadcast_in_dim_tile.8.bias_first_ref, ...), custom_call_target="tpu_custom_call" | custom-call | flops 37446746112 | bytes 16777216 | tf_op jit(solution)/shard_map/denoise/pallas_call | solution.py:236
  118.0 5.8 %all-to-all-start.2 = ((f32[32,2,2,8,128]{4,3,2,1,0:T(8,128)}), f32[32,2,2,8,128]{4,3,2,1,0:T(8,128)S(1)}, u32[]{:S(2)}, u32[]{:S(2)}) async-start(f32[32,2,2,8,128]{4,3,2,1,0:T(8,128)} %denoise.1.denoised_ref), calls=%async_computation.2 | async-start | bytes 1048576 | tf_op jit(solution)/shard_map/all_to_all | solution.py:681
  124.0 1.3 copy-done.3
  125.3 7.0 %adjoint.1.adjoint_ref = f32[32,2,2,8,128]{4,3,2,1,0:T(8,128)} custom-call(bf16[4,8,4,32,256]{4,3,2,1,0:T(8,128)(2,1)} %bitcast.3.spectra_real_ref.spectra_imag_ref, bf16[4,8,4,32,256]{4,3,2,1,0:T(8,128)(2,1)} %bitcast.3.spectra_real_ref.spectra_imag_ref, bf16[4,8,4,64,128]{4,3,2,1,0:T(8,128)(2,1)} %bitcast.maps_real_ref.maps_imag_ref, ...), custom_call_target="tpu_custom_call" | custom-call | flops 4831838208 | bytes 8388608 | tf_op jit(solution)/shard_map/adjoint/pallas_call | solution.py:583
  132.3 7.7 %all-to-all-done.2.denoised_ref = f32[32,2,2,8,128]{4,3,2,1,0:T(8,128)S(1)} async-done(((f32[32,2,2,8,128]{4,3,2,1,0:T(8,128)}), f32[32,2,2,8,128]{4,3,2,1,0:T(8,128)S(1)}, u32[]{:S(2)}, u32[]{:S(2)}) %all-to-all-start.2) | async-done | bytes 524320 | tf_op jit(solution)/shard_map/all_to_all | solution.py:681
  140.0 2.6 %all-to-all-start.3 = ((f32[32,2,2,8,128]{4,3,2,1,0:T(8,128)}), f32[32,2,2,8,128]{4,3,2,1,0:T(8,128)S(1)}, u32[]{:S(2)}, u32[]{:S(2)}) async-start(f32[32,2,2,8,128]{4,3,2,1,0:T(8,128)} %adjoint.1.adjoint_ref), calls=%async_computation.3 | async-start | bytes 1048576 | tf_op jit(solution)/shard_map/all_to_all | solution.py:681
  142.6 17.3 %products.1 = f32[32,9,8,128]{3,2,1,0:T(8,128)S(1)} custom-call(bf16[4,8,4,64,128]{4,3,2,1,0:T(8,128)(2,1)} %bitcast.maps_real_ref.maps_imag_ref, bf16[4,8,4,64,128]{4,3,2,1,0:T(8,128)(2,1)} %bitcast.maps_real_ref.maps_imag_ref, f32[32,2,2,8,128]{4,3,2,1,0:T(8,128)} %adjoint.1.adjoint_ref, f32[32,2,2,8,128]{4,3,2,1,0:T(8,128)S(1)} %all-to-all-done.2.denoised_ref, ...), custom_call_target="tpu_custom_call" | custom-call | flops 19327352832 | bytes 8388608 | tf_op jit(solution)/shard_map/products/pallas_call | solution.py:583
  159.9 36.0 %all_to_all.25.moved_ref = f32[32,9,8,128]{3,2,1,0:T(8,128)S(1)} all-to-all(f32[32,9,8,128]{3,2,1,0:T(8,128)S(1)} %products.1), channel_id=1, replica_groups=mesh['slab'=4,'coil'=8] {'slab','coil'}, dimensions={0} | all-to-all | bytes 2359296 | tf_op jit(solution)/shard_map/all_to_all | solution.py:681
  196.0 2.5 %finish.1 = (f32[8,128,128]{2,1,0:T(8,128)}, f32[8,128,128]{2,1,0:T(8,128)}) custom-call(f32[32,2,2,8,128]{4,3,2,1,0:T(8,128)S(1)} %all-to-all-done.3.adjoint_ref, f32[32,2,2,8,128]{4,3,2,1,0:T(8,128)} %denoise.1.denoised_ref, f32[32,9,8,128]{3,2,1,0:T(8,128)S(1)} %all_to_all.25.moved_ref), custom_call_target="tpu_custom_call" | custom-call | flops 1048576 | bytes 3145728 | tf_op jit(solution)/shard_map/finish/pallas_call | solution.py:741
  (91 shorter events, 7.4 us)
Async XLA Ops:
  5.9 7.5 %copy-start.7 = (bf16[8,128,128]{2,1,0:T(8,128)(2,1)S(1)}, bf16[8,128,128]{2,1,0:T(8,128)(2,1)}, u32[]{:S(2)}) copy-start(bf16[8,128,128]{2,1,0:T(8,128)(2,1)} %get-tuple-element.9) | copy-start | bytes 786436
  5.9 13.7 %copy-start.11 = (s32[32,256]{1,0:T(8,128)S(1)}, s32[32,256]{1,0:T(8,128)}, u32[]{:S(2)}) copy-start(s32[32,256]{1,0:T(8,128)} %param.18) | copy-start | bytes 98308
  5.9 13.7 %copy-start.12 = (bf16[3,3,3,32,2]{3,4,2,1,0:T(2,128)(2,1)S(1)}, bf16[3,3,3,32,2]{3,4,2,1,0:T(2,128)(2,1)}, u32[]{:S(2)}) copy-start(bf16[3,3,3,32,2]{3,4,2,1,0:T(2,128)(2,1)} %param.19) | copy-start | bytes 10372
  5.9 14.9 %copy-start.13 = (bf16[3,3,3,2,32]{4,3,2,1,0:T(2,128)(2,1)S(1)}, bf16[3,3,3,2,32]{4,3,2,1,0:T(2,128)(2,1)}, u32[]{:S(2)}) copy-start(bf16[3,3,3,2,32]{4,3,2,1,0:T(2,128)(2,1)} %param.23) | copy-start | bytes 10372
  5.9 58.5 %all-to-all-start = ((bf16[32,4,64,128]{3,2,1,0:T(8,128)(2,1)}), bf16[32,4,64,128]{3,2,1,0:T(8,128)(2,1)}, u32[]{:S(2)}, u32[]{:S(2)}) async-start(bf16[32,4,64,128]{3,2,1,0:T(8,128)(2,1)} %get-tuple-element.8), calls=%async_computation | async-start | bytes 4194304 | tf_op jit(solution)/shard_map/all_to_all | solution.py:681
  13.4 9.5 %copy-start.10 = (bf16[3,3,3,32,32]{4,3,2,1,0:T(8,128)(2,1)S(1)}, bf16[3,3,3,32,32]{4,3,2,1,0:T(8,128)(2,1)}, u32[]{:S(2)}) copy-start(bf16[3,3,3,32,32]{4,3,2,1,0:T(8,128)(2,1)} %param.21) | copy-start | bytes 165892
  14.1 54.1 %collective-permute-start = (bf16[3,128,128]{2,1,0:T(8,128)(2,1)}, bf16[3,128,128]{2,1,0:T(8,128)(2,1)}, u32[]{:S(2)}, u32[]{:S(2)}) collective-permute-start(bf16[3,128,128]{2,1,0:T(8,128)(2,1)} %get-tuple-element.16), channel_id=1, source_target_pairs={{0,1},{1,2},{2,3},{3,4},{4,5},{5,6},{6,7},{7,8},{8,9},{9,10},{10,1... | collective-permute-start | bytes 294920 | tf_op jit(solution)/shard_map/ppermute | solution.py:28
  18.3 49.8 %collective-permute-start.1 = (bf16[3,128,128]{2,1,0:T(8,128)(2,1)}, bf16[3,128,128]{2,1,0:T(8,128)(2,1)}, u32[]{:S(2)}, u32[]{:S(2)}) collective-permute-start(bf16[3,128,128]{2,1,0:T(8,128)(2,1)} %get-tuple-element.17), channel_id=1, source_target_pairs={{1,0},{2,1},{3,2},{4,3},{5,4},{6,5},{7,6},{8,7},{9,8},{10,9},{11,1... | collective-permute-start | bytes 294920 | tf_op jit(solution)/shard_map/ppermute | solution.py:29
  23.1 1.7 copy-start.14
  23.1 1.8 copy-start.15
  23.1 1.9 copy-start.16
  40.4 4.1 %copy-start.8 = (bf16[32,1152]{1,0:T(8,128)(2,1)S(1)}, bf16[32,1152]{1,0:T(8,128)(2,1)}, u32[]{:S(2)}) copy-start(bf16[32,1152]{1,0:T(8,128)(2,1)} %broadcast_in_dim.206) | copy-start | bytes 221188
  64.5 53.6 %all-to-all-start.1 = ((bf16[32,2,2,32,256]{4,3,2,1,0:T(8,128)(2,1)}), bf16[32,2,2,32,256]{4,3,2,1,0:T(8,128)(2,1)}, u32[]{:S(2)}, u32[]{:S(2)}) async-start(bf16[32,2,2,32,256]{4,3,2,1,0:T(8,128)(2,1)} %copy.35), calls=%async_computation.1 | async-start | bytes 4194304 | tf_op jit(solution)/shard_map/all_to_all | solution.py:681
  68.1 2.4 %copy-start = (bf16[64,32,1152]{2,1,0:T(8,128)(2,1)S(1)}, bf16[64,32,1152]{2,1,0:T(8,128)(2,1)}, u32[]{:S(2)}) copy-start(bf16[64,32,1152]{2,1,0:T(8,128)(2,1)} %select_select_fusion) | copy-start | bytes 14155780
  69.3 1.6 copy-start.2
  70.9 2.3 %copy-start.1 = (bf16[18,64,2048]{2,1,0:T(8,128)(2,1)S(1)}, bf16[18,64,2048]{2,1,0:T(8,128)(2,1)}, u32[]{:S(2)}) copy-start(bf16[18,64,2048]{2,1,0:T(8,128)(2,1)} %select_select_fusion.1) | copy-start | bytes 14155780
  73.3 50.6 %copy-start.9 = (bf16[128,256]{1,0:T(8,128)(2,1)S(1)}, bf16[128,256]{1,0:T(8,128)(2,1)}, u32[]{:S(2)}) copy-start(bf16[128,256]{1,0:T(8,128)(2,1)} %all_gather.3) | copy-start | bytes 196612
  118.0 21.9 %all-to-all-start.2 = ((f32[32,2,2,8,128]{4,3,2,1,0:T(8,128)}), f32[32,2,2,8,128]{4,3,2,1,0:T(8,128)S(1)}, u32[]{:S(2)}, u32[]{:S(2)}) async-start(f32[32,2,2,8,128]{4,3,2,1,0:T(8,128)} %denoise.1.denoised_ref), calls=%async_computation.2 | async-start | bytes 1048576 | tf_op jit(solution)/shard_map/all_to_all | solution.py:681
  124.0 1.3 copy-start.3
  125.3 17.3 %copy-start.4 = (bf16[256,512]{1,0:T(8,128)(2,1)S(1)}, bf16[256,512]{1,0:T(8,128)(2,1)}, u32[]{:S(2)}) copy-start(bf16[256,512]{1,0:T(8,128)(2,1)} %constant.70.clone.refs_1_) | copy-start | bytes 786436
  125.3 17.3 %copy-start.5 = (bf16[512,256]{1,0:T(8,128)(2,1)S(1)}, bf16[512,256]{1,0:T(8,128)(2,1)}, u32[]{:S(2)}) copy-start(bf16[512,256]{1,0:T(8,128)(2,1)} %constant.71.clone.refs_2_) | copy-start | bytes 786436
  125.3 17.3 %copy-start.6 = (f32[2,128,128]{2,1,0:T(8,128)S(1)}, f32[2,128,128]{2,1,0:T(8,128)}, u32[]{:S(2)}) copy-start(f32[2,128,128]{2,1,0:T(8,128)} %constant.72.clone.refs_3_) | copy-start | bytes 393220
  140.0 20.0 %all-to-all-start.3 = ((f32[32,2,2,8,128]{4,3,2,1,0:T(8,128)}), f32[32,2,2,8,128]{4,3,2,1,0:T(8,128)S(1)}, u32[]{:S(2)}, u32[]{:S(2)}) async-start(f32[32,2,2,8,128]{4,3,2,1,0:T(8,128)} %adjoint.1.adjoint_ref), calls=%async_computation.3 | async-start | bytes 1048576 | tf_op jit(solution)/shard_map/all_to_all | solution.py:681
